TPU v7x, 32 devices: a whole 2x2x4 slice. The times are simulated.
32 devices in a mesh: section: 2 (over core), seq: 4 (over z), wshard: 4 (over y, x).
Axes of the slice: x: 2, y: 2, z: 4, core: 2. Of those that a mesh axis runs over, the one named last changes fastest.
Arguments:
- layer_input: bfloat16 [2, 8192, 1024], P(None, ('wshard', 'seq')), may hold values from -6 to 6
- out_grad: bfloat16 [2, 8192, 1024], P(None, ('wshard', 'seq')), may hold values from -6 to 6
- doc_index: int32 [2, 8192], P(None, ('wshard', 'seq')), may hold values from 0 to 7, as said below
- doc_adapter: int32 [2, 4, 16], P(None, 'wshard'), may hold values from 0 to 7
- in_weight: bfloat16 [2, 1024, 4384], P('section', 'wshard'), may hold values from -0.1875 to 0.1875
- out_weight: bfloat16 [2, 2048, 1024], P('section', 'wshard'), may hold values from -0.125 to 0.125
- norm_gain: float32 [2, 1024], P('section'), may hold values from 0.5 to 1.5
- conv_weight: float32 [2, 4, 2304], P('section'), may hold values from -3 to 3
- conv_bias: float32 [2, 2304], P('section'), may hold values from -1.5 to 1.5
- dt_bias: float32 [2, 32], P('section'), may hold values from -11 to -3
- a_log: float32 [2, 32], P('section'), may hold values from 0 to 2.77
- skip_gain: float32 [2, 32], P('section'), may hold values from 0.5 to 1.5
- gate_gain: float32 [2, 2048], P('section'), may hold values from 0.5 to 1.5
- in_down: bfloat16 [2, 1024, 128], P('section'), may hold values from -0.1875 to 0.1875
- in_up: bfloat16 [2, 128, 4384], P('section'), may hold values from -0.75 to 0.75
- out_down: bfloat16 [2, 2048, 128], P('section'), may hold values from -0.125 to 0.125
- out_up: bfloat16 [2, 128, 1024], P('section'), may hold values from -0.75 to 0.75
Outputs:
- section_out: bfloat16 [2, 2, 8192, 1024], P('section', None, ('wshard', 'seq'))
- input_grad: bfloat16 [2, 2, 8192, 1024], P('section', None, ('wshard', 'seq'))
- in_down_grad: float32 [2, 1024, 128], P('section')
- in_up_grad: float32 [2, 128, 4384], P('section')
- out_down_grad: float32 [2, 2048, 128], P('section')
- out_up_grad: float32 [2, 128, 1024], P('section')
Inputs may be any that keep to these rules, and one draw needn't show every extreme that they name: `doc_index`: within each aligned block of 2048 tokens the numbers start at 0, never fall, and rise by one exactly once inside each eighth of the block after the first, so that each block holds 8 documents.
All inputs are finite; a program needn't handle non-finite values.
Results may differ from a plain program's by a relative error of at most 0.018.
Values may be sent and summed in bfloat16 or wider, within the bound.
No kernel may reach another device: no remote copies, remote signals or barrier semaphores. Data moves between devices by JAX's collectives and lax.ppermute only.
A program may use at most 256 MiB of HBM per device.

v0:
```python
import functools

import jax
import jax.numpy as jnp
from jax import lax
from jax.experimental import pallas as pl
from jax.experimental.pallas import tpu as pltpu
from jax.sharding import PartitionSpec as P

SPAN = 256
RANK = 16
LANES = 128
DOCS_PER_BLOCK = 8
EPSILON = 1e-05
EXACT = lax.Precision.HIGHEST
BF16 = jnp.bfloat16
F32 = jnp.float32
PARAMS = pltpu.CompilerParams(vmem_limit_bytes=56 * 1024 * 1024)


def from_behind(value, axis, steps):
    count = lax.axis_size(axis)
    initial, last = (max(0, -steps), min(count, count - steps))
    return lax.ppermute(value, axis, [(source, source + steps) for source in range(initial, last)])


def dot(left, right):
    return jnp.dot(left, right, preferred_element_type=F32)


def dot_last(left, right):
    return lax.dot_general(left, right, (((1,), (1,)), ((), ())), preferred_element_type=F32)


def dot_first(left, right):
    return lax.dot_general(left, right, (((0,), (0,)), ((), ())), preferred_element_type=F32)


def rms_rate(values):
    return lax.rsqrt(jnp.mean(values * values, axis=-1, keepdims=True) + EPSILON)


def sigmoid(v):
    return 1.0 / (1.0 + jnp.exp(-v))


def lower_ones(shape):
    rows = lax.broadcasted_iota(jnp.int32, shape, 0)
    columns = lax.broadcasted_iota(jnp.int32, shape, 1)
    return rows <= columns


def conv_rows(rows, rim, weight, offset, valid):
    length = rows.shape[0]
    extended = jnp.concatenate([rim, rows], axis=0)
    taps = weight.shape[0]
    total = offset + weight[taps - 1 : taps] * rows
    for back in range(1, taps):
        shifted = extended[8 - back : 8 - back + length]
        total = total + jnp.where(valid >= back, shifted, 0.0) * weight[taps - 1 - back : taps - back]
    gate = sigmoid(total)
    active = total * gate
    return active, gate + active * (1.0 - gate)


def conv_kernel(
    spans, head, heads, state,
    mixed_ref, mixed_bc_ref, rim_ref, rim_bc_ref, weight_ref, weight_bc_ref, offset_ref, offset_bc_ref,
    valid_ref, raw_ref, bias_ref, rate_ref, token_ref,
    values_ref, slope_ref, bc_ref, slope_bc_ref, state_ref, step_ref, decay_ref, sig_ref, tail_ref,
):
    group = pl.program_id(0)
    valid = valid_ref[:, :1]
    heads_here = mixed_ref.shape[1] // head

    @pl.when(group == 0)
    def _():
        active, slope = conv_rows(
            mixed_bc_ref[...].astype(F32), rim_bc_ref[...].astype(F32), weight_bc_ref[...], offset_bc_ref[...], valid
        )
        bc_ref[...] = active.astype(BF16)
        slope_bc_ref[...] = slope.astype(BF16)
        raw = (raw_ref[...].astype(F32) + bias_ref[...]).T[:heads]
        step = (jnp.maximum(raw, 0.0) + jnp.log1p(jnp.exp(-jnp.abs(raw)))).astype(BF16).astype(F32)
        step_ref[...] = step
        sig_ref[...] = sigmoid(raw)
        drop = -(step * rate_ref[:, :1])
        ones = lower_ones((SPAN, SPAN)).astype(F32)
        for span in range(spans):
            here = slice(span * SPAN, (span + 1) * SPAN)
            decay = jnp.dot(drop[:, here], ones, precision=EXACT, preferred_element_type=F32)
            decay_ref[:, here] = decay
            tail = jnp.exp(decay[:, SPAN - 1 :] - decay) * token_ref[span][1:2]
            tail_ref[:, here] = tail * step[:, here]

    active, slope = conv_rows(
        mixed_ref[...].astype(F32), rim_ref[...].astype(F32), weight_ref[...], offset_ref[...], valid
    )
    slope_ref[...] = slope.astype(BF16)
    turned = active.T
    low = turned.astype(BF16)
    values_ref[...] = low
    low = low.astype(F32)
    first = pl.multiple_of(group * heads_here, heads_here)
    tail_rows = tail_ref[pl.ds(first, heads_here), :]
    for span in range(spans):
        here = slice(span * SPAN, (span + 1) * SPAN)
        driven = jnp.concatenate(
            [
                (low[place * head : (place + 1) * head, here] * tail_rows[place : place + 1, here]).astype(BF16)
                for place in range(heads_here)
            ],
            axis=0,
        )
        state_ref[span] = dot(driven, bc_ref[here, :state]).astype(BF16)


def scan_kernel(
    head, state,
    values_ref, bc_ref, step_ref, decay_ref, token_ref, doc_column_ref, doc_row_ref, state_ref, skip_ref, gate_ref,
    gain_ref, *rest,
):
    mixed_ref, normed_ref, score_ref, scanned_ref = rest[-4:]
    group, groups = pl.program_id(0), pl.num_programs(0)
    width = values_ref.shape[0]
    heads_here = width // head

    @pl.when(group == 0)
    def _():
        score = dot_last(bc_ref[:, :state], bc_ref[:, state:])
        same = (doc_column_ref[:, :1] == doc_row_ref[:1]) & lower_ones((SPAN, SPAN))
        score_ref[...] = jnp.where(same, score, 0.0)

    decay, step = decay_ref[...], step_ref[...]
    carry = jnp.exp(decay) * token_ref[0][:1]
    columns = jnp.concatenate([decay] * (LANES // heads_here), axis=0).T
    out_map = bc_ref[:, state:]
    parts = []
    for place in range(heads_here):
        rows = slice(place * head, (place + 1) * head)
        one = slice(place, place + 1)
        kernel = (jnp.exp(jnp.minimum(decay[one] - columns[:, one], 0.0)) * score_ref[...]).astype(BF16)
        values = values_ref[rows].astype(F32)
        driven = (values * step[one]).astype(BF16)
        before = dot_last(state_ref[rows], out_map) * carry[one]
        parts.append(dot(driven, kernel) + before + skip_ref[one, :1] * values)
    turned = jnp.concatenate(parts, axis=0).T
    scanned_ref[:, pl.ds(pl.multiple_of(group * width, width), width)] = turned.astype(BF16)

    @pl.when(group == groups - 1)
    def _():
        def rows_at(index, _):
            rows = pl.ds(pl.multiple_of(index * 16, 16), 16)
            mixed = scanned_ref[rows, :]
            mixed_ref[rows, :] = mixed
            gate = gate_ref[rows, :].astype(F32)
            gated = mixed.astype(F32) * (gate * sigmoid(gate))
            normed_ref[rows, :] = (gated * rms_rate(gated) * gain_ref[...]).astype(BF16)
            return 0

        lax.fori_loop(0, SPAN // 16, rows_at, 0)


def out_back_kernel(
    head, heads, state,
    up_ref, lane_ref, up_out_ref, down_out_ref, first_ref, second_ref, third_ref, near_ref, far_ref, where_ref,
    mixed_ref, gate_ref, gain_ref, decay_ref, token_ref, bc_ref,
    project_ref, turned_ref, state_ref, narrow_ref, grad_ref, grad_mixed_ref,
):
    width = mixed_ref.shape[1]
    up = up_ref[...]
    narrow = (dot_last(up, up_out_ref[...]) * lane_ref[...]).astype(BF16)
    narrow_ref[...] = narrow
    left = jnp.concatenate([up, narrow], axis=1)
    for offset, part in out_places(where_ref, (first_ref, second_ref, third_ref), near_ref, far_ref):
        here = pl.ds(offset, part.shape[0])
        grad_ref[:, here] = dot_last(left, jnp.concatenate([part[...], down_out_ref[here, :]], axis=1))

    def rows_at(index, _):
        rows = pl.ds(pl.multiple_of(index * 16, 16), 16)
        mixed = mixed_ref[rows, :].astype(F32)
        gate = gate_ref[rows, :].astype(F32)
        share = sigmoid(gate)
        silu = gate * share
        gated = mixed * silu
        grad = grad_ref[rows, :] * gain_ref[...]
        rate = rms_rate(gated)
        pull = jnp.mean(gated * grad, axis=-1, keepdims=True) * rate * rate * rate
        grad_gated = rate * grad - gated * pull
        project_ref[rows, :] = (grad_gated * mixed * (share + silu * (1.0 - share))).astype(BF16)
        grad_mixed_ref[rows, :] = (grad_gated * silu).astype(BF16)
        return 0

    lax.fori_loop(0, SPAN // 16, rows_at, 0)
    carry = jnp.exp(decay_ref[...]) * token_ref[0][:1]
    out_map = bc_ref[:, state:]
    wide = 512
    for first in range(0, width, wide):
        low = grad_mixed_ref[:, first : first + wide].astype(F32).T
        turned_ref[first : first + wide, :] = low.astype(BF16)
        scaled = [
            (low[place * head : (place + 1) * head] * carry[first // head + place : first // head + place + 1]).astype(BF16)
            for place in range(wide // head)
        ]
        state_ref[0, first : first + wide, :] = dot(jnp.concatenate(scaled, axis=0), out_map).astype(BF16)


def aligned(value, unit):
    return pl.multiple_of(value * unit, unit)


def out_places(where_ref, parts, near, far):
    rows, half = parts[0].shape[0], near.shape[0]
    places = [(aligned(where_ref[place], rows), part) for place, part in enumerate(parts)]
    apart = where_ref[3] * 2
    places.append((aligned(apart + where_ref[4], half), near))
    places.append((aligned(apart + 1 - where_ref[4], half), far))
    return places


def in_columns(ref, where_ref, parts):
    columns = ref.shape[1] // parts
    return [ref[:, pl.ds(aligned(where_ref[place], columns), columns)] for place in range(parts)]


def mixed_kernel(
    main, lanes,
    input_ref, gain_ref, down_ref, lane_ref, up_ref, first_ref, second_ref, third_ref, near_ref, far_ref, where_ref,
    normed_ref, narrow_ref, mixed_ref, raw_ref,
):
    rows = input_ref.shape[0]
    inputs = input_ref[...].astype(F32)
    normed = (inputs * rms_rate(inputs) * gain_ref[...]).astype(BF16)
    normed_ref[...] = normed
    narrow = (dot(normed, down_ref[...]) * lane_ref[...]).astype(BF16)
    narrow_ref[...] = narrow
    left = jnp.concatenate(in_columns(normed_ref, where_ref, 4) + [narrow], axis=1)
    first = where_ref[4] == 0
    half, whole_rows = near_ref.shape[0], first_ref.shape[0]
    step = main // 6

    def product(start, size):
        here = slice(start, start + size)
        if start < main // 2:
            there = slice(start, start + size)
            apart = jnp.where(first, near_ref[there], far_ref[there])
        else:
            there = slice(start - whole_rows + half, start - whole_rows + half + size)
            apart = jnp.where(first, far_ref[there], near_ref[there])
        parts = [first_ref[here], second_ref[here], third_ref[here], apart, up_ref[here]]
        return dot_last(left, jnp.concatenate(parts, axis=1))

    for start in range(0, main, step):
        mixed_ref[:, start : start + step] = product(start, step).astype(BF16)
    extra = whole_rows - main
    raw_ref[...] = jnp.concatenate([product(main, extra), jnp.zeros((rows, lanes - extra), F32)], axis=1).astype(BF16)


def gate_kernel(normed_ref, narrow_ref, up_ref, first_ref, second_ref, third_ref, near_ref, far_ref, where_ref, gate_ref):
    tile, tiles = pl.program_id(0), pl.num_programs(0)
    near = (where_ref[4] == 0) == (tile < tiles // 2)
    left = jnp.concatenate(in_columns(normed_ref, where_ref, 4) + [narrow_ref[...]], axis=1)
    apart = jnp.where(near, near_ref[...], far_ref[...])
    right = jnp.concatenate([first_ref[...], second_ref[...], third_ref[...], apart, up_ref[...]], axis=1)
    gate_ref[...] = dot_last(left, right).astype(BF16)


def out_kernel(
    normed_ref, input_ref, down_ref, lane_ref, up_ref, first_ref, second_ref, third_ref, near_ref, far_ref, where_ref,
    narrow_ref, out_ref,
):
    narrow = (dot(normed_ref[...], down_ref[...]) * lane_ref[...]).astype(BF16)
    narrow_ref[...] = narrow
    places = out_places(where_ref, (first_ref, second_ref, third_ref), near_ref, far_ref)
    left = [normed_ref[:, pl.ds(offset, part.shape[0])] for offset, part in places]
    left = jnp.concatenate(left + [narrow], axis=1)
    wide = 256
    for start in range(0, out_ref.shape[1], wide):
        here = slice(start, start + wide)
        right = jnp.concatenate([part[:, here] for _, part in places] + [up_ref[:, here]], axis=0)
        out_ref[:, here] = (input_ref[:, here].astype(F32) + dot(left, right)).astype(BF16)


def gate_in_back_kernel(
    grad_ref, up_ref, first_ref, second_ref, third_ref, near_ref, far_ref, where_ref, out_ref
):
    tile, tiles = pl.program_id(0), pl.num_programs(0)
    near = (where_ref[4] == 0) == (tile < tiles // 2)
    apart = jnp.where(near, near_ref[...], far_ref[...])
    right = jnp.concatenate([first_ref[...], second_ref[...], third_ref[...], apart, up_ref[...]], axis=1)
    product = dot(grad_ref[...], right)

    @pl.when(tile == 0)
    def _():
        out_ref[...] = product

    @pl.when(tile > 0)
    def _():
        out_ref[...] += product


def mixed_in_back_kernel(
    main,
    grad_ref, raw_ref, part_ref, input_ref, up_stream_ref, gain_ref, lane_ref, down_ref, up_ref,
    first_ref, second_ref, third_ref, near_ref, far_ref, where_ref,
    out_ref, narrow_ref, total_ref,
):
    first = where_ref[4] == 0
    half, whole_rows = near_ref.shape[0], first_ref.shape[0]
    width = input_ref.shape[1]
    columns = width // 4

    def right(start, size):
        here = slice(start, start + size)
        if start < main // 2:
            there = slice(start, start + size)
            apart = jnp.where(first, near_ref[there], far_ref[there])
        else:
            there = slice(start - whole_rows + half, start - whole_rows + half + size)
            apart = jnp.where(first, far_ref[there], near_ref[there])
        return jnp.concatenate([first_ref[here], second_ref[here], third_ref[here], apart, up_ref[here]], axis=1)

    total = part_ref[...] + dot(grad_ref[:, : main // 2], right(0, main // 2))
    total = total + dot(grad_ref[:, main // 2 :], right(main // 2, main // 2))
    extra = whole_rows - main
    total = total + dot(raw_ref[:, :extra], right(main, extra))
    narrow = (total[:, width:] * lane_ref[...]).astype(BF16)
    narrow_ref[...] = narrow
    for place in range(4):
        total_ref[:, pl.ds(aligned(where_ref[place], columns), columns)] = total[:, place * columns : (place + 1) * columns]
    scaled = (total_ref[...] + dot_last(narrow, down_ref[...])) * gain_ref[...]
    inputs = input_ref[...].astype(F32)
    rate = rms_rate(inputs)
    pull = jnp.mean(inputs * scaled, axis=-1, keepdims=True) * rate * rate * rate
    out_ref[...] = (up_stream_ref[...].astype(F32) + rate * scaled - inputs * pull).astype(BF16)


def scan_back_kernel(
    head, heads, state,
    values_ref, grad_ref, bc_ref, step_ref, decay_ref, sig_ref, token_ref, doc_column_ref, doc_row_ref, state_ref,
    grad_state_ref, skip_ref, rate_ref, *rest,
):
    out_values_ref, out_bc_ref, out_raw_ref = rest[-9:-6]
    score_ref, grad_score_ref, pull_ref, direct_ref, grad_in_ref, grad_out_ref = rest[-6:]
    group, groups = pl.program_id(0), pl.num_programs(0)
    width = values_ref.shape[0]
    heads_here = width // head
    in_map, out_map = bc_ref[:, :state], bc_ref[:, state:]

    def same_doc():
        return (doc_column_ref[:, :1] == doc_row_ref[:1]) & lower_ones((SPAN, SPAN))

    @pl.when(group == 0)
    def _():
        score_ref[...] = jnp.where(same_doc(), dot_last(in_map, out_map), 0.0)
        grad_score_ref[...] = jnp.zeros_like(grad_score_ref)
        grad_in_ref[...] = jnp.zeros_like(grad_in_ref)
        grad_out_ref[...] = jnp.zeros_like(grad_out_ref)

    decay, step = decay_ref[...], step_ref[...]
    token = token_ref[0]
    last = decay[:, SPAN - 1 :]
    carry = jnp.exp(decay) * token[:1]
    tail = jnp.exp(last - decay) * token[1:2]
    keep = jnp.exp(last) * token[2:3, :1]
    columns = jnp.concatenate([decay] * (LANES // heads_here), axis=0).T
    at_end = lax.broadcasted_iota(jnp.int32, (1, SPAN), 1) == SPAN - 1
    grads, tails, carried, pulls, directs = [], [], [], [], []
    for place in range(heads_here):
        rows = slice(place * head, (place + 1) * head)
        one = slice(place, place + 1)
        fade = jnp.exp(jnp.minimum(decay[one] - columns[:, one], 0.0))
        kernel = (fade * score_ref[...]).astype(BF16)
        values = values_ref[rows].astype(F32)
        driven = (values * step[one]).astype(BF16)
        grad_low = grad_ref[rows]
        grad = grad_low.astype(F32)
        grad_score_ref[...] += dot_first(driven, grad_low) * fade
        state_here, grad_state = state_ref[rows], grad_state_ref[rows]
        output = dot(driven, kernel) + dot_last(state_here, out_map) * carry[one]
        by_state = dot_last(grad_state, in_map) * tail[one]
        grad_driven = dot_last(grad_low, kernel) + by_state
        driven = driven.astype(F32)
        pull = jnp.sum(grad * output - driven * grad_driven, axis=0, keepdims=True)
        ending = jnp.sum(jnp.sum(driven * by_state, axis=0, keepdims=True), axis=1, keepdims=True)
        kept = jnp.sum(state_here.astype(F32) * grad_state.astype(F32), axis=0, keepdims=True)
        ending = ending + keep[one] * jnp.sum(kept, axis=1, keepdims=True)
        pulls.append(pull + jnp.where(at_end, ending, 0.0))
        directs.append(jnp.sum(values * grad_driven, axis=0, keepdims=True))
        grads.append(step[one] * grad_driven + skip_ref[one, :1] * grad)
        tails.append((driven * tail[one]).astype(BF16))
        carried.append((grad * carry[one]).astype(BF16))
    grad_in_ref[...] += dot_first(jnp.concatenate(tails, axis=0), grad_state_ref[...])
    grad_out_ref[...] += dot_first(jnp.concatenate(carried, axis=0), state_ref[...])
    out_values_ref[...] = jnp.concatenate(grads, axis=0).T.astype(BF16)
    here = pl.ds(pl.multiple_of(group * heads_here, heads_here), heads_here)
    pull_ref[here, :] = jnp.concatenate(pulls, axis=0)
    direct_ref[here, :] = jnp.concatenate(directs, axis=0)

    @pl.when(group == groups - 1)
    def _():
        ones = lower_ones((SPAN, SPAN)).astype(F32)
        summed = lax.dot_general(
            pull_ref[...], ones, (((1,), (1,)), ((), ())), precision=EXACT, preferred_element_type=F32
        )
        grad_step = (direct_ref[...] - rate_ref[:, :1] * summed).astype(BF16).astype(F32)
        grad_raw = grad_step * sig_ref[...]
        padded = jnp.concatenate([grad_raw, jnp.zeros((LANES - heads, SPAN), F32)], axis=0)
        out_raw_ref[...] = padded.T.astype(BF16)
        grad_score = jnp.where(same_doc(), grad_score_ref[...], 0.0).astype(BF16)
        out_bc_ref[:, :state] = (grad_in_ref[...] + dot(grad_score, out_map)).astype(BF16)
        out_bc_ref[:, state:] = (grad_out_ref[...] + dot_first(grad_score, in_map)).astype(BF16)


def conv_back_kernel(
    value_blocks,
    grad_ref, grad_bc_ref, slope_ref, slope_bc_ref, next_ref, weight_ref, valid_ref, next_valid_ref, project_ref,
):
    block = pl.program_id(0)
    length = grad_ref.shape[0]

    def back(grad_low, slope_low):
        grad = grad_low.astype(F32) * slope_low.astype(F32)
        later = next_ref[...].astype(F32)
        weight = weight_ref[...]
        valid, next_valid = valid_ref[:, :1], next_valid_ref[:, :1]
        taps = weight.shape[0]
        total = weight[taps - 1 : taps] * grad
        for ahead in range(1, taps):
            extended = jnp.concatenate(
                [jnp.where(valid >= ahead, grad, 0.0), jnp.where(next_valid >= ahead, later, 0.0)], axis=0
            )
            total = total + weight[taps - 1 - ahead : taps - ahead] * extended[ahead : ahead + length]
        project_ref[...] = total.astype(BF16)

    @pl.when(block < value_blocks)
    def _():
        back(grad_ref[...], slope_ref[...])

    @pl.when(block == value_blocks)
    def _():
        back(grad_bc_ref[...], slope_bc_ref[...])


def spec(shape, index):
    return pl.BlockSpec(shape, index)


def whole(shape):
    return pl.BlockSpec(shape, lambda *_: (0,) * len(shape))


def cost(flops, moved, transcendentals):
    return pl.CostEstimate(flops=int(flops), bytes_accessed=int(moved), transcendentals=int(transcendentals))


class Sizes:
    def __init__(self, rows, inner, heads, state, columns, taps):
        self.rows, self.inner, self.heads, self.state, self.columns, self.taps = rows, inner, heads, state, columns, taps
        self.head = inner // heads
        self.spans = rows // SPAN
        self.mixed = inner + 2 * state
        self.group_heads = 8
        self.groups = heads // self.group_heads
        self.wide = self.group_heads * self.head


def conv_forward(sizes, mixed, raw, rim, level, tokens):
    s = sizes
    rows, wide, heads, state = s.rows, s.wide, s.heads, s.state
    maps = s.inner // (2 * state)
    shapes = [
        ((s.inner, rows), BF16), ((rows, s.inner), BF16), ((rows, 2 * state), BF16), ((rows, 2 * state), BF16),
        ((s.spans, s.inner, state), BF16), ((heads, rows), F32), ((heads, rows), F32), ((heads, rows), F32),
    ]
    return pl.pallas_call(
        functools.partial(conv_kernel, s.spans, s.head, heads, state),
        grid=(s.groups,),
        in_specs=[
            spec((rows, wide), lambda g: (0, g)), spec((rows, 2 * state), lambda g: (0, maps)),
            spec((8, wide), lambda g: (0, g)), spec((8, 2 * state), lambda g: (0, maps)),
            spec((s.taps, wide), lambda g: (0, g)), spec((s.taps, 2 * state), lambda g: (0, maps)),
            spec((1, wide), lambda g: (0, g)), spec((1, 2 * state), lambda g: (0, maps)),
            whole((rows, LANES)), whole((rows, LANES)), whole((1, LANES)), whole((heads, LANES)),
            whole((s.spans, 8, SPAN)),
        ],
        out_specs=[
            spec((wide, rows), lambda g: (g, 0)), spec((rows, wide), lambda g: (0, g)), whole((rows, 2 * state)),
            whole((rows, 2 * state)), spec((s.spans, wide, state), lambda g: (0, g, 0)), whole((heads, rows)),
            whole((heads, rows)), whole((heads, rows)),
        ],
        out_shape=[jax.ShapeDtypeStruct(*one) for one in shapes],
        scratch_shapes=[pltpu.VMEM((heads, rows), F32)],
        compiler_params=PARAMS,
        cost_estimate=cost(2 * rows * s.inner * state, 10 * rows * s.inner, 2 * rows * s.inner),
    )(
        mixed, mixed, rim, rim, level["conv_weight"], level["conv_weight"], level["conv_bias"], level["conv_bias"],
        tokens["valid"], raw, level["dt_bias"], level["rate"], tokens["flags"],
    )


def span_specs(sizes, span):
    s = sizes
    return dict(
        turned=spec((s.wide, SPAN), lambda g: (g, span)),
        maps=spec((SPAN, 2 * s.state), lambda g: (span, 0)),
        rows=spec((s.group_heads, SPAN), lambda g: (g, span)),
        flags=spec((1, 8, SPAN), lambda g: (span, 0, 0)),
        doc_column=spec((SPAN, LANES), lambda g: (span, 0)),
        doc_row=spec((8, SPAN), lambda g: (0, span)),
        state=spec((s.wide, s.state), lambda g: (g, 0)),
        head=spec((s.group_heads, LANES), lambda g: (g, 0)),
        full=spec((SPAN, s.inner), lambda g: (span, 0)),
    )


ANYWHERE = pl.BlockSpec(memory_space=pl.ANY)


def scan_forward(sizes, span, conv, state_in, gate, level, tokens, earlier):
    s = sizes
    at = span_specs(s, span)
    args = [
        conv["values"], conv["maps"], conv["step"], conv["decay"], tokens["flags"], tokens["column"], tokens["row"],
        state_in, level["skip"], gate, level["gate_gain"],
    ]
    in_specs = [
        at["turned"], at["maps"], at["rows"], at["rows"], at["flags"], at["doc_column"], at["doc_row"], at["state"],
        at["head"], at["full"], whole((1, s.inner)),
    ]
    aliases = {}
    if earlier is not None:
        aliases = {len(args): 0, len(args) + 1: 1}
        args, in_specs = args + list(earlier), in_specs + [ANYWHERE] * 2
    shape = jax.ShapeDtypeStruct((s.rows, s.inner), BF16)
    return pl.pallas_call(
        functools.partial(scan_kernel, s.head, s.state),
        grid=(s.groups,),
        in_specs=in_specs,
        out_specs=[at["full"], at["full"]],
        out_shape=[shape, shape],
        scratch_shapes=[pltpu.VMEM((SPAN, SPAN), F32), pltpu.VMEM((SPAN, s.inner), BF16)],
        input_output_aliases=aliases,
        compiler_params=PARAMS,
        cost_estimate=cost(
            2 * SPAN * s.inner * (SPAN * 4 + s.state), 8 * SPAN * s.inner, s.heads * SPAN * SPAN
        ),
    )(*args)


SMALL = pl.BlockSpec(memory_space=pltpu.SMEM)


def shape_of(shape, dtype=BF16):
    return jax.ShapeDtypeStruct(shape, dtype)


def whole_specs(*arrays):
    return [whole(array.shape) for array in arrays]


def project_mixed(sizes, inputs, level, lane_mask):
    s = sizes
    parts = level["mixed"]
    args = [inputs, level["norm_gain"], level["in_down"], lane_mask, level["up_mixed"], *parts]
    width = inputs.shape[1]
    shapes = [(s.rows, width), (s.rows, LANES), (s.rows, s.mixed), (s.rows, LANES)]
    return pl.pallas_call(
        functools.partial(mixed_kernel, s.mixed, LANES),
        grid=(1,),
        in_specs=whole_specs(*args) + [SMALL],
        out_specs=[whole(shape) for shape in shapes],
        out_shape=[shape_of(shape) for shape in shapes],
        compiler_params=PARAMS,
        cost_estimate=cost(2 * s.rows * width * s.mixed, 10 * width * s.mixed, s.rows),
    )(*args, level["where"])


def gate_tile_specs(sizes, tile):
    quarter = spec((tile, sizes.columns), lambda j: (j, 0))
    half = spec((tile, sizes.columns), lambda j: (lax.rem(j, sizes.inner // (2 * tile)), 0))
    return [spec((tile, LANES), lambda j: (j, 0)), quarter, quarter, quarter, half, half, SMALL]


def project_gate(sizes, normed, narrow, level):
    s = sizes
    tile = 512
    return pl.pallas_call(
        gate_kernel,
        grid=(s.inner // tile,),
        in_specs=whole_specs(normed, narrow) + gate_tile_specs(s, tile),
        out_specs=spec((s.rows, tile), lambda j: (0, j)),
        out_shape=shape_of((s.rows, s.inner)),
        compiler_params=PARAMS,
        cost_estimate=cost(2 * s.rows * normed.shape[1] * s.inner, 10 * s.inner * s.rows, 0),
    )(normed, narrow, level["up_gate"], *level["gate"], level["where"])


def project_out(sizes, normed_out, inputs, level, lane_mask):
    s = sizes
    args = [normed_out, inputs, level["out_down"], lane_mask, level["out_up"], *level["out"]]
    shapes = [(s.rows, LANES), inputs.shape]
    return pl.pallas_call(
        out_kernel,
        grid=(1,),
        in_specs=whole_specs(*args) + [SMALL],
        out_specs=[whole(shape) for shape in shapes],
        out_shape=[shape_of(shape) for shape in shapes],
        compiler_params=PARAMS,
        cost_estimate=cost(2 * s.rows * inputs.shape[1] * s.inner, 6 * inputs.shape[1] * s.inner, 0),
    )(*args, level["where"])


def out_backward(sizes, upstream, mixed, gate, conv, level, lane_mask, tokens):
    s = sizes
    full = spec((SPAN, s.inner), lambda k: (k, 0))
    parts = level["out"]
    width = upstream.shape[1]
    return pl.pallas_call(
        functools.partial(out_back_kernel, s.head, s.heads, s.state),
        grid=(s.spans,),
        in_specs=[
            spec((SPAN, width), lambda k: (k, 0)), spec((SPAN, LANES), lambda k: (k, 0)),
            *whole_specs(level["out_up"], level["out_down"], *parts), SMALL,
            full, full, whole((1, s.inner)), spec((s.heads, SPAN), lambda k: (0, k)),
            spec((1, 8, SPAN), lambda k: (k, 0, 0)), spec((SPAN, 2 * s.state), lambda k: (k, 0)),
        ],
        out_specs=[
            full, spec((s.inner, SPAN), lambda k: (0, k)), spec((1, s.inner, s.state), lambda k: (k, 0, 0)),
            spec((SPAN, LANES), lambda k: (k, 0)),
        ],
        out_shape=[
            shape_of((s.rows, s.inner)), shape_of((s.inner, s.rows)), shape_of((s.spans, s.inner, s.state)),
            shape_of((s.rows, LANES)),
        ],
        scratch_shapes=[pltpu.VMEM((SPAN, s.inner), F32), pltpu.VMEM((SPAN, s.inner), BF16)],
        compiler_params=PARAMS,
        cost_estimate=cost(
            2 * s.rows * s.inner * (s.state + width), 14 * s.rows * s.inner, 2 * s.rows * s.inner
        ),
    )(
        upstream, lane_mask, level["out_up"], level["out_down"], *parts, level["where"], mixed, gate,
        level["gate_gain"], conv["decay"], tokens["flags"], conv["maps"],
    )


def gate_in_backward(sizes, grad_gate, level):
    s = sizes
    tile = 512
    width = 4 * s.columns + LANES
    return pl.pallas_call(
        gate_in_back_kernel,
        grid=(s.inner // tile,),
        in_specs=[spec((s.rows, tile), lambda j: (0, j))] + gate_tile_specs(s, tile),
        out_specs=whole((s.rows, width)),
        out_shape=shape_of((s.rows, width), F32),
        compiler_params=PARAMS,
        cost_estimate=cost(2 * s.rows * width * s.inner, 10 * s.inner * s.rows, 0),
    )(grad_gate, level["up_gate"], *level["gate"], level["where"])


def mixed_in_backward(sizes, grad_mixed, raw, part, inputs, upstream, level, lane_mask):
    s = sizes
    width = inputs.shape[1]
    rows = lambda columns: spec((SPAN, columns), lambda k: (k, 0))
    fixed = [level["in_down"], level["up_mixed"], *level["mixed"]]
    return pl.pallas_call(
        functools.partial(mixed_in_back_kernel, s.mixed),
        grid=(s.spans,),
        in_specs=[
            rows(s.mixed), rows(LANES), rows(width + LANES), rows(width), rows(width), whole((1, width)), rows(LANES),
            *whole_specs(*fixed), SMALL,
        ],
        out_specs=[rows(width), rows(LANES)],
        out_shape=[shape_of((s.rows, width)), shape_of((s.rows, LANES))],
        scratch_shapes=[pltpu.VMEM((SPAN, width), F32)],
        compiler_params=PARAMS,
        cost_estimate=cost(2 * s.rows * width * s.mixed, 10 * width * s.mixed, s.rows),
    )(grad_mixed, raw, part, inputs, upstream, level["norm_gain"], lane_mask, *fixed, level["where"])


def scan_backward(sizes, span, conv, grad_turned, state_in, grad_state, level, tokens, earlier):
    s = sizes
    at = span_specs(s, span)
    args = [
        conv["values"], grad_turned, conv["maps"], conv["step"], conv["decay"], conv["sig"], tokens["flags"],
        tokens["column"], tokens["row"], state_in, grad_state, level["skip"], level["rate"],
    ]
    in_specs = [
        at["turned"], at["turned"], at["maps"], at["rows"], at["rows"], spec((s.heads, SPAN), lambda g: (0, span)),
        at["flags"], at["doc_column"], at["doc_row"], at["state"], at["state"], at["head"], whole((s.heads, LANES)),
    ]
    aliases = {}
    if earlier is not None:
        aliases = {len(args) + place: place for place in range(3)}
        args, in_specs = args + list(earlier), in_specs + [ANYWHERE] * 3
    return pl.pallas_call(
        functools.partial(scan_back_kernel, s.head, s.heads, s.state),
        grid=(s.groups,),
        in_specs=in_specs,
        out_specs=[spec((SPAN, s.wide), lambda g: (span, g)), at["maps"], spec((SPAN, LANES), lambda g: (span, 0))],
        out_shape=[
            jax.ShapeDtypeStruct((s.rows, s.inner), BF16), jax.ShapeDtypeStruct((s.rows, 2 * s.state), BF16),
            jax.ShapeDtypeStruct((s.rows, LANES), BF16),
        ],
        scratch_shapes=[
            pltpu.VMEM((SPAN, SPAN), F32), pltpu.VMEM((SPAN, SPAN), F32), pltpu.VMEM((s.heads, SPAN), F32),
            pltpu.VMEM((s.heads, SPAN), F32), pltpu.VMEM((SPAN, s.state), F32), pltpu.VMEM((SPAN, s.state), F32),
        ],
        input_output_aliases=aliases,
        compiler_params=PARAMS,
        cost_estimate=cost(
            2 * SPAN * s.inner * (SPAN * 12 + 4 * s.state), 10 * SPAN * s.inner, s.heads * SPAN * SPAN
        ),
    )(*args)


def conv_backward(sizes, grad_values, grad_maps, conv, later, level, tokens):
    s = sizes
    wide = 2 * s.state
    blocks = s.inner // wide
    values = spec((s.rows, wide), lambda i: (0, jnp.minimum(i, blocks - 1)))
    mixed = lambda i: (0, i)
    return pl.pallas_call(
        functools.partial(conv_back_kernel, blocks),
        grid=(blocks + 1,),
        in_specs=[
            values, whole((s.rows, wide)), values, whole((s.rows, wide)), spec((8, wide), mixed),
            spec((s.taps, wide), mixed), whole((s.rows, LANES)), whole((8, LANES)),
        ],
        out_specs=spec((s.rows, wide), mixed),
        out_shape=shape_of((s.rows, s.mixed)),
        compiler_params=PARAMS,
        cost_estimate=cost(10 * s.rows * s.mixed, 6 * s.rows * s.mixed, 0),
    )(
        grad_values, grad_maps, conv["slope"], conv["slope_maps"], later, level["conv_weight"], tokens["valid"],
        tokens["next_valid"],
    )


def early_grads_kernel(up_ref, narrow_out_ref, normed_out_ref, grad_narrow_ref, grad_gate_ref, narrow_ref, out_ref):
    block = pl.program_id(0)

    @pl.when(block == 0)
    def _():
        out_ref[...] = dot_first(up_ref[...], narrow_out_ref[...]).astype(BF16)

    @pl.when((block == 1) | (block == 2))
    def _():
        out_ref[...] = dot_first(normed_out_ref[...], grad_narrow_ref[...]).astype(BF16)

    @pl.when(block > 2)
    def _():
        out_ref[...] = dot_first(grad_gate_ref[...], narrow_ref[...]).astype(BF16)


def early_grads(sizes, upstream, kept, grad_narrow_out, grad_gate):
    s = sizes
    wide = upstream.shape[1]
    blocks = 1 + 2 * (s.inner // wide)
    args = [upstream, kept["narrow_out"], kept["normed_out"], grad_narrow_out, grad_gate, kept["narrow"]]
    narrow = whole((s.rows, LANES))
    return pl.pallas_call(
        early_grads_kernel,
        grid=(blocks,),
        in_specs=[
            whole((s.rows, wide)), narrow, spec((s.rows, wide), lambda i: (0, jnp.clip(i - 1, 0, 1))), narrow,
            spec((s.rows, wide), lambda i: (0, jnp.clip(i - 3, 0, 1))), narrow,
        ],
        out_specs=spec((wide, LANES), lambda i: (i, 0)),
        out_shape=shape_of((blocks * wide, LANES)),
        compiler_params=PARAMS,
        cost_estimate=cost(2 * s.rows * LANES * blocks * wide, 2 * s.rows * blocks * wide, 0),
    )(*args)


def late_grads_kernel(normed_ref, grad_narrow_ref, mixed_ref, raw_ref, narrow_ref, out_ref):
    first = 0
    for left, right in ((normed_ref, grad_narrow_ref), (mixed_ref, narrow_ref), (raw_ref, narrow_ref)):
        rows = left.shape[1]
        out_ref[first : first + rows, :] = dot_first(left[...], right[...]).astype(BF16)
        first += rows
    out_ref[first:, :] = jnp.zeros((out_ref.shape[0] - first, out_ref.shape[1]), BF16)


def late_grads(sizes, kept, grad_narrow, grad_mixed, raw):
    s = sizes
    args = [kept["normed"], grad_narrow, grad_mixed, raw, kept["narrow"]]
    rows = -(-(kept["normed"].shape[1] + s.mixed + LANES) // 512) * 512
    return pl.pallas_call(
        late_grads_kernel,
        grid=(1,),
        in_specs=whole_specs(*args),
        out_specs=whole((rows, LANES)),
        out_shape=shape_of((rows, LANES)),
        compiler_params=PARAMS,
        cost_estimate=cost(2 * s.rows * LANES * rows, 2 * s.rows * rows, 0),
    )(*args)


def token_tables(doc_ids, block_rows):
    rows = doc_ids.shape[0]
    before = from_behind(doc_ids[rows - 8 :], "seq", 1)
    after = from_behind(doc_ids[:8], "seq", -1)
    extended = jnp.concatenate([before, doc_ids, after])

    def taps_behind(first, count):
        here = extended[first : first + count]
        return sum((extended[first - back : first - back + count] == here).astype(jnp.int32) for back in (1, 2, 3))

    spans = rows // SPAN
    ends = extended[7 + SPAN :: SPAN][:spans]
    starts = extended[7::SPAN][:spans]
    by_span = doc_ids.reshape(spans, SPAN)
    flags = jnp.stack(
        [
            (by_span == starts[:, None]).astype(F32),
            (by_span == ends[:, None]).astype(F32),
            jnp.broadcast_to((starts == ends).astype(F32)[:, None], (spans, SPAN)),
        ]
        + [jnp.zeros((spans, SPAN), F32)] * 5,
        axis=1,
    )
    return dict(
        valid=jnp.broadcast_to(taps_behind(8, rows)[:, None], (rows, LANES)),
        next_valid=jnp.broadcast_to(taps_behind(8 + rows, 8)[:, None], (8, LANES)),
        column=jnp.broadcast_to(doc_ids[:, None], (rows, LANES)),
        row=jnp.broadcast_to(doc_ids[None, :], (8, rows)),
        flags=flags,
        keep=(starts == ends).astype(F32),
    )


def state_hops(rows, block_rows):
    eighth = block_rows // DOCS_PER_BLOCK
    if rows // SPAN > 1 and eighth > SPAN:
        raise ValueError("unsupported block")
    return 1 if rows >= eighth else 2 * eighth // rows - 1


def pass_states(sizes, local, conv, tokens, hops, direction):
    if hops > 1:
        keep = jnp.exp(conv["decay"][:, -1]) * tokens["keep"][0]
        keep = jnp.repeat(keep, sizes.head)[:, None]
        total = local.astype(F32)
        reach = 1
        while reach < hops:
            total = total + keep * from_behind(total.astype(BF16), "seq", direction * reach).astype(F32)
            keep = keep * from_behind(keep, "seq", direction * reach)
            reach *= 2
        local = total.astype(BF16)
    return from_behind(local, "seq", direction)


def layer_forward(sizes, inputs, level, lane_mask, tokens, hops):
    s = sizes
    normed, narrow, mixed, raw = project_mixed(s, inputs, level, lane_mask)
    rim = from_behind(mixed[s.rows - 8 :], "seq", 1)
    gate = project_gate(s, normed, narrow, level)
    values, slope, maps, slope_maps, states, step, decay, sig = conv_forward(s, mixed, raw, rim, level, tokens)
    conv = dict(values=values, slope=slope, maps=maps, slope_maps=slope_maps, step=step, decay=decay, sig=sig)
    states_in = [pass_states(s, states[s.spans - 1], conv, tokens, hops, 1)]
    states_in += [states[span] for span in range(s.spans - 1)]
    outputs = None
    for span in reversed(range(s.spans)):
        outputs = scan_forward(s, span, conv, states_in[span], gate, level, tokens, outputs)
    mixed_out, normed_out = outputs
    narrow_out, result = project_out(s, normed_out, inputs, level, lane_mask)
    kept = dict(
        inputs=inputs, normed=normed, narrow=narrow, gate=gate, conv=conv, states_in=states_in, mixed_out=mixed_out,
        normed_out=normed_out, narrow_out=narrow_out,
    )
    return result, kept


def layer_backward(sizes, upstream, kept, level, lane_mask, tokens, hops):
    s = sizes
    conv = kept["conv"]
    grad_gate, turned, local, grad_narrow_out = out_backward(
        s, upstream, kept["mixed_out"], kept["gate"], conv, level, lane_mask, tokens
    )
    early = early_grads(s, upstream, kept, grad_narrow_out, grad_gate)
    grad_states = [local[span] for span in range(1, s.spans)]
    grad_states.append(pass_states(s, local[0], conv, tokens, hops, -1))
    part = gate_in_backward(s, grad_gate, level)
    outputs = None
    for span in range(s.spans):
        outputs = scan_backward(
            s, span, conv, turned, kept["states_in"][span], grad_states[span], level, tokens, outputs
        )
        if span == 0:
            edge = jnp.concatenate([outputs[0][:8], outputs[1][:8]], axis=1).astype(F32)
            slopes = jnp.concatenate([conv["slope"][:8], conv["slope_maps"][:8]], axis=1).astype(F32)
            later = from_behind((edge * slopes).astype(BF16), "seq", -1)
    grad_values, grad_maps, raw = outputs
    grad_mixed = conv_backward(s, grad_values, grad_maps, conv, later, level, tokens)
    grad_inputs, grad_narrow = mixed_in_backward(
        s, grad_mixed, raw, part, kept["inputs"], upstream, level, lane_mask
    )
    return grad_inputs, early, late_grads(s, kept, grad_narrow, grad_mixed, raw)


def make_level(sizes, weights, section, place):
    s = sizes
    level = dict(weights)
    level["norm_gain"] = weights["norm_gain"][None, :]
    level["gate_gain"] = weights["gate_gain"][None, :]
    level["conv_bias"] = weights["conv_bias"][None, :]
    level["dt_bias"] = jnp.pad(weights["dt_bias"], (0, LANES - s.heads))[None, :]
    level["rate"] = jnp.broadcast_to(jnp.exp(weights["a_log"])[:, None], (s.heads, LANES))
    level["skip"] = jnp.broadcast_to(weights["skip_gain"][:, None], (s.heads, LANES))
    turned = weights["in_up"].T
    level["up_gate"], level["up_mixed"] = turned[: s.inner], turned[s.inner :]
    level["where"] = jnp.stack([place, place ^ (1 + section), place ^ (2 - section), place ^ 3, section]).astype(jnp.int32)
    return level


def swap(value):
    return lax.ppermute(value, "section", [(0, 1), (1, 0)])


def exchange(value, axis, distance):
    count = lax.axis_size(axis)
    return lax.ppermute(value, axis, [(place, place ^ distance) for place in range(count)])


def rows_at(value, index, rows):
    return lax.dynamic_slice_in_dim(value, index * rows, rows, axis=0)


def put_at(buffer, value, *index):
    start = list(index) + [0] * (buffer.ndim - len(index))
    return lax.dynamic_update_slice(buffer, value.reshape((1,) * len(index) + value.shape), start)


def across(value, second):
    count = lax.axis_size("wshard")
    pairs = []
    for section in range(2):
        distance = 2 - section if second else 1 + section
        pairs += [(section * count + place, section * count + (place ^ distance)) for place in range(count)]
    return lax.ppermute(value, ("section", "wshard"), pairs)


def spread(quarters):
    section = lax.axis_index("section")
    others = [swap(matrix) for matrix, _, _ in quarters]
    layers, before = [], None
    for layer in range(2):
        parts = []
        for (matrix, half, step), other in zip(quarters, others, strict=True):
            own = jnp.where(section == layer, matrix, other)
            if before is not None:
                own, _ = lax.optimization_barrier((own, before))
            near = across(own, False)
            before = near
            twin = swap(near)
            apart = across(lax.dynamic_slice_in_dim(near, section * step, half, axis=0), True)
            parts.append((own, near, twin, apart, swap(apart)))
        layers.append(parts)
    return layers


def reduce_rows(value, axis):
    count, place = lax.axis_size(axis), lax.axis_index(axis)
    rows = value.shape[0] // count
    total = rows_at(value, place, rows).astype(F32)
    for distance in range(1, count):
        total = total + exchange(rows_at(value, place ^ distance, rows), axis, distance).astype(F32)
    return total


def collect_rows(value, axis):
    count, place = lax.axis_size(axis), lax.axis_index(axis)
    buffer = jnp.zeros((count,) + value.shape, value.dtype)
    for distance in range(count):
        part = exchange(value, axis, distance) if distance else value
        buffer = put_at(buffer, part, place ^ distance)
    return buffer.reshape((count * value.shape[0],) + value.shape[1:])


def sum_everywhere(packed):
    section = lax.axis_index("section")
    half = packed.shape[0] // 2
    mine = rows_at(packed, section, half).astype(F32) + swap(rows_at(packed, 1 - section, half)).astype(F32)
    mine = mine.astype(BF16)
    if lax.axis_size("seq") == 4:
        part = reduce_rows(mine, "wshard").astype(BF16)
        part = reduce_rows(part, "seq").astype(BF16)
        mine = collect_rows(collect_rows(part, "seq"), "wshard")
    else:
        mine = lax.psum(mine, ("seq", "wshard"))
    other = swap(mine)
    return jnp.concatenate([jnp.where(section == 0, mine, other), jnp.where(section == 0, other, mine)], axis=0)


VECTORS = ("norm_gain", "conv_weight", "conv_bias", "gate_gain", "dt_bias", "a_log", "skip_gain")
ADAPTERS = ("in_down", "in_up", "out_down", "out_up")


def both_layers(own):
    section = lax.axis_index("section")
    other = jax.tree.map(swap, own)
    return [
        jax.tree.map(lambda here, there: jnp.where(section == layer, here, there), own, other) for layer in range(2)
    ]


def on_device(layer_input, out_grad, doc_index, doc_adapter, in_weight, out_weight, *parameters):
    names = ("norm_gain", "conv_weight", "conv_bias", "dt_bias", "a_log", "skip_gain", "gate_gain") + ADAPTERS
    own = {name: value[0] for name, value in zip(names, parameters, strict=True)}
    section = lax.axis_index("section")
    batches, rows, width = layer_input.shape
    heads, inner = own["dt_bias"].shape[0], own["gate_gain"].shape[0]
    taps, mixed = own["conv_weight"].shape
    sizes = Sizes(rows, inner, heads, (mixed - inner) // 2, in_weight.shape[1], taps)
    block_rows = rows * lax.axis_size("seq")
    hops = state_hops(rows, block_rows)

    pick = lambda array: lax.dynamic_index_in_dim(array, section, 0, keepdims=False)
    inputs, grads, doc_ids, table = pick(layer_input), pick(out_grad), pick(doc_index), pick(doc_adapter)[0]
    tokens = token_tables(doc_ids, block_rows)
    adapter = jnp.sum(jnp.where(doc_ids[:, None] == jnp.arange(table.shape[0])[None, :], table[None, :], 0), axis=1)
    lane_mask = (adapter[:, None] == (jnp.arange(own["in_down"].shape[1]) // RANK)[None, :]).astype(F32)

    turned = in_weight[0].T
    main = sizes.mixed // 2
    groups = spread(
        [
            (turned[inner:], main + heads, main),
            (turned[:inner], inner // 2, inner // 2),
            (out_weight[0], out_weight.shape[1] // 2, out_weight.shape[1] // 2),
        ]
    )
    packed = both_layers(jnp.concatenate([own[name].reshape(-1) for name in VECTORS]))
    adapters = both_layers({name: own[name] for name in ADAPTERS})
    levels = []
    for layer in range(2):
        weights, first = dict(adapters[layer]), 0
        for name in VECTORS:
            size = own[name].size
            weights[name] = packed[layer][first : first + size].reshape(own[name].shape)
            first += size
        weights["mixed"], weights["gate"], weights["out"] = groups[layer]
        levels.append(make_level(sizes, weights, section, lax.axis_index("wshard")))

    results, kept = [], []
    rows_now = inputs
    for layer in range(2):
        rows_now, stored = layer_forward(sizes, rows_now, levels[layer], lane_mask, tokens, hops)
        results.append(rows_now)
        kept.append(stored)
    upper_grad, upper_early, upper_late = layer_backward(sizes, grads, kept[1], levels[1], lane_mask, tokens, hops)
    lower_grad, lower_early, lower_late = layer_backward(sizes, upper_grad, kept[0], levels[0], lane_mask, tokens, hops)
    first = sum_everywhere(jnp.concatenate([lower_early, upper_early, upper_late], axis=0))
    early_rows = lower_early.shape[0]
    early = jnp.where(section == 0, first[:early_rows], first[early_rows : 2 * early_rows]).astype(F32)
    late = jnp.where(section == 0, sum_everywhere(lower_late), first[2 * early_rows :]).astype(F32)
    up_out, down_out, up_gate = early[:width], early[width : width + inner], early[width + inner :]
    down_in, up_mixed = late[:width], late[width : width + mixed + heads]

    def placed(pair):
        here = jnp.where(section == 0, pair[0], pair[1])
        there = swap(jnp.where(section == 0, pair[1], pair[0]))
        first, second = jnp.where(section == 0, here, there), jnp.where(section == 0, there, here)
        return jnp.stack([first, second])[None]

    return (
        placed(results),
        placed([lower_grad, upper_grad]),
        down_in[None],
        jnp.concatenate([up_gate, up_mixed], axis=0).T[None],
        down_out[None],
        up_out.T[None],
    )


def solution(mesh):
    tokens, matrix, vector = P(None, ("wshard", "seq"), None), P("section", None, None), P("section", None)
    in_specs = (tokens, tokens, P(None, ("wshard", "seq")), P(None, "wshard", None))
    in_specs += (P("section", "wshard", None),) * 2
    in_specs += (vector, matrix) + (vector,) * 5 + (matrix,) * 4
    out_specs = (P("section", None, ("wshard", "seq"), None),) * 2 + (matrix,) * 4
    return jax.shard_map(on_device, mesh=mesh, in_specs=in_specs, out_specs=out_specs, check_vma=False)
```

profile of v0, /device:TPU:17, one launch (start us, length us, event | category | flops | bytes accessed | tf_op | source)
XLA Modules:
  0.0 555.2 jit_solution(3079339886722864800)
XLA Ops:
  19.1 3.7 collective-permute-start.9
  37.7 5.8 %collective-permute-done.13.second_ref = bf16[2048,256]{1,0:T(8,128)(2,1)} collective-permute-done((bf16[2048,256]{1,0:T(8,128)(2,1)S(1)}, bf16[2048,256]{1,0:T(8,128)(2,1)}, u32[]{:S(2)}, u32[]{:S(2)}) %collective-permute-start.13) | collective-permute-done | bytes 1048608 | tf_op jit(solution)/shard_map/ppermute | solution.py:942
  48.3 3.0 collective-permute-start.18
  53.1 8.4 %collective-permute-done.6.near_ref = bf16[1184,256]{1,0:T(8,128)(2,1)S(1)} collective-permute-done((bf16[1184,256]{1,0:T(8,128)(2,1)S(1)}, bf16[1184,256]{1,0:T(8,128)(2,1)S(1)}, u32[]{:S(2)}, u32[]{:S(2)}) %collective-permute-start.6) | collective-permute-done | bytes 606240 | tf_op jit(solution)/shard_map/ppermute | solution.py:942
  72.2 9.6 %collective-permute-done.24.second_ref = bf16[2336,256]{1,0:T(8,128)(2,1)S(1)} collective-permute-done((bf16[2336,256]{1,0:T(8,128)(2,1)S(1)}, bf16[2336,256]{1,0:T(8,128)(2,1)S(1)}, u32[]{:S(2)}, u32[]{:S(2)}) %collective-permute-start.24) | collective-permute-done | bytes 1196064 | tf_op jit(solution)/shard_map/ppermute | solution.py:942
  83.7 9.2 %shard_map.208 = (bf16[512,1024]{1,0:T(8,128)(2,1)}, bf16[512,128]{1,0:T(8,128)(2,1)}, bf16[512,2304]{1,0:T(8,128)(2,1)}, bf16[512,128]{1,0:T(8,128)(2,1)}) custom-call(bf16[512,1024]{1,0:T(8,128)(2,1)} %dynamic-slice_bitcast_fusion.1.input_ref, f32[1,1024]{1,0:T(1,128)} %bitcast.165, bf16[1024,128]{1,0:T(8,128)(2,1)} %get-tuple-element.186.down_ref, ...), custom_call_target="tpu_custom_call" | custom-call | flops 2415919104 | bytes 23592960 | tf_op jit(solution)/shard_map/pallas_call | solution.py:568
  93.7 3.7 collective-permute-start.8
  103.7 9.4 %shard_map.209 = (bf16[2048,512]{1,0:T(8,128)(2,1)}, bf16[512,2048]{1,0:T(8,128)(2,1)}, bf16[512,256]{1,0:T(8,128)(2,1)}, bf16[512,256]{1,0:T(8,128)(2,1)}, bf16...) custom-call(bf16[512,2304]{1,0:T(8,128)(2,1)} %get-tuple-element.71.mixed_ref.mixed_bc_ref, ...), custom_call_target="tpu_custom_call" | custom-call | flops 268435456 | bytes 10485760 | tf_op jit(solution)/shard_map/pallas_call | solution.py:476
  115.1 3.2 collective-permute-start.11
  122.2 8.6 %collective-permute-done.11.state_ref = bf16[2048,128]{1,0:T(8,128)(2,1)S(1)} collective-permute-done((bf16[2048,128]{1,0:T(8,128)(2,1)S(1)}, bf16[2048,128]{1,0:T(8,128)(2,1)S(1)}, u32[]{:S(2)}, u32[]{:S(2)}) %collective-permute-start.11) | collective-permute-done | bytes 524320 | tf_op jit(solution)/shard_map/ppermute | solution.py:24
  138.7 7.0 %shard_map.210.gate_ref = bf16[512,2048]{1,0:T(8,128)(2,1)} custom-call(bf16[512,1024]{1,0:T(8,128)(2,1)} %get-tuple-element.78.normed_ref, bf16[512,128]{1,0:T(8,128)(2,1)} %get-tuple-element.79.narrow_ref, bf16[2048,128]{1,0:T(8,128)(2,1)} %slice.250.up_ref, bf16[2048,256]{1,0:T(8,128)(2,1)} %copy-done.7, ...), custom_call_target="tpu_custom_call" | custom-call | flops 2147483648 | bytes 10485760 | tf_op jit(solution)/shard_map/pallas_call | solution.py:588
  147.8 9.3 %shard_map.211 = (bf16[512,2048]{1,0:T(8,128)(2,1)}, bf16[512,2048]{1,0:T(8,128)(2,1)}) custom-call(bf16[2048,512]{1,0:T(8,128)(2,1)} %get-tuple-element.73.values_ref, bf16[512,256]{1,0:T(8,128)(2,1)} %get-tuple-element.74.bc_ref, f32[32,512]{1,0:T(8,128)} %get-tuple-element.75.step_ref, f32[32,512]{1,0:T(8,128)} %get-tuple-element.76.decay_ref, ...), custom_call_target="tpu_custom_call" | custom-call | flops 1207959552 | bytes 4194304 | tf_op jit(solution)/shard_map/pallas_call | solution.py:536
  157.1 9.2 %shard_map.212 = (bf16[512,2048]{1,0:T(8,128)(2,1)}, bf16[512,2048]{1,0:T(8,128)(2,1)}) custom-call(bf16[2048,512]{1,0:T(8,128)(2,1)} %get-tuple-element.73.values_ref, bf16[512,256]{1,0:T(8,128)(2,1)} %get-tuple-element.74.bc_ref, f32[32,512]{1,0:T(8,128)} %get-tuple-element.75.step_ref, ...), custom_call_target="tpu_custom_call", output_to_operand_aliasing={{0}: (11, {}), {1}: (12, {})} | custom-call | flops 1207959552 | bytes 4194304 | tf_op jit(solution)/shard_map/pallas_call | solution.py:536
  169.6 7.5 %shard_map.213 = (bf16[512,128]{1,0:T(8,128)(2,1)}, bf16[512,1024]{1,0:T(8,128)(2,1)}) custom-call(bf16[512,2048]{1,0:T(8,128)(2,1)} %get-tuple-element.83.normed_ref.normed_out_ref, bf16[512,1024]{1,0:T(8,128)(2,1)} %dynamic-slice_bitcast_fusion.1.input_ref, bf16[2048,128]{1,0:T(8,128)(2,1)} %get-tuple-element.176.down_ref.down_out_ref, ...), custom_call_target="tpu_custom_call" | custom-call | flops 2147483648 | bytes 12582912 | tf_op jit(solution)/shard_map/pallas_call | solution.py:603
  179.0 9.3 %shard_map.214 = (bf16[512,1024]{1,0:T(8,128)(2,1)}, bf16[512,128]{1,0:T(8,128)(2,1)}, bf16[512,2304]{1,0:T(8,128)(2,1)}, bf16[512,128]{1,0:T(8,128)(2,1)}) custom-call(bf16[512,1024]{1,0:T(8,128)(2,1)} %get-tuple-element.85.input_ref, f32[1,1024]{1,0:T(1,128)} %bitcast.167, bf16[1024,128]{1,0:T(8,128)(2,1)} %get-tuple-element.185.down_ref, ...), custom_call_target="tpu_custom_call" | custom-call | flops 2415919104 | bytes 23592960 | tf_op jit(solution)/shard_map/pallas_call | solution.py:568
  195.8 9.4 %shard_map.215 = (bf16[2048,512]{1,0:T(8,128)(2,1)}, bf16[512,2048]{1,0:T(8,128)(2,1)}, bf16[512,256]{1,0:T(8,128)(2,1)}, bf16[512,256]{1,0:T(8,128)(2,1)}, bf16...) custom-call(bf16[512,2304]{1,0:T(8,128)(2,1)} %get-tuple-element.87.mixed_ref.mixed_bc_ref, ...), custom_call_target="tpu_custom_call" | custom-call | flops 268435456 | bytes 10485760 | tf_op jit(solution)/shard_map/pallas_call | solution.py:476
  217.0 7.1 %shard_map.216.gate_ref = bf16[512,2048]{1,0:T(8,128)(2,1)} custom-call(bf16[512,1024]{1,0:T(8,128)(2,1)} %get-tuple-element.94.normed_ref, bf16[512,128]{1,0:T(8,128)(2,1)} %get-tuple-element.95.narrow_ref, bf16[2048,128]{1,0:T(8,128)(2,1)} %slice.260.up_ref, bf16[2048,256]{1,0:T(8,128)(2,1)} %copy-done.9, ...), custom_call_target="tpu_custom_call" | custom-call | flops 2147483648 | bytes 10485760 | tf_op jit(solution)/shard_map/pallas_call | solution.py:588
  224.7 9.2 %shard_map.217 = (bf16[512,2048]{1,0:T(8,128)(2,1)}, bf16[512,2048]{1,0:T(8,128)(2,1)}) custom-call(bf16[2048,512]{1,0:T(8,128)(2,1)} %get-tuple-element.89.values_ref, bf16[512,256]{1,0:T(8,128)(2,1)} %get-tuple-element.90.bc_ref, f32[32,512]{1,0:T(8,128)} %get-tuple-element.91.step_ref, f32[32,512]{1,0:T(8,128)} %get-tuple-element.92.decay_ref, ...), custom_call_target="tpu_custom_call" | custom-call | flops 1207959552 | bytes 4194304 | tf_op jit(solution)/shard_map/pallas_call | solution.py:536
  234.7 9.2 %shard_map.218 = (bf16[512,2048]{1,0:T(8,128)(2,1)}, bf16[512,2048]{1,0:T(8,128)(2,1)}) custom-call(bf16[2048,512]{1,0:T(8,128)(2,1)} %get-tuple-element.89.values_ref, bf16[512,256]{1,0:T(8,128)(2,1)} %get-tuple-element.90.bc_ref, f32[32,512]{1,0:T(8,128)} %get-tuple-element.91.step_ref, ...), custom_call_target="tpu_custom_call", output_to_operand_aliasing={{0}: (11, {}), {1}: (12, {})} | custom-call | flops 1207959552 | bytes 4194304 | tf_op jit(solution)/shard_map/pallas_call | solution.py:536
  245.1 15.5 %shard_map.220 = (bf16[512,2048]{1,0:T(8,128)(2,1)}, bf16[2048,512]{1,0:T(8,128)(2,1)}, bf16[2,2048,128]{2,1,0:T(8,128)(2,1)}, bf16[512,128]{1,0:T(8,128)(2,1)}) custom-call(bf16[512,1024]{1,0:T(8,128)(2,1)} %dynamic-slice_bitcast_fusion.up_ref.up_stream_ref, f32[512,128]{1,0:T(8,128)} %compare_convert_fusion.lane_ref, ...), custom_call_target="tpu_custom_call" | custom-call | flops 2415919104 | bytes 14680064 | tf_op jit(solution)/shard_map/pallas_call | solution.py:619
  262.7 10.6 %shard_map.221 = (bf16[512,2048]{1,0:T(8,128)(2,1)}, bf16[512,256]{1,0:T(8,128)(2,1)}, bf16[512,128]{1,0:T(8,128)(2,1)}) custom-call(bf16[2048,512]{1,0:T(8,128)(2,1)} %get-tuple-element.89.values_ref, bf16[2048,512]{1,0:T(8,128)(2,1)} %get-tuple-element.103.grad_ref, bf16[512,256]{1,0:T(8,128)(2,1)} %get-tuple-element.90.bc_ref, ...), custom_call_target="tpu_custom_call" | custom-call | flops 3758096384 | bytes 5242880 | tf_op jit(solution)/shard_map/pallas_call | solution.py:697
  274.8 3.6 collective-permute-start.40
  281.1 7.6 %shard_map.219 = (bf16[512,128]{1,0:T(8,128)(2,1)}, bf16[512,1024]{1,0:T(8,128)(2,1)}) custom-call(bf16[512,2048]{1,0:T(8,128)(2,1)} %get-tuple-element.99.normed_ref.normed_out_ref, bf16[512,1024]{1,0:T(8,128)(2,1)} %get-tuple-element.85.input_ref, bf16[2048,128]{1,0:T(8,128)(2,1)} %get-tuple-element.175.down_ref.down_out_ref, ...), custom_call_target="tpu_custom_call" | custom-call | flops 2147483648 | bytes 12582912 | tf_op jit(solution)/shard_map/pallas_call | solution.py:603
  290.7 7.1 %shard_map.234 = bf16[5120,128]{1,0:T(8,128)(2,1)} custom-call(bf16[512,1024]{1,0:T(8,128)(2,1)} %dynamic-slice_bitcast_fusion.up_ref.up_stream_ref, bf16[512,128]{1,0:T(8,128)(2,1)} %get-tuple-element.133.narrow_out_ref, bf16[512,2048]{1,0:T(8,128)(2,1)} %get-tuple-element.99.normed_ref.normed_out_ref, bf16[512,128]{1,0:T(8,128)(2,1)} %get-tuple-element.134.grad_narrow_ref, ...), custom_call_target="tpu_custom_call" | custom-call | flops 671088640 | bytes 5242880 | tf_op jit(solution)/shard_map/pallas_call | solution.py:763
  297.8 7.7 %shard_map.224.part_ref = f32[512,1152]{1,0:T(8,128)} custom-call(bf16[512,2048]{1,0:T(8,128)(2,1)} %get-tuple-element.114.grad_ref.grad_gate_ref, bf16[2048,128]{1,0:T(8,128)(2,1)} %slice.260.up_ref, bf16[2048,256]{1,0:T(8,128)(2,1)} %copy-done.9, bf16[2048,256]{1,0:T(8,128)(2,1)} %collective-permute-done.30.second_ref, bf16[2048,256]{1,0:T(8,128)(2,1)} %copy-done.20, ...), custom_call_target="tpu_custom_call" | custom-call | flops 2415919104 | bytes 10485760 | tf_op jit(solution)/shard_map/pallas_call | solution.py:651
  306.3 10.5 %shard_map.222 = (bf16[512,2048]{1,0:T(8,128)(2,1)}, bf16[512,256]{1,0:T(8,128)(2,1)}, bf16[512,128]{1,0:T(8,128)(2,1)}) custom-call(bf16[2048,512]{1,0:T(8,128)(2,1)} %get-tuple-element.89.values_ref, bf16[2048,512]{1,0:T(8,128)(2,1)} %get-tuple-element.103.grad_ref, ...), custom_call_target="tpu_custom_call", output_to_operand_aliasing={{0}: (13, {}), {1}: (14, {}), {2}: (15, {})} | custom-call | flops 3758096384 | bytes 5242880 | tf_op jit(solution)/shard_map/pallas_call | solution.py:697
  317.5 8.5 %shard_map.223.grad_ref.mixed_ref = bf16[512,2304]{1,0:T(8,128)(2,1)} custom-call(bf16[512,2048]{1,0:T(8,128)(2,1)} %get-tuple-element.109.grad_ref, bf16[512,256]{1,0:T(8,128)(2,1)} %get-tuple-element.110.grad_bc_ref, bf16[512,2048]{1,0:T(8,128)(2,1)} %get-tuple-element.111.slope_ref, bf16[512,256]{1,0:T(8,128)(2,1)} %get-tuple-element.112.slope_bc_ref, ...), custom_call_target="tpu_custom_call" | custom-call | flops 11796480 | bytes 7077888 | tf_op jit(solution)/shard_map/pallas_call | solution.py:724
  326.0 9.9 %shard_map.225 = (bf16[512,1024]{1,0:T(8,128)(2,1)}, bf16[512,128]{1,0:T(8,128)(2,1)}) custom-call(bf16[512,2304]{1,0:T(8,128)(2,1)} %shard_map.223.grad_ref.mixed_ref, bf16[512,128]{1,0:T(8,128)(2,1)} %get-tuple-element.113.raw_ref, f32[512,1152]{1,0:T(8,128)} %shard_map.224.part_ref, bf16[512,1024]{1,0:T(8,128)(2,1)} %get-tuple-element.85.input_ref, ...), custom_call_target="tpu_custom_call" | custom-call | flops 2415919104 | bytes 23592960 | tf_op jit(solution)/shard_map/pallas_call | solution.py:667
  336.0 4.2 shard_map.235
  340.2 15.5 %shard_map.226 = (bf16[512,2048]{1,0:T(8,128)(2,1)}, bf16[2048,512]{1,0:T(8,128)(2,1)}, bf16[2,2048,128]{2,1,0:T(8,128)(2,1)}, bf16[512,128]{1,0:T(8,128)(2,1)}) custom-call(bf16[512,1024]{1,0:T(8,128)(2,1)} %get-tuple-element.115.up_ref.up_stream_ref, f32[512,128]{1,0:T(8,128)} %compare_convert_fusion.lane_ref, ...), custom_call_target="tpu_custom_call" | custom-call | flops 2415919104 | bytes 14680064 | tf_op jit(solution)/shard_map/pallas_call | solution.py:619
  355.7 7.5 %shard_map.233 = bf16[5120,128]{1,0:T(8,128)(2,1)} custom-call(bf16[512,1024]{1,0:T(8,128)(2,1)} %get-tuple-element.115.up_ref.up_stream_ref, bf16[512,128]{1,0:T(8,128)(2,1)} %get-tuple-element.131.narrow_out_ref, bf16[512,2048]{1,0:T(8,128)(2,1)} %get-tuple-element.83.normed_ref.normed_out_ref, bf16[512,128]{1,0:T(8,128)(2,1)} %get-tuple-element.132.grad_narrow_ref, ...), custom_call_target="tpu_custom_call" | custom-call | flops 671088640 | bytes 5242880 | tf_op jit(solution)/shard_map/pallas_call | solution.py:763
  363.2 14.9 %pad_maximum_fusion = bf16[13824,128]{1,0:T(8,128)(2,1)S(1)} fusion(bf16[3584,128]{1,0:T(8,128)(2,1)S(1)} %copy-done.24, bf16[5120,128]{1,0:T(8,128)(2,1)S(1)} %copy-done.13, bf16[5120,128]{1,0:T(8,128)(2,1)} %shard_map.233), kind=kLoop, calls=%fused_computation | loop fusion | flops 10616832 | bytes 7077888 | tf_op jit(solution)/shard_map/concatenate | solution.py:1055
  381.0 10.5 %shard_map.227 = (bf16[512,2048]{1,0:T(8,128)(2,1)}, bf16[512,256]{1,0:T(8,128)(2,1)}, bf16[512,128]{1,0:T(8,128)(2,1)}) custom-call(bf16[2048,512]{1,0:T(8,128)(2,1)} %get-tuple-element.73.values_ref, bf16[2048,512]{1,0:T(8,128)(2,1)} %get-tuple-element.117.grad_ref, bf16[512,256]{1,0:T(8,128)(2,1)} %get-tuple-element.74.bc_ref, ...), custom_call_target="tpu_custom_call" | custom-call | flops 3758096384 | bytes 5242880 | tf_op jit(solution)/shard_map/pallas_call | solution.py:697
  396.8 7.9 %shard_map.230.part_ref = f32[512,1152]{1,0:T(8,128)} custom-call(bf16[512,2048]{1,0:T(8,128)(2,1)} %get-tuple-element.128.grad_ref.grad_gate_ref, bf16[2048,128]{1,0:T(8,128)(2,1)} %slice.250.up_ref, bf16[2048,256]{1,0:T(8,128)(2,1)} %copy-done.7, bf16[2048,256]{1,0:T(8,128)(2,1)} %collective-permute-done.13.second_ref, bf16[2048,256]{1,0:T(8,128)(2,1)} %copy-done.18, ...), custom_call_target="tpu_custom_call" | custom-call | flops 2415919104 | bytes 10485760 | tf_op jit(solution)/shard_map/pallas_call | solution.py:651
  404.7 3.6 collective-permute-done.41.grad_state_ref
  409.1 10.5 %shard_map.228 = (bf16[512,2048]{1,0:T(8,128)(2,1)}, bf16[512,256]{1,0:T(8,128)(2,1)}, bf16[512,128]{1,0:T(8,128)(2,1)}) custom-call(bf16[2048,512]{1,0:T(8,128)(2,1)} %get-tuple-element.73.values_ref, bf16[2048,512]{1,0:T(8,128)(2,1)} %get-tuple-element.117.grad_ref, ...), custom_call_target="tpu_custom_call", output_to_operand_aliasing={{0}: (13, {}), {1}: (14, {}), {2}: (15, {})} | custom-call | flops 3758096384 | bytes 5242880 | tf_op jit(solution)/shard_map/pallas_call | solution.py:697
  420.2 8.6 %shard_map.229.grad_ref.mixed_ref = bf16[512,2304]{1,0:T(8,128)(2,1)} custom-call(bf16[512,2048]{1,0:T(8,128)(2,1)} %get-tuple-element.123.grad_ref, bf16[512,256]{1,0:T(8,128)(2,1)} %get-tuple-element.124.grad_bc_ref, bf16[512,2048]{1,0:T(8,128)(2,1)} %get-tuple-element.125.slope_ref, bf16[512,256]{1,0:T(8,128)(2,1)} %get-tuple-element.126.slope_bc_ref, ...), custom_call_target="tpu_custom_call" | custom-call | flops 11796480 | bytes 7077888 | tf_op jit(solution)/shard_map/pallas_call | solution.py:724
  428.8 10.1 %shard_map.231 = (bf16[512,1024]{1,0:T(8,128)(2,1)}, bf16[512,128]{1,0:T(8,128)(2,1)}) custom-call(bf16[512,2304]{1,0:T(8,128)(2,1)} %shard_map.229.grad_ref.mixed_ref, bf16[512,128]{1,0:T(8,128)(2,1)} %get-tuple-element.127.raw_ref, f32[512,1152]{1,0:T(8,128)} %shard_map.230.part_ref, bf16[512,1024]{1,0:T(8,128)(2,1)} %dynamic-slice_bitcast_fusion.1.input_ref, ...), custom_call_target="tpu_custom_call" | custom-call | flops 2415919104 | bytes 23592960 | tf_op jit(solution)/shard_map/pallas_call | solution.py:667
  438.9 4.3 shard_map.232
  464.3 3.1 collective-permute-start.43
  472.2 8.8 %collective-permute-done.61 = bf16[1728,128]{1,0:T(8,128)(2,1)S(1)} collective-permute-done((bf16[1728,128]{1,0:T(8,128)(2,1)S(1)}, bf16[1728,128]{1,0:T(8,128)(2,1)S(1)}, u32[]{:S(2)}, u32[]{:S(2)}) %collective-permute-start.61) | collective-permute-done | bytes 442400 | tf_op jit(solution)/shard_map/ppermute | solution.py:924
  487.2 5.6 %collective-permute-done.64 = bf16[432,128]{1,0:T(8,128)(2,1)S(1)} collective-permute-done((bf16[432,128]{1,0:T(8,128)(2,1)S(1)}, bf16[432,128]{1,0:T(8,128)(2,1)S(1)}, u32[]{:S(2)}, u32[]{:S(2)}) %collective-permute-start.64) | collective-permute-done | bytes 110624 | tf_op jit(solution)/shard_map/ppermute | solution.py:924
  497.8 6.7 %collective-permute-done.67 = bf16[432,128]{1,0:T(8,128)(2,1)S(1)} collective-permute-done((bf16[432,128]{1,0:T(8,128)(2,1)S(1)}, bf16[432,128]{1,0:T(8,128)(2,1)S(1)}, u32[]{:S(2)}, u32[]{:S(2)}) %collective-permute-start.67) | collective-permute-done | bytes 110624 | tf_op jit(solution)/shard_map/ppermute | solution.py:924
  507.6 6.1 %collective-permute-done.68 = bf16[1728,128]{1,0:T(8,128)(2,1)S(1)} collective-permute-done((bf16[1728,128]{1,0:T(8,128)(2,1)S(1)}, bf16[1728,128]{1,0:T(8,128)(2,1)S(1)}, u32[]{:S(2)}, u32[]{:S(2)}) %collective-permute-start.68) | collective-permute-done | bytes 442400 | tf_op jit(solution)/shard_map/ppermute | solution.py:924
  514.6 9.9 %collective-permute-done.69 = bf16[1728,128]{1,0:T(8,128)(2,1)S(1)} collective-permute-done((bf16[1728,128]{1,0:T(8,128)(2,1)S(1)}, bf16[1728,128]{1,0:T(8,128)(2,1)S(1)}, u32[]{:S(2)}, u32[]{:S(2)}) %collective-permute-start.69) | collective-permute-done | bytes 442400 | tf_op jit(solution)/shard_map/ppermute | solution.py:924
  524.6 8.1 %collective-permute-done.70 = bf16[1728,128]{1,0:T(8,128)(2,1)S(1)} collective-permute-done((bf16[1728,128]{1,0:T(8,128)(2,1)S(1)}, bf16[1728,128]{1,0:T(8,128)(2,1)S(1)}, u32[]{:S(2)}, u32[]{:S(2)}) %collective-permute-start.70) | collective-permute-done | bytes 442400 | tf_op jit(solution)/shard_map/ppermute | solution.py:924
  532.8 10.1 %collective-permute-start.71 = (bf16[6912,128]{1,0:T(8,128)(2,1)S(1)}, bf16[6912,128]{1,0:T(8,128)(2,1)S(1)}, u32[]{:S(2)}, u32[]{:S(2)}) collective-permute-start(bf16[6912,128]{1,0:T(8,128)(2,1)S(1)} %bitcast.139), channel_id=1, source_target_pairs={{0,16},{16,0},{1,17},{17,1},{2,18},{18,2},{3,19},{19,3},{4,20},{20... | collective-permute-start | bytes 5308424 | tf_op jit(solution)/shard_map/ppermute | solution.py:919
  552.1 2.9 maximum_bitcast_fusion
  (408 shorter events, 171.6 us)
Async XLA Ops:
  3.8 42.0 %collective-permute-start = (f32[14688]{0:T(1024)}, f32[14688]{0:T(1024)}, u32[]{:S(2)}, u32[]{:S(2)}) collective-permute-start(f32[14688]{0:T(1024)} %concatenate.40), channel_id=1, source_target_pairs={{0,16},{16,0},{1,17},{17,1},{2,18},{18,2},{3,19},{19,3},{4,20},{20... | collective-permute-start | bytes 176264 | tf_op jit(solution)/shard_map/ppermute | solution.py:919
  3.8 62.4 %collective-permute-start.2 = (bf16[128,4384]{0,1:T(8,128)(2,1)}, bf16[128,4384]{0,1:T(8,128)(2,1)}, u32[]{:S(2)}, u32[]{:S(2)}) collective-permute-start(bf16[128,4384]{0,1:T(8,128)(2,1)} %bitcast.145), channel_id=1, source_target_pairs={{0,16},{16,0},{1,17},{17,1},{2,18},{18,2},{3,19},{19,3},{4,20},{20... | collective-permute-start | bytes 3366920 | tf_op jit(solution)/shard_map/ppermute | solution.py:919
  6.6 20.9 %collective-permute-start.12 = (bf16[2048,256]{1,0:T(8,128)(2,1)}, bf16[2048,256]{1,0:T(8,128)(2,1)}, u32[]{:S(2)}, u32[]{:S(2)}) collective-permute-start(bf16[2048,256]{1,0:T(8,128)(2,1)} %slice.251), channel_id=1, source_target_pairs={{0,16},{16,0},{1,17},{17,1},{2,18},{18,2},{3,19},{19,3},{4,20},{20... | collective-permute-start | bytes 3145736 | tf_op jit(solution)/shard_map/ppermute | solution.py:919
  7.2 11.9 %collective-permute-start.10 = (s32[8]{0:T(128)}, s32[8]{0:T(128)}, u32[]{:S(2)}, u32[]{:S(2)}) collective-permute-start(s32[8]{0:T(128)} %get-tuple-element.204), channel_id=1, source_target_pairs={{4,0},{8,4},{12,8},{5,1},{9,5},{13,9},{6,2},{10,6},{14,10},{7,3},{... | collective-permute-start | bytes 104 | tf_op jit(solution)/shard_map/ppermute | solution.py:24
  12.8 16.5 %collective-permute-start.4 = (bf16[2336,256]{1,0:T(8,128)(2,1)S(1)}, bf16[2336,256]{1,0:T(8,128)(2,1)}, u32[]{:S(2)}, u32[]{:S(2)}) collective-permute-start(bf16[2336,256]{1,0:T(8,128)(2,1)S(1)} %get-tuple-element.155.first_ref), channel_id=1, source_target_pairs={{0,1},{1,0},{2,3},{3,2},{16,18},{17,19},{18,16},{19,17},{4,5},{5,4... | collective-permute-start | bytes 3588104 | tf_op jit(solution)/shard_map/ppermute | solution.py:942
  23.8 24.5 %collective-permute-start.1 = (bf16[1024,128]{1,0:T(8,128)(2,1)S(1)}, bf16[1024,128]{1,0:T(8,128)(2,1)}, u32[]{:S(2)}, u32[]{:S(2)}) collective-permute-start(bf16[1024,128]{1,0:T(8,128)(2,1)S(1)} %bitcast.151), channel_id=1, source_target_pairs={{0,16},{16,0},{1,17},{17,1},{2,18},{18,2},{3,19},{19,3},{4,20},{20... | collective-permute-start | bytes 786440 | tf_op jit(solution)/shard_map/ppermute | solution.py:919
  29.3 14.1 %collective-permute-start.13 = (bf16[2048,256]{1,0:T(8,128)(2,1)S(1)}, bf16[2048,256]{1,0:T(8,128)(2,1)}, u32[]{:S(2)}, u32[]{:S(2)}) collective-permute-start(bf16[2048,256]{1,0:T(8,128)(2,1)S(1)} %get-tuple-element.80.first_ref), channel_id=1, source_target_pairs={{0,1},{1,0},{2,3},{3,2},{16,18},{17,19},{18,16},{19,17},{4,5},{5,4... | collective-permute-start | bytes 3145736 | tf_op jit(solution)/shard_map/ppermute | solution.py:942
  34.1 84.7 %collective-permute-start.17 = (bf16[2048,128]{1,0:T(8,128)(2,1)}, bf16[2048,128]{1,0:T(8,128)(2,1)}, u32[]{:S(2)}, u32[]{:S(2)}) collective-permute-start(bf16[2048,128]{1,0:T(8,128)(2,1)} %bitcast.146), channel_id=1, source_target_pairs={{0,16},{16,0},{1,17},{17,1},{2,18},{18,2},{3,19},{19,3},{4,20},{20... | collective-permute-start | bytes 1572872 | tf_op jit(solution)/shard_map/ppermute | solution.py:919
  43.4 20.8 %collective-permute-start.20 = (bf16[512,1024]{1,0:T(8,128)(2,1)S(1)}, bf16[512,1024]{1,0:T(8,128)(2,1)S(1)}, u32[]{:S(2)}, u32[]{:S(2)}) collective-permute-start(bf16[512,1024]{1,0:T(8,128)(2,1)S(1)} %get-tuple-element.84.first_ref), channel_id=1, source_target_pairs={{0,1},{1,0},{2,3},{3,2},{16,18},{17,19},{18,16},{19,17},{4,5},{5,4... | collective-permute-start | bytes 3145736 | tf_op jit(solution)/shard_map/ppermute | solution.py:942
  45.8 15.7 %collective-permute-start.6 = (bf16[1184,256]{1,0:T(8,128)(2,1)S(1)}, bf16[1184,256]{1,0:T(8,128)(2,1)S(1)}, u32[]{:S(2)}, u32[]{:S(2)}) collective-permute-start(bf16[1184,256]{1,0:T(8,128)(2,1)S(1)} %constant_dynamic-slice_fusion.19), channel_id=1, source_target_pairs={{0,2},{1,3},{2,0},{3,1},{16,17},{17,16},{18,19},{19,18},{4,6},{5,7... | collective-permute-start | bytes 1818632 | tf_op jit(solution)/shard_map/ppermute | solution.py:942
  48.3 66.9 %collective-permute-start.18 = (bf16[128,1024]{1,0:T(8,128)(2,1)}, bf16[128,1024]{1,0:T(8,128)(2,1)}, u32[]{:S(2)}, u32[]{:S(2)}) collective-permute-start(bf16[128,1024]{1,0:T(8,128)(2,1)} %bitcast.28), channel_id=1, source_target_pairs={{0,16},{16,0},{1,17},{17,1},{2,18},{18,2},{3,19},{19,3},{4,20},{20... | collective-permute-start | bytes 786440 | tf_op jit(solution)/shard_map/ppermute | solution.py:919
  61.5 21.0 %collective-permute-start.5 = (bf16[2336,256]{1,0:T(8,128)(2,1)}, bf16[2336,256]{1,0:T(8,128)(2,1)S(1)}, u32[]{:S(2)}, u32[]{:S(2)}) collective-permute-start(bf16[2336,256]{1,0:T(8,128)(2,1)} %collective-permute-done.4.second_ref), channel_id=1, source_target_pairs={{0,16},{16,0},{1,17},{17,1},{2,18},{18,2},{3,19},{19,3},{4,20},{20... | collective-permute-start | bytes 3588104 | tf_op jit(solution)/shard_map/ppermute | solution.py:919
  64.3 18.5 %collective-permute-start.7 = (bf16[1184,256]{1,0:T(8,128)(2,1)S(1)}, bf16[1184,256]{1,0:T(8,128)(2,1)S(1)}, u32[]{:S(2)}, u32[]{:S(2)}) collective-permute-start(bf16[1184,256]{1,0:T(8,128)(2,1)S(1)} %collective-permute-done.6.near_ref), channel_id=1, source_target_pairs={{0,16},{16,0},{1,17},{17,1},{2,18},{18,2},{3,19},{19,3},{4,20},{20... | collective-permute-start | bytes 1818632 | tf_op jit(solution)/shard_map/ppermute | solution.py:919
  66.3 15.5 %collective-permute-start.24 = (bf16[2336,256]{1,0:T(8,128)(2,1)S(1)}, bf16[2336,256]{1,0:T(8,128)(2,1)S(1)}, u32[]{:S(2)}, u32[]{:S(2)}) collective-permute-start(bf16[2336,256]{1,0:T(8,128)(2,1)S(1)} %copy-done.15), channel_id=1, source_target_pairs={{0,1},{1,0},{2,3},{3,2},{16,18},{17,19},{18,16},{19,17},{4,5},{5,4... | collective-permute-start | bytes 3588104 | tf_op jit(solution)/shard_map/ppermute | solution.py:942
  81.8 36.6 %collective-permute-start.15 = (bf16[1024,256]{1,0:T(8,128)(2,1)}, bf16[1024,256]{1,0:T(8,128)(2,1)}, u32[]{:S(2)}, u32[]{:S(2)}) collective-permute-start(bf16[1024,256]{1,0:T(8,128)(2,1)} %constant_dynamic-slice_fusion.18), channel_id=1, source_target_pairs={{0,2},{1,3},{2,0},{3,1},{16,17},{17,16},{18,19},{19,18},{4,6},{5,7... | collective-permute-start | bytes 1572872 | tf_op jit(solution)/shard_map/ppermute | solution.py:942
  82.5 37.6 %collective-permute-start.30 = (bf16[2048,256]{1,0:T(8,128)(2,1)S(1)}, bf16[2048,256]{1,0:T(8,128)(2,1)}, u32[]{:S(2)}, u32[]{:S(2)}) collective-permute-start(bf16[2048,256]{1,0:T(8,128)(2,1)S(1)} %get-tuple-element.96.first_ref), channel_id=1, source_target_pairs={{0,1},{1,0},{2,3},{3,2},{16,18},{17,19},{18,16},{19,17},{4,5},{5,4... | collective-permute-start | bytes 3145736 | tf_op jit(solution)/shard_map/ppermute | solution.py:942
  100.4 31.1 %collective-permute-start.14 = (bf16[2048,256]{1,0:T(8,128)(2,1)}, bf16[2048,256]{1,0:T(8,128)(2,1)S(1)}, u32[]{:S(2)}, u32[]{:S(2)}) collective-permute-start(bf16[2048,256]{1,0:T(8,128)(2,1)} %collective-permute-done.13.second_ref), channel_id=1, source_target_pairs={{0,16},{16,0},{1,17},{17,1},{2,18},{18,2},{3,19},{19,3},{4,20},{20... | collective-permute-start | bytes 3145736 | tf_op jit(solution)/shard_map/ppermute | solution.py:919
  115.1 15.7 %collective-permute-start.11 = (bf16[2048,128]{1,0:T(8,128)(2,1)S(1)}, bf16[2048,128]{1,0:T(8,128)(2,1)S(1)}, u32[]{:S(2)}, u32[]{:S(2)}) collective-permute-start(bf16[2048,128]{1,0:T(8,128)(2,1)S(1)} %get-tuple-element.180), channel_id=1, source_target_pairs={{0,4},{4,8},{8,12},{1,5},{5,9},{9,13},{2,6},{6,10},{10,14},{3,7},{... | collective-permute-start | bytes 1572872 | tf_op jit(solution)/shard_map/ppermute | solution.py:24
  118.4 13.1 %collective-permute-start.16 = (bf16[1024,256]{1,0:T(8,128)(2,1)}, bf16[1024,256]{1,0:T(8,128)(2,1)S(1)}, u32[]{:S(2)}, u32[]{:S(2)}) collective-permute-start(bf16[1024,256]{1,0:T(8,128)(2,1)} %collective-permute-done.15.near_ref), channel_id=1, source_target_pairs={{0,16},{16,0},{1,17},{17,1},{2,18},{18,2},{3,19},{19,3},{4,20},{20... | collective-permute-start | bytes 1572872 | tf_op jit(solution)/shard_map/ppermute | solution.py:919
  118.8 19.0 %collective-permute-start.22 = (bf16[256,1024]{1,0:T(8,128)(2,1)S(1)}, bf16[256,1024]{1,0:T(8,128)(2,1)S(1)}, u32[]{:S(2)}, u32[]{:S(2)}) collective-permute-start(bf16[256,1024]{1,0:T(8,128)(2,1)S(1)} %constant_dynamic-slice_fusion.17), channel_id=1, source_target_pairs={{0,2},{1,3},{2,0},{3,1},{16,17},{17,16},{18,19},{19,18},{4,6},{5,7... | collective-permute-start | bytes 1572872 | tf_op jit(solution)/shard_map/ppermute | solution.py:942
  120.1 18.5 %collective-permute-start.26 = (bf16[1184,256]{1,0:T(8,128)(2,1)S(1)}, bf16[1184,256]{1,0:T(8,128)(2,1)}, u32[]{:S(2)}, u32[]{:S(2)}) collective-permute-start(bf16[1184,256]{1,0:T(8,128)(2,1)S(1)} %constant_dynamic-slice_fusion.16), channel_id=1, source_target_pairs={{0,2},{1,3},{2,0},{3,1},{16,17},{17,16},{18,19},{19,18},{4,6},{5,7... | collective-permute-start | bytes 1818632 | tf_op jit(solution)/shard_map/ppermute | solution.py:942
  130.8 37.8 %collective-permute-start.21 = (bf16[512,1024]{1,0:T(8,128)(2,1)S(1)}, bf16[512,1024]{1,0:T(8,128)(2,1)S(1)}, u32[]{:S(2)}, u32[]{:S(2)}) collective-permute-start(bf16[512,1024]{1,0:T(8,128)(2,1)S(1)} %collective-permute-done.20.second_ref), channel_id=1, source_target_pairs={{0,16},{16,0},{1,17},{17,1},{2,18},{18,2},{3,19},{19,3},{4,20},{20... | collective-permute-start | bytes 3145736 | tf_op jit(solution)/shard_map/ppermute | solution.py:919
  131.5 46.6 %collective-permute-start.25 = (bf16[2336,256]{1,0:T(8,128)(2,1)}, bf16[2336,256]{1,0:T(8,128)(2,1)}, u32[]{:S(2)}, u32[]{:S(2)}) collective-permute-start(bf16[2336,256]{1,0:T(8,128)(2,1)} %copy-done.26), channel_id=1, source_target_pairs={{0,16},{16,0},{1,17},{17,1},{2,18},{18,2},{3,19},{19,3},{4,20},{20... | collective-permute-start | bytes 3588104 | tf_op jit(solution)/shard_map/ppermute | solution.py:919
  131.6 60.2 %collective-permute-start.34 = (bf16[512,1024]{1,0:T(8,128)(2,1)S(1)}, bf16[512,1024]{1,0:T(8,128)(2,1)S(1)}, u32[]{:S(2)}, u32[]{:S(2)}) collective-permute-start(bf16[512,1024]{1,0:T(8,128)(2,1)S(1)} %copy-done.10), channel_id=1, source_target_pairs={{0,1},{1,0},{2,3},{3,2},{16,18},{17,19},{18,16},{19,17},{4,5},{5,4... | collective-permute-start | bytes 3145736 | tf_op jit(solution)/shard_map/ppermute | solution.py:942
  137.8 30.3 %collective-permute-start.23 = (bf16[256,1024]{1,0:T(8,128)(2,1)S(1)}, bf16[256,1024]{1,0:T(8,128)(2,1)S(1)}, u32[]{:S(2)}, u32[]{:S(2)}) collective-permute-start(bf16[256,1024]{1,0:T(8,128)(2,1)S(1)} %collective-permute-done.22.near_ref), channel_id=1, source_target_pairs={{0,16},{16,0},{1,17},{17,1},{2,18},{18,2},{3,19},{19,3},{4,20},{20... | collective-permute-start | bytes 1572872 | tf_op jit(solution)/shard_map/ppermute | solution.py:919
  138.6 39.5 %collective-permute-start.27 = (bf16[1184,256]{1,0:T(8,128)(2,1)}, bf16[1184,256]{1,0:T(8,128)(2,1)S(1)}, u32[]{:S(2)}, u32[]{:S(2)}) collective-permute-start(bf16[1184,256]{1,0:T(8,128)(2,1)} %collective-permute-done.26.near_ref), channel_id=1, source_target_pairs={{0,16},{16,0},{1,17},{17,1},{2,18},{18,2},{3,19},{19,3},{4,20},{20... | collective-permute-start | bytes 1818632 | tf_op jit(solution)/shard_map/ppermute | solution.py:919
  168.1 37.1 %collective-permute-start.32 = (bf16[1024,256]{1,0:T(8,128)(2,1)}, bf16[1024,256]{1,0:T(8,128)(2,1)}, u32[]{:S(2)}, u32[]{:S(2)}) collective-permute-start(bf16[1024,256]{1,0:T(8,128)(2,1)} %constant_dynamic-slice_fusion.15), channel_id=1, source_target_pairs={{0,2},{1,3},{2,0},{3,1},{16,17},{17,16},{18,19},{19,18},{4,6},{5,7... | collective-permute-start | bytes 1572872 | tf_op jit(solution)/shard_map/ppermute | solution.py:942
  177.1 38.6 %collective-permute-start.31 = (bf16[2048,256]{1,0:T(8,128)(2,1)}, bf16[2048,256]{1,0:T(8,128)(2,1)S(1)}, u32[]{:S(2)}, u32[]{:S(2)}) collective-permute-start(bf16[2048,256]{1,0:T(8,128)(2,1)} %collective-permute-done.30.second_ref), channel_id=1, source_target_pairs={{0,16},{16,0},{1,17},{17,1},{2,18},{18,2},{3,19},{19,3},{4,20},{20... | collective-permute-start | bytes 3145736 | tf_op jit(solution)/shard_map/ppermute | solution.py:919
  192.7 17.3 %collective-permute-start.36 = (bf16[256,1024]{1,0:T(8,128)(2,1)}, bf16[256,1024]{1,0:T(8,128)(2,1)}, u32[]{:S(2)}, u32[]{:S(2)}) collective-permute-start(bf16[256,1024]{1,0:T(8,128)(2,1)} %constant_dynamic-slice_fusion.14), channel_id=1, source_target_pairs={{0,2},{1,3},{2,0},{3,1},{16,17},{17,16},{18,19},{19,18},{4,6},{5,7... | collective-permute-start | bytes 1572872 | tf_op jit(solution)/shard_map/ppermute | solution.py:942
  205.9 38.1 %collective-permute-start.35 = (bf16[512,1024]{1,0:T(8,128)(2,1)S(1)}, bf16[512,1024]{1,0:T(8,128)(2,1)S(1)}, u32[]{:S(2)}, u32[]{:S(2)}) collective-permute-start(bf16[512,1024]{1,0:T(8,128)(2,1)S(1)} %collective-permute-done.34.second_ref), channel_id=1, source_target_pairs={{0,16},{16,0},{1,17},{17,1},{2,18},{18,2},{3,19},{19,3},{4,20},{20... | collective-permute-start | bytes 3145736 | tf_op jit(solution)/shard_map/ppermute | solution.py:919
  208.0 25.9 %collective-permute-start.29 = (bf16[2048,128]{1,0:T(8,128)(2,1)S(1)}, bf16[2048,128]{1,0:T(8,128)(2,1)S(1)}, u32[]{:S(2)}, u32[]{:S(2)}) collective-permute-start(bf16[2048,128]{1,0:T(8,128)(2,1)S(1)} %get-tuple-element.178), channel_id=1, source_target_pairs={{0,4},{4,8},{8,12},{1,5},{5,9},{9,13},{2,6},{6,10},{10,14},{3,7},{... | collective-permute-start | bytes 1572872 | tf_op jit(solution)/shard_map/ppermute | solution.py:24
  210.0 34.0 %collective-permute-start.37 = (bf16[256,1024]{1,0:T(8,128)(2,1)}, bf16[256,1024]{1,0:T(8,128)(2,1)S(1)}, u32[]{:S(2)}, u32[]{:S(2)}) collective-permute-start(bf16[256,1024]{1,0:T(8,128)(2,1)} %collective-permute-done.36.near_ref), channel_id=1, source_target_pairs={{0,16},{16,0},{1,17},{17,1},{2,18},{18,2},{3,19},{19,3},{4,20},{20... | collective-permute-start | bytes 1572872 | tf_op jit(solution)/shard_map/ppermute | solution.py:919
  274.8 42.0 %collective-permute-start.40 = (bf16[8,2304]{1,0:T(8,128)(2,1)S(1)}, bf16[8,2304]{1,0:T(8,128)(2,1)S(1)}, u32[]{:S(2)}, u32[]{:S(2)}) collective-permute-start(bf16[8,2304]{1,0:T(8,128)(2,1)S(1)} %multiply_convert_fusion.1), channel_id=1, source_target_pairs={{4,0},{8,4},{12,8},{5,1},{9,5},{13,9},{6,2},{10,6},{14,10},{7,3},{... | collective-permute-start | bytes 110600 | tf_op jit(solution)/shard_map/ppermute | solution.py:24
  278.3 27.2 %collective-permute-start.39 = (bf16[2048,128]{1,0:T(8,128)(2,1)S(1)}, bf16[2048,128]{1,0:T(8,128)(2,1)S(1)}, u32[]{:S(2)}, u32[]{:S(2)}) collective-permute-start(bf16[2048,128]{1,0:T(8,128)(2,1)S(1)} %get-tuple-element.174), channel_id=1, source_target_pairs={{4,0},{8,4},{12,8},{5,1},{9,5},{13,9},{6,2},{10,6},{14,10},{7,3},{... | collective-permute-start | bytes 1572872 | tf_op jit(solution)/shard_map/ppermute | solution.py:24
  288.9 157.4 %collective-permute-start.38 = (bf16[512,1024]{1,0:T(8,128)(2,1)S(1)}, bf16[512,1024]{1,0:T(8,128)(2,1)}, u32[]{:S(2)}, u32[]{:S(2)}) collective-permute-start(bf16[512,1024]{1,0:T(8,128)(2,1)S(1)} %broadcast_select_fusion.9), channel_id=1, source_target_pairs={{0,16},{16,0},{1,17},{17,1},{2,18},{18,2},{3,19},{19,3},{4,20},{20... | collective-permute-start | bytes 3145736 | tf_op jit(solution)/shard_map/ppermute | solution.py:919
  379.5 79.8 %collective-permute-start.58 = (bf16[6912,128]{1,0:T(8,128)(2,1)}, bf16[6912,128]{1,0:T(8,128)(2,1)}, u32[]{:S(2)}, u32[]{:S(2)}) collective-permute-start(bf16[6912,128]{1,0:T(8,128)(2,1)} %constant_dynamic-slice_fusion.6), channel_id=1, source_target_pairs={{0,16},{16,0},{1,17},{17,1},{2,18},{18,2},{3,19},{19,3},{4,20},{20... | collective-permute-start | bytes 5308424 | tf_op jit(solution)/shard_map/ppermute | solution.py:919
  392.9 15.4 %collective-permute-start.41 = (bf16[2048,128]{1,0:T(8,128)(2,1)S(1)}, bf16[2048,128]{1,0:T(8,128)(2,1)S(1)}, u32[]{:S(2)}, u32[]{:S(2)}) collective-permute-start(bf16[2048,128]{1,0:T(8,128)(2,1)S(1)} %get-tuple-element.172), channel_id=1, source_target_pairs={{4,0},{8,4},{12,8},{5,1},{9,5},{13,9},{6,2},{10,6},{14,10},{7,3},{... | collective-permute-start | bytes 1572872 | tf_op jit(solution)/shard_map/ppermute | solution.py:24
  394.9 24.7 %collective-permute-start.42 = (bf16[8,2304]{1,0:T(8,128)(2,1)S(1)}, bf16[8,2304]{1,0:T(8,128)(2,1)S(1)}, u32[]{:S(2)}, u32[]{:S(2)}) collective-permute-start(bf16[8,2304]{1,0:T(8,128)(2,1)S(1)} %multiply_convert_fusion), channel_id=1, source_target_pairs={{4,0},{8,4},{12,8},{5,1},{9,5},{13,9},{6,2},{10,6},{14,10},{7,3},{... | collective-permute-start | bytes 110600 | tf_op jit(solution)/shard_map/ppermute | solution.py:24
  462.6 18.4 %collective-permute-start.61 = (bf16[1728,128]{1,0:T(8,128)(2,1)S(1)}, bf16[1728,128]{1,0:T(8,128)(2,1)S(1)}, u32[]{:S(2)}, u32[]{:S(2)}) collective-permute-start(bf16[1728,128]{1,0:T(8,128)(2,1)S(1)} %get-tuple-element.169), channel_id=1, source_target_pairs={{0,3},{1,2},{2,1},{3,0},{4,7},{5,6},{6,5},{7,4},{8,11},{9,10},{10,... | collective-permute-start | bytes 1327112 | tf_op jit(solution)/shard_map/ppermute | solution.py:924
  464.3 78.9 %collective-permute-start.43 = (bf16[512,1024]{1,0:T(8,128)(2,1)S(1)}, bf16[512,1024]{1,0:T(8,128)(2,1)S(1)}, u32[]{:S(2)}, u32[]{:S(2)}) collective-permute-start(bf16[512,1024]{1,0:T(8,128)(2,1)S(1)} %broadcast_select_fusion.7), channel_id=1, source_target_pairs={{0,16},{16,0},{1,17},{17,1},{2,18},{18,2},{3,19},{19,3},{4,20},{20... | collective-permute-start | bytes 3145736 | tf_op jit(solution)/shard_map/ppermute | solution.py:919
  467.5 15.3 %collective-permute-start.51 = (bf16[112,128]{1,0:T(8,128)(2,1)S(1)}, bf16[112,128]{1,0:T(8,128)(2,1)S(1)}, u32[]{:S(2)}, u32[]{:S(2)}) collective-permute-start(bf16[112,128]{1,0:T(8,128)(2,1)S(1)} %get-tuple-element.149), channel_id=1, source_target_pairs={{0,4},{4,0},{8,12},{12,8},{1,5},{5,1},{9,13},{13,9},{2,6},{6,2},{1... | collective-permute-start | bytes 86024 | tf_op jit(solution)/shard_map/ppermute | solution.py:924
  471.0 22.1 %collective-permute-start.52 = (bf16[112,128]{1,0:T(8,128)(2,1)S(1)}, bf16[112,128]{1,0:T(8,128)(2,1)S(1)}, u32[]{:S(2)}, u32[]{:S(2)}) collective-permute-start(bf16[112,128]{1,0:T(8,128)(2,1)S(1)} %get-tuple-element.149), channel_id=1, source_target_pairs={{0,8},{4,12},{8,0},{12,4},{1,9},{5,13},{9,1},{13,5},{2,10},{6,14},... | collective-permute-start | bytes 86024 | tf_op jit(solution)/shard_map/ppermute | solution.py:924
  485.0 19.6 %collective-permute-start.53 = (bf16[112,128]{1,0:T(8,128)(2,1)S(1)}, bf16[112,128]{1,0:T(8,128)(2,1)S(1)}, u32[]{:S(2)}, u32[]{:S(2)}) collective-permute-start(bf16[112,128]{1,0:T(8,128)(2,1)S(1)} %get-tuple-element.149), channel_id=1, source_target_pairs={{0,12},{4,8},{8,4},{12,0},{1,13},{5,9},{9,5},{13,1},{2,14},{6,10},... | collective-permute-start | bytes 86024 | tf_op jit(solution)/shard_map/ppermute | solution.py:924
  504.6 38.4 %collective-permute-start.54 = (bf16[448,128]{1,0:T(8,128)(2,1)S(1)}, bf16[448,128]{1,0:T(8,128)(2,1)S(1)}, u32[]{:S(2)}, u32[]{:S(2)}) collective-permute-start(bf16[448,128]{1,0:T(8,128)(2,1)S(1)} %bitcast.147), channel_id=1, source_target_pairs={{0,1},{1,0},{2,3},{3,2},{4,5},{5,4},{6,7},{7,6},{8,9},{9,8},{10,11... | collective-permute-start | bytes 344072 | tf_op jit(solution)/shard_map/ppermute | solution.py:924
  506.1 37.0 %collective-permute-start.55 = (bf16[448,128]{1,0:T(8,128)(2,1)S(1)}, bf16[448,128]{1,0:T(8,128)(2,1)S(1)}, u32[]{:S(2)}, u32[]{:S(2)}) collective-permute-start(bf16[448,128]{1,0:T(8,128)(2,1)S(1)} %bitcast.148), channel_id=1, source_target_pairs={{0,2},{1,3},{2,0},{3,1},{4,6},{5,7},{6,4},{7,5},{8,10},{9,11},{10,... | collective-permute-start | bytes 344072 | tf_op jit(solution)/shard_map/ppermute | solution.py:924
  506.7 36.4 %collective-permute-start.56 = (bf16[448,128]{1,0:T(8,128)(2,1)S(1)}, bf16[448,128]{1,0:T(8,128)(2,1)S(1)}, u32[]{:S(2)}, u32[]{:S(2)}) collective-permute-start(bf16[448,128]{1,0:T(8,128)(2,1)S(1)} %bitcast.149), channel_id=1, source_target_pairs={{0,3},{1,2},{2,1},{3,0},{4,7},{5,6},{6,5},{7,4},{8,11},{9,10},{10,... | collective-permute-start | bytes 344072 | tf_op jit(solution)/shard_map/ppermute | solution.py:924
  513.8 10.8 %collective-permute-start.69 = (bf16[1728,128]{1,0:T(8,128)(2,1)S(1)}, bf16[1728,128]{1,0:T(8,128)(2,1)S(1)}, u32[]{:S(2)}, u32[]{:S(2)}) collective-permute-start(bf16[1728,128]{1,0:T(8,128)(2,1)S(1)} %bitcast.143), channel_id=1, source_target_pairs={{0,2},{1,3},{2,0},{3,1},{4,6},{5,7},{6,4},{7,5},{8,10},{9,11},{10,... | collective-permute-start | bytes 1327112 | tf_op jit(solution)/shard_map/ppermute | solution.py:924
  532.8 14.2 %collective-permute-start.71 = (bf16[6912,128]{1,0:T(8,128)(2,1)S(1)}, bf16[6912,128]{1,0:T(8,128)(2,1)S(1)}, u32[]{:S(2)}, u32[]{:S(2)}) collective-permute-start(bf16[6912,128]{1,0:T(8,128)(2,1)S(1)} %bitcast.139), channel_id=1, source_target_pairs={{0,16},{16,0},{1,17},{17,1},{2,18},{18,2},{3,19},{19,3},{4,20},{20... | collective-permute-start | bytes 5308424 | tf_op jit(solution)/shard_map/ppermute | solution.py:919
  (101 other events, 857.2 us)
where the time goes:
time: 566 us; the launch traced here: 555 us
  Pallas kernels  252 us (45%)
  waiting for transfers between devices  95.4 us (17%)
  starting transfers between devices  90.9 us (16%)
  local copies, waits for them, and re-layouts  64.9 us (11%)
  other arithmetic  49.7 us (9%)
    ppermute x24, waiting for transfers between devices, exchange(): lax.ppermute(value, axis, [(place, place ^ distance) for place in range(c...  56.1 us
    pallas_call x4, Pallas kernels, scan_backward(): pl.pallas_call(functools.partial(scan_back_kernel, s.head, s.heads, s.sta...  42 us
    pallas_call x4, Pallas kernels, scan_forward(): pl.pallas_call(functools.partial(scan_kernel, s.head, s.state), grid=(s.g...  36.8 us
    ppermute x26, starting transfers between devices, swap(): return lax.ppermute(value, 'section', [(0, 1), (1, 0)])  34.2 us
    pallas_call x2, Pallas kernels, out_backward(): pl.pallas_call(functools.partial(out_back_kernel, s.head, s.heads, s.stat...  31.1 us
    ppermute x10, starting transfers between devices, from_behind(): lax.ppermute(value, axis, [(source, source + steps) for source in range(i...  27.5 us
    ppermute x12, waiting for transfers between devices, across(): return lax.ppermute(value, ('section', 'wshard'), pairs)  23.8 us
    pallas_call x2, Pallas kernels, mixed_in_backward(): pl.pallas_call(functools.partial(mixed_in_back_kernel, s.mixed), grid=(s....  20 us
  transfers between devices with their start and end apart: 72, of which 22 were waited for; matrix products, arithmetic and copies ran while one was open for 17% of the time, Pallas kernels for 41%

commit v1 on v0

v1 whole, which is shorter than its diff:
```python
import functools

import jax
import jax.numpy as jnp
from jax import lax
from jax.experimental import pallas as pl
from jax.experimental.pallas import tpu as pltpu
from jax.sharding import PartitionSpec as P

SPAN = 256
RANK = 16
LANES = 128
DOCS_PER_BLOCK = 8
EPSILON = 1e-05
EXACT = lax.Precision.HIGHEST
SEQ, WSHARD, SECTION = "seq", "wshard", "section"
BF16 = jnp.bfloat16
F32 = jnp.float32
PARAMS = pltpu.CompilerParams(vmem_limit_bytes=20 * 1024 * 1024)


class Bag:
    def __init__(self, **fields):
        self.__dict__.update(fields)


def tie(value, *others):
    return lax.optimization_barrier((value, *others))[0]


def from_behind(value, axis, steps):
    count = lax.axis_size(axis)
    initial, last = (max(0, -steps), min(count, count - steps))
    return lax.ppermute(value, axis, [(source, source + steps) for source in range(initial, last)])


def dot(left, right):
    return jnp.dot(left, right, preferred_element_type=F32)


def dot_last(left, right):
    return lax.dot_general(left, right, (((1,), (1,)), ((), ())), preferred_element_type=F32)


def dot_first(left, right):
    return lax.dot_general(left, right, (((0,), (0,)), ((), ())), preferred_element_type=F32)


def rms_rate(values):
    return lax.rsqrt(jnp.mean(values * values, axis=-1, keepdims=True) + EPSILON)


def sigmoid(v):
    return 1.0 / (1.0 + jnp.exp(-v))


def lower_ones(shape):
    rows = lax.broadcasted_iota(jnp.int32, shape, 0)
    columns = lax.broadcasted_iota(jnp.int32, shape, 1)
    return rows <= columns


def conv_rows(rows, rim, weight, offset, valid):
    length = rows.shape[0]
    extended = jnp.concatenate([rim, rows], axis=0)
    taps = weight.shape[0]
    total = offset + weight[taps - 1 : taps] * rows
    for back in range(1, taps):
        shifted = extended[8 - back : 8 - back + length]
        total = total + jnp.where(valid >= back, shifted, 0.0) * weight[taps - 1 - back : taps - back]
    gate = sigmoid(total)
    active = total * gate
    return active, gate + active * (1.0 - gate)


def taps_at(vector_ref, places, first, width):
    rows = [vector_ref[:, pl.ds(pl.multiple_of(place + first, LANES), width)] for place in places]
    return jnp.concatenate(rows[:-1], axis=0), rows[-1]


def conv_kernel(
    spans, head, heads, state, places,
    mixed_ref, mixed_bc_ref, rim_ref, rim_bc_ref, vector_ref, valid_ref, raw_ref, head_ref, token_ref,
    values_ref, slope_ref, bc_ref, slope_bc_ref, step_ref, decay_ref, sig_ref, *rest,
):
    state_refs, tail_ref = rest[:-1], rest[-1]
    group = pl.program_id(0)
    valid = valid_ref[:, :1]
    width = mixed_ref.shape[1]
    heads_here = width // head

    @pl.when(group == 0)
    def _():
        weight, offset = taps_at(vector_ref, places, pl.num_programs(0) * width, 2 * state)
        active, slope = conv_rows(
            mixed_bc_ref[...].astype(F32), rim_bc_ref[...].astype(F32), weight, offset, valid
        )
        bc_ref[...] = active.astype(BF16)
        slope_bc_ref[...] = slope.astype(BF16)
        raw = raw_ref[...].astype(F32).T[:heads] + head_ref[:, 2:3]
        step = (jnp.maximum(raw, 0.0) + jnp.log1p(jnp.exp(-jnp.abs(raw)))).astype(BF16).astype(F32)
        step_ref[...] = step
        sig_ref[...] = sigmoid(raw)
        drop = -(step * head_ref[:, :1])
        ones = lower_ones((SPAN, SPAN)).astype(F32)
        for span in range(spans):
            here = slice(span * SPAN, (span + 1) * SPAN)
            decay = jnp.dot(drop[:, here], ones, precision=EXACT, preferred_element_type=F32)
            decay_ref[:, here] = decay
            tail = jnp.exp(decay[:, SPAN - 1 :] - decay) * token_ref[span][1:2]
            tail_ref[:, here] = tail * step[:, here]

    weight, offset = taps_at(vector_ref, places, group * width, width)
    active, slope = conv_rows(
        mixed_ref[...].astype(F32), rim_ref[...].astype(F32), weight, offset, valid
    )
    slope_ref[...] = slope.astype(BF16)
    turned = active.T
    low = turned.astype(BF16)
    values_ref[...] = low
    low = low.astype(F32)
    first = pl.multiple_of(group * heads_here, heads_here)
    tail_rows = tail_ref[pl.ds(first, heads_here), :]
    for span in range(spans):
        here = slice(span * SPAN, (span + 1) * SPAN)
        driven = jnp.concatenate(
            [
                (low[place * head : (place + 1) * head, here] * tail_rows[place : place + 1, here]).astype(BF16)
                for place in range(heads_here)
            ],
            axis=0,
        )
        state_refs[span][...] = dot(driven, bc_ref[here, :state]).astype(BF16)


def scan_kernel(
    head, state, gain,
    values_ref, bc_ref, step_ref, decay_ref, token_ref, doc_column_ref, doc_row_ref, state_ref, head_ref, gate_ref,
    vector_ref, *rest,
):
    mixed_ref, normed_ref, score_ref, scanned_ref = rest[-4:]
    group, groups = pl.program_id(0), pl.num_programs(0)
    width = values_ref.shape[0]
    heads_here = width // head

    @pl.when(group == 0)
    def _():
        score = dot_last(bc_ref[:, :state], bc_ref[:, state:])
        same = (doc_column_ref[:, :1] == doc_row_ref[:1]) & lower_ones((SPAN, SPAN))
        score_ref[...] = jnp.where(same, score, 0.0)

    decay, step = decay_ref[...], step_ref[...]
    carry = jnp.exp(decay) * token_ref[0][:1]
    columns = jnp.concatenate([decay] * (LANES // heads_here), axis=0).T
    out_map = bc_ref[:, state:]
    parts = []
    for place in range(heads_here):
        rows = slice(place * head, (place + 1) * head)
        one = slice(place, place + 1)
        kernel = (jnp.exp(jnp.minimum(decay[one] - columns[:, one], 0.0)) * score_ref[...]).astype(BF16)
        values = values_ref[rows].astype(F32)
        driven = (values * step[one]).astype(BF16)
        before = dot_last(state_ref[rows], out_map) * carry[one]
        parts.append(dot(driven, kernel) + before + head_ref[one, 1:2] * values)
    turned = jnp.concatenate(parts, axis=0).T
    scanned_ref[:, pl.ds(pl.multiple_of(group * width, width), width)] = turned.astype(BF16)

    @pl.when(group == groups - 1)
    def _():
        def rows_at(index, _):
            rows = pl.ds(pl.multiple_of(index * 16, 16), 16)
            mixed = scanned_ref[rows, :]
            mixed_ref[rows, :] = mixed
            gate = gate_ref[rows, :].astype(F32)
            gated = mixed.astype(F32) * (gate * sigmoid(gate))
            normed_ref[rows, :] = (gated * rms_rate(gated) * vector_ref[:, gain : gain + gated.shape[1]]).astype(BF16)
            return 0

        lax.fori_loop(0, SPAN // 16, rows_at, 0)


def out_back_kernel(
    head, heads, state, gain,
    up_ref, lane_ref, up_out_ref, down_out_ref, first_ref, second_ref, third_ref, near_ref, far_ref, where_ref,
    mixed_ref, gate_ref, vector_ref, decay_ref, token_ref, bc_ref,
    project_ref, turned_ref, narrow_ref, *rest,
):
    state_refs, grad_ref, grad_mixed_ref = rest[:-2], rest[-2], rest[-1]
    width = mixed_ref.shape[1]
    up = up_ref[...]
    narrow = (dot_last(up, up_out_ref[...]) * lane_ref[...]).astype(BF16)
    narrow_ref[...] = narrow
    left = jnp.concatenate([up, narrow], axis=1)
    for offset, part in out_places(where_ref, (first_ref, second_ref, third_ref), near_ref, far_ref):
        here = pl.ds(offset, part.shape[0])
        grad_ref[:, here] = dot_last(left, jnp.concatenate([part[...], down_out_ref[here, :]], axis=1))

    def rows_at(index, _):
        rows = pl.ds(pl.multiple_of(index * 16, 16), 16)
        mixed = mixed_ref[rows, :].astype(F32)
        gate = gate_ref[rows, :].astype(F32)
        share = sigmoid(gate)
        silu = gate * share
        gated = mixed * silu
        grad = grad_ref[rows, :] * vector_ref[:, gain : gain + width]
        rate = rms_rate(gated)
        pull = jnp.mean(gated * grad, axis=-1, keepdims=True) * rate * rate * rate
        grad_gated = rate * grad - gated * pull
        project_ref[rows, :] = (grad_gated * mixed * (share + silu * (1.0 - share))).astype(BF16)
        grad_mixed_ref[rows, :] = (grad_gated * silu).astype(BF16)
        return 0

    lax.fori_loop(0, SPAN // 16, rows_at, 0)
    carry = jnp.exp(decay_ref[...]) * token_ref[0][:1]
    out_map = bc_ref[:, state:]
    wide = 512
    for first in range(0, width, wide):
        low = grad_mixed_ref[:, first : first + wide].astype(F32).T
        turned_ref[first : first + wide, :] = low.astype(BF16)
        scaled = [
            (low[place * head : (place + 1) * head] * carry[first // head + place : first // head + place + 1]).astype(BF16)
            for place in range(wide // head)
        ]
        local = dot(jnp.concatenate(scaled, axis=0), out_map).astype(BF16)
        for span, state_ref in enumerate(state_refs):

            @pl.when(pl.program_id(0) == span)
            def _(state_ref=state_ref, first=first, local=local):
                state_ref[first : first + wide, :] = local


def aligned(value, unit):
    return pl.multiple_of(value * unit, unit)


def out_places(where_ref, parts, near, far):
    rows, half = parts[0].shape[0], near.shape[0]
    places = [(aligned(where_ref[place], rows), part) for place, part in enumerate(parts)]
    apart = where_ref[3] * 2
    places.append((aligned(apart + where_ref[4], half), near))
    places.append((aligned(apart + 1 - where_ref[4], half), far))
    return places


def in_columns(ref, where_ref, parts):
    columns = ref.shape[1] // parts
    return [ref[:, pl.ds(aligned(where_ref[place], columns), columns)] for place in range(parts)]


def mixed_kernel(
    main, lanes, gain,
    input_ref, vector_ref, down_ref, lane_ref, up_ref, first_ref, second_ref, third_ref, near_ref, far_ref, where_ref,
    normed_ref, narrow_ref, mixed_ref, raw_ref, rim_ref,
):
    rows = input_ref.shape[0]
    inputs = input_ref[...].astype(F32)
    normed = (inputs * rms_rate(inputs) * vector_ref[:, gain : gain + inputs.shape[1]]).astype(BF16)
    normed_ref[...] = normed
    narrow = (dot(normed, down_ref[...]) * lane_ref[...]).astype(BF16)
    narrow_ref[...] = narrow
    left = jnp.concatenate(in_columns(normed_ref, where_ref, 4) + [narrow], axis=1)
    first = where_ref[4] == 0
    half, whole_rows = near_ref.shape[0], first_ref.shape[0]
    before = up_ref.shape[0] - whole_rows
    step = main // 6

    def product(start, size):
        here = slice(start, start + size)
        if start < main // 2:
            there = slice(start, start + size)
            apart = jnp.where(first, near_ref[there], far_ref[there])
        else:
            there = slice(start - whole_rows + half, start - whole_rows + half + size)
            apart = jnp.where(first, far_ref[there], near_ref[there])
        up = up_ref[before + start : before + start + size]
        parts = [first_ref[here], second_ref[here], third_ref[here], apart, up]
        return dot_last(left, jnp.concatenate(parts, axis=1))

    for start in range(0, main, step):
        low = product(start, step).astype(BF16)
        mixed_ref[:, start : start + step] = low
        rim_ref[:, start : start + step] = low[rows - 8 :]
    extra = whole_rows - main
    raw_ref[...] = jnp.concatenate([product(main, extra), jnp.zeros((rows, lanes - extra), F32)], axis=1).astype(BF16)


def gate_kernel(normed_ref, narrow_ref, up_ref, first_ref, second_ref, third_ref, near_ref, far_ref, where_ref, gate_ref):
    tile, tiles = pl.program_id(0), pl.num_programs(0)
    near = (where_ref[4] == 0) == (tile < tiles // 2)
    left = jnp.concatenate(in_columns(normed_ref, where_ref, 4) + [narrow_ref[...]], axis=1)
    apart = jnp.where(near, near_ref[...], far_ref[...])
    right = jnp.concatenate([first_ref[...], second_ref[...], third_ref[...], apart, up_ref[...]], axis=1)
    gate_ref[...] = dot_last(left, right).astype(BF16)


def out_kernel(
    normed_ref, input_ref, down_ref, lane_ref, up_ref, first_ref, second_ref, third_ref, near_ref, far_ref, where_ref,
    narrow_ref, out_ref,
):
    narrow = (dot(normed_ref[...], down_ref[...]) * lane_ref[...]).astype(BF16)
    narrow_ref[...] = narrow
    places = out_places(where_ref, (first_ref, second_ref, third_ref), near_ref, far_ref)
    left = [normed_ref[:, pl.ds(offset, part.shape[0])] for offset, part in places]
    left = jnp.concatenate(left + [narrow], axis=1)
    wide = 256
    for start in range(0, out_ref.shape[1], wide):
        here = slice(start, start + wide)
        right = jnp.concatenate([part[:, here] for _, part in places] + [up_ref[:, here]], axis=0)
        out_ref[:, here] = (input_ref[:, here].astype(F32) + dot(left, right)).astype(BF16)


def gate_in_back_kernel(
    grad_ref, up_ref, first_ref, second_ref, third_ref, near_ref, far_ref, where_ref, out_ref
):
    tile, tiles = pl.program_id(0), pl.num_programs(0)
    near = (where_ref[4] == 0) == (tile < tiles // 2)
    apart = jnp.where(near, near_ref[...], far_ref[...])
    right = jnp.concatenate([first_ref[...], second_ref[...], third_ref[...], apart, up_ref[...]], axis=1)
    product = dot(grad_ref[...], right)

    @pl.when(tile == 0)
    def _():
        out_ref[...] = product

    @pl.when(tile > 0)
    def _():
        out_ref[...] += product


def mixed_in_back_kernel(
    main, gain,
    grad_ref, raw_ref, part_ref, input_ref, up_stream_ref, vector_ref, lane_ref, down_ref, up_ref,
    first_ref, second_ref, third_ref, near_ref, far_ref, where_ref,
    out_ref, narrow_ref, total_ref,
):
    first = where_ref[4] == 0
    half, whole_rows = near_ref.shape[0], first_ref.shape[0]
    before = up_ref.shape[0] - whole_rows
    width = input_ref.shape[1]
    columns = width // 4

    def right(start, size):
        here = slice(start, start + size)
        if start < main // 2:
            there = slice(start, start + size)
            apart = jnp.where(first, near_ref[there], far_ref[there])
        else:
            there = slice(start - whole_rows + half, start - whole_rows + half + size)
            apart = jnp.where(first, far_ref[there], near_ref[there])
        up = up_ref[before + start : before + start + size]
        return jnp.concatenate([first_ref[here], second_ref[here], third_ref[here], apart, up], axis=1)

    total = part_ref[...] + dot(grad_ref[:, : main // 2], right(0, main // 2))
    total = total + dot(grad_ref[:, main // 2 :], right(main // 2, main // 2))
    extra = whole_rows - main
    total = total + dot(raw_ref[:, :extra], right(main, extra))
    narrow = (total[:, width:] * lane_ref[...]).astype(BF16)
    narrow_ref[...] = narrow
    for place in range(4):
        total_ref[:, pl.ds(aligned(where_ref[place], columns), columns)] = total[:, place * columns : (place + 1) * columns]
    scaled = (total_ref[...] + dot_last(narrow, down_ref[...])) * vector_ref[:, gain : gain + width]
    inputs = input_ref[...].astype(F32)
    rate = rms_rate(inputs)
    pull = jnp.mean(inputs * scaled, axis=-1, keepdims=True) * rate * rate * rate
    out_ref[...] = (up_stream_ref[...].astype(F32) + rate * scaled - inputs * pull).astype(BF16)


def scan_back_kernel(
    head, heads, state, edge,
    values_ref, grad_ref, bc_ref, step_ref, decay_ref, sig_ref, token_ref, doc_column_ref, doc_row_ref, state_ref,
    grad_state_ref, head_ref, rate_ref, slope_ref, slope_bc_ref, *rest,
):
    outputs = rest[:-6]
    if edge:
        outputs, edge_ref = outputs[:-1], outputs[-1]
    out_values_ref, out_bc_ref, out_raw_ref = outputs[-3:]
    score_ref, grad_score_ref, pull_ref, direct_ref, grad_in_ref, grad_out_ref = rest[-6:]
    group, groups = pl.program_id(0), pl.num_programs(0)
    width = values_ref.shape[0]
    heads_here = width // head
    in_map, out_map = bc_ref[:, :state], bc_ref[:, state:]

    def same_doc():
        return (doc_column_ref[:, :1] == doc_row_ref[:1]) & lower_ones((SPAN, SPAN))

    @pl.when(group == 0)
    def _():
        score_ref[...] = jnp.where(same_doc(), dot_last(in_map, out_map), 0.0)
        grad_score_ref[...] = jnp.zeros_like(grad_score_ref)
        grad_in_ref[...] = jnp.zeros_like(grad_in_ref)
        grad_out_ref[...] = jnp.zeros_like(grad_out_ref)

    decay, step = decay_ref[...], step_ref[...]
    token = token_ref[0]
    last = decay[:, SPAN - 1 :]
    carry = jnp.exp(decay) * token[:1]
    tail = jnp.exp(last - decay) * token[1:2]
    keep = jnp.exp(last) * token[2:3, :1]
    columns = jnp.concatenate([decay] * (LANES // heads_here), axis=0).T
    at_end = lax.broadcasted_iota(jnp.int32, (1, SPAN), 1) == SPAN - 1
    grads, tails, carried, pulls, directs = [], [], [], [], []
    for place in range(heads_here):
        rows = slice(place * head, (place + 1) * head)
        one = slice(place, place + 1)
        fade = jnp.exp(jnp.minimum(decay[one] - columns[:, one], 0.0))
        kernel = (fade * score_ref[...]).astype(BF16)
        values = values_ref[rows].astype(F32)
        driven = (values * step[one]).astype(BF16)
        grad_low = grad_ref[rows]
        grad = grad_low.astype(F32)
        grad_score_ref[...] += dot_first(driven, grad_low) * fade
        state_here, grad_state = state_ref[rows], grad_state_ref[rows]
        output = dot(driven, kernel) + dot_last(state_here, out_map) * carry[one]
        by_state = dot_last(grad_state, in_map) * tail[one]
        grad_driven = dot_last(grad_low, kernel) + by_state
        driven = driven.astype(F32)
        pull = jnp.sum(grad * output - driven * grad_driven, axis=0, keepdims=True)
        ending = jnp.sum(jnp.sum(driven * by_state, axis=0, keepdims=True), axis=1, keepdims=True)
        kept = jnp.sum(state_here.astype(F32) * grad_state.astype(F32), axis=0, keepdims=True)
        ending = ending + keep[one] * jnp.sum(kept, axis=1, keepdims=True)
        pulls.append(pull + jnp.where(at_end, ending, 0.0))
        directs.append(jnp.sum(values * grad_driven, axis=0, keepdims=True))
        grads.append(step[one] * grad_driven + head_ref[one, 1:2] * grad)
        tails.append((driven * tail[one]).astype(BF16))
        carried.append((grad * carry[one]).astype(BF16))
    grad_in_ref[...] += dot_first(jnp.concatenate(tails, axis=0), grad_state_ref[...])
    grad_out_ref[...] += dot_first(jnp.concatenate(carried, axis=0), state_ref[...])
    grads = jnp.concatenate(grads, axis=0).T.astype(BF16)
    out_values_ref[...] = grads
    if edge:
        product = grads[:8].astype(F32) * slope_ref[...][:8].astype(F32)
        edge_ref[:, pl.ds(pl.multiple_of(group * width, width), width)] = product.astype(BF16)
    here = pl.ds(pl.multiple_of(group * heads_here, heads_here), heads_here)
    pull_ref[here, :] = jnp.concatenate(pulls, axis=0)
    direct_ref[here, :] = jnp.concatenate(directs, axis=0)

    @pl.when(group == groups - 1)
    def _():
        ones = lower_ones((SPAN, SPAN)).astype(F32)
        summed = lax.dot_general(
            pull_ref[...], ones, (((1,), (1,)), ((), ())), precision=EXACT, preferred_element_type=F32
        )
        grad_step = (direct_ref[...] - rate_ref[:, :1] * summed).astype(BF16).astype(F32)
        grad_raw = grad_step * sig_ref[...]
        padded = jnp.concatenate([grad_raw, jnp.zeros((LANES - heads, SPAN), F32)], axis=0)
        out_raw_ref[...] = padded.T.astype(BF16)
        grad_score = jnp.where(same_doc(), grad_score_ref[...], 0.0).astype(BF16)
        grad_in = grad_in_ref[...] + dot(grad_score, out_map)
        grad_out = grad_out_ref[...] + dot_first(grad_score, in_map)
        low = jnp.concatenate([grad_in, grad_out], axis=1).astype(BF16)
        out_bc_ref[...] = low
        if edge:
            product = low[:8].astype(F32) * slope_bc_ref[...][:8].astype(F32)
            edge_ref[:, groups * width :] = product.astype(BF16)


def conv_back_kernel(
    value_blocks, places,
    grad_ref, grad_bc_ref, slope_ref, slope_bc_ref, next_ref, vector_ref, valid_ref, next_valid_ref, project_ref,
):
    block = pl.program_id(0)
    length = grad_ref.shape[0]

    def back(grad_low, slope_low):
        grad = grad_low.astype(F32) * slope_low.astype(F32)
        later = next_ref[...].astype(F32)
        weight, _ = taps_at(vector_ref, places, block * grad.shape[1], grad.shape[1])
        valid, next_valid = valid_ref[:, :1], next_valid_ref[:, :1]
        taps = weight.shape[0]
        total = weight[taps - 1 : taps] * grad
        for ahead in range(1, taps):
            extended = jnp.concatenate(
                [jnp.where(valid >= ahead, grad, 0.0), jnp.where(next_valid >= ahead, later, 0.0)], axis=0
            )
            total = total + weight[taps - 1 - ahead : taps - ahead] * extended[ahead : ahead + length]
        project_ref[...] = total.astype(BF16)

    @pl.when(block < value_blocks)
    def _():
        back(grad_ref[...], slope_ref[...])

    @pl.when(block == value_blocks)
    def _():
        back(grad_bc_ref[...], slope_bc_ref[...])


def spec(shape, index):
    return pl.BlockSpec(shape, index)


def whole(shape):
    return pl.BlockSpec(shape, lambda *_: (0,) * len(shape))


def cost(flops, moved, transcendentals):
    return pl.CostEstimate(flops=int(flops), bytes_accessed=int(moved), transcendentals=int(transcendentals))


class Sizes:
    def __init__(self, rows, inner, heads, state, columns, taps):
        self.rows, self.inner, self.heads, self.state, self.columns, self.taps = rows, inner, heads, state, columns, taps
        self.head = inner // heads
        self.spans = rows // SPAN
        self.mixed = inner + 2 * state
        self.group_heads = 8
        self.groups = heads // self.group_heads
        self.wide = self.group_heads * self.head
        self.places = tuple(tap * self.mixed for tap in range(taps + 1))
        self.gate_gain = (taps + 1) * self.mixed
        self.norm_gain = self.gate_gain + inner


def conv_forward(sizes, mixed, raw, rim, level, tokens):
    s = sizes
    rows, wide, heads, state = s.rows, s.wide, s.heads, s.state
    maps = s.inner // (2 * state)
    shapes = [
        ((s.inner, rows), BF16), ((rows, s.inner), BF16), ((rows, 2 * state), BF16), ((rows, 2 * state), BF16),
        ((heads, rows), F32), ((heads, rows), F32), ((heads, rows), F32),
    ] + [((s.inner, state), BF16)] * s.spans
    args = [level.vector, tokens.valid, raw, level.heads, tokens.flags]
    outputs = pl.pallas_call(
        functools.partial(conv_kernel, s.spans, s.head, heads, state, s.places),
        grid=(s.groups,),
        in_specs=[
            spec((rows, wide), lambda g: (0, g)), spec((rows, 2 * state), lambda g: (0, maps)),
            spec((8, wide), lambda g: (0, g)), spec((8, 2 * state), lambda g: (0, maps)), *whole_specs(*args),
        ],
        out_specs=[
            spec((wide, rows), lambda g: (g, 0)), spec((rows, wide), lambda g: (0, g)), whole((rows, 2 * state)),
            whole((rows, 2 * state)), whole((heads, rows)), whole((heads, rows)), whole((heads, rows)),
        ] + [spec((wide, state), lambda g: (g, 0))] * s.spans,
        out_shape=[jax.ShapeDtypeStruct(*one) for one in shapes],
        scratch_shapes=[pltpu.VMEM((heads, rows), F32)],
        compiler_params=PARAMS,
        cost_estimate=cost(2 * rows * s.inner * state, 10 * rows * s.inner, 2 * rows * s.inner),
    )(mixed, mixed, rim, rim, *args)
    return outputs[:7], outputs[7:]


def span_specs(sizes, span):
    s = sizes
    return Bag(
        turned=spec((s.wide, SPAN), lambda g: (g, span)),
        maps=spec((SPAN, 2 * s.state), lambda g: (span, 0)),
        rows=spec((s.group_heads, SPAN), lambda g: (g, span)),
        flags=spec((1, 8, SPAN), lambda g: (span, 0, 0)),
        doc_column=spec((SPAN, LANES), lambda g: (span, 0)),
        doc_row=spec((8, SPAN), lambda g: (0, span)),
        state=spec((s.wide, s.state), lambda g: (g, 0)),
        head=spec((s.group_heads, LANES), lambda g: (g, 0)),
        full=spec((SPAN, s.inner), lambda g: (span, 0)),
    )


ANYWHERE = pl.BlockSpec(memory_space=pl.ANY)


def scan_forward(sizes, span, conv, state_in, gate, level, tokens, earlier):
    s = sizes
    at = span_specs(s, span)
    args = [
        conv.values, conv.maps, conv.step, conv.decay, tokens.flags, tokens.column, tokens.row,
        state_in, level.heads, gate, level.vector,
    ]
    in_specs = [
        at.turned, at.maps, at.rows, at.rows, at.flags, at.doc_column, at.doc_row, at.state,
        at.head, at.full, whole(level.vector.shape),
    ]
    aliases = {}
    if earlier is not None:
        aliases = {len(args): 0, len(args) + 1: 1}
        args, in_specs = args + list(earlier), in_specs + [ANYWHERE] * 2
    shape = jax.ShapeDtypeStruct((s.rows, s.inner), BF16)
    return pl.pallas_call(
        functools.partial(scan_kernel, s.head, s.state, s.gate_gain),
        grid=(s.groups,),
        in_specs=in_specs,
        out_specs=[at.full, at.full],
        out_shape=[shape, shape],
        scratch_shapes=[pltpu.VMEM((SPAN, SPAN), F32), pltpu.VMEM((SPAN, s.inner), BF16)],
        input_output_aliases=aliases,
        compiler_params=PARAMS,
        cost_estimate=cost(
            2 * SPAN * s.inner * (SPAN * 4 + s.state), 8 * SPAN * s.inner, s.heads * SPAN * SPAN
        ),
    )(*args)


SMALL = pl.BlockSpec(memory_space=pltpu.SMEM)


def shape_of(shape, dtype=BF16):
    return jax.ShapeDtypeStruct(shape, dtype)


def whole_specs(*arrays):
    return [whole(array.shape) for array in arrays]


def project_mixed(sizes, inputs, level, lane_mask):
    s = sizes
    parts = level.mixed
    args = [inputs, level.vector, level.in_down, lane_mask, level.in_up, *parts]
    width = inputs.shape[1]
    shapes = [(s.rows, width), (s.rows, LANES), (s.rows, s.mixed), (s.rows, LANES), (8, s.mixed)]
    return pl.pallas_call(
        functools.partial(mixed_kernel, s.mixed, LANES, s.norm_gain),
        grid=(1,),
        in_specs=whole_specs(*args) + [SMALL],
        out_specs=[whole(shape) for shape in shapes],
        out_shape=[shape_of(shape) for shape in shapes],
        compiler_params=PARAMS,
        cost_estimate=cost(2 * s.rows * width * s.mixed, 10 * width * s.mixed, s.rows),
    )(*args, level.where)


def gate_tile_specs(sizes, tile):
    quarter = spec((tile, sizes.columns), lambda j: (j, 0))
    half = spec((tile, sizes.columns), lambda j: (lax.rem(j, sizes.inner // (2 * tile)), 0))
    return [spec((tile, LANES), lambda j: (j, 0)), quarter, quarter, quarter, half, half, SMALL]


def project_gate(sizes, normed, narrow, level):
    s = sizes
    tile = 512
    return pl.pallas_call(
        gate_kernel,
        grid=(s.inner // tile,),
        in_specs=whole_specs(normed, narrow) + gate_tile_specs(s, tile),
        out_specs=spec((s.rows, tile), lambda j: (0, j)),
        out_shape=shape_of((s.rows, s.inner)),
        compiler_params=PARAMS,
        cost_estimate=cost(2 * s.rows * normed.shape[1] * s.inner, 10 * s.inner * s.rows, 0),
    )(normed, narrow, level.in_up, *level.gate, level.where)


def project_out(sizes, normed_out, inputs, level, lane_mask):
    s = sizes
    args = [normed_out, inputs, level.out_down, lane_mask, level.out_up, *level.out]
    shapes = [(s.rows, LANES), inputs.shape]
    return pl.pallas_call(
        out_kernel,
        grid=(1,),
        in_specs=whole_specs(*args) + [SMALL],
        out_specs=[whole(shape) for shape in shapes],
        out_shape=[shape_of(shape) for shape in shapes],
        compiler_params=PARAMS,
        cost_estimate=cost(2 * s.rows * inputs.shape[1] * s.inner, 6 * inputs.shape[1] * s.inner, 0),
    )(*args, level.where)


def out_backward(sizes, upstream, mixed, gate, conv, level, lane_mask, tokens):
    s = sizes
    full = spec((SPAN, s.inner), lambda k: (k, 0))
    parts = level.out
    width = upstream.shape[1]
    return pl.pallas_call(
        functools.partial(out_back_kernel, s.head, s.heads, s.state, s.gate_gain),
        grid=(s.spans,),
        in_specs=[
            spec((SPAN, width), lambda k: (k, 0)), spec((SPAN, LANES), lambda k: (k, 0)),
            *whole_specs(level.out_up, level.out_down, *parts), SMALL,
            full, full, whole(level.vector.shape), spec((s.heads, SPAN), lambda k: (0, k)),
            spec((1, 8, SPAN), lambda k: (k, 0, 0)), spec((SPAN, 2 * s.state), lambda k: (k, 0)),
        ],
        out_specs=[
            full, spec((s.inner, SPAN), lambda k: (0, k)), spec((SPAN, LANES), lambda k: (k, 0)),
        ] + [whole((s.inner, s.state))] * s.spans,
        out_shape=[
            shape_of((s.rows, s.inner)), shape_of((s.inner, s.rows)), shape_of((s.rows, LANES)),
        ] + [shape_of((s.inner, s.state))] * s.spans,
        scratch_shapes=[pltpu.VMEM((SPAN, s.inner), F32), pltpu.VMEM((SPAN, s.inner), BF16)],
        compiler_params=PARAMS,
        cost_estimate=cost(
            2 * s.rows * s.inner * (s.state + width), 14 * s.rows * s.inner, 2 * s.rows * s.inner
        ),
    )(
        upstream, lane_mask, level.out_up, level.out_down, *parts, level.where, mixed, gate,
        level.vector, conv.decay, tokens.flags, conv.maps,
    )


def gate_in_backward(sizes, grad_gate, level):
    s = sizes
    tile = 512
    width = 4 * s.columns + LANES
    return pl.pallas_call(
        gate_in_back_kernel,
        grid=(s.inner // tile,),
        in_specs=[spec((s.rows, tile), lambda j: (0, j))] + gate_tile_specs(s, tile),
        out_specs=whole((s.rows, width)),
        out_shape=shape_of((s.rows, width), F32),
        compiler_params=PARAMS,
        cost_estimate=cost(2 * s.rows * width * s.inner, 10 * s.inner * s.rows, 0),
    )(grad_gate, level.in_up, *level.gate, level.where)


def mixed_in_backward(sizes, grad_mixed, raw, part, inputs, upstream, level, lane_mask):
    s = sizes
    width = inputs.shape[1]
    rows = lambda columns: spec((SPAN, columns), lambda k: (k, 0))
    fixed = [level.in_down, level.in_up, *level.mixed]
    return pl.pallas_call(
        functools.partial(mixed_in_back_kernel, s.mixed, s.norm_gain),
        grid=(s.spans,),
        in_specs=[
            rows(s.mixed), rows(LANES), rows(width + LANES), rows(width), rows(width), whole(level.vector.shape), rows(LANES),
            *whole_specs(*fixed), SMALL,
        ],
        out_specs=[rows(width), rows(LANES)],
        out_shape=[shape_of((s.rows, width)), shape_of((s.rows, LANES))],
        scratch_shapes=[pltpu.VMEM((SPAN, width), F32)],
        compiler_params=PARAMS,
        cost_estimate=cost(2 * s.rows * width * s.mixed, 10 * width * s.mixed, s.rows),
    )(grad_mixed, raw, part, inputs, upstream, level.vector, lane_mask, *fixed, level.where)


def scan_backward(sizes, span, conv, grad_turned, state_in, grad_state, level, tokens, earlier):
    s = sizes
    at = span_specs(s, span)
    args = [
        conv.values, grad_turned, conv.maps, conv.step, conv.decay, conv.sig, tokens.flags, tokens.column, tokens.row,
        state_in, grad_state, level.heads, level.heads, conv.slope, conv.slope_maps,
    ]
    in_specs = [
        at.turned, at.turned, at.maps, at.rows, at.rows, spec((s.heads, SPAN), lambda g: (0, span)), at.flags,
        at.doc_column, at.doc_row, at.state, at.state, at.head, whole((s.heads, LANES)),
        spec((16, s.wide), lambda g: (0, g)), spec((16, 2 * s.state), lambda g: (0, 0)),
    ]
    aliases = {}
    if earlier is not None:
        aliases = {len(args) + place: place for place in range(3)}
        args, in_specs = args + list(earlier[:3]), in_specs + [ANYWHERE] * 3
    out_specs = [spec((SPAN, s.wide), lambda g: (span, g)), at.maps, spec((SPAN, LANES), lambda g: (span, 0))]
    out_shape = [shape_of((s.rows, s.inner)), shape_of((s.rows, 2 * s.state)), shape_of((s.rows, LANES))]
    if span == 0:
        out_specs, out_shape = out_specs + [whole((8, s.mixed))], out_shape + [shape_of((8, s.mixed))]
    return pl.pallas_call(
        functools.partial(scan_back_kernel, s.head, s.heads, s.state, span == 0),
        grid=(s.groups,),
        in_specs=in_specs,
        out_specs=out_specs,
        out_shape=out_shape,
        scratch_shapes=[
            pltpu.VMEM((SPAN, SPAN), F32), pltpu.VMEM((SPAN, SPAN), F32), pltpu.VMEM((s.heads, SPAN), F32),
            pltpu.VMEM((s.heads, SPAN), F32), pltpu.VMEM((SPAN, s.state), F32), pltpu.VMEM((SPAN, s.state), F32),
        ],
        input_output_aliases=aliases,
        compiler_params=PARAMS,
        cost_estimate=cost(
            2 * SPAN * s.inner * (SPAN * 12 + 4 * s.state), 10 * SPAN * s.inner, s.heads * SPAN * SPAN
        ),
    )(*args)


def conv_backward(sizes, grad_values, grad_maps, conv, later, level, tokens):
    s = sizes
    wide = 2 * s.state
    blocks = s.inner // wide
    values = spec((s.rows, wide), lambda i: (0, jnp.minimum(i, blocks - 1)))
    maps = whole((s.rows, wide))
    fixed = [level.vector, tokens.valid, tokens.next_valid]
    return pl.pallas_call(
        functools.partial(conv_back_kernel, blocks, s.places),
        grid=(blocks + 1,),
        in_specs=[values, maps, values, maps, spec((8, wide), lambda i: (0, i)), *whole_specs(*fixed)],
        out_specs=spec((s.rows, wide), lambda i: (0, i)),
        out_shape=shape_of((s.rows, s.mixed)),
        compiler_params=PARAMS,
        cost_estimate=cost(10 * s.rows * s.mixed, 6 * s.rows * s.mixed, 0),
    )(grad_values, grad_maps, conv.slope, conv.slope_maps, later, *fixed)


GRAD_ROWS = 512


def early_grads_kernel(
    up_blocks, out_blocks, up_ref, narrow_out_ref, normed_out_ref, grad_narrow_ref, grad_gate_ref, narrow_ref, *rest
):
    out_ref = rest[-1]
    block = pl.program_id(0)

    @pl.when(block < up_blocks)
    def _():
        out_ref[...] = dot_first(up_ref[...], narrow_out_ref[...]).astype(BF16)

    @pl.when((block >= up_blocks) & (block < up_blocks + out_blocks))
    def _():
        out_ref[...] = dot_first(normed_out_ref[...], grad_narrow_ref[...]).astype(BF16)

    @pl.when(block >= up_blocks + out_blocks)
    def _():
        out_ref[...] = dot_first(grad_gate_ref[...], narrow_ref[...]).astype(BF16)


def grad_blocks(sizes, width):
    late = -(-(width + sizes.mixed + LANES) // GRAD_ROWS)
    return (width + 2 * sizes.inner) // GRAD_ROWS, late


def early_grads(sizes, upstream, kept, grad_narrow_out, grad_gate, rows, first, buffer):
    s = sizes
    wide = GRAD_ROWS
    up_blocks, out_blocks = upstream.shape[1] // wide, s.inner // wide
    args = [upstream, kept.narrow_out, kept.normed_out, grad_narrow_out, grad_gate, kept.narrow]
    narrow = whole((s.rows, LANES))
    at = lambda start, count: spec((s.rows, wide), lambda i: (0, jnp.clip(i - start, 0, count - 1)))
    in_specs = [
        at(0, up_blocks), narrow, at(up_blocks, out_blocks), narrow, at(up_blocks + out_blocks, out_blocks), narrow
    ]
    aliases = {}
    if buffer is not None:
        aliases = {len(args): 0}
        args, in_specs = args + [buffer], in_specs + [ANYWHERE]
    blocks = up_blocks + 2 * out_blocks
    return pl.pallas_call(
        functools.partial(early_grads_kernel, up_blocks, out_blocks),
        grid=(blocks,),
        in_specs=in_specs,
        out_specs=spec((wide, LANES), lambda i: (first + i, 0)),
        out_shape=shape_of((rows, LANES)),
        input_output_aliases=aliases,
        compiler_params=PARAMS,
        cost_estimate=cost(2 * s.rows * LANES * blocks * wide, 2 * s.rows * blocks * wide, 0),
    )(*args)


def late_grads_kernel(normed_ref, grad_narrow_ref, mixed_ref, raw_ref, narrow_ref, *rest):
    out_ref = rest[-1]
    first = 0
    for left, right in ((normed_ref, grad_narrow_ref), (mixed_ref, narrow_ref), (raw_ref, narrow_ref)):
        rows = left.shape[1]
        out_ref[first : first + rows, :] = dot_first(left[...], right[...]).astype(BF16)
        first += rows
    out_ref[first:, :] = jnp.zeros((out_ref.shape[0] - first, out_ref.shape[1]), BF16)


def late_grads(sizes, kept, grad_narrow, grad_mixed, raw, buffer):
    s = sizes
    args = [kept.normed, grad_narrow, grad_mixed, raw, kept.narrow]
    in_specs = whole_specs(*args)
    rows = grad_blocks(s, kept.normed.shape[1])[1] * GRAD_ROWS
    all_rows, aliases = rows, {}
    if buffer is not None:
        all_rows, aliases = buffer.shape[0], {len(args): 0}
        args, in_specs = args + [buffer], in_specs + [ANYWHERE]
    return pl.pallas_call(
        late_grads_kernel,
        grid=(1,),
        in_specs=in_specs,
        out_specs=whole((rows, LANES)),
        out_shape=shape_of((all_rows, LANES)),
        input_output_aliases=aliases,
        compiler_params=PARAMS,
        cost_estimate=cost(2 * s.rows * LANES * rows, 2 * s.rows * rows, 0),
    )(*args)


def token_tables(doc_ids, block_rows):
    rows = doc_ids.shape[0]
    before = from_behind(doc_ids[rows - 8 :], SEQ, 1)
    after = from_behind(doc_ids[:8], SEQ, -1)
    extended = jnp.concatenate([before, doc_ids, after])

    def taps_behind(first, count):
        here = extended[first : first + count]
        return sum((extended[first - back : first - back + count] == here).astype(jnp.int32) for back in (1, 2, 3))

    spans = rows // SPAN
    ends = extended[7 + SPAN :: SPAN][:spans]
    starts = extended[7::SPAN][:spans]
    by_span = doc_ids.reshape(spans, SPAN)
    flags = jnp.stack(
        [
            (by_span == starts[:, None]).astype(F32),
            (by_span == ends[:, None]).astype(F32),
            jnp.broadcast_to((starts == ends).astype(F32)[:, None], (spans, SPAN)),
        ]
        + [jnp.zeros((spans, SPAN), F32)] * 5,
        axis=1,
    )
    return Bag(
        valid=jnp.broadcast_to(taps_behind(8, rows)[:, None], (rows, LANES)),
        next_valid=jnp.broadcast_to(taps_behind(8 + rows, 8)[:, None], (8, LANES)),
        column=jnp.broadcast_to(doc_ids[:, None], (rows, LANES)),
        row=jnp.broadcast_to(doc_ids[None, :], (8, rows)),
        flags=flags,
        keep=(starts == ends).astype(F32),
    )


def state_hops(rows, block_rows):
    eighth = block_rows // DOCS_PER_BLOCK
    if rows // SPAN > 1 and eighth > SPAN:
        raise ValueError("unsupported block")
    return 1 if rows >= eighth else 2 * eighth // rows - 1


def pass_states(sizes, local, conv, tokens, hops, direction):
    if hops > 1:
        keep = jnp.exp(conv.decay[:, -1]) * tokens.keep[0]
        keep = jnp.repeat(keep, sizes.head)[:, None]
        total = local.astype(F32)
        reach = 1
        while reach < hops:
            total = total + keep * from_behind(total.astype(BF16), SEQ, direction * reach).astype(F32)
            keep = keep * from_behind(keep, SEQ, direction * reach)
            reach *= 2
        local = total.astype(BF16)
    return from_behind(local, SEQ, direction)


def layer_forward(sizes, inputs, level, lane_mask, tokens, hops):
    s = sizes
    normed, narrow, mixed, raw, rim = project_mixed(s, inputs, level, lane_mask)
    rim = from_behind(rim, SEQ, 1)
    outputs, states = conv_forward(s, mixed, raw, rim, level, tokens)
    values, slope, maps, slope_maps, step, decay, sig = outputs
    conv = Bag(values=values, slope=slope, maps=maps, slope_maps=slope_maps, step=step, decay=decay, sig=sig)
    states_in = [pass_states(s, states[-1], conv, tokens, hops, 1)] + list(states[:-1])
    gate = project_gate(s, normed, narrow, level)
    outputs = None
    for span in reversed(range(s.spans)):
        outputs = scan_forward(s, span, conv, states_in[span], gate, level, tokens, outputs)
    mixed_out, normed_out = outputs
    narrow_out, result = project_out(s, normed_out, inputs, level, lane_mask)
    kept = Bag(
        inputs=inputs, normed=normed, narrow=narrow, gate=gate, conv=conv, states_in=states_in, mixed_out=mixed_out,
        normed_out=normed_out, narrow_out=narrow_out,
    )
    return result, kept


def layer_backward(sizes, upstream, kept, level, lane_mask, tokens, hops, buffer, rows, first, last):
    s = sizes
    conv = kept.conv
    grad_gate, turned, grad_narrow_out, *local = out_backward(
        s, upstream, kept.mixed_out, kept.gate, conv, level, lane_mask, tokens
    )
    grad_states = list(local[1:]) + [pass_states(s, local[0], conv, tokens, hops, -1)]
    buffer = early_grads(s, upstream, kept, grad_narrow_out, grad_gate, rows, first, buffer)
    part = gate_in_backward(s, grad_gate, level)
    outputs = None
    for span in range(s.spans):
        outputs = scan_backward(
            s, span, conv, turned, kept.states_in[span], grad_states[span], level, tokens, outputs
        )
        if span == 0:
            later = from_behind(outputs[3], SEQ, -1)
    grad_values, grad_maps, raw = outputs[:3]
    grad_mixed = conv_backward(s, grad_values, grad_maps, conv, later, level, tokens)
    grad_inputs, grad_narrow = mixed_in_backward(s, grad_mixed, raw, part, kept.inputs, upstream, level, lane_mask)
    late = late_grads(s, kept, grad_narrow, grad_mixed, raw, None if last else buffer)
    return grad_inputs, buffer, late


def make_level(sizes, vector, numbers, adapters, section, place):
    s = sizes
    in_down, in_up, out_down, out_up = adapters
    dt_bias, a_log, skip_gain = numbers
    table = jnp.stack([jnp.exp(a_log), skip_gain, dt_bias], axis=1)
    where = jnp.stack([place, place ^ (1 + section), place ^ (2 - section), place ^ 3, section]).astype(jnp.int32)
    return Bag(
        vector=vector, heads=jnp.pad(table, ((0, 0), (0, LANES - 3))), in_down=in_down, in_up=in_up, out_down=out_down,
        out_up=out_up, where=where,
    )


def swap(value):
    return lax.ppermute(value, SECTION, [(0, 1), (1, 0)])


def exchange(value, axis, distance):
    count = lax.axis_size(axis)
    return lax.ppermute(value, axis, [(place, place ^ distance) for place in range(count)])


def rows_at(value, index, rows):
    return lax.dynamic_slice_in_dim(value, index * rows, rows, axis=0)


def put_at(buffer, value, *index):
    start = list(index) + [0] * (buffer.ndim - len(index))
    return lax.dynamic_update_slice(buffer, value.reshape((1,) * len(index) + value.shape), start)


def across(value, second):
    count = lax.axis_size(WSHARD)
    pairs = []
    for section in range(2):
        distance = 2 - section if second else 1 + section
        pairs += [(section * count + place, section * count + (place ^ distance)) for place in range(count)]
    return lax.ppermute(value, (SECTION, WSHARD), pairs)


def spread(quarters):
    section = lax.axis_index(SECTION)
    layers, before, others = [], None, []
    for layer in range(2):
        parts = []
        for index, (matrix, half, step) in enumerate(quarters):
            if layer == 0:
                others.append(swap(matrix if before is None else tie(matrix, before.own)))
            own = jnp.where(section == layer, matrix, others[index])
            ready = own
            if before is not None:
                ready = tie(own, before.apart if before.first else before.near)
            near = across(ready, False)
            pass_on = near if before is None else tie(near, before.apart)
            apart = across(lax.dynamic_slice_in_dim(pass_on, section * step, half, axis=0), True)
            parts.append((own, near, swap(pass_on), apart, swap(apart)))
            before = Bag(own=own, near=near, apart=apart, first=before is None)
        layers.append(parts)
    return layers


def reduce_rows(value, axis):
    count, place = lax.axis_size(axis), lax.axis_index(axis)
    rows = value.shape[0] // count
    total = rows_at(value, place, rows).astype(F32)
    for distance in range(1, count):
        total = total + exchange(rows_at(value, place ^ distance, rows), axis, distance).astype(F32)
    return total


def collect_rows(value, axis):
    count, place = lax.axis_size(axis), lax.axis_index(axis)
    buffer = jnp.zeros((count,) + value.shape, value.dtype)
    for distance in range(count):
        part = exchange(value, axis, distance) if distance else value
        buffer = put_at(buffer, part, place ^ distance)
    return buffer.reshape((count * value.shape[0],) + value.shape[1:])


def sum_everywhere(packed):
    section = lax.axis_index(SECTION)
    half = packed.shape[0] // 2
    mine = rows_at(packed, section, half).astype(F32) + swap(rows_at(packed, 1 - section, half)).astype(F32)
    mine = mine.astype(BF16)
    if lax.axis_size(SEQ) == 4:
        part = reduce_rows(mine, WSHARD).astype(BF16)
        part = reduce_rows(part, SEQ).astype(BF16)
        mine = collect_rows(collect_rows(part, SEQ), WSHARD)
    else:
        mine = lax.psum(mine, (SEQ, WSHARD))
    other = swap(mine)
    return jnp.concatenate([jnp.where(section == 0, mine, other), jnp.where(section == 0, other, mine)], axis=0)


def both_layers(own):
    section = lax.axis_index(SECTION)
    other = swap(own)
    return [jnp.where(section == layer, own, other) for layer in range(2)]


def on_device(
    layer_input, out_grad, doc_index, doc_adapter, in_weight, out_weight, norm_gain, conv_weight, conv_bias, dt_bias,
    a_log, skip_gain, gate_gain, *adapters,
):
    section, place = lax.axis_index(SECTION), lax.axis_index(WSHARD)
    batches, rows, width = layer_input.shape
    heads, inner = dt_bias.shape[1], gate_gain.shape[1]
    taps, mixed = conv_weight.shape[1:]
    sizes = Sizes(rows, inner, heads, (mixed - inner) // 2, in_weight.shape[1], taps)
    block_rows = rows * lax.axis_size(SEQ)
    hops = state_hops(rows, block_rows)

    pick = lambda array: lax.dynamic_index_in_dim(array, section, 0, keepdims=False)
    inputs, grads, doc_ids, table = pick(layer_input), pick(out_grad), pick(doc_index), pick(doc_adapter)[0]
    turned = in_weight[0].T
    main = mixed // 2
    groups = spread(
        [
            (turned[inner:], main + heads, main),
            (turned[:inner], inner // 2, inner // 2),
            (out_weight[0], out_weight.shape[1] // 2, out_weight.shape[1] // 2),
        ]
    )
    tokens = token_tables(doc_ids, block_rows)
    adapter = jnp.sum(jnp.where(doc_ids[:, None] == jnp.arange(table.shape[0])[None, :], table[None, :], 0), axis=1)
    lane_mask = (adapter[:, None] == (jnp.arange(LANES) // RANK)[None, :]).astype(F32)
    vectors = both_layers(jnp.concatenate([conv_weight[0].reshape(1, -1), conv_bias, gate_gain, norm_gain], axis=1))
    numbers = both_layers(jnp.concatenate([dt_bias, a_log, skip_gain], axis=0))
    in_down, in_up, out_down, out_up = adapters
    both = [both_layers(array) for array in (in_down[0], in_up[0].T, out_down[0], out_up[0])]
    levels = [
        make_level(sizes, vectors[layer], numbers[layer], [pair[layer] for pair in both], section, place)
        for layer in range(2)
    ]
    small = [inputs, grads, lane_mask, tokens.__dict__] + [level.__dict__ for level in levels]
    first_parts = groups[0][0]
    (inputs, grads, lane_mask, token_fields, *level_fields), first_parts = lax.optimization_barrier((small, first_parts))
    tokens, levels = Bag(**token_fields), [Bag(**fields) for fields in level_fields]
    groups[0][0] = first_parts
    for layer in range(2):
        levels[layer].mixed, levels[layer].gate, levels[layer].out = groups[layer]

    results, kept = [], []
    rows_now = inputs
    for layer in range(2):
        rows_now, stored = layer_forward(sizes, rows_now, levels[layer], lane_mask, tokens, hops)
        results.append(rows_now)
        kept.append(stored)
    early_blocks, late_blocks = grad_blocks(sizes, width)
    early_rows, late_rows = early_blocks * GRAD_ROWS, late_blocks * GRAD_ROWS
    all_rows = late_rows + 2 * early_rows
    upper_grad, _, buffer = layer_backward(
        sizes, grads, kept[1], levels[1], lane_mask, tokens, hops, None, all_rows, late_blocks, False
    )
    lower_grad, buffer, lower_late = layer_backward(
        sizes, upper_grad, kept[0], levels[0], lane_mask, tokens, hops, buffer, all_rows, late_blocks + early_blocks, True
    )
    first = sum_everywhere(buffer)
    upper_early, lower_early = first[late_rows : late_rows + early_rows], first[late_rows + early_rows :]
    early = jnp.where(section == 0, lower_early, upper_early).astype(F32)
    late = jnp.where(section == 0, sum_everywhere(lower_late), first[:late_rows]).astype(F32)
    up_out, down_out, up_gate = early[:width], early[width : width + inner], early[width + inner :]
    down_in, up_mixed = late[:width], late[width : width + mixed + heads]

    def placed(pair):
        here = jnp.where(section == 0, pair[0], pair[1])
        there = swap(jnp.where(section == 0, pair[1], pair[0]))
        first, second = jnp.where(section == 0, here, there), jnp.where(section == 0, there, here)
        return jnp.stack([first, second])[None]

    return (
        placed(results),
        placed([lower_grad, upper_grad]),
        down_in[None],
        jnp.concatenate([up_gate, up_mixed], axis=0).T[None],
        down_out[None],
        up_out.T[None],
    )


def solution(mesh):
    tokens, matrix, vector = P(None, (WSHARD, SEQ), None), P(SECTION, None, None), P(SECTION, None)
    in_specs = (tokens, tokens, P(None, (WSHARD, SEQ)), P(None, WSHARD, None))
    in_specs += (P(SECTION, WSHARD, None),) * 2
    in_specs += (vector, matrix) + (vector,) * 5 + (matrix,) * 4
    out_specs = (P(SECTION, None, (WSHARD, SEQ), None),) * 2 + (matrix,) * 4
    return jax.shard_map(on_device, mesh=mesh, in_specs=in_specs, out_specs=out_specs, check_vma=False)
```

time: 566 us -> 475 us (0.84)
  the two profiles are of different devices: /device:TPU:17 before, /device:TPU:0 now
where the time goes in v1:
time: 475 us; the launch traced here: 466 us
  Pallas kernels  178 us (37%)
  waiting for transfers between devices  129 us (27%)
  starting transfers between devices  94.6 us (20%)
  local copies, waits for them, and re-layouts  36.1 us (8%)
  other arithmetic  24.7 us (5%)
    ppermute x12, waiting for transfers between devices, across(): return lax.ppermute(value, (SECTION, WSHARD), pairs)  65.5 us
    ppermute x24, waiting for transfers between devices, exchange(): lax.ppermute(value, axis, [(place, place ^ distance) for place in range(c...  47.7 us
    ppermute x24, starting transfers between devices, exchange(): lax.ppermute(value, axis, [(place, place ^ distance) for place in range(c...  41.5 us
    pallas_call x4, Pallas kernels, scan_backward(): pl.pallas_call(functools.partial(scan_back_kernel, s.head, s.heads, s.sta...  34 us
    ppermute x10, starting transfers between devices, from_behind(): lax.ppermute(value, axis, [(source, source + steps) for source in range(i...  29.5 us
    pallas_call x2, Pallas kernels, out_backward(): pl.pallas_call(functools.partial(out_back_kernel, s.head, s.heads, s.stat...  27.1 us
    pallas_call x4, Pallas kernels, scan_forward(): pl.pallas_call(functools.partial(scan_kernel, s.head, s.state, s.gate_gai...  25.6 us
    unnamed x321, local copies, waits for them, and re-layouts  20.3 us
  transfers between devices with their start and end apart: 73, of which 25 were waited for; matrix products, arithmetic and copies ran while one was open for 7% of the time, Pallas kernels for 35%

profile of v1, /device:TPU:0, one launch (start us, length us, event | category | flops | bytes accessed | tf_op | source)
XLA Modules:
  0.0 465.5 jit_solution(18112955579567050647)
XLA Ops:
  4.0 5.1 %collective-permute-start = (s32[8]{0:T(128)S(1)}, s32[8]{0:T(128)S(1)}, u32[]{:S(2)}, u32[]{:S(2)}) collective-permute-start(s32[8]{0:T(128)S(1)} %get-tuple-element.280), channel_id=1, source_target_pairs={{0,4},{4,8},{8,12},{1,5},{5,9},{9,13},{2,6},{6,10},{10,14},{3,7},{... | collective-permute-start | bytes 104 | tf_op jit(solution)/shard_map/ppermute | solution.py:34
  19.5 9.7 %collective-permute-done.9.second_ref = bf16[2336,256]{1,0:T(8,128)(2,1)} collective-permute-done((bf16[2336,256]{1,0:T(8,128)(2,1)S(1)}, bf16[2336,256]{1,0:T(8,128)(2,1)}, u32[]{:S(2)}, u32[]{:S(2)}) %collective-permute-start.9) | collective-permute-done | bytes 1196064 | tf_op jit(solution)/shard_map/ppermute | solution.py:994
  34.9 5.5 %collective-permute-done.11.near_ref = bf16[1184,256]{1,0:T(8,128)(2,1)S(1)} collective-permute-done((bf16[1184,256]{1,0:T(8,128)(2,1)S(1)}, bf16[1184,256]{1,0:T(8,128)(2,1)S(1)}, u32[]{:S(2)}, u32[]{:S(2)}) %collective-permute-start.11) | collective-permute-done | bytes 606240 | tf_op jit(solution)/shard_map/ppermute | solution.py:994
  45.0 10.3 %collective-permute-done.16.second_ref = bf16[2048,256]{1,0:T(8,128)(2,1)} collective-permute-done((bf16[2048,256]{1,0:T(8,128)(2,1)S(1)}, bf16[2048,256]{1,0:T(8,128)(2,1)}, u32[]{:S(2)}, u32[]{:S(2)}) %collective-permute-start.16) | collective-permute-done | bytes 1048608 | tf_op jit(solution)/shard_map/ppermute | solution.py:994
  57.3 12.9 %collective-permute-done.21.second_ref = bf16[512,1024]{1,0:T(8,128)(2,1)S(1)} collective-permute-done((bf16[512,1024]{1,0:T(8,128)(2,1)S(1)}, bf16[512,1024]{1,0:T(8,128)(2,1)S(1)}, u32[]{:S(2)}, u32[]{:S(2)}) %collective-permute-start.21) | collective-permute-done | bytes 1048608 | tf_op jit(solution)/shard_map/ppermute | solution.py:994
  78.2 10.6 %collective-permute-done.18.near_ref = bf16[1024,256]{1,0:T(8,128)(2,1)S(1)} collective-permute-done((bf16[1024,256]{1,0:T(8,128)(2,1)S(1)}, bf16[1024,256]{1,0:T(8,128)(2,1)S(1)}, u32[]{:S(2)}, u32[]{:S(2)}) %collective-permute-start.18) | collective-permute-done | bytes 524320 | tf_op jit(solution)/shard_map/ppermute | solution.py:994
  90.4 3.9 collective-permute-done.25.second_ref
  98.3 4.3 collective-permute-done.23.near_ref
  103.9 6.2 %shard_map.208 = (bf16[512,1024]{1,0:T(8,128)(2,1)S(1)}, bf16[512,128]{1,0:T(8,128)(2,1)S(1)}, bf16[512,2304]{1,0:T(8,128)(2,1)S(1)}, bf16[512,128]{1,0:T(8,128)(2,1)S(1)}, bf16[8,2304]{1,0:T(8,128)(2,1)S(1)}) custom-call(bf16[512,1024]{1,0:T(8,128)(2,1)S(1)} %copy-done.22, f32[1,14592]{1,0:T(1,128)S(1)} %get-tuple-element.114.vector_ref, ...), custom_call_target="tpu_custom_call" | custom-call | flops 2415919104 | bytes 23592960 | tf_op jit(solution)/shard_map/pallas_call | solution.py:607
  110.2 3.5 collective-permute-start.13
  115.3 7.1 %shard_map.209 = (bf16[2048,512]{1,0:T(8,128)(2,1)S(1)}, bf16[512,2048]{1,0:T(8,128)(2,1)S(1)}, bf16[512,256]{1,0:T(8,128)(2,1)S(1)}, bf16[512,256]{1,0:T(8,128)...) custom-call(bf16[512,2304]{1,0:T(8,128)(2,1)S(1)} %get-tuple-element, ...), custom_call_target="tpu_custom_call" | custom-call | flops 268435456 | bytes 10485760 | tf_op jit(solution)/shard_map/pallas_call | solution.py:522
  125.2 4.5 collective-permute-start.14
  131.6 9.7 %collective-permute-done.14.state_ref = bf16[2048,128]{1,0:T(8,128)(2,1)S(1)} collective-permute-done((bf16[2048,128]{1,0:T(8,128)(2,1)S(1)}, bf16[2048,128]{1,0:T(8,128)(2,1)S(1)}, u32[]{:S(2)}, u32[]{:S(2)}) %collective-permute-start.14) | collective-permute-done | bytes 524320 | tf_op jit(solution)/shard_map/ppermute | solution.py:34
  142.3 8.3 %collective-permute-done.33.near_ref = bf16[1024,256]{1,0:T(8,128)(2,1)} collective-permute-done((bf16[1024,256]{1,0:T(8,128)(2,1)S(1)}, bf16[1024,256]{1,0:T(8,128)(2,1)}, u32[]{:S(2)}, u32[]{:S(2)}) %collective-permute-start.33) | collective-permute-done | bytes 524320 | tf_op jit(solution)/shard_map/ppermute | solution.py:994
  150.6 4.7 %shard_map.210.gate_ref = bf16[512,2048]{1,0:T(8,128)(2,1)S(1)} custom-call(bf16[512,1024]{1,0:T(8,128)(2,1)S(1)} %get-tuple-element.137.normed_ref, bf16[512,128]{1,0:T(8,128)(2,1)S(1)} %get-tuple-element.138.narrow_ref, bf16[4384,128]{1,0:T(8,128)(2,1)S(1)} %get-tuple-element.117.up_ref, bf16[2048,256]{1,0:T(8,128)(2,1)S(1)} %copy-done.25, ...), custom_call_target="tpu_custom_call" | custom-call | flops 2147483648 | bytes 10485760 | tf_op jit(solution)/shard_map/pallas_call | solution.py:627
  155.9 6.1 %shard_map.211 = (bf16[512,2048]{1,0:T(8,128)(2,1)S(1)}, bf16[512,2048]{1,0:T(8,128)(2,1)S(1)}) custom-call(bf16[2048,512]{1,0:T(8,128)(2,1)S(1)} %get-tuple-element.130.values_ref, bf16[512,256]{1,0:T(8,128)(2,1)S(1)} %get-tuple-element.131.bc_ref, f32[32,512]{1,0:T(8,128)S(1)} %get-tuple-element.132.step_ref, f32[32,512]{1,0:T(8,128)S(1)} %get-tuple-element.133.decay_ref, ...), custom_call_target="tpu_custom_call" | custom-call | flops 1207959552 | bytes 4194304 | tf_op jit(solution)/shard_map/pallas_call | solution.py:575
  162.1 6.2 %shard_map.212 = (bf16[512,2048]{1,0:T(8,128)(2,1)S(1)}, bf16[512,2048]{1,0:T(8,128)(2,1)S(1)}) custom-call(bf16[2048,512]{1,0:T(8,128)(2,1)S(1)} %get-tuple-element.130.values_ref, bf16[512,256]{1,0:T(8,128)(2,1)S(1)} %get-tuple-element.131.bc_ref, f32[32,512]{1,0:T(8,128)S(1)} %get-tuple-element.132.step_ref, ...), custom_call_target="tpu_custom_call", output_to_operand_aliasing={{0}: (11, {}), {1}: (12, {})} | custom-call | flops 1207959552 | bytes 4194304 | tf_op jit(solution)/shard_map/pallas_call | solution.py:575
  172.3 3.7 shard_map.213
  176.1 5.4 %shard_map.214 = (bf16[512,1024]{1,0:T(8,128)(2,1)S(1)}, bf16[512,128]{1,0:T(8,128)(2,1)S(1)}, bf16[512,2304]{1,0:T(8,128)(2,1)S(1)}, bf16[512,128]{1,0:T(8,128)(2,1)S(1)}, bf16[8,2304]{1,0:T(8,128)(2,1)S(1)}) custom-call(bf16[512,1024]{1,0:T(8,128)(2,1)S(1)} %get-tuple-element.151.input_ref, f32[1,14592]{1,0:T(1,128)S(1)} %get-tuple-element.152.vector_ref, ...), custom_call_target="tpu_custom_call" | custom-call | flops 2415919104 | bytes 23592960 | tf_op jit(solution)/shard_map/pallas_call | solution.py:607
  182.5 4.8 %collective-permute-start.29 = (bf16[8,2304]{1,0:T(8,128)(2,1)S(1)}, bf16[8,2304]{1,0:T(8,128)(2,1)S(1)}, u32[]{:S(2)}, u32[]{:S(2)}) collective-permute-start(bf16[8,2304]{1,0:T(8,128)(2,1)S(1)} %get-tuple-element.159), channel_id=1, source_target_pairs={{0,4},{4,8},{8,12},{1,5},{5,9},{9,13},{2,6},{6,10},{10,14},{3,7},{... | collective-permute-start | bytes 110600 | tf_op jit(solution)/shard_map/ppermute | solution.py:34
  188.5 7.7 %shard_map.215 = (bf16[2048,512]{1,0:T(8,128)(2,1)S(1)}, bf16[512,2048]{1,0:T(8,128)(2,1)S(1)}, bf16[512,256]{1,0:T(8,128)(2,1)S(1)}, bf16[512,256]{1,0:T(8,128)...) custom-call(bf16[512,2304]{1,0:T(8,128)(2,1)S(1)} %get-tuple-element, ...), custom_call_target="tpu_custom_call" | custom-call | flops 268435456 | bytes 10485760 | tf_op jit(solution)/shard_map/pallas_call | solution.py:522
  203.5 5.0 %collective-permute-start.30 = (bf16[2048,128]{1,0:T(8,128)(2,1)}, bf16[2048,128]{1,0:T(8,128)(2,1)}, u32[]{:S(2)}, u32[]{:S(2)}) collective-permute-start(bf16[2048,128]{1,0:T(8,128)(2,1)} %get-tuple-element.166), channel_id=1, source_target_pairs={{0,4},{4,8},{8,12},{1,5},{5,9},{9,13},{2,6},{6,10},{10,14},{3,7},{... | collective-permute-start | bytes 1572872 | tf_op jit(solution)/shard_map/ppermute | solution.py:34
  212.0 5.4 %shard_map.216.gate_ref = bf16[512,2048]{1,0:T(8,128)(2,1)S(1)} custom-call(bf16[512,1024]{1,0:T(8,128)(2,1)S(1)} %copy-done.60, bf16[512,128]{1,0:T(8,128)(2,1)S(1)} %copy-done.97, bf16[4384,128]{1,0:T(8,128)(2,1)S(1)} %get-tuple-element.154.up_ref, bf16[2048,256]{1,0:T(8,128)(2,1)S(1)} %copy-done.28, bf16[2048,256]{1,0:T(8,128)(2,1)} %collective-permute-done.31.second_ref, ...), custom_call_target="tpu_custom_call" | custom-call | flops 2147483648 | bytes 10485760 | tf_op jit(solution)/shard_map/pallas_call | solution.py:627
  217.5 6.1 %shard_map.217 = (bf16[512,2048]{1,0:T(8,128)(2,1)S(1)}, bf16[512,2048]{1,0:T(8,128)(2,1)S(1)}) custom-call(bf16[2048,512]{1,0:T(8,128)(2,1)S(1)} %copy-done.35, bf16[512,256]{1,0:T(8,128)(2,1)S(1)} %copy-done.76, f32[32,512]{1,0:T(8,128)S(1)} %copy-done.129, f32[32,512]{1,0:T(8,128)S(1)} %copy-done.117, f32[2,8,256]{2,1,0:T(8,128)S(1)} %copy-done.91, ...), custom_call_target="tpu_custom_call" | custom-call | flops 1207959552 | bytes 4194304 | tf_op jit(solution)/shard_map/pallas_call | solution.py:575
  223.7 7.2 %shard_map.218 = (bf16[512,2048]{1,0:T(8,128)(2,1)S(1)}, bf16[512,2048]{1,0:T(8,128)(2,1)S(1)}) custom-call(bf16[2048,512]{1,0:T(8,128)(2,1)S(1)} %copy-done.35, bf16[512,256]{1,0:T(8,128)(2,1)S(1)} %copy-done.76, f32[32,512]{1,0:T(8,128)S(1)} %copy-done.129, f32[32,512]{1,0:T(8,128)S(1)} %copy-done.117, ...), custom_call_target="tpu_custom_call", output_to_operand_aliasing={{0}: (11, {}), {1}: (12, {})} | custom-call | flops 1207959552 | bytes 4194304 | tf_op jit(solution)/shard_map/pallas_call | solution.py:575
  230.9 14.3 %shard_map.220 = (bf16[512,2048]{1,0:T(8,128)(2,1)S(1)}, bf16[2048,512]{1,0:T(8,128)(2,1)S(1)}, bf16[512,128]{1,0:T(8,128)(2,1)S(1)}, bf16[2048,128]{1,0:T(8,128)(2,1)S(1)}, bf16[2048,128]{1,0:T(8,128)(2,1)S(1)}) custom-call(bf16[512,1024]{1,0:T(8,128)(2,1)S(1)} %get-tuple-element.180.up_ref.up_stream_ref, f32[512,128]{1,0:T(8,128)S(1)} %compare_convert_fusion.lane_ref, ...), custom_call_target="tpu_custom_call" | custom-call | flops 2415919104 | bytes 14680064 | tf_op jit(solution)/shard_map/pallas_call | solution.py:658
  246.5 9.1 %shard_map.221 = (bf16[512,2048]{1,0:T(8,128)(2,1)S(1)}, bf16[512,256]{1,0:T(8,128)(2,1)S(1)}, bf16[512,128]{1,0:T(8,128)(2,1)S(1)}, bf16[8,2304]{1,0:T(8,128)(2,1)S(1)}) custom-call(bf16[2048,512]{1,0:T(8,128)(2,1)S(1)} %copy-done.35, bf16[2048,512]{1,0:T(8,128)(2,1)S(1)} %get-tuple-element.182.grad_ref, bf16[512,256]{1,0:T(8,128)(2,1)S(1)} %copy-done.76, ...), custom_call_target="tpu_custom_call" | custom-call | flops 3758096384 | bytes 5242880 | tf_op jit(solution)/shard_map/pallas_call | solution.py:739
  257.0 5.0 %shard_map.219 = (bf16[512,128]{1,0:T(8,128)(2,1)S(1)}, bf16[512,1024]{1,0:T(8,128)(2,1)S(1)}) custom-call(bf16[512,2048]{1,0:T(8,128)(2,1)S(1)} %get-tuple-element.174.normed_ref.normed_out_ref, bf16[512,1024]{1,0:T(8,128)(2,1)S(1)} %get-tuple-element.151.input_ref, bf16[2048,128]{1,0:T(8,128)(2,1)S(1)} %copy-done.49, ...), custom_call_target="tpu_custom_call" | custom-call | flops 2147483648 | bytes 12582912 | tf_op jit(solution)/shard_map/pallas_call | solution.py:642
  264.0 4.5 shard_map.233.rest_0_
  268.5 5.9 %shard_map.224.part_ref = f32[512,1152]{1,0:T(8,128)S(1)} custom-call(bf16[512,2048]{1,0:T(8,128)(2,1)S(1)} %get-tuple-element.196.grad_ref.grad_gate_ref, bf16[4384,128]{1,0:T(8,128)(2,1)S(1)} %copy-done.11, bf16[2048,256]{1,0:T(8,128)(2,1)S(1)} %copy-done.29, bf16[2048,256]{1,0:T(8,128)(2,1)} %collective-permute-done.31.second_ref, ...), custom_call_target="tpu_custom_call" | custom-call | flops 2415919104 | bytes 10485760 | tf_op jit(solution)/shard_map/pallas_call | solution.py:688
  274.5 8.2 %shard_map.222 = (bf16[512,2048]{1,0:T(8,128)(2,1)S(1)}, bf16[512,256]{1,0:T(8,128)(2,1)S(1)}, bf16[512,128]{1,0:T(8,128)(2,1)S(1)}) custom-call(bf16[2048,512]{1,0:T(8,128)(2,1)S(1)} %copy-done.35, bf16[2048,512]{1,0:T(8,128)(2,1)S(1)} %get-tuple-element.182.grad_ref, ...), custom_call_target="tpu_custom_call", output_to_operand_aliasing={{0}: (15, {}), {1}: (16, {}), {2}: (17, {})} | custom-call | flops 3758096384 | bytes 5242880 | tf_op jit(solution)/shard_map/pallas_call | solution.py:739
  282.9 4.9 %shard_map.223.grad_ref.mixed_ref = bf16[512,2304]{1,0:T(8,128)(2,1)S(1)} custom-call(bf16[512,2048]{1,0:T(8,128)(2,1)S(1)} %get-tuple-element.191.grad_ref, bf16[512,256]{1,0:T(8,128)(2,1)S(1)} %get-tuple-element.192.grad_bc_ref, bf16[512,2048]{1,0:T(8,128)(2,1)S(1)} %copy-done.88, bf16[512,256]{1,0:T(8,128)(2,1)S(1)} %copy-done.137, ...), custom_call_target="tpu_custom_call" | custom-call | flops 11796480 | bytes 7077888 | tf_op jit(solution)/shard_map/pallas_call | solution.py:764
  287.9 6.0 %shard_map.225 = (bf16[512,1024]{1,0:T(8,128)(2,1)S(1)}, bf16[512,128]{1,0:T(8,128)(2,1)S(1)}) custom-call(bf16[512,2304]{1,0:T(8,128)(2,1)S(1)} %shard_map.223.grad_ref.mixed_ref, bf16[512,128]{1,0:T(8,128)(2,1)S(1)} %get-tuple-element.195.raw_ref, f32[512,1152]{1,0:T(8,128)S(1)} %shard_map.224.part_ref, bf16[512,1024]{1,0:T(8,128)(2,1)S(1)} %copy-done.15, ...), custom_call_target="tpu_custom_call" | custom-call | flops 2415919104 | bytes 23592960 | tf_op jit(solution)/shard_map/pallas_call | solution.py:704
  298.0 12.8 %shard_map.226 = (bf16[512,2048]{1,0:T(8,128)(2,1)S(1)}, bf16[2048,512]{1,0:T(8,128)(2,1)S(1)}, bf16[512,128]{1,0:T(8,128)(2,1)S(1)}, bf16[2048,128]{1,0:T(8,128)(2,1)S(1)}, bf16[2048,128]{1,0:T(8,128)(2,1)S(1)}) custom-call(bf16[512,1024]{1,0:T(8,128)(2,1)S(1)} %get-tuple-element.197.up_ref.up_stream_ref, f32[512,128]{1,0:T(8,128)S(1)} %copy-done.17, ...), custom_call_target="tpu_custom_call" | custom-call | flops 2415919104 | bytes 14680064 | tf_op jit(solution)/shard_map/pallas_call | solution.py:658
  310.8 4.6 shard_map.235
  318.7 8.3 %shard_map.227 = (bf16[512,2048]{1,0:T(8,128)(2,1)S(1)}, bf16[512,256]{1,0:T(8,128)(2,1)S(1)}, bf16[512,128]{1,0:T(8,128)(2,1)S(1)}, bf16[8,2304]{1,0:T(8,128)(2,1)S(1)}) custom-call(bf16[2048,512]{1,0:T(8,128)(2,1)S(1)} %copy-done.33, bf16[2048,512]{1,0:T(8,128)(2,1)S(1)} %get-tuple-element.199.grad_ref, bf16[512,256]{1,0:T(8,128)(2,1)S(1)} %copy-done.73, ...), custom_call_target="tpu_custom_call" | custom-call | flops 3758096384 | bytes 5242880 | tf_op jit(solution)/shard_map/pallas_call | solution.py:739
  328.5 5.6 %shard_map.230.part_ref = f32[512,1152]{1,0:T(8,128)S(1)} custom-call(bf16[512,2048]{1,0:T(8,128)(2,1)S(1)} %get-tuple-element.212.grad_ref.grad_gate_ref, bf16[4384,128]{1,0:T(8,128)(2,1)S(1)} %copy-done.9, bf16[2048,256]{1,0:T(8,128)(2,1)S(1)} %copy-done.26, bf16[2048,256]{1,0:T(8,128)(2,1)} %collective-permute-done.16.second_ref, ...), custom_call_target="tpu_custom_call" | custom-call | flops 2415919104 | bytes 10485760 | tf_op jit(solution)/shard_map/pallas_call | solution.py:688
  334.8 8.3 %shard_map.228 = (bf16[512,2048]{1,0:T(8,128)(2,1)S(1)}, bf16[512,256]{1,0:T(8,128)(2,1)S(1)}, bf16[512,128]{1,0:T(8,128)(2,1)S(1)}) custom-call(bf16[2048,512]{1,0:T(8,128)(2,1)S(1)} %copy-done.33, bf16[2048,512]{1,0:T(8,128)(2,1)S(1)} %get-tuple-element.199.grad_ref, ...), custom_call_target="tpu_custom_call", output_to_operand_aliasing={{0}: (15, {}), {1}: (16, {}), {2}: (17, {})} | custom-call | flops 3758096384 | bytes 5242880 | tf_op jit(solution)/shard_map/pallas_call | solution.py:739
  343.2 4.9 %shard_map.229.grad_ref.mixed_ref = bf16[512,2304]{1,0:T(8,128)(2,1)S(1)} custom-call(bf16[512,2048]{1,0:T(8,128)(2,1)S(1)} %get-tuple-element.208.grad_ref, bf16[512,256]{1,0:T(8,128)(2,1)S(1)} %get-tuple-element.209.grad_bc_ref, bf16[512,2048]{1,0:T(8,128)(2,1)S(1)} %copy-done.86, bf16[512,256]{1,0:T(8,128)(2,1)S(1)} %copy-done.135, ...), custom_call_target="tpu_custom_call" | custom-call | flops 11796480 | bytes 7077888 | tf_op jit(solution)/shard_map/pallas_call | solution.py:764
  348.2 7.0 %shard_map.231 = (bf16[512,1024]{1,0:T(8,128)(2,1)S(1)}, bf16[512,128]{1,0:T(8,128)(2,1)S(1)}) custom-call(bf16[512,2304]{1,0:T(8,128)(2,1)S(1)} %shard_map.229.grad_ref.mixed_ref, bf16[512,128]{1,0:T(8,128)(2,1)S(1)} %get-tuple-element.211.raw_ref, f32[512,1152]{1,0:T(8,128)S(1)} %shard_map.230.part_ref, bf16[512,1024]{1,0:T(8,128)(2,1)S(1)} %copy-done.23, ...), custom_call_target="tpu_custom_call" | custom-call | flops 2415919104 | bytes 23592960 | tf_op jit(solution)/shard_map/pallas_call | solution.py:704
  369.6 3.8 collective-permute-start.49
  383.3 8.7 %collective-permute-done.60 = bf16[1728,128]{1,0:T(8,128)(2,1)S(1)} collective-permute-done((bf16[1728,128]{1,0:T(8,128)(2,1)S(1)}, bf16[1728,128]{1,0:T(8,128)(2,1)S(1)}, u32[]{:S(2)}, u32[]{:S(2)}) %collective-permute-start.60) | collective-permute-done | bytes 442400 | tf_op jit(solution)/shard_map/ppermute | solution.py:976
  393.6 5.7 %collective-permute-done.61 = bf16[1728,128]{1,0:T(8,128)(2,1)S(1)} collective-permute-done((bf16[1728,128]{1,0:T(8,128)(2,1)S(1)}, bf16[1728,128]{1,0:T(8,128)(2,1)S(1)}, u32[]{:S(2)}, u32[]{:S(2)}) %collective-permute-start.61) | collective-permute-done | bytes 442400 | tf_op jit(solution)/shard_map/ppermute | solution.py:976
  400.2 3.5 collective-permute-start.64
  404.6 4.7 %collective-permute-start.54 = (bf16[112,128]{1,0:T(8,128)(2,1)S(1)}, bf16[112,128]{1,0:T(8,128)(2,1)S(1)}, u32[]{:S(2)}, u32[]{:S(2)}) collective-permute-start(bf16[112,128]{1,0:T(8,128)(2,1)S(1)} %get-tuple-element.239), channel_id=1, source_target_pairs={{0,12},{4,8},{8,4},{12,0},{1,13},{5,9},{9,5},{13,1},{2,14},{6,10},... | collective-permute-start | bytes 86024 | tf_op jit(solution)/shard_map/ppermute | solution.py:976
  410.9 5.2 %collective-permute-start.66 = (bf16[432,128]{1,0:T(8,128)(2,1)S(1)}, bf16[432,128]{1,0:T(8,128)(2,1)S(1)}, u32[]{:S(2)}, u32[]{:S(2)}) collective-permute-start(bf16[432,128]{1,0:T(8,128)(2,1)S(1)} %get-tuple-element.241), channel_id=1, source_target_pairs={{0,4},{4,0},{8,12},{12,8},{1,5},{5,1},{9,13},{13,9},{2,6},{6,2},{1... | collective-permute-start | bytes 331784 | tf_op jit(solution)/shard_map/ppermute | solution.py:976
  434.3 11.4 %collective-permute-done.70 = bf16[1728,128]{1,0:T(8,128)(2,1)S(1)} collective-permute-done((bf16[1728,128]{1,0:T(8,128)(2,1)S(1)}, bf16[1728,128]{1,0:T(8,128)(2,1)S(1)}, u32[]{:S(2)}, u32[]{:S(2)}) %collective-permute-start.70) | collective-permute-done | bytes 442400 | tf_op jit(solution)/shard_map/ppermute | solution.py:976
  446.8 8.1 %collective-permute-done.71 = bf16[1728,128]{1,0:T(8,128)(2,1)S(1)} collective-permute-done((bf16[1728,128]{1,0:T(8,128)(2,1)S(1)}, bf16[1728,128]{1,0:T(8,128)(2,1)S(1)}, u32[]{:S(2)}, u32[]{:S(2)}) %collective-permute-start.71) | collective-permute-done | bytes 442400 | tf_op jit(solution)/shard_map/ppermute | solution.py:976
  (542 shorter events, 137.4 us)
Async XLA Ops:
  2.7 15.7 %collective-permute-start.1 = (s32[8]{0:T(128)S(1)}, s32[8]{0:T(128)S(1)}, u32[]{:S(2)}, u32[]{:S(2)}) collective-permute-start(s32[8]{0:T(128)S(1)} %get-tuple-element.281), channel_id=1, source_target_pairs={{4,0},{8,4},{12,8},{5,1},{9,5},{13,9},{6,2},{10,6},{14,10},{7,3},{... | collective-permute-start | bytes 104 | tf_op jit(solution)/shard_map/ppermute | solution.py:34
  4.0 14.8 %collective-permute-start = (s32[8]{0:T(128)S(1)}, s32[8]{0:T(128)S(1)}, u32[]{:S(2)}, u32[]{:S(2)}) collective-permute-start(s32[8]{0:T(128)S(1)} %get-tuple-element.280), channel_id=1, source_target_pairs={{0,4},{4,8},{8,12},{1,5},{5,9},{9,13},{2,6},{6,10},{10,14},{3,7},{... | collective-permute-start | bytes 104 | tf_op jit(solution)/shard_map/ppermute | solution.py:34
  9.2 33.1 %collective-permute-start.2 = (f32[3,32]{1,0:T(4,128)S(1)}, f32[3,32]{1,0:T(4,128)S(1)}, u32[]{:S(2)}, u32[]{:S(2)}) collective-permute-start(f32[3,32]{1,0:T(4,128)S(1)} %pad_maximum_fusion.1), channel_id=1, source_target_pairs={{0,16},{16,0},{1,17},{17,1},{2,18},{18,2},{3,19},{19,3},{4,20},{20... | collective-permute-start | bytes 1160 | tf_op jit(solution)/shard_map/ppermute | solution.py:971
  12.7 16.5 %collective-permute-start.9 = (bf16[2336,256]{1,0:T(8,128)(2,1)S(1)}, bf16[2336,256]{1,0:T(8,128)(2,1)}, u32[]{:S(2)}, u32[]{:S(2)}) collective-permute-start(bf16[2336,256]{1,0:T(8,128)(2,1)S(1)} %get-tuple-element.118.first_ref), channel_id=1, source_target_pairs={{0,1},{1,0},{2,3},{3,2},{16,18},{17,19},{18,16},{19,17},{4,5},{5,4... | collective-permute-start | bytes 3588104 | tf_op jit(solution)/shard_map/ppermute | solution.py:994
  16.9 15.3 %collective-permute-start.15 = (bf16[2048,256]{1,0:T(8,128)(2,1)}, bf16[2048,256]{1,0:T(8,128)(2,1)}, u32[]{:S(2)}, u32[]{:S(2)}) collective-permute-start(bf16[2048,256]{1,0:T(8,128)(2,1)} %slice.99), channel_id=1, source_target_pairs={{0,16},{16,0},{1,17},{17,1},{2,18},{18,2},{3,19},{19,3},{4,20},{20... | collective-permute-start | bytes 3145736 | tf_op jit(solution)/shard_map/ppermute | solution.py:971
  18.4 36.9 %collective-permute-start.7 = (f32[1,14592]{1,0:T(1,128)S(1)}, f32[1,14592]{1,0:T(1,128)S(1)}, u32[]{:S(2)}, u32[]{:S(2)}) collective-permute-start(f32[1,14592]{1,0:T(1,128)S(1)} %constant_dynamic-update-slice_fusion), channel_id=1, source_target_pairs={{0,16},{16,0},{1,17},{17,1},{2,18},{18,2},{3,19},{19,3},{4,20},{20... | collective-permute-start | bytes 175112 | tf_op jit(solution)/shard_map/ppermute | solution.py:971
  18.8 77.7 %collective-permute-start.4 = (bf16[4384,128]{1,0:T(8,128)(2,1)}, bf16[4384,128]{1,0:T(8,128)(2,1)}, u32[]{:S(2)}, u32[]{:S(2)}) collective-permute-start(bf16[4384,128]{1,0:T(8,128)(2,1)} %bitcast.128), channel_id=1, source_target_pairs={{0,16},{16,0},{1,17},{17,1},{2,18},{18,2},{3,19},{19,3},{4,20},{20... | collective-permute-start | bytes 3366920 | tf_op jit(solution)/shard_map/ppermute | solution.py:971
  40.4 14.9 %collective-permute-start.16 = (bf16[2048,256]{1,0:T(8,128)(2,1)S(1)}, bf16[2048,256]{1,0:T(8,128)(2,1)}, u32[]{:S(2)}, u32[]{:S(2)}) collective-permute-start(bf16[2048,256]{1,0:T(8,128)(2,1)S(1)} %get-tuple-element.140.first_ref), channel_id=1, source_target_pairs={{0,1},{1,0},{2,3},{3,2},{16,18},{17,19},{18,16},{19,17},{4,5},{5,4... | collective-permute-start | bytes 3145736 | tf_op jit(solution)/shard_map/ppermute | solution.py:994
  42.3 33.3 %collective-permute-start.5 = (bf16[2048,128]{1,0:T(8,128)(2,1)}, bf16[2048,128]{1,0:T(8,128)(2,1)}, u32[]{:S(2)}, u32[]{:S(2)}) collective-permute-start(bf16[2048,128]{1,0:T(8,128)(2,1)} %bitcast.129), channel_id=1, source_target_pairs={{0,16},{16,0},{1,17},{17,1},{2,18},{18,2},{3,19},{19,3},{4,20},{20... | collective-permute-start | bytes 1572872 | tf_op jit(solution)/shard_map/ppermute | solution.py:971
  42.7 29.3 %collective-permute-start.6 = (bf16[128,1024]{1,0:T(8,128)(2,1)}, bf16[128,1024]{1,0:T(8,128)(2,1)S(1)}, u32[]{:S(2)}, u32[]{:S(2)}) collective-permute-start(bf16[128,1024]{1,0:T(8,128)(2,1)} %bitcast.134), channel_id=1, source_target_pairs={{0,16},{16,0},{1,17},{17,1},{2,18},{18,2},{3,19},{19,3},{4,20},{20... | collective-permute-start | bytes 786440 | tf_op jit(solution)/shard_map/ppermute | solution.py:971
  55.3 20.2 %collective-permute-start.3 = (bf16[1024,128]{1,0:T(8,128)(2,1)S(1)}, bf16[1024,128]{1,0:T(8,128)(2,1)S(1)}, u32[]{:S(2)}, u32[]{:S(2)}) collective-permute-start(bf16[1024,128]{1,0:T(8,128)(2,1)S(1)} %bitcast.135), channel_id=1, source_target_pairs={{0,16},{16,0},{1,17},{17,1},{2,18},{18,2},{3,19},{19,3},{4,20},{20... | collective-permute-start | bytes 786440 | tf_op jit(solution)/shard_map/ppermute | solution.py:971
  55.3 14.9 %collective-permute-start.21 = (bf16[512,1024]{1,0:T(8,128)(2,1)S(1)}, bf16[512,1024]{1,0:T(8,128)(2,1)S(1)}, u32[]{:S(2)}, u32[]{:S(2)}) collective-permute-start(bf16[512,1024]{1,0:T(8,128)(2,1)S(1)} %get-tuple-element.149.first_ref), channel_id=1, source_target_pairs={{0,1},{1,0},{2,3},{3,2},{16,18},{17,19},{18,16},{19,17},{4,5},{5,4... | collective-permute-start | bytes 3145736 | tf_op jit(solution)/shard_map/ppermute | solution.py:994
  70.2 24.1 %collective-permute-start.25 = (bf16[2336,256]{1,0:T(8,128)(2,1)S(1)}, bf16[2336,256]{1,0:T(8,128)(2,1)S(1)}, u32[]{:S(2)}, u32[]{:S(2)}) collective-permute-start(bf16[2336,256]{1,0:T(8,128)(2,1)S(1)} %copy-done.45), channel_id=1, source_target_pairs={{0,1},{1,0},{2,3},{3,2},{16,18},{17,19},{18,16},{19,17},{4,5},{5,4... | collective-permute-start | bytes 3588104 | tf_op jit(solution)/shard_map/ppermute | solution.py:994
  73.9 14.9 %collective-permute-start.18 = (bf16[1024,256]{1,0:T(8,128)(2,1)S(1)}, bf16[1024,256]{1,0:T(8,128)(2,1)S(1)}, u32[]{:S(2)}, u32[]{:S(2)}) collective-permute-start(bf16[1024,256]{1,0:T(8,128)(2,1)S(1)} %constant_dynamic-slice_fusion.18), channel_id=1, source_target_pairs={{0,2},{1,3},{2,0},{3,1},{16,17},{17,16},{18,19},{19,18},{4,6},{5,7... | collective-permute-start | bytes 1572872 | tf_op jit(solution)/shard_map/ppermute | solution.py:994
  77.7 20.1 %collective-permute-start.10 = (bf16[2336,256]{1,0:T(8,128)(2,1)}, bf16[2336,256]{1,0:T(8,128)(2,1)S(1)}, u32[]{:S(2)}, u32[]{:S(2)}) collective-permute-start(bf16[2336,256]{1,0:T(8,128)(2,1)} %collective-permute-done.9.second_ref), channel_id=1, source_target_pairs={{0,16},{16,0},{1,17},{17,1},{2,18},{18,2},{3,19},{19,3},{4,20},{20... | collective-permute-start | bytes 3588104 | tf_op jit(solution)/shard_map/ppermute | solution.py:971
  77.7 20.2 %collective-permute-start.12 = (bf16[1184,256]{1,0:T(8,128)(2,1)S(1)}, bf16[1184,256]{1,0:T(8,128)(2,1)S(1)}, u32[]{:S(2)}, u32[]{:S(2)}) collective-permute-start(bf16[1184,256]{1,0:T(8,128)(2,1)S(1)} %copy-done.106), channel_id=1, source_target_pairs={{0,16},{16,0},{1,17},{17,1},{2,18},{18,2},{3,19},{19,3},{4,20},{20... | collective-permute-start | bytes 1818632 | tf_op jit(solution)/shard_map/ppermute | solution.py:971
  88.9 13.7 %collective-permute-start.23 = (bf16[256,1024]{1,0:T(8,128)(2,1)S(1)}, bf16[256,1024]{1,0:T(8,128)(2,1)S(1)}, u32[]{:S(2)}, u32[]{:S(2)}) collective-permute-start(bf16[256,1024]{1,0:T(8,128)(2,1)S(1)} %constant_dynamic-slice_fusion.17), channel_id=1, source_target_pairs={{0,2},{1,3},{2,0},{3,1},{16,17},{17,16},{18,19},{19,18},{4,6},{5,7... | collective-permute-start | bytes 1572872 | tf_op jit(solution)/shard_map/ppermute | solution.py:994
  94.3 35.6 %collective-permute-start.31 = (bf16[2048,256]{1,0:T(8,128)(2,1)S(1)}, bf16[2048,256]{1,0:T(8,128)(2,1)}, u32[]{:S(2)}, u32[]{:S(2)}) collective-permute-start(bf16[2048,256]{1,0:T(8,128)(2,1)S(1)} %copy-done.27), channel_id=1, source_target_pairs={{0,1},{1,0},{2,3},{3,2},{16,18},{17,19},{18,16},{19,17},{4,5},{5,4... | collective-permute-start | bytes 3145736 | tf_op jit(solution)/shard_map/ppermute | solution.py:994
  102.6 27.3 %collective-permute-start.27 = (bf16[1184,256]{1,0:T(8,128)(2,1)S(1)}, bf16[1184,256]{1,0:T(8,128)(2,1)S(1)}, u32[]{:S(2)}, u32[]{:S(2)}) collective-permute-start(bf16[1184,256]{1,0:T(8,128)(2,1)S(1)} %constant_dynamic-slice_fusion.16), channel_id=1, source_target_pairs={{0,2},{1,3},{2,0},{3,1},{16,17},{17,16},{18,19},{19,18},{4,6},{5,7... | collective-permute-start | bytes 1818632 | tf_op jit(solution)/shard_map/ppermute | solution.py:994
  125.1 16.7 %collective-permute-start.17 = (bf16[2048,256]{1,0:T(8,128)(2,1)}, bf16[2048,256]{1,0:T(8,128)(2,1)S(1)}, u32[]{:S(2)}, u32[]{:S(2)}) collective-permute-start(bf16[2048,256]{1,0:T(8,128)(2,1)} %collective-permute-done.16.second_ref), channel_id=1, source_target_pairs={{0,16},{16,0},{1,17},{17,1},{2,18},{18,2},{3,19},{19,3},{4,20},{20... | collective-permute-start | bytes 3145736 | tf_op jit(solution)/shard_map/ppermute | solution.py:971
  125.2 16.0 %collective-permute-start.14 = (bf16[2048,128]{1,0:T(8,128)(2,1)S(1)}, bf16[2048,128]{1,0:T(8,128)(2,1)S(1)}, u32[]{:S(2)}, u32[]{:S(2)}) collective-permute-start(bf16[2048,128]{1,0:T(8,128)(2,1)S(1)} %get-tuple-element.136), channel_id=1, source_target_pairs={{0,4},{4,8},{8,12},{1,5},{5,9},{9,13},{2,6},{6,10},{10,14},{3,7},{... | collective-permute-start | bytes 1572872 | tf_op jit(solution)/shard_map/ppermute | solution.py:34
  129.9 25.4 %collective-permute-start.35 = (bf16[512,1024]{1,0:T(8,128)(2,1)S(1)}, bf16[512,1024]{1,0:T(8,128)(2,1)}, u32[]{:S(2)}, u32[]{:S(2)}) collective-permute-start(bf16[512,1024]{1,0:T(8,128)(2,1)S(1)} %get-tuple-element.177.first_ref), channel_id=1, source_target_pairs={{0,1},{1,0},{2,3},{3,2},{16,18},{17,19},{18,16},{19,17},{4,5},{5,4... | collective-permute-start | bytes 3145736 | tf_op jit(solution)/shard_map/ppermute | solution.py:994
  130.0 41.7 %collective-permute-start.26 = (bf16[2336,256]{1,0:T(8,128)(2,1)S(1)}, bf16[2336,256]{1,0:T(8,128)(2,1)S(1)}, u32[]{:S(2)}, u32[]{:S(2)}) collective-permute-start(bf16[2336,256]{1,0:T(8,128)(2,1)S(1)} %collective-permute-done.25.second_ref), channel_id=1, source_target_pairs={{0,16},{16,0},{1,17},{17,1},{2,18},{18,2},{3,19},{19,3},{4,20},{20... | collective-permute-start | bytes 3588104 | tf_op jit(solution)/shard_map/ppermute | solution.py:971
  141.8 29.5 %collective-permute-start.22 = (bf16[512,1024]{1,0:T(8,128)(2,1)S(1)}, bf16[512,1024]{1,0:T(8,128)(2,1)S(1)}, u32[]{:S(2)}, u32[]{:S(2)}) collective-permute-start(bf16[512,1024]{1,0:T(8,128)(2,1)S(1)} %collective-permute-done.21.second_ref), channel_id=1, source_target_pairs={{0,16},{16,0},{1,17},{17,1},{2,18},{18,2},{3,19},{19,3},{4,20},{20... | collective-permute-start | bytes 3145736 | tf_op jit(solution)/shard_map/ppermute | solution.py:971
  141.8 29.3 %collective-permute-start.24 = (bf16[256,1024]{1,0:T(8,128)(2,1)S(1)}, bf16[256,1024]{1,0:T(8,128)(2,1)S(1)}, u32[]{:S(2)}, u32[]{:S(2)}) collective-permute-start(bf16[256,1024]{1,0:T(8,128)(2,1)S(1)} %collective-permute-done.23.near_ref), channel_id=1, source_target_pairs={{0,16},{16,0},{1,17},{17,1},{2,18},{18,2},{3,19},{19,3},{4,20},{20... | collective-permute-start | bytes 1572872 | tf_op jit(solution)/shard_map/ppermute | solution.py:971
  150.5 25.5 %collective-permute-start.28 = (bf16[1184,256]{1,0:T(8,128)(2,1)S(1)}, bf16[1184,256]{1,0:T(8,128)(2,1)S(1)}, u32[]{:S(2)}, u32[]{:S(2)}) collective-permute-start(bf16[1184,256]{1,0:T(8,128)(2,1)S(1)} %collective-permute-done.27.near_ref), channel_id=1, source_target_pairs={{0,16},{16,0},{1,17},{17,1},{2,18},{18,2},{3,19},{19,3},{4,20},{20... | collective-permute-start | bytes 1818632 | tf_op jit(solution)/shard_map/ppermute | solution.py:971
  155.4 53.2 %collective-permute-start.32 = (bf16[2048,256]{1,0:T(8,128)(2,1)}, bf16[2048,256]{1,0:T(8,128)(2,1)}, u32[]{:S(2)}, u32[]{:S(2)}) collective-permute-start(bf16[2048,256]{1,0:T(8,128)(2,1)} %collective-permute-done.31.second_ref), channel_id=1, source_target_pairs={{0,16},{16,0},{1,17},{17,1},{2,18},{18,2},{3,19},{19,3},{4,20},{20... | collective-permute-start | bytes 3145736 | tf_op jit(solution)/shard_map/ppermute | solution.py:971
  171.1 37.4 %collective-permute-start.34 = (bf16[1024,256]{1,0:T(8,128)(2,1)}, bf16[1024,256]{1,0:T(8,128)(2,1)}, u32[]{:S(2)}, u32[]{:S(2)}) collective-permute-start(bf16[1024,256]{1,0:T(8,128)(2,1)} %collective-permute-done.33.near_ref), channel_id=1, source_target_pairs={{0,16},{16,0},{1,17},{17,1},{2,18},{18,2},{3,19},{19,3},{4,20},{20... | collective-permute-start | bytes 1572872 | tf_op jit(solution)/shard_map/ppermute | solution.py:971
  171.3 59.6 %collective-permute-start.36 = (bf16[512,1024]{1,0:T(8,128)(2,1)}, bf16[512,1024]{1,0:T(8,128)(2,1)}, u32[]{:S(2)}, u32[]{:S(2)}) collective-permute-start(bf16[512,1024]{1,0:T(8,128)(2,1)} %collective-permute-done.35.second_ref), channel_id=1, source_target_pairs={{0,16},{16,0},{1,17},{17,1},{2,18},{18,2},{3,19},{19,3},{4,20},{20... | collective-permute-start | bytes 3145736 | tf_op jit(solution)/shard_map/ppermute | solution.py:971
  171.7 36.8 %collective-permute-start.37 = (bf16[256,1024]{1,0:T(8,128)(2,1)S(1)}, bf16[256,1024]{1,0:T(8,128)(2,1)}, u32[]{:S(2)}, u32[]{:S(2)}) collective-permute-start(bf16[256,1024]{1,0:T(8,128)(2,1)S(1)} %constant_dynamic-slice_fusion.14), channel_id=1, source_target_pairs={{0,2},{1,3},{2,0},{3,1},{16,17},{17,16},{18,19},{19,18},{4,6},{5,7... | collective-permute-start | bytes 1572872 | tf_op jit(solution)/shard_map/ppermute | solution.py:994
  203.5 20.1 %collective-permute-start.30 = (bf16[2048,128]{1,0:T(8,128)(2,1)}, bf16[2048,128]{1,0:T(8,128)(2,1)}, u32[]{:S(2)}, u32[]{:S(2)}) collective-permute-start(bf16[2048,128]{1,0:T(8,128)(2,1)} %get-tuple-element.166), channel_id=1, source_target_pairs={{0,4},{4,8},{8,12},{1,5},{5,9},{9,13},{2,6},{6,10},{10,14},{3,7},{... | collective-permute-start | bytes 1572872 | tf_op jit(solution)/shard_map/ppermute | solution.py:34
  208.6 22.3 %collective-permute-start.38 = (bf16[256,1024]{1,0:T(8,128)(2,1)}, bf16[256,1024]{1,0:T(8,128)(2,1)}, u32[]{:S(2)}, u32[]{:S(2)}) collective-permute-start(bf16[256,1024]{1,0:T(8,128)(2,1)} %collective-permute-done.37.near_ref), channel_id=1, source_target_pairs={{0,16},{16,0},{1,17},{17,1},{2,18},{18,2},{3,19},{19,3},{4,20},{20... | collective-permute-start | bytes 1572872 | tf_op jit(solution)/shard_map/ppermute | solution.py:971
  245.2 29.3 %collective-permute-start.40 = (bf16[2048,128]{1,0:T(8,128)(2,1)S(1)}, bf16[2048,128]{1,0:T(8,128)(2,1)S(1)}, u32[]{:S(2)}, u32[]{:S(2)}) collective-permute-start(bf16[2048,128]{1,0:T(8,128)(2,1)S(1)} %get-tuple-element.184), channel_id=1, source_target_pairs={{4,0},{8,4},{12,8},{5,1},{9,5},{13,9},{6,2},{10,6},{14,10},{7,3},{... | collective-permute-start | bytes 1572872 | tf_op jit(solution)/shard_map/ppermute | solution.py:34
  255.7 27.1 %collective-permute-start.41 = (bf16[8,2304]{1,0:T(8,128)(2,1)S(1)}, bf16[8,2304]{1,0:T(8,128)(2,1)S(1)}, u32[]{:S(2)}, u32[]{:S(2)}) collective-permute-start(bf16[8,2304]{1,0:T(8,128)(2,1)S(1)} %get-tuple-element.193), channel_id=1, source_target_pairs={{4,0},{8,4},{12,8},{5,1},{9,5},{13,9},{6,2},{10,6},{14,10},{7,3},{... | collective-permute-start | bytes 110600 | tf_op jit(solution)/shard_map/ppermute | solution.py:34
  263.1 94.3 %collective-permute-start.39 = (bf16[512,1024]{1,0:T(8,128)(2,1)}, bf16[512,1024]{1,0:T(8,128)(2,1)}, u32[]{:S(2)}, u32[]{:S(2)}) collective-permute-start(bf16[512,1024]{1,0:T(8,128)(2,1)} %broadcast_select_fusion.11), channel_id=1, source_target_pairs={{0,16},{16,0},{1,17},{17,1},{2,18},{18,2},{3,19},{19,3},{4,20},{20... | collective-permute-start | bytes 3145736 | tf_op jit(solution)/shard_map/ppermute | solution.py:971
  316.7 60.0 %collective-permute-start.59 = (bf16[6912,128]{1,0:T(8,128)(2,1)}, bf16[6912,128]{1,0:T(8,128)(2,1)}, u32[]{:S(2)}, u32[]{:S(2)}) collective-permute-start(bf16[6912,128]{1,0:T(8,128)(2,1)} %constant_dynamic-slice_fusion.6), channel_id=1, source_target_pairs={{0,16},{16,0},{1,17},{17,1},{2,18},{18,2},{3,19},{19,3},{4,20},{20... | collective-permute-start | bytes 5308424 | tf_op jit(solution)/shard_map/ppermute | solution.py:971
  317.3 17.6 %collective-permute-start.42 = (bf16[2048,128]{1,0:T(8,128)(2,1)S(1)}, bf16[2048,128]{1,0:T(8,128)(2,1)S(1)}, u32[]{:S(2)}, u32[]{:S(2)}) collective-permute-start(bf16[2048,128]{1,0:T(8,128)(2,1)S(1)} %get-tuple-element.201), channel_id=1, source_target_pairs={{4,0},{8,4},{12,8},{5,1},{9,5},{13,9},{6,2},{10,6},{14,10},{7,3},{... | collective-permute-start | bytes 1572872 | tf_op jit(solution)/shard_map/ppermute | solution.py:34
  327.0 16.1 %collective-permute-start.43 = (bf16[8,2304]{1,0:T(8,128)(2,1)S(1)}, bf16[8,2304]{1,0:T(8,128)(2,1)S(1)}, u32[]{:S(2)}, u32[]{:S(2)}) collective-permute-start(bf16[8,2304]{1,0:T(8,128)(2,1)S(1)} %get-tuple-element.210), channel_id=1, source_target_pairs={{4,0},{8,4},{12,8},{5,1},{9,5},{13,9},{6,2},{10,6},{14,10},{7,3},{... | collective-permute-start | bytes 110600 | tf_op jit(solution)/shard_map/ppermute | solution.py:34
  378.8 13.2 %collective-permute-start.60 = (bf16[1728,128]{1,0:T(8,128)(2,1)S(1)}, bf16[1728,128]{1,0:T(8,128)(2,1)S(1)}, u32[]{:S(2)}, u32[]{:S(2)}) collective-permute-start(bf16[1728,128]{1,0:T(8,128)(2,1)S(1)} %get-tuple-element.258), channel_id=1, source_target_pairs={{0,1},{1,0},{2,3},{3,2},{4,5},{5,4},{6,7},{7,6},{8,9},{9,8},{10,11... | collective-permute-start | bytes 1327112 | tf_op jit(solution)/shard_map/ppermute | solution.py:976
  379.7 19.6 %collective-permute-start.61 = (bf16[1728,128]{1,0:T(8,128)(2,1)S(1)}, bf16[1728,128]{1,0:T(8,128)(2,1)S(1)}, u32[]{:S(2)}, u32[]{:S(2)}) collective-permute-start(bf16[1728,128]{1,0:T(8,128)(2,1)S(1)} %get-tuple-element.260), channel_id=1, source_target_pairs={{0,2},{1,3},{2,0},{3,1},{4,6},{5,7},{6,4},{7,5},{8,10},{9,11},{10,... | collective-permute-start | bytes 1327112 | tf_op jit(solution)/shard_map/ppermute | solution.py:976
  381.2 18.1 %collective-permute-start.62 = (bf16[1728,128]{1,0:T(8,128)(2,1)S(1)}, bf16[1728,128]{1,0:T(8,128)(2,1)S(1)}, u32[]{:S(2)}, u32[]{:S(2)}) collective-permute-start(bf16[1728,128]{1,0:T(8,128)(2,1)S(1)} %get-tuple-element.259), channel_id=1, source_target_pairs={{0,3},{1,2},{2,1},{3,0},{4,7},{5,6},{6,5},{7,4},{8,11},{9,10},{10,... | collective-permute-start | bytes 1327112 | tf_op jit(solution)/shard_map/ppermute | solution.py:976
  382.5 73.3 %collective-permute-start.44 = (bf16[512,1024]{1,0:T(8,128)(2,1)S(1)}, bf16[512,1024]{1,0:T(8,128)(2,1)S(1)}, u32[]{:S(2)}, u32[]{:S(2)}) collective-permute-start(bf16[512,1024]{1,0:T(8,128)(2,1)S(1)} %broadcast_select_fusion.9), channel_id=1, source_target_pairs={{0,16},{16,0},{1,17},{17,1},{2,18},{18,2},{3,19},{19,3},{4,20},{20... | collective-permute-start | bytes 3145736 | tf_op jit(solution)/shard_map/ppermute | solution.py:971
  382.6 21.1 %collective-permute-start.52 = (bf16[112,128]{1,0:T(8,128)(2,1)S(1)}, bf16[112,128]{1,0:T(8,128)(2,1)S(1)}, u32[]{:S(2)}, u32[]{:S(2)}) collective-permute-start(bf16[112,128]{1,0:T(8,128)(2,1)S(1)} %get-tuple-element.239), channel_id=1, source_target_pairs={{0,4},{4,0},{8,12},{12,8},{1,5},{5,1},{9,13},{13,9},{2,6},{6,2},{1... | collective-permute-start | bytes 86024 | tf_op jit(solution)/shard_map/ppermute | solution.py:976
  392.0 24.1 %collective-permute-start.53 = (bf16[112,128]{1,0:T(8,128)(2,1)S(1)}, bf16[112,128]{1,0:T(8,128)(2,1)S(1)}, u32[]{:S(2)}, u32[]{:S(2)}) collective-permute-start(bf16[112,128]{1,0:T(8,128)(2,1)S(1)} %get-tuple-element.239), channel_id=1, source_target_pairs={{0,8},{4,12},{8,0},{12,4},{1,9},{5,13},{9,1},{13,5},{2,10},{6,14},... | collective-permute-start | bytes 86024 | tf_op jit(solution)/shard_map/ppermute | solution.py:976
  404.6 21.0 %collective-permute-start.54 = (bf16[112,128]{1,0:T(8,128)(2,1)S(1)}, bf16[112,128]{1,0:T(8,128)(2,1)S(1)}, u32[]{:S(2)}, u32[]{:S(2)}) collective-permute-start(bf16[112,128]{1,0:T(8,128)(2,1)S(1)} %get-tuple-element.239), channel_id=1, source_target_pairs={{0,12},{4,8},{8,4},{12,0},{1,13},{5,9},{9,5},{13,1},{2,14},{6,10},... | collective-permute-start | bytes 86024 | tf_op jit(solution)/shard_map/ppermute | solution.py:976
  425.6 29.5 %collective-permute-start.55 = (bf16[448,128]{1,0:T(8,128)(2,1)S(1)}, bf16[448,128]{1,0:T(8,128)(2,1)S(1)}, u32[]{:S(2)}, u32[]{:S(2)}) collective-permute-start(bf16[448,128]{1,0:T(8,128)(2,1)S(1)} %bitcast.130), channel_id=1, source_target_pairs={{0,1},{1,0},{2,3},{3,2},{4,5},{5,4},{6,7},{7,6},{8,9},{9,8},{10,11... | collective-permute-start | bytes 344072 | tf_op jit(solution)/shard_map/ppermute | solution.py:976
  426.5 28.7 %collective-permute-start.56 = (bf16[448,128]{1,0:T(8,128)(2,1)S(1)}, bf16[448,128]{1,0:T(8,128)(2,1)S(1)}, u32[]{:S(2)}, u32[]{:S(2)}) collective-permute-start(bf16[448,128]{1,0:T(8,128)(2,1)S(1)} %bitcast.131), channel_id=1, source_target_pairs={{0,2},{1,3},{2,0},{3,1},{4,6},{5,7},{6,4},{7,5},{8,10},{9,11},{10,... | collective-permute-start | bytes 344072 | tf_op jit(solution)/shard_map/ppermute | solution.py:976
  428.1 27.1 %collective-permute-start.57 = (bf16[448,128]{1,0:T(8,128)(2,1)S(1)}, bf16[448,128]{1,0:T(8,128)(2,1)S(1)}, u32[]{:S(2)}, u32[]{:S(2)}) collective-permute-start(bf16[448,128]{1,0:T(8,128)(2,1)S(1)} %bitcast.132), channel_id=1, source_target_pairs={{0,3},{1,2},{2,1},{3,0},{4,7},{5,6},{6,5},{7,4},{8,11},{9,10},{10,... | collective-permute-start | bytes 344072 | tf_op jit(solution)/shard_map/ppermute | solution.py:976
  (183 other events, 3689.0 us)

commit v2 on v1

v2 whole, which is shorter than its diff:
```python
import functools

import jax
import jax.numpy as jnp
from jax import lax
from jax.experimental import pallas as pl
from jax.experimental.pallas import tpu as pltpu
from jax.sharding import PartitionSpec as P

SPAN = 256
RANK = 16
LANES = 128
DOCS_PER_BLOCK = 8
EPSILON = 1e-05
LOG2E = 1.4426950408889634
EXACT = lax.Precision.HIGHEST
SEQ, WSHARD, SECTION = "seq", "wshard", "section"
BF16 = jnp.bfloat16
F32 = jnp.float32
PARAMS = pltpu.CompilerParams(vmem_limit_bytes=20 * 1024 * 1024)


class Bag:
    def __init__(self, **fields):
        self.__dict__.update(fields)


def tie(value, *others):
    return lax.optimization_barrier((value, *others))[0]


def from_behind(value, axis, steps):
    count = lax.axis_size(axis)
    initial, last = (max(0, -steps), min(count, count - steps))
    return lax.ppermute(value, axis, [(source, source + steps) for source in range(initial, last)])


def dot(left, right):
    return jnp.dot(left, right, preferred_element_type=F32)


def dot_last(left, right):
    return lax.dot_general(left, right, (((1,), (1,)), ((), ())), preferred_element_type=F32)


def dot_first(left, right):
    return lax.dot_general(left, right, (((0,), (0,)), ((), ())), preferred_element_type=F32)


def rms_rate(values):
    return lax.rsqrt(jnp.mean(values * values, axis=-1, keepdims=True) + EPSILON)


def sigmoid(v):
    return 0.5 + 0.5 * jnp.tanh(0.5 * v)


def lower_ones(shape):
    rows = lax.broadcasted_iota(jnp.int32, shape, 0)
    columns = lax.broadcasted_iota(jnp.int32, shape, 1)
    return rows <= columns


def conv_rows(rows, rim, weight, offset, valid):
    length = rows.shape[0]
    valid = jnp.concatenate([valid] * (rows.shape[1] // LANES), axis=1)
    extended = jnp.concatenate([rim, rows], axis=0)
    taps = weight.shape[0]
    total = offset + weight[taps - 1 : taps] * rows
    for back in range(1, taps):
        shifted = extended[8 - back : 8 - back + length]
        total = total + jnp.where(valid >= back, shifted, 0.0) * weight[taps - 1 - back : taps - back]
    gate = sigmoid(total)
    active = total * gate
    return active, gate + active * (1.0 - gate)


def taps_at(vector_ref, places, first, width):
    rows = [vector_ref[:, pl.ds(pl.multiple_of(place + first, LANES), width)] for place in places]
    return jnp.concatenate(rows[:-1], axis=0), rows[-1]


def conv_kernel(
    spans, head, heads, state, places,
    mixed_ref, mixed_bc_ref, rim_ref, rim_bc_ref, vector_ref, valid_ref, raw_ref, head_ref, token_ref,
    values_ref, slope_ref, bc_ref, step_ref, *rest,
):
    state_refs, tail_ref = rest[:-1], rest[-1]
    group = pl.program_id(0)
    valid = valid_ref[...]
    width = mixed_ref.shape[1]
    heads_here = width // head

    @pl.when(group == 0)
    def _():
        weight, offset = taps_at(vector_ref, places, pl.num_programs(0) * width, 2 * state)
        active, slope = conv_rows(
            mixed_bc_ref[...].astype(F32), rim_bc_ref[...].astype(F32), weight, offset, valid
        )
        bc_ref[...] = jnp.concatenate([active, slope], axis=1).astype(BF16)
        raw = raw_ref[...].astype(F32).T[:heads] + head_ref[:, 2:3]
        step = (jnp.maximum(raw, 0.0) + jnp.log1p(jnp.exp(-jnp.abs(raw)))).astype(BF16).astype(F32)
        step_ref[:heads, :] = step
        step_ref[2 * heads :, :] = sigmoid(raw)
        drop = step * head_ref[:, :1]
        ones = lower_ones((SPAN, SPAN)).astype(F32)
        for span in range(spans):
            here = slice(span * SPAN, (span + 1) * SPAN)
            decay = jnp.dot(drop[:, here], ones, precision=EXACT, preferred_element_type=F32)
            step_ref[heads : 2 * heads, here] = decay
            tail = jnp.exp2(decay[:, SPAN - 1 :] - decay) * token_ref[span][1:2]
            tail_ref[:, here] = tail * step[:, here]

    weight, offset = taps_at(vector_ref, places, group * width, width)
    active, slope = conv_rows(
        mixed_ref[...].astype(F32), rim_ref[...].astype(F32), weight, offset, valid
    )
    slope_ref[...] = slope.astype(BF16)
    low = active.T.astype(BF16)
    values_ref[...] = low
    low = low.astype(F32)
    first = pl.multiple_of(group * heads_here, heads_here)
    tail_rows = tail_ref[pl.ds(first, heads_here), :]
    for span in range(spans):
        here = slice(span * SPAN, (span + 1) * SPAN)
        driven = jnp.concatenate(
            [
                (low[place * head : (place + 1) * head, here] * tail_rows[place : place + 1, here]).astype(BF16)
                for place in range(heads_here)
            ],
            axis=0,
        )
        state_refs[span][...] = dot(driven, bc_ref[here, :state]).astype(BF16)


def faded(row, column, score_ref):
    half = SPAN // 2
    upper = jnp.exp2(jnp.minimum(row - column[:half], 0.0))
    lower = jnp.exp2(jnp.minimum(row[:, half:] - column[half:], 0.0))
    lower = jnp.concatenate([jnp.zeros_like(lower), lower], axis=1)
    return (upper, lower), (upper * score_ref[:half, :], lower * score_ref[half:, :])


def scan_kernel(
    head, state, gain,
    values_ref, bc_ref, step_ref, decay_ref, token_ref, doc_column_ref, doc_row_ref, state_ref, head_ref, gate_ref,
    vector_ref, *rest,
):
    mixed_ref, normed_ref, score_ref, scanned_ref = rest[-4:]
    group, groups = pl.program_id(0), pl.num_programs(0)
    width = values_ref.shape[0]
    heads_here = width // head

    @pl.when(group == 0)
    def _():
        score = dot_last(bc_ref[:, :state], bc_ref[:, state:])
        same = (jnp.concatenate([doc_column_ref[...]] * (SPAN // LANES), axis=1) == doc_row_ref[:1]) & lower_ones((SPAN, SPAN))
        score_ref[...] = jnp.where(same, score, 0.0)

    decay, step = decay_ref[...], step_ref[...]
    carry = jnp.exp2(decay) * token_ref[0][:1]
    columns = jnp.concatenate([decay] * (LANES // heads_here), axis=0).T
    out_map = bc_ref[:, state:]
    parts = []
    for place in range(heads_here):
        rows = slice(place * head, (place + 1) * head)
        one = slice(place, place + 1)
        kernel = jnp.concatenate([part.astype(BF16) for part in faded(decay[one], columns[:, one], score_ref)[1]], axis=0)
        values = values_ref[rows].astype(F32)
        driven = (values * step[one]).astype(BF16)
        before = dot_last(state_ref[rows], out_map) * carry[one]
        parts.append(dot(driven, kernel) + before + head_ref[one, 1:2] * values)
    turned = jnp.concatenate(parts, axis=0).T
    low = turned.astype(BF16)
    mixed_ref[...] = low
    scanned_ref[:, pl.ds(pl.multiple_of(group * width, width), width)] = low

    @pl.when(group == groups - 1)
    def _():
        def rows_at(index, _):
            rows = pl.ds(pl.multiple_of(index * 16, 16), 16)
            mixed = scanned_ref[rows, :]
            gate = gate_ref[rows, :].astype(F32)
            gated = mixed.astype(F32) * (gate * sigmoid(gate))
            normed_ref[rows, :] = (gated * rms_rate(gated) * vector_ref[:, gain : gain + gated.shape[1]]).astype(BF16)
            return 0

        lax.fori_loop(0, SPAN // 16, rows_at, 0)


def out_back_kernel(
    head, heads, state, gain, count,
    up_ref, lane_ref, up_out_ref, down_out_ref, mixed_ref, gate_ref, vector_ref, decay_ref, token_ref, bc_ref, where_ref,
    *rest,
):
    parts, rest = rest[:count], rest[count:]
    (project_ref, turned_ref, narrow_ref), state_refs, (grad_ref, grad_mixed_ref) = rest[:3], rest[3:-2], rest[-2:]
    width = mixed_ref.shape[1]
    up = up_ref[...]
    narrow = (dot_last(up, up_out_ref[...]) * lane_ref[...]).astype(BF16)
    narrow_ref[...] = narrow
    left = jnp.concatenate([up, narrow], axis=1)
    for offset, part in out_places(where_ref, parts):
        here = pl.ds(offset, part.shape[0])
        grad_ref[:, here] = dot_last(left, jnp.concatenate([part[...], down_out_ref[here, :]], axis=1))

    def rows_at(index, _):
        rows = pl.ds(pl.multiple_of(index * 16, 16), 16)
        mixed = mixed_ref[rows, :].astype(F32)
        gate = gate_ref[rows, :].astype(F32)
        share = sigmoid(gate)
        silu = gate * share
        gated = mixed * silu
        grad = grad_ref[rows, :] * vector_ref[:, gain : gain + width]
        rate = rms_rate(gated)
        pull = jnp.mean(gated * grad, axis=-1, keepdims=True) * rate * rate * rate
        grad_gated = rate * grad - gated * pull
        project_ref[rows, :] = (grad_gated * mixed * (share + silu * (1.0 - share))).astype(BF16)
        grad_mixed_ref[rows, :] = (grad_gated * silu).astype(BF16)
        return 0

    lax.fori_loop(0, SPAN // 16, rows_at, 0)
    carry = jnp.exp2(decay_ref[...]) * token_ref[0][:1]
    out_map = bc_ref[:, state:]
    wide = 512
    for first in range(0, width, wide):
        low = grad_mixed_ref[:, first : first + wide].astype(F32).T
        turned_ref[first : first + wide, :] = low.astype(BF16)
        scaled = [
            (low[place * head : (place + 1) * head] * carry[first // head + place : first // head + place + 1]).astype(BF16)
            for place in range(wide // head)
        ]
        local = dot(jnp.concatenate(scaled, axis=0), out_map).astype(BF16)
        for span, state_ref in enumerate(state_refs):

            @pl.when(pl.program_id(0) == span)
            def _(state_ref=state_ref, first=first, local=local):
                state_ref[first : first + wide, :] = local


def aligned(value, unit):
    return pl.multiple_of(value * unit, unit)


def out_places(where_ref, parts):
    if len(parts) == 1:
        half = parts[0].shape[1]
        return [((2 * place + side) * half, parts[0].at[4 * side + place]) for place in range(4) for side in range(2)]
    rows, half = parts[0].shape[0], parts[3].shape[0]
    places = [(aligned(where_ref[place], rows), part) for place, part in enumerate(parts[:3])]
    apart = where_ref[3] * 2
    places.append((aligned(apart + where_ref[4], half), parts[3]))
    places.append((aligned(apart + 1 - where_ref[4], half), parts[4]))
    return places


def in_rows(where_ref, parts, step, start, size):
    side = int(start >= step)
    there = slice(start - side * step, start - side * step + size)
    if len(parts) == 1:
        return [parts[0][4 * side + place, there, :] for place in range(4)]
    pair = (parts[3][there], parts[4][there])
    apart = jnp.where(where_ref[4] == 0, pair[side], pair[1 - side])
    return [part[start : start + size] for part in parts[:3]] + [apart]


def in_columns(ref, where_ref, parts):
    columns = (ref.shape[1] - LANES) // parts
    places = [pl.ds(aligned(where_ref[place], columns), columns) for place in range(parts)]
    return jnp.concatenate([ref[:, here] for here in places + [pl.ds(parts * columns, LANES)]], axis=1)


def mixed_kernel(
    main, lanes, gain, count, input_ref, vector_ref, down_ref, lane_ref, up_ref, where_ref, *rest
):
    parts, (normed_ref, mixed_ref, raw_ref, rim_ref) = rest[:count], rest[count:]
    rows = input_ref.shape[0]
    inputs = input_ref[...].astype(F32)
    normed = (inputs * rms_rate(inputs) * vector_ref[:, gain : gain + inputs.shape[1]]).astype(BF16)
    narrow = (dot(normed, down_ref[...]) * lane_ref[...]).astype(BF16)
    normed_ref[...] = jnp.concatenate([normed, narrow], axis=1)
    left = in_columns(normed_ref, where_ref, 4)
    step, extra = main // 6, raw_ref.shape[1] // 4
    before = up_ref.shape[0] - main - extra

    def product(start, size):
        right = in_rows(where_ref, parts, main // 2, start, size)
        right.append(up_ref[before + start : before + start + size])
        return dot_last(left, jnp.concatenate(right, axis=1))

    for start in range(0, main, step):
        low = product(start, step).astype(BF16)
        mixed_ref[:, start : start + step] = low
        rim_ref[:, start : start + step] = low[rows - 8 :]
    raw_ref[...] = jnp.concatenate([product(main, extra), jnp.zeros((rows, lanes - extra), F32)], axis=1).astype(BF16)


def gate_kernel(count, normed_ref, up_ref, where_ref, *rest):
    parts, gate_ref = rest[:count], rest[count]
    left = in_columns(normed_ref, where_ref, 4)
    wide = 512
    inner = gate_ref.shape[1]
    for start in range(0, inner, wide):
        right = in_rows(where_ref, parts, inner // 2, start, wide) + [up_ref[start : start + wide]]
        gate_ref[:, start : start + wide] = dot_last(left, jnp.concatenate(right, axis=1)).astype(BF16)


def out_kernel(count, normed_ref, input_ref, down_ref, lane_ref, up_ref, where_ref, *rest):
    parts, (narrow_ref, out_ref) = rest[:count], rest[count:]
    narrow = (dot(normed_ref[...], down_ref[...]) * lane_ref[...]).astype(BF16)
    narrow_ref[...] = narrow
    places = out_places(where_ref, parts)
    left = [normed_ref[:, pl.ds(offset, part.shape[0])] for offset, part in places]
    left = jnp.concatenate(left + [narrow], axis=1)
    wide = 256
    for start in range(0, out_ref.shape[1], wide):
        here = slice(start, start + wide)
        right = jnp.concatenate([part[:, here] for _, part in places] + [up_ref[:, here]], axis=0)
        out_ref[:, here] = (input_ref[:, here].astype(F32) + dot(left, right)).astype(BF16)


def gate_in_back_kernel(count, grad_ref, up_ref, where_ref, *rest):
    parts, out_ref = rest[:count], rest[count]
    grad = grad_ref[...]
    half = grad.shape[1] // 2
    lower, upper = [in_rows(where_ref, parts, half, side * half, half) for side in range(2)]
    columns = lower[0].shape[1]
    for place in range(4):
        product = dot(grad[:, :half], lower[place]) + dot(grad[:, half:], upper[place])
        out_ref[:, place * columns : (place + 1) * columns] = product
    out_ref[:, 4 * columns :] = dot(grad, up_ref[...])


def narrow_back_kernel(main, extra, grad_ref, raw_ref, part_ref, lane_ref, up_ref, narrow_ref):
    before = up_ref.shape[0] - main - extra
    total = part_ref[...] + dot(grad_ref[...], up_ref[before : before + main])
    total = total + dot(raw_ref[...][:, :extra], up_ref[before + main :])
    narrow_ref[...] = (total * lane_ref[...]).astype(BF16)


def mixed_in_back_kernel(
    main, extra, gain, count,
    grad_ref, raw_ref, part_ref, input_ref, up_stream_ref, vector_ref, narrow_ref, down_ref, where_ref, *rest
):
    parts, (out_ref, total_ref) = rest[:count], rest[count:]
    width = input_ref.shape[1]
    columns = width // 4
    half = main // 2
    left = jnp.concatenate([grad_ref[...], raw_ref[...][:, :extra]], axis=1)
    lower = in_rows(where_ref, parts, half, 0, half)
    upper = in_rows(where_ref, parts, half, half, half + extra)
    for place in range(4):
        product = dot(left[:, :half], lower[place]) + dot(left[:, half:], upper[place])
        here = slice(place * columns, (place + 1) * columns)
        total_ref[:, pl.ds(aligned(where_ref[place], columns), columns)] = part_ref[:, here] + product
    scaled = (total_ref[...] + dot_last(narrow_ref[...], down_ref[...])) * vector_ref[:, gain : gain + width]
    inputs = input_ref[...].astype(F32)
    rate = rms_rate(inputs)
    pull = jnp.mean(inputs * scaled, axis=-1, keepdims=True) * rate * rate * rate
    out_ref[...] = (up_stream_ref[...].astype(F32) + rate * scaled - inputs * pull).astype(BF16)


def scan_back_kernel(
    head, heads, state, edge,
    values_ref, grad_ref, bc_ref, step_ref, decay_ref, sig_ref, token_ref, doc_column_ref, doc_row_ref, state_ref,
    grad_state_ref, head_ref, rate_ref, slope_ref, slope_bc_ref, *rest,
):
    outputs = rest[:-6]
    if edge:
        outputs, edge_ref = outputs[:-1], outputs[-1]
    out_values_ref, out_bc_ref, out_raw_ref = outputs[-3:]
    score_ref, grad_score_ref, pull_ref, direct_ref, grad_in_ref, grad_out_ref = rest[-6:]
    group, groups = pl.program_id(0), pl.num_programs(0)
    width = values_ref.shape[0]
    heads_here = width // head
    in_map, out_map = bc_ref[:, :state], bc_ref[:, state:]

    def same_doc():
        return (jnp.concatenate([doc_column_ref[...]] * (SPAN // LANES), axis=1) == doc_row_ref[:1]) & lower_ones((SPAN, SPAN))

    @pl.when(group == 0)
    def _():
        score_ref[...] = jnp.where(same_doc(), dot_last(in_map, out_map), 0.0)
        grad_score_ref[...] = jnp.zeros_like(grad_score_ref)
        grad_in_ref[...] = jnp.zeros_like(grad_in_ref)
        grad_out_ref[...] = jnp.zeros_like(grad_out_ref)

    decay, step = decay_ref[...], step_ref[...]
    token = token_ref[0]
    last = decay[:, SPAN - 1 :]
    carry = jnp.exp2(decay) * token[:1]
    tail = jnp.exp2(last - decay) * token[1:2]
    keep = jnp.exp2(last) * token[2:3, :1]
    columns = jnp.concatenate([decay] * (LANES // heads_here), axis=0).T
    at_end = lax.broadcasted_iota(jnp.int32, (1, SPAN), 1) == SPAN - 1
    grads, tails, carried, pulls, directs = [], [], [], [], []
    for place in range(heads_here):
        rows = slice(place * head, (place + 1) * head)
        one = slice(place, place + 1)
        fade, kernel = faded(decay[one], columns[:, one], score_ref)
        kernel = jnp.concatenate([part.astype(BF16) for part in kernel], axis=0)
        values = values_ref[rows].astype(F32)
        driven = (values * step[one]).astype(BF16)
        grad_low = grad_ref[rows]
        grad = grad_low.astype(F32)
        grad_kernel = dot_first(driven, grad_low)
        half = SPAN // 2
        grad_score_ref[:half, :] += grad_kernel[:half] * fade[0]
        grad_score_ref[half:, half:] += grad_kernel[half:, half:] * fade[1][:, half:]
        state_here, grad_state = state_ref[rows], grad_state_ref[rows]
        output = dot(driven, kernel) + dot_last(state_here, out_map) * carry[one]
        by_state = dot_last(grad_state, in_map) * tail[one]
        grad_driven = dot_last(grad_low, kernel) + by_state
        driven = driven.astype(F32)
        pull = jnp.sum(grad * output - driven * grad_driven, axis=0, keepdims=True)
        ending = jnp.sum(jnp.sum(driven * by_state, axis=0, keepdims=True), axis=1, keepdims=True)
        kept = jnp.sum(state_here.astype(F32) * grad_state.astype(F32), axis=0, keepdims=True)
        ending = ending + keep[one] * jnp.sum(kept, axis=1, keepdims=True)
        pulls.append(pull + jnp.where(at_end, ending, 0.0))
        directs.append(jnp.sum(values * grad_driven, axis=0, keepdims=True))
        grads.append(step[one] * grad_driven + head_ref[one, 1:2] * grad)
        tails.append((driven * tail[one]).astype(BF16))
        carried.append((grad * carry[one]).astype(BF16))
    grad_in_ref[...] += dot_first(jnp.concatenate(tails, axis=0), grad_state_ref[...])
    grad_out_ref[...] += dot_first(jnp.concatenate(carried, axis=0), state_ref[...])
    grads = jnp.concatenate(grads, axis=0).T.astype(BF16)
    out_values_ref[...] = grads
    if edge:
        product = grads[:8].astype(F32) * slope_ref[...][:8].astype(F32)
        edge_ref[:, pl.ds(pl.multiple_of(group * width, width), width)] = product.astype(BF16)
    here = pl.ds(pl.multiple_of(group * heads_here, heads_here), heads_here)
    pull_ref[here, :] = jnp.concatenate(pulls, axis=0)
    direct_ref[here, :] = jnp.concatenate(directs, axis=0)

    @pl.when(group == groups - 1)
    def _():
        ones = lower_ones((SPAN, SPAN)).astype(F32)
        summed = lax.dot_general(
            pull_ref[...], ones, (((1,), (1,)), ((), ())), precision=EXACT, preferred_element_type=F32
        )
        grad_step = (direct_ref[...] + rate_ref[:, 3:4] * summed).astype(BF16).astype(F32)
        grad_raw = grad_step * sig_ref[...]
        padded = jnp.concatenate([grad_raw, jnp.zeros((LANES - heads, SPAN), F32)], axis=0)
        out_raw_ref[...] = padded.T.astype(BF16)
        grad_score = jnp.where(same_doc(), grad_score_ref[...], 0.0).astype(BF16)
        grad_in = grad_in_ref[...] + dot(grad_score, out_map)
        grad_out = grad_out_ref[...] + dot_first(grad_score, in_map)
        low = jnp.concatenate([grad_in, grad_out], axis=1).astype(BF16)
        out_bc_ref[...] = low
        if edge:
            product = low[:8].astype(F32) * slope_bc_ref[...][:8].astype(F32)
            edge_ref[:, groups * width :] = product.astype(BF16)


def conv_back_kernel(
    value_blocks, places,
    grad_ref, grad_bc_ref, slope_ref, slope_bc_ref, next_ref, vector_ref, valid_ref, next_valid_ref, project_ref,
):
    block = pl.program_id(0)
    length = grad_ref.shape[0]

    def back(grad_low, slope_low):
        grad = grad_low.astype(F32) * slope_low.astype(F32)
        later = next_ref[...].astype(F32)
        weight, _ = taps_at(vector_ref, places, block * grad.shape[1], grad.shape[1])
        valid, next_valid = [jnp.concatenate([ref[...]] * (grad.shape[1] // LANES), axis=1) for ref in (valid_ref, next_valid_ref)]
        taps = weight.shape[0]
        total = weight[taps - 1 : taps] * grad
        for ahead in range(1, taps):
            extended = jnp.concatenate(
                [jnp.where(valid >= ahead, grad, 0.0), jnp.where(next_valid >= ahead, later, 0.0)], axis=0
            )
            total = total + weight[taps - 1 - ahead : taps - ahead] * extended[ahead : ahead + length]
        project_ref[...] = total.astype(BF16)

    @pl.when(block < value_blocks)
    def _():
        back(grad_ref[...], slope_ref[...])

    @pl.when(block == value_blocks)
    def _():
        back(grad_bc_ref[...], slope_bc_ref[...])


def spec(shape, index):
    return pl.BlockSpec(shape, index)


def whole(shape):
    return pl.BlockSpec(shape, lambda *_: (0,) * len(shape))


def cost(microseconds):
    return pl.CostEstimate(flops=int(microseconds * 1.15e9), bytes_accessed=1 << 16, transcendentals=0)


class Sizes:
    def __init__(self, rows, inner, heads, state, columns, taps):
        self.rows, self.inner, self.heads, self.state, self.columns, self.taps = rows, inner, heads, state, columns, taps
        self.head = inner // heads
        self.spans = rows // SPAN
        self.mixed = inner + 2 * state
        self.group_heads = 8
        self.groups = heads // self.group_heads
        self.wide = self.group_heads * self.head
        self.places = tuple(tap * self.mixed for tap in range(taps + 1))
        self.gate_gain = (taps + 1) * self.mixed
        self.norm_gain = self.gate_gain + inner


def conv_forward(sizes, mixed, raw, rim, level, tokens):
    s = sizes
    rows, wide, heads, state = s.rows, s.wide, s.heads, s.state
    maps = s.inner // (2 * state)
    shapes = [(s.inner, rows), (rows, s.inner), (rows, 4 * state)]
    args = [level.vector, tokens.valid, raw, level.heads, tokens.flags]
    outputs = pl.pallas_call(
        functools.partial(conv_kernel, s.spans, s.head, heads, state, s.places),
        grid=(s.groups,),
        in_specs=[
            spec((rows, wide), lambda g: (0, g)), spec((rows, 2 * state), lambda g: (0, maps)),
            spec((8, wide), lambda g: (0, g)), spec((8, 2 * state), lambda g: (0, maps)), *whole_specs(*args),
        ],
        out_specs=[
            spec((wide, rows), lambda g: (g, 0)), spec((rows, wide), lambda g: (0, g)), whole(shapes[2]),
            whole((3 * heads, rows)),
        ] + [spec((wide, state), lambda g: (g, 0))] * s.spans,
        out_shape=[shape_of(shapes[0]), far_shape(shapes[1]), shape_of(shapes[2]), shape_of((3 * heads, rows), F32)]
        + [shape_of((s.inner, state))] * s.spans,
        scratch_shapes=[pltpu.VMEM((heads, rows), F32)],
        compiler_params=PARAMS,
        cost_estimate=cost(8.5),
    )(mixed, mixed, rim, rim, *args)
    return outputs[:4], outputs[4:]


def span_specs(sizes, span):
    s = sizes
    return Bag(
        turned=spec((s.wide, SPAN), lambda g: (g, span)),
        maps=spec((SPAN, 2 * s.state), lambda g: (span, 0)),
        rows=spec((s.group_heads, SPAN), lambda g: (g, span)),
        decay=spec((s.group_heads, SPAN), lambda g: (s.groups + g, span)),
        flags=spec((1, 8, SPAN), lambda g: (span, 0, 0)),
        doc_column=spec((SPAN, LANES), lambda g: (span, 0)),
        doc_row=spec((8, SPAN), lambda g: (0, span)),
        state=spec((s.wide, s.state), lambda g: (g, 0)),
        head=spec((s.group_heads, LANES), lambda g: (g, 0)),
        full=spec((SPAN, s.inner), lambda g: (span, 0)),
    )


ANYWHERE = pl.BlockSpec(memory_space=pl.ANY)


def scan_forward(sizes, span, conv, state_in, gate, level, tokens, earlier):
    s = sizes
    at = span_specs(s, span)
    args = [
        conv.values, conv.maps, conv.step, conv.step, tokens.flags, tokens.column, tokens.row, state_in, level.heads,
        gate, level.vector,
    ]
    in_specs = [
        at.turned, at.maps, at.rows, at.decay, at.flags, at.doc_column, at.doc_row, at.state,
        at.head, at.full, whole(level.vector.shape),
    ]
    aliases = {}
    if earlier is not None:
        aliases = {len(args): 0, len(args) + 1: 1}
        args, in_specs = args + list(earlier), in_specs + [ANYWHERE] * 2
    shape = (s.rows, s.inner)
    return pl.pallas_call(
        functools.partial(scan_kernel, s.head, s.state, s.gate_gain),
        grid=(s.groups,),
        in_specs=in_specs,
        out_specs=[spec((SPAN, s.wide), lambda g: (span, g)), at.full],
        out_shape=[shape_of(shape), shape_of(shape)],
        scratch_shapes=[pltpu.VMEM((SPAN, SPAN), F32), pltpu.VMEM((SPAN, s.inner), BF16)],
        input_output_aliases=aliases,
        compiler_params=PARAMS,
        cost_estimate=cost(6.5),
    )(*args)


SMALL = pl.BlockSpec(memory_space=pltpu.SMEM)


def shape_of(shape, dtype=BF16):
    return jax.ShapeDtypeStruct(shape, dtype)


def far_shape(shape, dtype=BF16):
    return pltpu.HBM(shape, dtype)


def whole_specs(*arrays):
    return [whole(array.shape) for array in arrays]


def project_mixed(sizes, inputs, level, lane_mask):
    s = sizes
    args = [inputs, level.vector, level.in_down, lane_mask, level.in_up]
    width = inputs.shape[1]
    shapes = [(s.rows, width + LANES), (s.rows, s.mixed), (s.rows, LANES), (8, s.mixed)]
    return pl.pallas_call(
        functools.partial(mixed_kernel, s.mixed, LANES, s.norm_gain, len(level.mixed)),
        grid=(1,),
        in_specs=whole_specs(*args) + [SMALL] + whole_specs(*level.mixed),
        out_specs=[whole(shape) for shape in shapes],
        out_shape=[shape_of(shape) for shape in shapes],
        compiler_params=PARAMS,
        cost_estimate=cost(6),
    )(*args, level.mixed_where, *level.mixed)


def gate_specs(sizes, level):
    return [whole((sizes.inner, LANES)), SMALL] + whole_specs(*level.gate)


def project_gate(sizes, normed, level):
    s = sizes
    return pl.pallas_call(
        functools.partial(gate_kernel, len(level.gate)),
        grid=(1,),
        in_specs=whole_specs(normed) + gate_specs(s, level),
        out_specs=whole((s.rows, s.inner)),
        out_shape=shape_of((s.rows, s.inner)),
        compiler_params=PARAMS,
        cost_estimate=cost(3.6),
    )(normed, level.in_up, level.where, *level.gate)


def project_out(sizes, normed_out, inputs, level, lane_mask):
    s = sizes
    args = [normed_out, inputs, level.out_down, lane_mask, level.out_up]
    shapes = [(s.rows, LANES), inputs.shape]
    return pl.pallas_call(
        functools.partial(out_kernel, len(level.out)),
        grid=(1,),
        in_specs=whole_specs(*args) + [SMALL] + whole_specs(*level.out),
        out_specs=[whole(shape) for shape in shapes],
        out_shape=[shape_of(shape) for shape in shapes],
        compiler_params=PARAMS,
        cost_estimate=cost(4),
    )(*args, level.where, *level.out)


def out_backward(sizes, upstream, mixed, gate, conv, level, lane_mask, tokens):
    s = sizes
    full = spec((SPAN, s.inner), lambda k: (k, 0))
    width = upstream.shape[1]
    return pl.pallas_call(
        functools.partial(out_back_kernel, s.head, s.heads, s.state, s.gate_gain, len(level.out)),
        grid=(s.spans,),
        in_specs=[
            spec((SPAN, width), lambda k: (k, 0)), spec((SPAN, LANES), lambda k: (k, 0)),
            *whole_specs(level.out_up, level.out_down), full, full, whole(level.vector.shape),
            spec((s.heads, SPAN), lambda k: (1, k)), spec((1, 8, SPAN), lambda k: (k, 0, 0)),
            spec((SPAN, 2 * s.state), lambda k: (k, 0)), SMALL, *whole_specs(*level.out),
        ],
        out_specs=[
            full, spec((s.inner, SPAN), lambda k: (0, k)), spec((SPAN, LANES), lambda k: (k, 0)),
        ] + [whole((s.inner, s.state))] * s.spans,
        out_shape=[
            shape_of((s.rows, s.inner)), shape_of((s.inner, s.rows)), shape_of((s.rows, LANES)),
        ] + [shape_of((s.inner, s.state))] * s.spans,
        scratch_shapes=[pltpu.VMEM((SPAN, s.inner), F32), pltpu.VMEM((SPAN, s.inner), BF16)],
        compiler_params=PARAMS,
        cost_estimate=cost(13.5),
    )(
        upstream, lane_mask, level.out_up, level.out_down, mixed, gate, level.vector, conv.step, tokens.flags, conv.maps,
        level.where, *level.out,
    )


def gate_in_backward(sizes, grad_gate, level):
    s = sizes
    width = 4 * s.columns + LANES
    return pl.pallas_call(
        functools.partial(gate_in_back_kernel, len(level.gate)),
        grid=(1,),
        in_specs=whole_specs(grad_gate) + gate_specs(s, level),
        out_specs=whole((s.rows, width)),
        out_shape=shape_of((s.rows, width), F32),
        compiler_params=PARAMS,
        cost_estimate=cost(3.5),
    )(grad_gate, level.in_up, level.where, *level.gate)


def narrow_backward(sizes, grad_mixed, raw, part, level, lane_mask):
    s = sizes
    args = [grad_mixed, raw, part, lane_mask, level.in_up]
    in_specs = whole_specs(*args)
    in_specs[2] = spec((s.rows, LANES), lambda _: (0, part.shape[1] // LANES - 1))
    return pl.pallas_call(
        functools.partial(narrow_back_kernel, s.mixed, s.heads),
        grid=(1,),
        in_specs=in_specs,
        out_specs=whole((s.rows, LANES)),
        out_shape=shape_of((s.rows, LANES)),
        compiler_params=PARAMS,
        cost_estimate=cost(0.9),
    )(*args)


def mixed_in_backward(sizes, grad_mixed, raw, part, inputs, upstream, narrow, level):
    s = sizes
    width = inputs.shape[1]
    rows = lambda columns: spec((SPAN, columns), lambda k: (k, 0))
    return pl.pallas_call(
        functools.partial(mixed_in_back_kernel, s.mixed, s.heads, s.norm_gain, len(level.mixed)),
        grid=(s.spans,),
        in_specs=[
            rows(s.mixed), rows(LANES), rows(width + LANES), rows(width), rows(width), whole(level.vector.shape),
            rows(LANES), *whole_specs(level.in_down), SMALL, *whole_specs(*level.mixed),
        ],
        out_specs=rows(width),
        out_shape=shape_of((s.rows, width)),
        scratch_shapes=[pltpu.VMEM((SPAN, width), F32)],
        compiler_params=PARAMS,
        cost_estimate=cost(4.7),
    )(grad_mixed, raw, part, inputs, upstream, level.vector, narrow, level.in_down, level.mixed_where, *level.mixed)


def scan_backward(sizes, span, conv, grad_turned, state_in, grad_state, level, tokens, earlier):
    s = sizes
    at = span_specs(s, span)
    args = [
        conv.values, grad_turned, conv.maps, conv.step, conv.step, conv.step, tokens.flags, tokens.column, tokens.row,
        state_in, grad_state, level.heads, level.heads, conv.slope, conv.maps,
    ]
    in_specs = [
        at.turned, at.turned, at.maps, at.rows, at.decay, spec((s.heads, SPAN), lambda g: (2, span)), at.flags,
        at.doc_column, at.doc_row, at.state, at.state, at.head, whole((s.heads, LANES)),
        spec((16, s.wide), lambda g: (0, g)), spec((16, 2 * s.state), lambda g: (0, 1)),
    ]
    aliases = {}
    if earlier is not None:
        aliases = {len(args) + place: place for place in range(3)}
        args, in_specs = args + list(earlier[:3]), in_specs + [ANYWHERE] * 3
    out_specs = [spec((SPAN, s.wide), lambda g: (span, g)), at.maps, spec((SPAN, LANES), lambda g: (span, 0))]
    out_shape = [shape_of((s.rows, s.inner)), shape_of((s.rows, 2 * s.state)), shape_of((s.rows, LANES))]
    if span == 0:
        out_specs, out_shape = out_specs + [whole((8, s.mixed))], out_shape + [shape_of((8, s.mixed))]
    return pl.pallas_call(
        functools.partial(scan_back_kernel, s.head, s.heads, s.state, span == 0),
        grid=(s.groups,),
        in_specs=in_specs,
        out_specs=out_specs,
        out_shape=out_shape,
        scratch_shapes=[
            pltpu.VMEM((SPAN, SPAN), F32), pltpu.VMEM((SPAN, SPAN), F32), pltpu.VMEM((s.heads, SPAN), F32),
            pltpu.VMEM((s.heads, SPAN), F32), pltpu.VMEM((SPAN, s.state), F32), pltpu.VMEM((SPAN, s.state), F32),
        ],
        input_output_aliases=aliases,
        compiler_params=PARAMS,
        cost_estimate=cost(8.5),
    )(*args)


def conv_backward(sizes, grad_values, grad_maps, conv, later, level, tokens):
    s = sizes
    wide = 2 * s.state
    blocks = s.inner // wide
    values = spec((s.rows, wide), lambda i: (0, jnp.minimum(i, blocks - 1)))
    maps, slopes = whole((s.rows, wide)), spec((s.rows, wide), lambda i: (0, 1))
    fixed = [level.vector, tokens.valid, tokens.next_valid]
    return pl.pallas_call(
        functools.partial(conv_back_kernel, blocks, s.places),
        grid=(blocks + 1,),
        in_specs=[values, maps, values, slopes, spec((8, wide), lambda i: (0, i)), *whole_specs(*fixed)],
        out_specs=spec((s.rows, wide), lambda i: (0, i)),
        out_shape=shape_of((s.rows, s.mixed)),
        compiler_params=PARAMS,
        cost_estimate=cost(4.4),
    )(grad_values, grad_maps, conv.slope, conv.maps, later, *fixed)


def stacked_kernel(places, *refs):
    out_ref = refs[-1]
    first = 0
    for left, right in places:
        rows = refs[left].shape[1]
        out_ref[first : first + rows, :] = dot_first(refs[left][...], refs[right][...]).astype(BF16)
        first += rows
    if first < out_ref.shape[0]:
        out_ref[first:, :] = jnp.zeros((out_ref.shape[0] - first, out_ref.shape[1]), BF16)


def stacked(sizes, args, places, columns, rows, first, buffer, all_rows):
    s = sizes
    in_specs = [spec((s.rows, width), functools.partial(lambda at, _: (0, at), at)) for at, width in columns]
    aliases = {}
    if buffer is not None:
        aliases = {len(args): 0}
        args, in_specs = args + [buffer], in_specs + [ANYWHERE]
    return pl.pallas_call(
        functools.partial(stacked_kernel, places),
        grid=(1,),
        in_specs=in_specs,
        out_specs=pl.BlockSpec((pl.Element(rows), pl.Element(LANES)), lambda _: (first, 0)),
        out_shape=shape_of((all_rows, LANES)),
        input_output_aliases=aliases,
        compiler_params=PARAMS,
        cost_estimate=cost(1.6),
    )(*args)


def grad_rows(sizes, width):
    return width + 2 * sizes.inner, -(-(width + sizes.mixed + LANES) // 512) * 512


def early_grads(sizes, upstream, kept, grad_narrow_out, grad_gate, first, buffer, all_rows):
    s = sizes
    width = upstream.shape[1]
    args = [upstream, kept.narrow_out, kept.normed_out, grad_narrow_out, grad_gate, kept.normed]
    columns = [(0, width), (0, LANES), (0, s.inner), (0, LANES), (0, s.inner), (width // LANES, LANES)]
    return stacked(
        s, args, ((0, 1), (2, 3), (4, 5)), columns, grad_rows(s, width)[0], first, buffer, all_rows
    )


def late_grads(sizes, kept, grad_narrow, grad_mixed, raw, first, buffer, all_rows):
    s = sizes
    width = kept.inputs.shape[1]
    args = [kept.normed, grad_narrow, grad_mixed, raw, kept.normed]
    columns = [(0, width), (0, LANES), (0, s.mixed), (0, LANES), (width // LANES, LANES)]
    return stacked(s, args, ((0, 1), (2, 4), (3, 4)), columns, grad_rows(s, width)[1], first, buffer, all_rows)


def final_kernel(width, inner, where_ref, *refs):
    upper, upper_other, lower, lower_other, down_in_ref, in_up_ref, down_out_ref, out_up_ref = refs
    first = where_ref[0] == 0
    half = upper.shape[0]

    def rows(start, stop):
        pieces = []
        for side, (mine, yours) in enumerate(((lower, upper_other), (lower_other, upper))):
            low, high = max(start - side * half, 0), min(stop - side * half, half)
            if low < high:
                pieces.append(jnp.where(first, mine[low:high], yours[low:high]).astype(F32))
        return pieces

    def put(ref, at, start, stop):
        for piece in rows(start, stop):
            ref[at : at + piece.shape[0], :] = piece
            at += piece.shape[0]

    out_up_ref[...] = jnp.concatenate(rows(0, width), axis=0).T
    put(down_out_ref, 0, width, width + inner)
    put(in_up_ref, 0, width + inner, width + 2 * inner)
    late = width + 2 * inner
    put(down_in_ref, 0, late, late + width)
    put(in_up_ref, inner, late + width, late + width + in_up_ref.shape[0] - inner)


def final_sums(sizes, width, section, *sums):
    s = sizes
    shapes = [(width, LANES), (s.inner + s.mixed + s.heads, LANES), (s.inner, LANES), (LANES, width)]
    return pl.pallas_call(
        functools.partial(final_kernel, width, s.inner),
        grid=(1,),
        in_specs=[SMALL] + whole_specs(*sums),
        out_specs=[whole(shape) for shape in shapes],
        out_shape=[shape_of(shape, F32) for shape in shapes],
        compiler_params=PARAMS,
    )(section[None], *sums)


def token_kernel(spans, row_ref, before_ref, after_ref, table_ref, valid_ref, next_ref, column_ref, mask_ref, flags_ref):
    length = row_ref.shape[1]
    row = row_ref[...].astype(F32)
    ids = jnp.concatenate([before_ref[...].astype(F32), row, after_ref[...].astype(F32)], axis=1)
    behind = jnp.zeros((1, length + LANES), F32)
    for back in (1, 2, 3):
        same = ids[:, LANES - back : 2 * LANES - back + length] == ids[:, LANES : 2 * LANES + length]
        behind = behind + jnp.where(same, 1.0, 0.0)
    adapter = jnp.zeros_like(row)
    for document in range(table_ref.shape[0]):
        adapter = jnp.where(row == document, table_ref[document].astype(F32), adapter)
    rows = jnp.concatenate([behind[:, :length], row, adapter, jnp.zeros((5, length), F32)], axis=0).T
    wide = (length, LANES)
    valid_ref[...] = jnp.broadcast_to(rows[:, :1], wide).astype(jnp.int32)
    column_ref[...] = jnp.broadcast_to(rows[:, 1:2], wide).astype(jnp.int32)
    lanes = lax.broadcasted_iota(jnp.int32, wide, 1) // RANK
    mask_ref[...] = jnp.where(lanes == jnp.broadcast_to(rows[:, 2:3], wide).astype(jnp.int32), 1.0, 0.0)
    last = jnp.concatenate([behind[:, length:], jnp.zeros((7, LANES), F32)], axis=0).T
    next_ref[...] = jnp.broadcast_to(last[:8, :1], (8, LANES)).astype(jnp.int32)
    zeros = jnp.zeros((5, SPAN), F32)
    for span in range(spans):
        here = row[:, span * SPAN : (span + 1) * SPAN]
        start = ids[:, LANES + span * SPAN - 1 : LANES + span * SPAN]
        end = here[:, SPAN - 1 :]
        keep = jnp.broadcast_to(jnp.where(start == end, 1.0, 0.0), here.shape)
        flags_ref[span] = jnp.concatenate(
            [jnp.where(here == start, 1.0, 0.0), jnp.where(here == end, 1.0, 0.0), keep, zeros], axis=0
        )


def token_tables(doc_ids, table):
    rows = doc_ids.shape[1]
    before = from_behind(doc_ids[:, rows - LANES :], SEQ, 1)
    after = from_behind(doc_ids[:, :LANES], SEQ, -1)
    shapes = [((rows, LANES), jnp.int32), ((8, LANES), jnp.int32), ((rows, LANES), jnp.int32), ((rows, LANES), F32)]
    shapes.append(((rows // SPAN, 8, SPAN), F32))
    valid, next_valid, column, mask, flags = pl.pallas_call(
        functools.partial(token_kernel, rows // SPAN),
        grid=(1,),
        in_specs=whole_specs(doc_ids, before, after) + [SMALL],
        out_specs=[whole(shape) for shape, _ in shapes],
        out_shape=[jax.ShapeDtypeStruct(*one) for one in shapes],
        compiler_params=PARAMS,
    )(doc_ids, before, after, table)
    row = jnp.broadcast_to(doc_ids, (8, rows))
    return Bag(valid=valid, next_valid=next_valid, column=column, row=row, flags=flags), mask


def state_hops(rows, block_rows):
    eighth = block_rows // DOCS_PER_BLOCK
    if rows // SPAN > 1 and eighth > SPAN:
        raise ValueError("unsupported block")
    return 1 if rows >= eighth else 2 * eighth // rows - 1


def pass_states(sizes, local, conv, tokens, hops, direction):
    if hops > 1:
        keep = jnp.exp2(conv.step[sizes.heads : 2 * sizes.heads, -1]) * tokens.flags[0, 2, 0]
        keep = jnp.repeat(keep, sizes.head)[:, None]
        total = local.astype(F32)
        reach = 1
        while reach < hops:
            total = total + keep * from_behind(total.astype(BF16), SEQ, direction * reach).astype(F32)
            keep = keep * from_behind(keep, SEQ, direction * reach)
            reach *= 2
        local = total.astype(BF16)
    return from_behind(local, SEQ, direction)


def layer_forward(sizes, inputs, level, lane_mask, tokens, hops):
    s = sizes
    normed, mixed, raw, rim = project_mixed(s, inputs, level, lane_mask)
    rim = from_behind(rim, SEQ, 1)
    yield mixed
    gate = None
    if level.gate_first:
        gate = project_gate(s, normed, level)
        rim = tie(rim, gate)
    (values, slope, maps, step), states = conv_forward(s, mixed, raw, rim, level, tokens)
    conv = Bag(values=values, slope=slope, maps=maps, step=step)
    states_in = [pass_states(s, states[-1], conv, tokens, hops, 1)] + list(states[:-1])
    yield values
    if gate is None:
        gate = project_gate(s, normed, level)
    outputs = None
    for span in reversed(range(s.spans)):
        outputs = scan_forward(s, span, conv, states_in[span], gate, level, tokens, outputs)
        if span == s.spans - 1:
            yield outputs[0]
    mixed_out, normed_out = outputs
    narrow_out, result = project_out(s, normed_out, inputs, level, lane_mask)
    yield result
    kept = Bag(
        inputs=inputs, normed=normed, gate=gate, conv=conv, states_in=states_in, mixed_out=mixed_out,
        normed_out=normed_out, narrow_out=narrow_out,
    )
    return result, kept


def layer_backward(sizes, upstream, kept, level, lane_mask, tokens, hops):
    s = sizes
    conv = kept.conv
    early_rows, late_rows = grad_rows(s, upstream.shape[1])
    all_rows = early_rows + late_rows
    grad_gate, turned, grad_narrow_out, *local = out_backward(
        s, upstream, kept.mixed_out, kept.gate, conv, level, lane_mask, tokens
    )
    grad_states = list(local[1:]) + [pass_states(s, local[0], conv, tokens, hops, -1)]
    buffer = early_grads(s, upstream, kept, grad_narrow_out, grad_gate, 0, None, all_rows)
    outputs = None
    for span in range(s.spans):
        outputs = scan_backward(
            s, span, conv, turned, kept.states_in[span], grad_states[span], level, tokens, outputs
        )
        if span == 0:
            later = from_behind(outputs[3], SEQ, -1)
            turned = yield outputs[0], turned
    grad_values, grad_maps, raw = outputs[:3]
    grad_values = yield grad_values, grad_values
    grad_mixed = conv_backward(s, grad_values, grad_maps, conv, later, level, tokens)
    part = gate_in_backward(s, grad_gate, level)
    grad_mixed = yield grad_mixed, grad_mixed
    narrow = narrow_backward(s, grad_mixed, raw, part, level, lane_mask)
    buffer = late_grads(s, kept, narrow, grad_mixed, raw, early_rows, buffer, all_rows)
    grad_mixed = yield buffer, grad_mixed
    return mixed_in_backward(s, grad_mixed, raw, part, kept.inputs, upstream, narrow, level)


def make_level(sizes, vector, numbers, adapters, where):
    s = sizes
    in_down, in_up, out_down, out_up = adapters
    dt_bias, a_log, skip_gain = numbers
    rate = -jnp.exp(a_log)[:, None]
    lane = jnp.arange(LANES)[None, :]
    table = jnp.where(lane == 1, skip_gain[:, None], jnp.where(lane == 2, dt_bias[:, None], rate))
    table = jnp.where(lane == 0, rate * LOG2E, table)
    return Bag(
        vector=vector, heads=table, in_down=in_down, in_up=in_up, out_down=out_down,
        out_up=out_up, where=where, mixed_where=where,
    )


def swap(value):
    return lax.ppermute(value, SECTION, [(0, 1), (1, 0)])


def exchange(value, axis, distance):
    count = lax.axis_size(axis)
    return lax.ppermute(value, axis, [(place, place ^ distance) for place in range(count)])


def rows_at(value, index, rows):
    return lax.dynamic_slice_in_dim(value, index * rows, rows, axis=0)


def put_at(buffer, value, *index):
    start = list(index) + [0] * (buffer.ndim - len(index))
    return lax.dynamic_update_slice(buffer, value.reshape((1,) * len(index) + value.shape), start)


def across(value, second):
    count = lax.axis_size(WSHARD)
    pairs = []
    for section in range(2):
        distance = 2 - section if second else 1 + section
        pairs += [(section * count + place, section * count + (place ^ distance)) for place in range(count)]
    return lax.ppermute(value, (SECTION, WSHARD), pairs)


class Parts:
    def __init__(self, quarters):
        self.section = lax.axis_index(SECTION)
        self.quarters, self.near, self.parts = quarters, {}, {}
        other = swap(quarters[0][0])
        self.own = [jnp.where(self.section == 0, quarters[0][0], other)]
        others = [other] + [swap(tie(matrix, self.own[0])) for matrix, _, _ in quarters[1:]]
        for layer in range(2):
            for (matrix, _, _), other in list(zip(quarters, others, strict=True))[1 - layer :]:
                self.own.append(jnp.where(self.section == layer, matrix, other))

    def start(self, index, *after):
        self.near[index] = across(tie(self.own[index], *after), False)

    def forward(self, index, *after):
        _, half, step = self.quarters[index % len(self.quarters)]
        near = tie(self.near[index], *after)
        apart = across(lax.dynamic_slice_in_dim(near, self.section * step, half, axis=0), True)
        self.parts[index] = (self.own[index], near, swap(near), apart, swap(apart))


def scatter_start(value, axis):
    count, place = lax.axis_size(axis), lax.axis_index(axis)
    rows = value.shape[0] // count
    sent = [exchange(rows_at(value, place ^ away, rows), axis, away) for away in range(1, count)]
    return rows_at(value, place, rows), sent


def scatter_done(parts, *after):
    own, received = parts
    total = own.astype(F32)
    for part in tie(received, *after):
        total = total + part.astype(F32)
    return total.astype(BF16)


def gather_start(value, axis):
    return value, [exchange(value, axis, away) for away in range(1, lax.axis_size(axis))]


def gather_done(parts, axis, *after):
    own, received = parts
    count, place = lax.axis_size(axis), lax.axis_index(axis)
    buffer = jnp.zeros((count,) + own.shape, own.dtype)
    for away, part in enumerate([own] + tie(received, *after)):
        buffer = put_at(buffer, part, place ^ away)
    return buffer.reshape((count * own.shape[0],) + own.shape[1:])


def chip_start(packed):
    section = lax.axis_index(SECTION)
    half = packed.shape[0] // 2
    return rows_at(packed, section, half), [swap(rows_at(packed, 1 - section, half))]


def both_layers(own):
    section = lax.axis_index(SECTION)
    other = swap(own)
    return [jnp.where(section == layer, own, other) for layer in range(2)]


def on_device(
    layer_input, out_grad, doc_index, doc_adapter, in_weight, out_weight, norm_gain, conv_weight, conv_bias, dt_bias,
    a_log, skip_gain, gate_gain, *adapters,
):
    section, place = lax.axis_index(SECTION), lax.axis_index(WSHARD)
    batches, rows, width = layer_input.shape
    heads, inner = dt_bias.shape[1], gate_gain.shape[1]
    taps, mixed = conv_weight.shape[1:]
    sizes = Sizes(rows, inner, heads, (mixed - inner) // 2, in_weight.shape[1], taps)
    block_rows = rows * lax.axis_size(SEQ)
    hops = state_hops(rows, block_rows)

    pick = lambda array: lax.dynamic_index_in_dim(array, section, 0, keepdims=False)
    turned = in_weight[0].T
    main = mixed // 2
    weights = Parts(
        [
            (turned[inner:], main + heads, main),
            (turned[:inner], inner // 2, inner // 2),
            (out_weight[0], out_weight.shape[1] // 2, out_weight.shape[1] // 2),
        ]
    )
    weights.start(0)
    weights.forward(0)
    weights.start(1, weights.parts[0][3])
    rest = (layer_input, out_grad, doc_index, doc_adapter, norm_gain, conv_weight, conv_bias, dt_bias, a_log, skip_gain)
    rest, gate_gain, adapters = tie((rest, gate_gain, adapters), weights.own[0])
    layer_input, out_grad, doc_index, doc_adapter, norm_gain, conv_weight, conv_bias, dt_bias, a_log, skip_gain = rest
    inputs, grads, doc_ids, table = pick(layer_input), pick(out_grad), pick(doc_index), pick(doc_adapter)[0]
    tokens, lane_mask = token_tables(doc_ids[None, :], table)
    vectors = both_layers(jnp.concatenate([conv_weight[0].reshape(1, -1), conv_bias, gate_gain, norm_gain], axis=1))
    numbers = both_layers(jnp.concatenate([dt_bias, a_log, skip_gain], axis=0))
    in_down, in_up, out_down, out_up = adapters
    both = [both_layers(array) for array in (in_down[0], in_up[0].T, out_down[0], out_up[0])]
    where = jnp.stack([place, place ^ (1 + section), place ^ (2 - section), place ^ 3, section]).astype(jnp.int32)
    levels = [
        make_level(sizes, vectors[layer], numbers[layer], [pair[layer] for pair in both], where)
        for layer in range(2)
    ]
    small = [inputs, grads, lane_mask, tokens.__dict__, weights.own[1:]] + [level.__dict__ for level in levels]
    small, weights.parts[0] = lax.optimization_barrier((small, weights.parts[0]))
    inputs, grads, lane_mask, token_fields, weights.own[1:], *level_fields = small
    tokens, levels = Bag(**token_fields), [Bag(**fields) for fields in level_fields]
    levels[0].mixed = weights.parts[0]
    levels[0].gate_first = levels[1].gate_first = False

    moves = {(0, 0): 1, (0, 1): 2, (0, 2): 3, (0, 4): 4, (1, 1): 5}
    results, kept = [], []
    rows_now = inputs
    for layer in range(2):
        stages = layer_forward(sizes, rows_now, levels[layer], lane_mask, tokens, hops)
        for stage in range(5):
            try:
                token = next(stages)
            except StopIteration as end:
                rows_now, stored = end.value
            move = moves.get((layer, stage))
            if move is not None:
                weights.forward(move, token)
                owner, parts = levels[move // 3], weights.parts[move]
                if move % 3 == 0:
                    owner.mixed = parts
                elif move % 3 == 1:
                    owner.gate = parts
                else:
                    owner.out = parts
                if move < 5:
                    weights.start(move + 1, weights.near[move], token)
        results.append(rows_now)
        kept.append(stored)

    direct = lax.axis_size(SEQ) == 4
    both_axes = (WSHARD, SEQ)

    def finish(stages, value):
        try:
            stages.send(value)
        except StopIteration as end:
            return end.value

    stages = layer_backward(sizes, tie(grads, rows_now), kept[1], levels[1], lane_mask, tokens, hops)
    _, pending = next(stages)
    for _ in range(2):
        _, pending = stages.send(pending)
    upper, pending = stages.send(pending)
    upper = chip_start(upper)
    upper_grad = finish(stages, pending)
    upper = scatter_done(upper, upper_grad)
    upper_grad = tie(upper_grad, upper)
    upper = scatter_start(upper, WSHARD) if direct else lax.psum(upper, both_axes)

    stages = layer_backward(sizes, upper_grad, kept[0], levels[0], lane_mask, tokens, hops)
    token, pending = next(stages)
    if direct:
        upper = scatter_start(scatter_done(upper, token), SEQ)
    token, pending = stages.send(tie(pending, upper[0]))
    if direct:
        upper = gather_start(scatter_done(upper, token), SEQ)
    token, pending = stages.send(tie(pending, upper[0]))
    if direct:
        upper = gather_start(gather_done(upper, SEQ, token), WSHARD)
    lower, pending = stages.send(tie(pending, upper[0]))
    lower = chip_start(lower)
    if direct:
        upper = gather_done(upper, WSHARD, lower[0])
    lower = scatter_done(lower, upper)
    if direct:
        lower = scatter_start(lower, WSHARD)
    lower_grad = finish(stages, tie(pending, lower[0]))
    if direct:
        lower = scatter_start(scatter_done(lower, lower_grad), SEQ)
        lower = gather_start(scatter_done(lower), SEQ)
        lower = gather_start(gather_done(lower, SEQ), WSHARD)
        lower = gather_done(lower, WSHARD)
    else:
        lower = lax.psum(lower, both_axes)
    sums = final_sums(sizes, width, section, upper, swap(upper), lower, swap(lower))
    def placed(pair):
        here = jnp.where(section == 0, pair[0], pair[1])
        there = swap(jnp.where(section == 0, pair[1], pair[0]))
        first, second = jnp.where(section == 0, here, there), jnp.where(section == 0, there, here)
        return jnp.stack([first, second])[None]

    down_in, in_up, down_out, out_up = sums
    return (
        placed(results), placed([lower_grad, upper_grad]), down_in[None], in_up.T[None], down_out[None], out_up[None],
    )


def solution(mesh):
    tokens, matrix, vector = P(None, (WSHARD, SEQ), None), P(SECTION, None, None), P(SECTION, None)
    in_specs = (tokens, tokens, P(None, (WSHARD, SEQ)), P(None, WSHARD, None))
    in_specs += (P(SECTION, WSHARD, None),) * 2
    in_specs += (vector, matrix) + (vector,) * 5 + (matrix,) * 4
    out_specs = (P(SECTION, None, (WSHARD, SEQ), None),) * 2 + (matrix,) * 4
    return jax.shard_map(on_device, mesh=mesh, in_specs=in_specs, out_specs=out_specs, check_vma=False)
```

time: 475 us -> 403 us (0.85)
  waiting for transfers between devices: 129 us -> 77.2 us
  starting transfers between devices: 94.6 us -> 86.1 us
  other arithmetic: 24.7 us -> 17.1 us
  Pallas kernels: 178 us -> 171 us
    ppermute x12, waiting for transfers between devices: 65.5 us -> 43.7 us  [across(): return lax.ppermute(value, (SECTION, WSHARD), pairs)]
    ppermute x24, waiting for transfers between devices: 47.7 us -> 28.8 us  [exchange(): lax.ppermute(value, axis, [(place, place ^ distance) for place in range(c...]
    ppermute x10, waiting for transfers between devices: 13.2 us -> 2.37 us  [from_behind(): lax.ppermute(value, axis, [(source, source + steps) for source in range(i...]
    unnamed x321 -> x294, local copies, waits for them, and re-layouts: 20.3 us -> 29 us
    pallas_call x12 -> x16, Pallas kernels: 54.9 us -> 48.8 us  [the longest x2 10.1 us: mixed_in_backward(): pl.pallas_call(functools.partial(mixed_in_back_kernel, s.mixed, s.heads,...]
    ppermute x24, starting transfers between devices: 41.5 us -> 35.3 us  [exchange(): lax.ppermute(value, axis, [(place, place ^ distance) for place in range(c...]
  transfers between devices with their start and end apart: 73 -> 73, of which waited for: 25 -> 22; matrix products, arithmetic and copies ran while one was open for 7% -> 5% of each run, Pallas kernels for 35% -> 36%
where the time goes in v2:
time: 403 us; the launch traced here: 395 us
  Pallas kernels  171 us (42%)
  starting transfers between devices  86.1 us (21%)
  waiting for transfers between devices  77.2 us (19%)
  local copies, waits for them, and re-layouts  40.8 us (10%)
  other arithmetic  17.1 us (4%)
    ppermute x12, waiting for transfers between devices, across(): return lax.ppermute(value, (SECTION, WSHARD), pairs)  43.7 us
    ppermute x24, starting transfers between devices, exchange(): lax.ppermute(value, axis, [(place, place ^ distance) for place in range(c...  35.3 us
    pallas_call x4, Pallas kernels, scan_backward(): pl.pallas_call(functools.partial(scan_back_kernel, s.head, s.heads, s.sta...  33.7 us
    ppermute x10, starting transfers between devices, from_behind(): lax.ppermute(value, axis, [(source, source + steps) for source in range(i...  29.1 us
    unnamed x294, local copies, waits for them, and re-layouts  29 us
    ppermute x24, waiting for transfers between devices, exchange(): lax.ppermute(value, axis, [(place, place ^ distance) for place in range(c...  28.8 us
    pallas_call x2, Pallas kernels, out_backward(): pl.pallas_call(functools.partial(out_back_kernel, s.head, s.heads, s.stat...  26.8 us
    pallas_call x4, Pallas kernels, scan_forward(): pl.pallas_call(functools.partial(scan_kernel, s.head, s.state, s.gate_gai...  23.3 us
  transfers between devices with their start and end apart: 73, of which 22 were waited for; matrix products, arithmetic and copies ran while one was open for 5% of the time, Pallas kernels for 36%

profile of v2, /device:TPU:0, one launch (start us, length us, event | category | flops | bytes accessed | tf_op | source)
XLA Modules:
  0.0 395.4 jit_solution(11488848596137959194)
XLA Ops:
  5.3 2.5 broadcast_select_fusion
  8.5 4.6 %collective-permute-start.1 = (s32[1,128]{1,0:T(1,128)S(1)}, s32[1,128]{1,0:T(1,128)S(1)}, u32[]{:S(2)}, u32[]{:S(2)}) collective-permute-start(s32[1,128]{1,0:T(1,128)S(1)} %get-tuple-element.363), channel_id=1, source_target_pairs={{0,4},{4,8},{8,12},{1,5},{5,9},{9,13},{2,6},{6,10},{10,14},{3,7},{... | collective-permute-start | bytes 1544 | tf_op jit(solution)/shard_map/ppermute | solution.py:35
  24.9 11.5 %collective-permute-done.11.rest_1_ = bf16[2336,256]{1,0:T(8,128)(2,1)S(1)} collective-permute-done((bf16[2336,256]{1,0:T(8,128)(2,1)S(1)}, bf16[2336,256]{1,0:T(8,128)(2,1)S(1)}, u32[]{:S(2)}, u32[]{:S(2)}) %collective-permute-start.11) | collective-permute-done | bytes 1196064 | tf_op jit(solution)/shard_map/ppermute | solution.py:1036
  39.1 2.7 broadcast_select_fusion.5
  41.8 4.7 %collective-permute-done.13.rest_3_ = bf16[1184,256]{1,0:T(8,128)(2,1)S(1)} collective-permute-done((bf16[1184,256]{1,0:T(8,128)(2,1)S(1)}, bf16[1184,256]{1,0:T(8,128)(2,1)S(1)}, u32[]{:S(2)}, u32[]{:S(2)}) %collective-permute-start.13) | collective-permute-done | bytes 606240 | tf_op jit(solution)/shard_map/ppermute | solution.py:1036
  50.1 5.6 %shard_map.209 = (bf16[512,1152]{1,0:T(8,128)(2,1)S(1)}, bf16[512,2304]{1,0:T(8,128)(2,1)S(1)}, bf16[512,128]{1,0:T(8,128)(2,1)S(1)}, bf16[8,2304]{1,0:T(8,128)(2,1)S(1)}) custom-call(bf16[512,1024]{1,0:T(8,128)(2,1)S(1)} %get-tuple-element.186.input_ref, f32[1,14592]{1,0:T(1,128)S(1)} %get-tuple-element.187.vector_ref, ...), custom_call_target="tpu_custom_call" | custom-call | flops 6899999744 | bytes 65536 | tf_op jit(solution)/shard_map/pallas_call | solution.py:605
  55.7 5.7 %collective-permute-done.17.rest_1_ = bf16[2048,256]{1,0:T(8,128)(2,1)} collective-permute-done((bf16[2048,256]{1,0:T(8,128)(2,1)S(1)}, bf16[2048,256]{1,0:T(8,128)(2,1)}, u32[]{:S(2)}, u32[]{:S(2)}) %collective-permute-start.17) | collective-permute-done | bytes 1048608 | tf_op jit(solution)/shard_map/ppermute | solution.py:1036
  65.6 4.4 %collective-permute-start.15 = (bf16[8,2304]{1,0:T(8,128)(2,1)S(1)}, bf16[8,2304]{1,0:T(8,128)(2,1)S(1)}, u32[]{:S(2)}, u32[]{:S(2)}) collective-permute-start(bf16[8,2304]{1,0:T(8,128)(2,1)S(1)} %get-tuple-element.198), channel_id=1, source_target_pairs={{0,4},{4,8},{8,12},{1,5},{5,9},{9,13},{2,6},{6,10},{10,14},{3,7},{... | collective-permute-start | bytes 110600 | tf_op jit(solution)/shard_map/ppermute | solution.py:35
  70.0 7.5 %collective-permute-done.19.rest_3_ = bf16[1024,256]{1,0:T(8,128)(2,1)} collective-permute-done((bf16[1024,256]{1,0:T(8,128)(2,1)S(1)}, bf16[1024,256]{1,0:T(8,128)(2,1)}, u32[]{:S(2)}, u32[]{:S(2)}) %collective-permute-start.19) | collective-permute-done | bytes 524320 | tf_op jit(solution)/shard_map/ppermute | solution.py:1036
  77.5 8.1 %shard_map.210 = (bf16[2048,512]{1,0:T(8,128)(2,1)S(1)}, bf16[512,2048]{1,0:T(8,128)(2,1)}, bf16[512,512]{1,0:T(8,128)(2,1)S(1)}, f32[96,512]{1,0:T(8,128)S(1)},...) custom-call(bf16[512,2304]{1,0:T(8,128)(2,1)S(1)} %get-tuple-element.197.mixed_ref.mixed_bc_ref, ...), custom_call_target="tpu_custom_call" | custom-call | flops 9774999552 | bytes 65536 | tf_op jit(solution)/shard_map/pallas_call | solution.py:517
  93.9 4.9 %shard_map.211.gate_ref = bf16[512,2048]{1,0:T(8,128)(2,1)S(1)} custom-call(bf16[512,1152]{1,0:T(8,128)(2,1)S(1)} %get-tuple-element.209.normed_ref.refs_5_.refs_0_.refs_4_, bf16[4384,128]{1,0:T(8,128)(2,1)S(1)} %get-tuple-element.190.up_ref, s32[5]{0:T(128)S(1)} %stack.41.where_ref, bf16[2048,256]{1,0:T(8,128)(2,1)S(1)} %copy-done.29, ...), custom_call_target="tpu_custom_call" | custom-call | flops 4140000000 | bytes 65536 | tf_op jit(solution)/shard_map/pallas_call | solution.py:622
  98.9 5.8 %shard_map.212 = (bf16[512,2048]{1,0:T(8,128)(2,1)S(1)}, bf16[512,2048]{1,0:T(8,128)(2,1)S(1)}) custom-call(bf16[2048,512]{1,0:T(8,128)(2,1)S(1)} %copy-done.114, bf16[512,512]{1,0:T(8,128)(2,1)S(1)} %copy-done.119, f32[96,512]{1,0:T(8,128)S(1)} %copy-done.125, f32[96,512]{1,0:T(8,128)S(1)} %copy-done.125, f32[2,8,256]{2,1,0:T(8,128)S(1)} %copy-done.101, ...), custom_call_target="tpu_custom_call" | custom-call | flops 7474999808 | bytes 65536 | tf_op jit(solution)/shard_map/pallas_call | solution.py:572
  104.7 3.1 collective-permute-done.25.rest_1_
  111.1 4.5 %collective-permute-start.16 = (bf16[2048,128]{1,0:T(8,128)(2,1)S(1)}, bf16[2048,128]{1,0:T(8,128)(2,1)S(1)}, u32[]{:S(2)}, u32[]{:S(2)}) collective-permute-start(bf16[2048,128]{1,0:T(8,128)(2,1)S(1)} %copy-done.91), channel_id=1, source_target_pairs={{0,4},{4,8},{8,12},{1,5},{5,9},{9,13},{2,6},{6,10},{10,14},{3,7},{... | collective-permute-start | bytes 1572872 | tf_op jit(solution)/shard_map/ppermute | solution.py:35
  115.7 9.0 %collective-permute-done.23.rest_3_ = bf16[256,1024]{1,0:T(8,128)(2,1)S(1)} collective-permute-done((bf16[256,1024]{1,0:T(8,128)(2,1)S(1)}, bf16[256,1024]{1,0:T(8,128)(2,1)S(1)}, u32[]{:S(2)}, u32[]{:S(2)}) %collective-permute-start.23) | collective-permute-done | bytes 524320 | tf_op jit(solution)/shard_map/ppermute | solution.py:1036
  127.3 5.8 %shard_map.213 = (bf16[512,2048]{1,0:T(8,128)(2,1)S(1)}, bf16[512,2048]{1,0:T(8,128)(2,1)S(1)}) custom-call(bf16[2048,512]{1,0:T(8,128)(2,1)S(1)} %copy-done.114, bf16[512,512]{1,0:T(8,128)(2,1)S(1)} %copy-done.119, f32[96,512]{1,0:T(8,128)S(1)} %copy-done.125, f32[96,512]{1,0:T(8,128)S(1)} %copy-done.125, ...), custom_call_target="tpu_custom_call", output_to_operand_aliasing={{0}: (11, {}), {1}: (12, {})} | custom-call | flops 7474999808 | bytes 65536 | tf_op jit(solution)/shard_map/pallas_call | solution.py:572
  134.6 3.7 shard_map.214
  145.6 7.8 %shard_map.215 = (bf16[512,1152]{1,0:T(8,128)(2,1)S(1)}, bf16[512,2304]{1,0:T(8,128)(2,1)S(1)}, bf16[512,128]{1,0:T(8,128)(2,1)S(1)}, bf16[8,2304]{1,0:T(8,128)(2,1)}) custom-call(bf16[512,1024]{1,0:T(8,128)(2,1)S(1)} %get-tuple-element.223.input_ref, f32[1,14592]{1,0:T(1,128)S(1)} %get-tuple-element.224.vector_ref, bf16[1024,128]{1,0:T(8,128)(2,1)S(1)} %copy-done.51, ...), custom_call_target="tpu_custom_call" | custom-call | flops 6899999744 | bytes 65536 | tf_op jit(solution)/shard_map/pallas_call | solution.py:605
  155.5 4.4 %collective-permute-start.29 = (bf16[8,2304]{1,0:T(8,128)(2,1)}, bf16[8,2304]{1,0:T(8,128)(2,1)S(1)}, u32[]{:S(2)}, u32[]{:S(2)}) collective-permute-start(bf16[8,2304]{1,0:T(8,128)(2,1)} %get-tuple-element.232), channel_id=1, source_target_pairs={{0,4},{4,8},{8,12},{1,5},{5,9},{9,13},{2,6},{6,10},{10,14},{3,7},{... | collective-permute-start | bytes 110600 | tf_op jit(solution)/shard_map/ppermute | solution.py:35
  166.1 8.0 %shard_map.216 = (bf16[2048,512]{1,0:T(8,128)(2,1)S(1)}, bf16[512,2048]{1,0:T(8,128)(2,1)}, bf16[512,512]{1,0:T(8,128)(2,1)S(1)}, f32[96,512]{1,0:T(8,128)S(1)},...) custom-call(bf16[512,2304]{1,0:T(8,128)(2,1)S(1)} %copy-done.112, bf16[512,2304]{1,0:T(8,128)(2,1)S(1)} %copy-done.112, ...), custom_call_target="tpu_custom_call" | custom-call | flops 9774999552 | bytes 65536 | tf_op jit(solution)/shard_map/pallas_call | solution.py:517
  174.1 4.6 %collective-permute-start.30 = (bf16[2048,128]{1,0:T(8,128)(2,1)S(1)}, bf16[2048,128]{1,0:T(8,128)(2,1)S(1)}, u32[]{:S(2)}, u32[]{:S(2)}) collective-permute-start(bf16[2048,128]{1,0:T(8,128)(2,1)S(1)} %get-tuple-element.238), channel_id=1, source_target_pairs={{0,4},{4,8},{8,12},{1,5},{5,9},{9,13},{2,6},{6,10},{10,14},{3,7},{... | collective-permute-start | bytes 1572872 | tf_op jit(solution)/shard_map/ppermute | solution.py:35
  180.6 4.7 %shard_map.217.gate_ref = bf16[512,2048]{1,0:T(8,128)(2,1)S(1)} custom-call(bf16[512,1152]{1,0:T(8,128)(2,1)S(1)} %get-tuple-element.239.normed_ref.refs_5_.refs_0_.refs_4_, bf16[4384,128]{1,0:T(8,128)(2,1)S(1)} %copy-done.9, s32[5]{0:T(128)S(1)} %stack.41.where_ref, bf16[2048,256]{1,0:T(8,128)(2,1)S(1)} %copy-done.35, ...), custom_call_target="tpu_custom_call" | custom-call | flops 4140000000 | bytes 65536 | tf_op jit(solution)/shard_map/pallas_call | solution.py:622
  185.3 5.8 %shard_map.218 = (bf16[512,2048]{1,0:T(8,128)(2,1)S(1)}, bf16[512,2048]{1,0:T(8,128)(2,1)S(1)}) custom-call(bf16[2048,512]{1,0:T(8,128)(2,1)S(1)} %get-tuple-element.235.values_ref, bf16[512,512]{1,0:T(8,128)(2,1)S(1)} %get-tuple-element.236.bc_ref.slope_bc_ref, f32[96,512]{1,0:T(8,128)S(1)} %get-tuple-element.237.step_ref.decay_ref.sig_ref, ...), custom_call_target="tpu_custom_call" | custom-call | flops 7474999808 | bytes 65536 | tf_op jit(solution)/shard_map/pallas_call | solution.py:572
  191.5 5.8 %shard_map.219 = (bf16[512,2048]{1,0:T(8,128)(2,1)S(1)}, bf16[512,2048]{1,0:T(8,128)(2,1)S(1)}) custom-call(bf16[2048,512]{1,0:T(8,128)(2,1)S(1)} %get-tuple-element.235.values_ref, bf16[512,512]{1,0:T(8,128)(2,1)S(1)} %get-tuple-element.236.bc_ref.slope_bc_ref, ...), custom_call_target="tpu_custom_call", output_to_operand_aliasing={{0}: (11, {}), {1}: (12, {})} | custom-call | flops 7474999808 | bytes 65536 | tf_op jit(solution)/shard_map/pallas_call | solution.py:572
  197.3 4.7 %shard_map.220 = (bf16[512,128]{1,0:T(8,128)(2,1)S(1)}, bf16[512,1024]{1,0:T(8,128)(2,1)S(1)}) custom-call(bf16[512,2048]{1,0:T(8,128)(2,1)S(1)} %get-tuple-element.247.normed_ref.refs_2_, bf16[512,1024]{1,0:T(8,128)(2,1)S(1)} %copy-done.14, bf16[2048,128]{1,0:T(8,128)(2,1)S(1)} %copy-done.44, f32[512,128]{1,0:T(8,128)S(1)} %copy-done.38, ...), custom_call_target="tpu_custom_call" | custom-call | flops 4600000000 | bytes 65536 | tf_op jit(solution)/shard_map/pallas_call | solution.py:637
  203.0 14.0 %shard_map.221 = (bf16[512,2048]{1,0:T(8,128)(2,1)S(1)}, bf16[2048,512]{1,0:T(8,128)(2,1)S(1)}, bf16[512,128]{1,0:T(8,128)(2,1)S(1)}, bf16[2048,128]{1,0:T(8,128)(2,1)S(1)}, bf16[2048,128]{1,0:T(8,128)(2,1)S(1)}) custom-call(bf16[512,1024]{1,0:T(8,128)(2,1)S(1)} %get-tuple-element.255.up_ref.up_stream_ref.refs_0_, f32[512,128]{1,0:T(8,128)S(1)} %copy-done.38, ...), custom_call_target="tpu_custom_call" | custom-call | flops 15525000192 | bytes 65536 | tf_op jit(solution)/shard_map/pallas_call | solution.py:652
  218.4 8.4 %shard_map.222 = (bf16[512,2048]{1,0:T(8,128)(2,1)S(1)}, bf16[512,256]{1,0:T(8,128)(2,1)S(1)}, bf16[512,128]{1,0:T(8,128)(2,1)S(1)}, bf16[8,2304]{1,0:T(8,128)(2,1)S(1)}) custom-call(bf16[2048,512]{1,0:T(8,128)(2,1)S(1)} %get-tuple-element.235.values_ref, bf16[2048,512]{1,0:T(8,128)(2,1)S(1)} %get-tuple-element.257.grad_ref, ...), custom_call_target="tpu_custom_call" | custom-call | flops 9774999552 | bytes 65536 | tf_op jit(solution)/shard_map/pallas_call | solution.py:745
  230.1 4.6 %shard_map.225.part_ref = f32[512,1152]{1,0:T(8,128)S(1)} custom-call(bf16[512,2048]{1,0:T(8,128)(2,1)S(1)} %get-tuple-element.269.grad_ref.refs_4_, bf16[4384,128]{1,0:T(8,128)(2,1)S(1)} %copy-done.9, s32[5]{0:T(128)S(1)} %stack.41.where_ref, bf16[2048,256]{1,0:T(8,128)(2,1)S(1)} %copy-done.35, bf16[2048,256]{1,0:T(8,128)(2,1)} %collective-permute-done.31.rest_1_, ...), custom_call_target="tpu_custom_call" | custom-call | flops 4024999936 | bytes 65536 | tf_op jit(solution)/shard_map/pallas_call | solution.py:679
  234.7 8.3 %shard_map.223 = (bf16[512,2048]{1,0:T(8,128)(2,1)S(1)}, bf16[512,256]{1,0:T(8,128)(2,1)S(1)}, bf16[512,128]{1,0:T(8,128)(2,1)S(1)}) custom-call(bf16[2048,512]{1,0:T(8,128)(2,1)S(1)} %get-tuple-element.235.values_ref, bf16[2048,512]{1,0:T(8,128)(2,1)S(1)} %get-tuple-element.257.grad_ref, ...), custom_call_target="tpu_custom_call", output_to_operand_aliasing={{0}: (15, {}), {1}: (16, {}), {2}: (17, {})} | custom-call | flops 9774999552 | bytes 65536 | tf_op jit(solution)/shard_map/pallas_call | solution.py:745
  243.0 4.4 %shard_map.224.grad_ref.refs_2_ = bf16[512,2304]{1,0:T(8,128)(2,1)S(1)} custom-call(bf16[512,2048]{1,0:T(8,128)(2,1)S(1)} %get-tuple-element.264.grad_ref, bf16[512,256]{1,0:T(8,128)(2,1)S(1)} %get-tuple-element.265.grad_bc_ref, bf16[512,2048]{1,0:T(8,128)(2,1)S(1)} %copy-done.110, bf16[512,512]{1,0:T(8,128)(2,1)S(1)} %get-tuple-element.236.bc_ref.slope_bc_ref, ...), custom_call_target="tpu_custom_call" | custom-call | flops 5059999744 | bytes 65536 | tf_op jit(solution)/shard_map/pallas_call | solution.py:768
  263.9 5.7 %shard_map.227.up_ref.refs_0_.up_stream_ref = bf16[512,1024]{1,0:T(8,128)(2,1)S(1)} custom-call(bf16[512,2304]{1,0:T(8,128)(2,1)S(1)} %copy-done.5, bf16[512,128]{1,0:T(8,128)(2,1)S(1)} %copy-done.41, f32[512,1152]{1,0:T(8,128)S(1)} %copy-done.20, bf16[512,1024]{1,0:T(8,128)(2,1)S(1)} %copy-done.15, bf16[512,1024]{1,0:T(8,128)(2,1)S(1)} %copy-done.12, ...), custom_call_target="tpu_custom_call" | custom-call | flops 5405000192 | bytes 65536 | tf_op jit(solution)/shard_map/pallas_call | solution.py:710
  275.2 12.8 %shard_map.230 = (bf16[512,2048]{1,0:T(8,128)(2,1)S(1)}, bf16[2048,512]{1,0:T(8,128)(2,1)S(1)}, bf16[512,128]{1,0:T(8,128)(2,1)S(1)}, bf16[2048,128]{1,0:T(8,128)(2,1)S(1)}, bf16[2048,128]{1,0:T(8,128)(2,1)S(1)}) custom-call(bf16[512,1024]{1,0:T(8,128)(2,1)S(1)} %shard_map.227.up_ref.refs_0_.up_stream_ref, f32[512,128]{1,0:T(8,128)S(1)} %copy-done.39, ...), custom_call_target="tpu_custom_call" | custom-call | flops 15525000192 | bytes 65536 | tf_op jit(solution)/shard_map/pallas_call | solution.py:652
  289.4 8.5 %shard_map.231 = (bf16[512,2048]{1,0:T(8,128)(2,1)S(1)}, bf16[512,256]{1,0:T(8,128)(2,1)S(1)}, bf16[512,128]{1,0:T(8,128)(2,1)S(1)}, bf16[8,2304]{1,0:T(8,128)(2,1)S(1)}) custom-call(bf16[2048,512]{1,0:T(8,128)(2,1)S(1)} %copy-done.115, bf16[2048,512]{1,0:T(8,128)(2,1)S(1)} %get-tuple-element.282.grad_ref, bf16[512,512]{1,0:T(8,128)(2,1)S(1)} %copy-done.120, ...), custom_call_target="tpu_custom_call" | custom-call | flops 9774999552 | bytes 65536 | tf_op jit(solution)/shard_map/pallas_call | solution.py:745
  301.0 4.7 %shard_map.234.part_ref = f32[512,1152]{1,0:T(8,128)S(1)} custom-call(bf16[512,2048]{1,0:T(8,128)(2,1)S(1)} %get-tuple-element.298.grad_ref.refs_4_, bf16[4384,128]{1,0:T(8,128)(2,1)S(1)} %copy-done.7, s32[5]{0:T(128)S(1)} %copy-done.69, bf16[2048,256]{1,0:T(8,128)(2,1)S(1)} %copy-done.30, bf16[2048,256]{1,0:T(8,128)(2,1)} %collective-permute-done.17.rest_1_, ...), custom_call_target="tpu_custom_call" | custom-call | flops 4024999936 | bytes 65536 | tf_op jit(solution)/shard_map/pallas_call | solution.py:679
  306.0 4.3 %collective-permute-start.47 = (bf16[272,128]{1,0:T(8,128)(2,1)S(1)}, bf16[272,128]{1,0:T(8,128)(2,1)S(1)}, u32[]{:S(2)}, u32[]{:S(2)}) collective-permute-start(bf16[272,128]{1,0:T(8,128)(2,1)S(1)} %get-tuple-element.358), channel_id=1, source_target_pairs={{0,4},{4,0},{8,12},{12,8},{1,5},{5,1},{9,13},{13,9},{2,6},{6,2},{1... | collective-permute-start | bytes 208904 | tf_op jit(solution)/shard_map/ppermute | solution.py:1018
  310.3 3.5 collective-permute-start.48
  313.8 8.4 %shard_map.232 = (bf16[512,2048]{1,0:T(8,128)(2,1)S(1)}, bf16[512,256]{1,0:T(8,128)(2,1)S(1)}, bf16[512,128]{1,0:T(8,128)(2,1)S(1)}) custom-call(bf16[2048,512]{1,0:T(8,128)(2,1)S(1)} %copy-done.115, bf16[2048,512]{1,0:T(8,128)(2,1)S(1)} %get-tuple-element.282.grad_ref, ...), custom_call_target="tpu_custom_call", output_to_operand_aliasing={{0}: (15, {}), {1}: (16, {}), {2}: (17, {})} | custom-call | flops 9774999552 | bytes 65536 | tf_op jit(solution)/shard_map/pallas_call | solution.py:745
  323.0 3.8 collective-permute-start.52
  326.9 4.4 %shard_map.233.grad_ref.refs_2_ = bf16[512,2304]{1,0:T(8,128)(2,1)S(1)} custom-call(bf16[512,2048]{1,0:T(8,128)(2,1)S(1)} %get-tuple-element.290.grad_ref, bf16[512,256]{1,0:T(8,128)(2,1)S(1)} %get-tuple-element.291.grad_bc_ref, bf16[512,2048]{1,0:T(8,128)(2,1)S(1)} %copy-done.109, bf16[512,512]{1,0:T(8,128)(2,1)S(1)} %copy-done.120, ...), custom_call_target="tpu_custom_call" | custom-call | flops 5059999744 | bytes 65536 | tf_op jit(solution)/shard_map/pallas_call | solution.py:768
  339.0 2.7 collective-permute-done.55
  341.7 4.1 %collective-permute-done.56 = bf16[1088,128]{1,0:T(8,128)(2,1)S(1)} collective-permute-done((bf16[1088,128]{1,0:T(8,128)(2,1)S(1)}, bf16[1088,128]{1,0:T(8,128)(2,1)S(1)}, u32[]{:S(2)}, u32[]{:S(2)}) %collective-permute-start.56) | collective-permute-done | bytes 278560 | tf_op jit(solution)/shard_map/ppermute | solution.py:1018
  350.1 4.5 %shard_map.238 = bf16[512,1024]{1,0:T(8,128)(2,1)S(1)} custom-call(bf16[512,2304]{1,0:T(8,128)(2,1)S(1)} %shard_map.233.grad_ref.refs_2_, bf16[512,128]{1,0:T(8,128)(2,1)S(1)} %get-tuple-element.297.raw_ref.refs_3_, f32[512,1152]{1,0:T(8,128)S(1)} %shard_map.234.part_ref, bf16[512,1024]{1,0:T(8,128)(2,1)S(1)} %copy-done.27, ...), custom_call_target="tpu_custom_call" | custom-call | flops 5405000192 | bytes 65536 | tf_op jit(solution)/shard_map/pallas_call | solution.py:710
  354.6 3.4 collective-permute-done.61
  358.2 3.3 collective-permute-start.64
  363.9 4.3 %collective-permute-done.65 = bf16[272,128]{1,0:T(8,128)(2,1)S(1)} collective-permute-done((bf16[272,128]{1,0:T(8,128)(2,1)S(1)}, bf16[272,128]{1,0:T(8,128)(2,1)S(1)}, u32[]{:S(2)}, u32[]{:S(2)}) %collective-permute-start.65) | collective-permute-done | bytes 69664 | tf_op jit(solution)/shard_map/ppermute | solution.py:1018
  380.6 4.7 %collective-permute-done.69 = bf16[1088,128]{1,0:T(8,128)(2,1)S(1)} collective-permute-done((bf16[1088,128]{1,0:T(8,128)(2,1)S(1)}, bf16[1088,128]{1,0:T(8,128)(2,1)S(1)}, u32[]{:S(2)}, u32[]{:S(2)}) %collective-permute-start.69) | collective-permute-done | bytes 278560 | tf_op jit(solution)/shard_map/ppermute | solution.py:1018
  385.3 3.4 collective-permute-done.70
  392.4 2.6 shard_map.239
  (490 shorter events, 123.2 us)
Async XLA Ops:
  7.9 8.9 %collective-permute-start.5 = (f32[3,32]{1,0:T(4,128)S(1)}, f32[3,32]{1,0:T(4,128)S(1)}, u32[]{:S(2)}, u32[]{:S(2)}) collective-permute-start(f32[3,32]{1,0:T(4,128)S(1)} %pad_maximum_fusion), channel_id=1, source_target_pairs={{0,16},{16,0},{1,17},{17,1},{2,18},{18,2},{3,19},{19,3},{4,20},{20... | collective-permute-start | bytes 1160 | tf_op jit(solution)/shard_map/ppermute | solution.py:1013
  8.5 9.2 %collective-permute-start.1 = (s32[1,128]{1,0:T(1,128)S(1)}, s32[1,128]{1,0:T(1,128)S(1)}, u32[]{:S(2)}, u32[]{:S(2)}) collective-permute-start(s32[1,128]{1,0:T(1,128)S(1)} %get-tuple-element.363), channel_id=1, source_target_pairs={{0,4},{4,8},{8,12},{1,5},{5,9},{9,13},{2,6},{6,10},{10,14},{3,7},{... | collective-permute-start | bytes 1544 | tf_op jit(solution)/shard_map/ppermute | solution.py:35
  14.4 33.6 %collective-permute-start.7 = (bf16[4384,128]{1,0:T(8,128)(2,1)S(1)}, bf16[4384,128]{1,0:T(8,128)(2,1)S(1)}, u32[]{:S(2)}, u32[]{:S(2)}) collective-permute-start(bf16[4384,128]{1,0:T(8,128)(2,1)S(1)} %bitcast.115), channel_id=1, source_target_pairs={{0,16},{16,0},{1,17},{17,1},{2,18},{18,2},{3,19},{19,3},{4,20},{20... | collective-permute-start | bytes 3366920 | tf_op jit(solution)/shard_map/ppermute | solution.py:1013
  19.9 16.4 %collective-permute-start.11 = (bf16[2336,256]{1,0:T(8,128)(2,1)S(1)}, bf16[2336,256]{1,0:T(8,128)(2,1)S(1)}, u32[]{:S(2)}, u32[]{:S(2)}) collective-permute-start(bf16[2336,256]{1,0:T(8,128)(2,1)S(1)} %get-tuple-element.192.rest_0_), channel_id=1, source_target_pairs={{0,1},{1,0},{2,3},{3,2},{16,18},{17,19},{18,16},{19,17},{4,5},{5,4... | collective-permute-start | bytes 3588104 | tf_op jit(solution)/shard_map/ppermute | solution.py:1036
  21.6 16.4 %collective-permute-start.4 = (bf16[512,1024]{1,0:T(8,128)(2,1)S(1)}, bf16[512,1024]{1,0:T(8,128)(2,1)S(1)}, u32[]{:S(2)}, u32[]{:S(2)}) collective-permute-start(bf16[512,1024]{1,0:T(8,128)(2,1)S(1)} %bitcast.124), channel_id=1, source_target_pairs={{0,16},{16,0},{1,17},{17,1},{2,18},{18,2},{3,19},{19,3},{4,20},{20... | collective-permute-start | bytes 3145736 | tf_op jit(solution)/shard_map/ppermute | solution.py:1013
  22.7 16.3 %collective-permute-start.3 = (bf16[2048,256]{1,0:T(8,128)(2,1)S(1)}, bf16[2048,256]{1,0:T(8,128)(2,1)S(1)}, u32[]{:S(2)}, u32[]{:S(2)}) collective-permute-start(bf16[2048,256]{1,0:T(8,128)(2,1)S(1)} %copy-done.132), channel_id=1, source_target_pairs={{0,16},{16,0},{1,17},{17,1},{2,18},{18,2},{3,19},{19,3},{4,20},{20... | collective-permute-start | bytes 3145736 | tf_op jit(solution)/shard_map/ppermute | solution.py:1013
  36.4 10.1 %collective-permute-start.13 = (bf16[1184,256]{1,0:T(8,128)(2,1)S(1)}, bf16[1184,256]{1,0:T(8,128)(2,1)S(1)}, u32[]{:S(2)}, u32[]{:S(2)}) collective-permute-start(bf16[1184,256]{1,0:T(8,128)(2,1)S(1)} %constant_dynamic-slice_fusion.23), channel_id=1, source_target_pairs={{0,2},{1,3},{2,0},{3,1},{16,17},{17,16},{18,19},{19,18},{4,6},{5,7... | collective-permute-start | bytes 1818632 | tf_op jit(solution)/shard_map/ppermute | solution.py:1036
  46.5 14.9 %collective-permute-start.17 = (bf16[2048,256]{1,0:T(8,128)(2,1)S(1)}, bf16[2048,256]{1,0:T(8,128)(2,1)}, u32[]{:S(2)}, u32[]{:S(2)}) collective-permute-start(bf16[2048,256]{1,0:T(8,128)(2,1)S(1)} %get-tuple-element.211.rest_0_), channel_id=1, source_target_pairs={{0,1},{1,0},{2,3},{3,2},{16,18},{17,19},{18,16},{19,17},{4,5},{5,4... | collective-permute-start | bytes 3145736 | tf_op jit(solution)/shard_map/ppermute | solution.py:1036
  62.5 15.0 %collective-permute-start.19 = (bf16[1024,256]{1,0:T(8,128)(2,1)S(1)}, bf16[1024,256]{1,0:T(8,128)(2,1)}, u32[]{:S(2)}, u32[]{:S(2)}) collective-permute-start(bf16[1024,256]{1,0:T(8,128)(2,1)S(1)} %constant_dynamic-slice_fusion.22), channel_id=1, source_target_pairs={{0,2},{1,3},{2,0},{3,1},{16,17},{17,16},{18,19},{19,18},{4,6},{5,7... | collective-permute-start | bytes 1572872 | tf_op jit(solution)/shard_map/ppermute | solution.py:1036
  64.1 26.0 %collective-permute-start.21 = (bf16[512,1024]{1,0:T(8,128)(2,1)S(1)}, bf16[512,1024]{1,0:T(8,128)(2,1)S(1)}, u32[]{:S(2)}, u32[]{:S(2)}) collective-permute-start(bf16[512,1024]{1,0:T(8,128)(2,1)S(1)} %get-tuple-element.221.rest_0_), channel_id=1, source_target_pairs={{0,1},{1,0},{2,3},{3,2},{16,18},{17,19},{18,16},{19,17},{4,5},{5,4... | collective-permute-start | bytes 3145736 | tf_op jit(solution)/shard_map/ppermute | solution.py:1036
  65.6 12.0 %collective-permute-start.15 = (bf16[8,2304]{1,0:T(8,128)(2,1)S(1)}, bf16[8,2304]{1,0:T(8,128)(2,1)S(1)}, u32[]{:S(2)}, u32[]{:S(2)}) collective-permute-start(bf16[8,2304]{1,0:T(8,128)(2,1)S(1)} %get-tuple-element.198), channel_id=1, source_target_pairs={{0,4},{4,8},{8,12},{1,5},{5,9},{9,13},{2,6},{6,10},{10,14},{3,7},{... | collective-permute-start | bytes 110600 | tf_op jit(solution)/shard_map/ppermute | solution.py:35
  70.0 22.7 %collective-permute-start.18 = (bf16[2048,256]{1,0:T(8,128)(2,1)}, bf16[2048,256]{1,0:T(8,128)(2,1)}, u32[]{:S(2)}, u32[]{:S(2)}) collective-permute-start(bf16[2048,256]{1,0:T(8,128)(2,1)} %collective-permute-done.17.rest_1_), channel_id=1, source_target_pairs={{0,16},{16,0},{1,17},{17,1},{2,18},{18,2},{3,19},{19,3},{4,20},{20... | collective-permute-start | bytes 3145736 | tf_op jit(solution)/shard_map/ppermute | solution.py:1013
  77.5 15.1 %collective-permute-start.20 = (bf16[1024,256]{1,0:T(8,128)(2,1)}, bf16[1024,256]{1,0:T(8,128)(2,1)}, u32[]{:S(2)}, u32[]{:S(2)}) collective-permute-start(bf16[1024,256]{1,0:T(8,128)(2,1)} %collective-permute-done.19.rest_3_), channel_id=1, source_target_pairs={{0,16},{16,0},{1,17},{17,1},{2,18},{18,2},{3,19},{19,3},{4,20},{20... | collective-permute-start | bytes 1572872 | tf_op jit(solution)/shard_map/ppermute | solution.py:1013
  91.1 16.7 %collective-permute-start.25 = (bf16[2336,256]{1,0:T(8,128)(2,1)}, bf16[2336,256]{1,0:T(8,128)(2,1)}, u32[]{:S(2)}, u32[]{:S(2)}) collective-permute-start(bf16[2336,256]{1,0:T(8,128)(2,1)} %get-tuple-element.229.rest_0_), channel_id=1, source_target_pairs={{0,1},{1,0},{2,3},{3,2},{16,18},{17,19},{18,16},{19,17},{4,5},{5,4... | collective-permute-start | bytes 3588104 | tf_op jit(solution)/shard_map/ppermute | solution.py:1036
  108.9 18.3 %collective-permute-start.27 = (bf16[1184,256]{1,0:T(8,128)(2,1)S(1)}, bf16[1184,256]{1,0:T(8,128)(2,1)S(1)}, u32[]{:S(2)}, u32[]{:S(2)}) collective-permute-start(bf16[1184,256]{1,0:T(8,128)(2,1)S(1)} %constant_dynamic-slice_fusion.20), channel_id=1, source_target_pairs={{0,2},{1,3},{2,0},{3,1},{16,17},{17,16},{18,19},{19,18},{4,6},{5,7... | collective-permute-start | bytes 1818632 | tf_op jit(solution)/shard_map/ppermute | solution.py:1036
  110.6 14.1 %collective-permute-start.23 = (bf16[256,1024]{1,0:T(8,128)(2,1)S(1)}, bf16[256,1024]{1,0:T(8,128)(2,1)S(1)}, u32[]{:S(2)}, u32[]{:S(2)}) collective-permute-start(bf16[256,1024]{1,0:T(8,128)(2,1)S(1)} %constant_dynamic-slice_fusion.21), channel_id=1, source_target_pairs={{0,2},{1,3},{2,0},{3,1},{16,17},{17,16},{18,19},{19,18},{4,6},{5,7... | collective-permute-start | bytes 1572872 | tf_op jit(solution)/shard_map/ppermute | solution.py:1036
  111.1 14.6 %collective-permute-start.16 = (bf16[2048,128]{1,0:T(8,128)(2,1)S(1)}, bf16[2048,128]{1,0:T(8,128)(2,1)S(1)}, u32[]{:S(2)}, u32[]{:S(2)}) collective-permute-start(bf16[2048,128]{1,0:T(8,128)(2,1)S(1)} %copy-done.91), channel_id=1, source_target_pairs={{0,4},{4,8},{8,12},{1,5},{5,9},{9,13},{2,6},{6,10},{10,14},{3,7},{... | collective-permute-start | bytes 1572872 | tf_op jit(solution)/shard_map/ppermute | solution.py:35
  115.6 18.9 %collective-permute-start.22 = (bf16[512,1024]{1,0:T(8,128)(2,1)S(1)}, bf16[512,1024]{1,0:T(8,128)(2,1)S(1)}, u32[]{:S(2)}, u32[]{:S(2)}) collective-permute-start(bf16[512,1024]{1,0:T(8,128)(2,1)S(1)} %copy-done.55), channel_id=1, source_target_pairs={{0,16},{16,0},{1,17},{17,1},{2,18},{18,2},{3,19},{19,3},{4,20},{20... | collective-permute-start | bytes 3145736 | tf_op jit(solution)/shard_map/ppermute | solution.py:1013
  124.7 9.8 %collective-permute-start.24 = (bf16[256,1024]{1,0:T(8,128)(2,1)S(1)}, bf16[256,1024]{1,0:T(8,128)(2,1)S(1)}, u32[]{:S(2)}, u32[]{:S(2)}) collective-permute-start(bf16[256,1024]{1,0:T(8,128)(2,1)S(1)} %collective-permute-done.23.rest_3_), channel_id=1, source_target_pairs={{0,16},{16,0},{1,17},{17,1},{2,18},{18,2},{3,19},{19,3},{4,20},{20... | collective-permute-start | bytes 1572872 | tf_op jit(solution)/shard_map/ppermute | solution.py:1013
  124.7 20.9 %collective-permute-start.26 = (bf16[2336,256]{1,0:T(8,128)(2,1)}, bf16[2336,256]{1,0:T(8,128)(2,1)S(1)}, u32[]{:S(2)}, u32[]{:S(2)}) collective-permute-start(bf16[2336,256]{1,0:T(8,128)(2,1)} %collective-permute-done.25.rest_1_), channel_id=1, source_target_pairs={{0,16},{16,0},{1,17},{17,1},{2,18},{18,2},{3,19},{19,3},{4,20},{20... | collective-permute-start | bytes 3588104 | tf_op jit(solution)/shard_map/ppermute | solution.py:1013
  125.7 14.9 %collective-permute-start.31 = (bf16[2048,256]{1,0:T(8,128)(2,1)S(1)}, bf16[2048,256]{1,0:T(8,128)(2,1)}, u32[]{:S(2)}, u32[]{:S(2)}) collective-permute-start(bf16[2048,256]{1,0:T(8,128)(2,1)S(1)} %copy-done.34), channel_id=1, source_target_pairs={{0,1},{1,0},{2,3},{3,2},{16,18},{17,19},{18,16},{19,17},{4,5},{5,4... | collective-permute-start | bytes 3145736 | tf_op jit(solution)/shard_map/ppermute | solution.py:1036
  127.2 18.3 %collective-permute-start.28 = (bf16[1184,256]{1,0:T(8,128)(2,1)S(1)}, bf16[1184,256]{1,0:T(8,128)(2,1)S(1)}, u32[]{:S(2)}, u32[]{:S(2)}) collective-permute-start(bf16[1184,256]{1,0:T(8,128)(2,1)S(1)} %collective-permute-done.27.rest_3_), channel_id=1, source_target_pairs={{0,16},{16,0},{1,17},{17,1},{2,18},{18,2},{3,19},{19,3},{4,20},{20... | collective-permute-start | bytes 1818632 | tf_op jit(solution)/shard_map/ppermute | solution.py:1013
  140.6 38.1 %collective-permute-start.35 = (bf16[512,1024]{1,0:T(8,128)(2,1)}, bf16[512,1024]{1,0:T(8,128)(2,1)}, u32[]{:S(2)}, u32[]{:S(2)}) collective-permute-start(bf16[512,1024]{1,0:T(8,128)(2,1)} %get-tuple-element.251.rest_0_), channel_id=1, source_target_pairs={{0,1},{1,0},{2,3},{3,2},{16,18},{17,19},{18,16},{19,17},{4,5},{5,4... | collective-permute-start | bytes 3145736 | tf_op jit(solution)/shard_map/ppermute | solution.py:1036
  144.0 16.0 %collective-permute-start.33 = (bf16[1024,256]{1,0:T(8,128)(2,1)}, bf16[1024,256]{1,0:T(8,128)(2,1)}, u32[]{:S(2)}, u32[]{:S(2)}) collective-permute-start(bf16[1024,256]{1,0:T(8,128)(2,1)} %constant_dynamic-slice_fusion.19), channel_id=1, source_target_pairs={{0,2},{1,3},{2,0},{3,1},{16,17},{17,16},{18,19},{19,18},{4,6},{5,7... | collective-permute-start | bytes 1572872 | tf_op jit(solution)/shard_map/ppermute | solution.py:1036
  159.9 20.6 %collective-permute-start.32 = (bf16[2048,256]{1,0:T(8,128)(2,1)}, bf16[2048,256]{1,0:T(8,128)(2,1)}, u32[]{:S(2)}, u32[]{:S(2)}) collective-permute-start(bf16[2048,256]{1,0:T(8,128)(2,1)} %collective-permute-done.31.rest_1_), channel_id=1, source_target_pairs={{0,16},{16,0},{1,17},{17,1},{2,18},{18,2},{3,19},{19,3},{4,20},{20... | collective-permute-start | bytes 3145736 | tf_op jit(solution)/shard_map/ppermute | solution.py:1013
  160.0 20.5 %collective-permute-start.34 = (bf16[1024,256]{1,0:T(8,128)(2,1)}, bf16[1024,256]{1,0:T(8,128)(2,1)S(1)}, u32[]{:S(2)}, u32[]{:S(2)}) collective-permute-start(bf16[1024,256]{1,0:T(8,128)(2,1)} %collective-permute-done.33.rest_3_), channel_id=1, source_target_pairs={{0,16},{16,0},{1,17},{17,1},{2,18},{18,2},{3,19},{19,3},{4,20},{20... | collective-permute-start | bytes 1572872 | tf_op jit(solution)/shard_map/ppermute | solution.py:1013
  174.1 17.3 %collective-permute-start.30 = (bf16[2048,128]{1,0:T(8,128)(2,1)S(1)}, bf16[2048,128]{1,0:T(8,128)(2,1)S(1)}, u32[]{:S(2)}, u32[]{:S(2)}) collective-permute-start(bf16[2048,128]{1,0:T(8,128)(2,1)S(1)} %get-tuple-element.238), channel_id=1, source_target_pairs={{0,4},{4,8},{8,12},{1,5},{5,9},{9,13},{2,6},{6,10},{10,14},{3,7},{... | collective-permute-start | bytes 1572872 | tf_op jit(solution)/shard_map/ppermute | solution.py:35
  178.7 18.5 %collective-permute-start.36 = (bf16[512,1024]{1,0:T(8,128)(2,1)}, bf16[512,1024]{1,0:T(8,128)(2,1)S(1)}, u32[]{:S(2)}, u32[]{:S(2)}) collective-permute-start(bf16[512,1024]{1,0:T(8,128)(2,1)} %collective-permute-done.35.rest_1_), channel_id=1, source_target_pairs={{0,16},{16,0},{1,17},{17,1},{2,18},{18,2},{3,19},{19,3},{4,20},{20... | collective-permute-start | bytes 3145736 | tf_op jit(solution)/shard_map/ppermute | solution.py:1013
  179.9 11.2 %collective-permute-start.37 = (bf16[256,1024]{1,0:T(8,128)(2,1)S(1)}, bf16[256,1024]{1,0:T(8,128)(2,1)S(1)}, u32[]{:S(2)}, u32[]{:S(2)}) collective-permute-start(bf16[256,1024]{1,0:T(8,128)(2,1)S(1)} %constant_dynamic-slice_fusion.18), channel_id=1, source_target_pairs={{0,2},{1,3},{2,0},{3,1},{16,17},{17,16},{18,19},{19,18},{4,6},{5,7... | collective-permute-start | bytes 1572872 | tf_op jit(solution)/shard_map/ppermute | solution.py:1036
  217.0 17.6 %collective-permute-start.40 = (bf16[2048,128]{1,0:T(8,128)(2,1)S(1)}, bf16[2048,128]{1,0:T(8,128)(2,1)S(1)}, u32[]{:S(2)}, u32[]{:S(2)}) collective-permute-start(bf16[2048,128]{1,0:T(8,128)(2,1)S(1)} %get-tuple-element.258), channel_id=1, source_target_pairs={{4,0},{8,4},{12,8},{5,1},{9,5},{13,9},{6,2},{10,6},{14,10},{7,3},{... | collective-permute-start | bytes 1572872 | tf_op jit(solution)/shard_map/ppermute | solution.py:35
  226.8 16.2 %collective-permute-start.41 = (bf16[8,2304]{1,0:T(8,128)(2,1)S(1)}, bf16[8,2304]{1,0:T(8,128)(2,1)S(1)}, u32[]{:S(2)}, u32[]{:S(2)}) collective-permute-start(bf16[8,2304]{1,0:T(8,128)(2,1)S(1)} %get-tuple-element.266), channel_id=1, source_target_pairs={{4,0},{8,4},{12,8},{5,1},{9,5},{13,9},{6,2},{10,6},{14,10},{7,3},{... | collective-permute-start | bytes 110600 | tf_op jit(solution)/shard_map/ppermute | solution.py:35
  251.1 18.5 %collective-permute-start.42 = (bf16[4352,128]{1,0:T(8,128)(2,1)}, bf16[4352,128]{1,0:T(8,128)(2,1)}, u32[]{:S(2)}, u32[]{:S(2)}) collective-permute-start(bf16[4352,128]{1,0:T(8,128)(2,1)} %constant_dynamic-slice_fusion.17), channel_id=1, source_target_pairs={{0,16},{16,0},{1,17},{17,1},{2,18},{18,2},{3,19},{19,3},{4,20},{20... | collective-permute-start | bytes 3342344 | tf_op jit(solution)/shard_map/ppermute | solution.py:1013
  271.5 34.3 %collective-permute-start.43 = (bf16[1088,128]{1,0:T(8,128)(2,1)S(1)}, bf16[1088,128]{1,0:T(8,128)(2,1)S(1)}, u32[]{:S(2)}, u32[]{:S(2)}) collective-permute-start(bf16[1088,128]{1,0:T(8,128)(2,1)S(1)} %get-tuple-element.346), channel_id=1, source_target_pairs={{0,1},{1,0},{2,3},{3,2},{4,5},{5,4},{6,7},{7,6},{8,9},{9,8},{10,11... | collective-permute-start | bytes 835592 | tf_op jit(solution)/shard_map/ppermute | solution.py:1018
  272.8 33.0 %collective-permute-start.44 = (bf16[1088,128]{1,0:T(8,128)(2,1)S(1)}, bf16[1088,128]{1,0:T(8,128)(2,1)S(1)}, u32[]{:S(2)}, u32[]{:S(2)}) collective-permute-start(bf16[1088,128]{1,0:T(8,128)(2,1)S(1)} %get-tuple-element.345), channel_id=1, source_target_pairs={{0,2},{1,3},{2,0},{3,1},{4,6},{5,7},{6,4},{7,5},{8,10},{9,11},{10,... | collective-permute-start | bytes 835592 | tf_op jit(solution)/shard_map/ppermute | solution.py:1018
  273.6 32.2 %collective-permute-start.45 = (bf16[1088,128]{1,0:T(8,128)(2,1)S(1)}, bf16[1088,128]{1,0:T(8,128)(2,1)S(1)}, u32[]{:S(2)}, u32[]{:S(2)}) collective-permute-start(bf16[1088,128]{1,0:T(8,128)(2,1)S(1)} %get-tuple-element.344), channel_id=1, source_target_pairs={{0,3},{1,2},{2,1},{3,0},{4,7},{5,6},{6,5},{7,4},{8,11},{9,10},{10,... | collective-permute-start | bytes 835592 | tf_op jit(solution)/shard_map/ppermute | solution.py:1018
  288.1 25.7 %collective-permute-start.46 = (bf16[2048,128]{1,0:T(8,128)(2,1)S(1)}, bf16[2048,128]{1,0:T(8,128)(2,1)S(1)}, u32[]{:S(2)}, u32[]{:S(2)}) collective-permute-start(bf16[2048,128]{1,0:T(8,128)(2,1)S(1)} %get-tuple-element.283), channel_id=1, source_target_pairs={{4,0},{8,4},{12,8},{5,1},{9,5},{13,9},{6,2},{10,6},{14,10},{7,3},{... | collective-permute-start | bytes 1572872 | tf_op jit(solution)/shard_map/ppermute | solution.py:35
  298.0 28.9 %collective-permute-start.50 = (bf16[8,2304]{1,0:T(8,128)(2,1)S(1)}, bf16[8,2304]{1,0:T(8,128)(2,1)S(1)}, u32[]{:S(2)}, u32[]{:S(2)}) collective-permute-start(bf16[8,2304]{1,0:T(8,128)(2,1)S(1)} %get-tuple-element.292), channel_id=1, source_target_pairs={{4,0},{8,4},{12,8},{5,1},{9,5},{13,9},{6,2},{10,6},{14,10},{7,3},{... | collective-permute-start | bytes 110600 | tf_op jit(solution)/shard_map/ppermute | solution.py:35
  306.0 16.3 %collective-permute-start.47 = (bf16[272,128]{1,0:T(8,128)(2,1)S(1)}, bf16[272,128]{1,0:T(8,128)(2,1)S(1)}, u32[]{:S(2)}, u32[]{:S(2)}) collective-permute-start(bf16[272,128]{1,0:T(8,128)(2,1)S(1)} %get-tuple-element.358), channel_id=1, source_target_pairs={{0,4},{4,0},{8,12},{12,8},{1,5},{5,1},{9,13},{13,9},{2,6},{6,2},{1... | collective-permute-start | bytes 208904 | tf_op jit(solution)/shard_map/ppermute | solution.py:1018
  310.3 12.0 %collective-permute-start.48 = (bf16[272,128]{1,0:T(8,128)(2,1)S(1)}, bf16[272,128]{1,0:T(8,128)(2,1)S(1)}, u32[]{:S(2)}, u32[]{:S(2)}) collective-permute-start(bf16[272,128]{1,0:T(8,128)(2,1)S(1)} %get-tuple-element.357), channel_id=1, source_target_pairs={{0,8},{4,12},{8,0},{12,4},{1,9},{5,13},{9,1},{13,5},{2,10},{6,14},... | collective-permute-start | bytes 208904 | tf_op jit(solution)/shard_map/ppermute | solution.py:1018
  322.4 8.9 %collective-permute-start.51 = (bf16[272,128]{1,0:T(8,128)(2,1)S(1)}, bf16[272,128]{1,0:T(8,128)(2,1)S(1)}, u32[]{:S(2)}, u32[]{:S(2)}) collective-permute-start(bf16[272,128]{1,0:T(8,128)(2,1)S(1)} %get-tuple-element.325), channel_id=1, source_target_pairs={{0,4},{4,0},{8,12},{12,8},{1,5},{5,1},{9,13},{13,9},{2,6},{6,2},{1... | collective-permute-start | bytes 208904 | tf_op jit(solution)/shard_map/ppermute | solution.py:1018
  334.6 11.3 %collective-permute-start.56 = (bf16[1088,128]{1,0:T(8,128)(2,1)S(1)}, bf16[1088,128]{1,0:T(8,128)(2,1)S(1)}, u32[]{:S(2)}, u32[]{:S(2)}) collective-permute-start(bf16[1088,128]{1,0:T(8,128)(2,1)S(1)} %bitcast.121), channel_id=1, source_target_pairs={{0,2},{1,3},{2,0},{3,1},{4,6},{5,7},{6,4},{7,5},{8,10},{9,11},{10,... | collective-permute-start | bytes 835592 | tf_op jit(solution)/shard_map/ppermute | solution.py:1018
  335.1 10.7 %collective-permute-start.57 = (bf16[1088,128]{1,0:T(8,128)(2,1)S(1)}, bf16[1088,128]{1,0:T(8,128)(2,1)S(1)}, u32[]{:S(2)}, u32[]{:S(2)}) collective-permute-start(bf16[1088,128]{1,0:T(8,128)(2,1)S(1)} %bitcast.122), channel_id=1, source_target_pairs={{0,3},{1,2},{2,1},{3,0},{4,7},{5,6},{6,5},{7,4},{8,11},{9,10},{10,... | collective-permute-start | bytes 835592 | tf_op jit(solution)/shard_map/ppermute | solution.py:1018
  347.1 10.9 %collective-permute-start.61 = (bf16[1088,128]{1,0:T(8,128)(2,1)S(1)}, bf16[1088,128]{1,0:T(8,128)(2,1)S(1)}, u32[]{:S(2)}, u32[]{:S(2)}) collective-permute-start(bf16[1088,128]{1,0:T(8,128)(2,1)S(1)} %get-tuple-element.341), channel_id=1, source_target_pairs={{0,2},{1,3},{2,0},{3,1},{4,6},{5,7},{6,4},{7,5},{8,10},{9,11},{10,... | collective-permute-start | bytes 835592 | tf_op jit(solution)/shard_map/ppermute | solution.py:1018
  348.6 9.4 %collective-permute-start.62 = (bf16[1088,128]{1,0:T(8,128)(2,1)S(1)}, bf16[1088,128]{1,0:T(8,128)(2,1)S(1)}, u32[]{:S(2)}, u32[]{:S(2)}) collective-permute-start(bf16[1088,128]{1,0:T(8,128)(2,1)S(1)} %get-tuple-element.340), channel_id=1, source_target_pairs={{0,3},{1,2},{2,1},{3,0},{4,7},{5,6},{6,5},{7,4},{8,11},{9,10},{10,... | collective-permute-start | bytes 835592 | tf_op jit(solution)/shard_map/ppermute | solution.py:1018
  372.9 16.0 %collective-permute-start.39 = (bf16[512,1024]{1,0:T(8,128)(2,1)S(1)}, bf16[512,1024]{1,0:T(8,128)(2,1)S(1)}, u32[]{:S(2)}, u32[]{:S(2)}) collective-permute-start(bf16[512,1024]{1,0:T(8,128)(2,1)S(1)} %broadcast_select_fusion.9), channel_id=1, source_target_pairs={{0,16},{16,0},{1,17},{17,1},{2,18},{18,2},{3,19},{19,3},{4,20},{20... | collective-permute-start | bytes 3145736 | tf_op jit(solution)/shard_map/ppermute | solution.py:1013
  373.0 19.4 %collective-permute-start.59 = (bf16[4352,128]{1,0:T(8,128)(2,1)S(1)}, bf16[4352,128]{1,0:T(8,128)(2,1)S(1)}, u32[]{:S(2)}, u32[]{:S(2)}) collective-permute-start(bf16[4352,128]{1,0:T(8,128)(2,1)S(1)} %bitcast.108), channel_id=1, source_target_pairs={{0,16},{16,0},{1,17},{17,1},{2,18},{18,2},{3,19},{19,3},{4,20},{20... | collective-permute-start | bytes 3342344 | tf_op jit(solution)/shard_map/ppermute | solution.py:1013
  378.2 10.5 %collective-permute-start.70 = (bf16[1088,128]{1,0:T(8,128)(2,1)S(1)}, bf16[1088,128]{1,0:T(8,128)(2,1)S(1)}, u32[]{:S(2)}, u32[]{:S(2)}) collective-permute-start(bf16[1088,128]{1,0:T(8,128)(2,1)S(1)} %bitcast.117), channel_id=1, source_target_pairs={{0,2},{1,3},{2,0},{3,1},{4,6},{5,7},{6,4},{7,5},{8,10},{9,11},{10,... | collective-permute-start | bytes 835592 | tf_op jit(solution)/shard_map/ppermute | solution.py:1018
  378.3 10.4 %collective-permute-start.71 = (bf16[1088,128]{1,0:T(8,128)(2,1)S(1)}, bf16[1088,128]{1,0:T(8,128)(2,1)S(1)}, u32[]{:S(2)}, u32[]{:S(2)}) collective-permute-start(bf16[1088,128]{1,0:T(8,128)(2,1)S(1)} %bitcast.118), channel_id=1, source_target_pairs={{0,3},{1,2},{2,1},{3,0},{4,7},{5,6},{6,5},{7,4},{8,11},{9,10},{10,... | collective-permute-start | bytes 835592 | tf_op jit(solution)/shard_map/ppermute | solution.py:1018
  (170 other events, 2405.4 us)

commit v3 on v2

--- a/solution.py
+++ b/solution.py
@@ -170,8 +170,7 @@
         driven = (values * step[one]).astype(BF16)
         before = dot_last(state_ref[rows], out_map) * carry[one]
         parts.append(dot(driven, kernel) + before + head_ref[one, 1:2] * values)
-    turned = jnp.concatenate(parts, axis=0).T
-    low = turned.astype(BF16)
+    low = jnp.concatenate(parts, axis=0).astype(BF16).T
     mixed_ref[...] = low
     scanned_ref[:, pl.ds(pl.multiple_of(group * width, width), width)] = low
 
@@ -185,7 +184,7 @@
             normed_ref[rows, :] = (gated * rms_rate(gated) * vector_ref[:, gain : gain + gated.shape[1]]).astype(BF16)
             return 0
 
-        lax.fori_loop(0, SPAN // 16, rows_at, 0)
+        lax.fori_loop(0, SPAN // 16, rows_at, 0, unroll=4)
 
 
 def out_back_kernel(
@@ -219,7 +218,7 @@
         grad_mixed_ref[rows, :] = (grad_gated * silu).astype(BF16)
         return 0
 
-    lax.fori_loop(0, SPAN // 16, rows_at, 0)
+    lax.fori_loop(0, SPAN // 16, rows_at, 0, unroll=4)
     carry = jnp.exp2(decay_ref[...]) * token_ref[0][:1]
     out_map = bc_ref[:, state:]
     wide = 512
@@ -491,7 +490,7 @@
 
 
 def cost(microseconds):
-    return pl.CostEstimate(flops=int(microseconds * 1.15e9), bytes_accessed=1 << 16, transcendentals=0)
+    return pl.CostEstimate(flops=int(microseconds * 3.45e+09), bytes_accessed=1 << 16, transcendentals=0)
 
 
 class Sizes:
@@ -1043,6 +1042,7 @@
         other = swap(quarters[0][0])
         self.own = [jnp.where(self.section == 0, quarters[0][0], other)]
         others = [other] + [swap(tie(matrix, self.own[0])) for matrix, _, _ in quarters[1:]]
+        self.later = others[1]
         for layer in range(2):
             for (matrix, _, _), other in list(zip(quarters, others, strict=True))[1 - layer :]:
                 self.own.append(jnp.where(self.section == layer, matrix, other))
@@ -1054,7 +1054,11 @@
         _, half, step = self.quarters[index % len(self.quarters)]
         near = tie(self.near[index], *after)
         apart = across(lax.dynamic_slice_in_dim(near, self.section * step, half, axis=0), True)
-        self.parts[index] = (self.own[index], near, swap(near), apart, swap(apart))
+        self.halfway = (self.own[index], near, swap(near), apart)
+        return apart
+
+    def finish(self, index, *after):
+        self.parts[index] = self.halfway + (swap(tie(self.halfway[3], *after)),)
 
 
 def scatter_start(value, axis):
@@ -1120,10 +1124,10 @@
         ]
     )
     weights.start(0)
-    weights.forward(0)
-    weights.start(1, weights.parts[0][3])
+    weights.start(1, weights.forward(0))
+    weights.finish(0)
     rest = (layer_input, out_grad, doc_index, doc_adapter, norm_gain, conv_weight, conv_bias, dt_bias, a_log, skip_gain)
-    rest, gate_gain, adapters = tie((rest, gate_gain, adapters), weights.own[0])
+    rest, gate_gain, adapters = tie((rest, gate_gain, adapters), weights.later)
     layer_input, out_grad, doc_index, doc_adapter, norm_gain, conv_weight, conv_bias, dt_bias, a_log, skip_gain = rest
     inputs, grads, doc_ids, table = pick(layer_input), pick(out_grad), pick(doc_index), pick(doc_adapter)[0]
     tokens, lane_mask = token_tables(doc_ids[None, :], table)
@@ -1143,7 +1147,8 @@
     levels[0].mixed = weights.parts[0]
     levels[0].gate_first = levels[1].gate_first = False
 
-    moves = {(0, 0): 1, (0, 1): 2, (0, 2): 3, (0, 4): 4, (1, 1): 5}
+    passes = {(0, 0): 1, (0, 1): 2, (0, 2): 3, (0, 4): 4, (1, 1): 5}
+    ends = {(0, 1): 1, (0, 2): 2, (0, 3): 3, (1, 0): 4, (1, 2): 5}
     results, kept = [], []
     rows_now = inputs
     for layer in range(2):
@@ -1153,9 +1158,9 @@
                 token = next(stages)
             except StopIteration as end:
                 rows_now, stored = end.value
-            move = moves.get((layer, stage))
+            move = ends.get((layer, stage))
             if move is not None:
-                weights.forward(move, token)
+                weights.finish(move, token)
                 owner, parts = levels[move // 3], weights.parts[move]
                 if move % 3 == 0:
                     owner.mixed = parts
@@ -1163,10 +1168,19 @@
                     owner.gate = parts
                 else:
                     owner.out = parts
+            move = passes.get((layer, stage))
+            if move is not None:
+                weights.forward(move, token)
                 if move < 5:
-                    weights.start(move + 1, weights.near[move], token)
+                    weights.start(move + 1, token)
         results.append(rows_now)
         kept.append(stored)
+
+    def placed(pair):
+        here = jnp.where(section == 0, pair[0], pair[1])
+        there = swap(jnp.where(section == 0, pair[1], pair[0]))
+        first, second = jnp.where(section == 0, here, there), jnp.where(section == 0, there, here)
+        return jnp.stack([first, second])[None]
 
     direct = lax.axis_size(SEQ) == 4
     both_axes = (WSHARD, SEQ)
@@ -1206,23 +1220,18 @@
     if direct:
         lower = scatter_start(lower, WSHARD)
     lower_grad = finish(stages, tie(pending, lower[0]))
+    outputs = (placed(results), placed([lower_grad, upper_grad]))
     if direct:
         lower = scatter_start(scatter_done(lower, lower_grad), SEQ)
         lower = gather_start(scatter_done(lower), SEQ)
         lower = gather_start(gather_done(lower, SEQ), WSHARD)
-        lower = gather_done(lower, WSHARD)
+        lower = gather_done(lower, WSHARD, outputs)
     else:
         lower = lax.psum(lower, both_axes)
     sums = final_sums(sizes, width, section, upper, swap(upper), lower, swap(lower))
-    def placed(pair):
-        here = jnp.where(section == 0, pair[0], pair[1])
-        there = swap(jnp.where(section == 0, pair[1], pair[0]))
-        first, second = jnp.where(section == 0, here, there), jnp.where(section == 0, there, here)
-        return jnp.stack([first, second])[None]
-
     down_in, in_up, down_out, out_up = sums
     return (
-        placed(results), placed([lower_grad, upper_grad]), down_in[None], in_up.T[None], down_out[None], out_up[None],
+        *outputs, down_in[None], in_up.T[None], down_out[None], out_up[None],
     )
 
 

time: 403 us -> 356 us (0.88)
  waiting for transfers between devices: 77.2 us -> 49.1 us
  local copies, waits for them, and re-layouts: 40.8 us -> 27.7 us
  Pallas kernels: 171 us -> 160 us
  starting transfers between devices: 86.1 us -> 94.3 us
    ppermute x12, waiting for transfers between devices: 43.7 us -> 17.2 us  [across(): return lax.ppermute(value, (SECTION, WSHARD), pairs)]
    unnamed x294 -> x242, local copies, waits for them, and re-layouts: 29 us -> 16.1 us
    ppermute x10, starting transfers between devices: 29.1 us -> 34.9 us  [from_behind(): lax.ppermute(value, axis, [(source, source + steps) for source in range(i...]
    pallas_call x4, Pallas kernels: 23.3 us -> 18.5 us  [scan_forward(): pl.pallas_call(functools.partial(scan_kernel, s.head, s.state, s.gate_gai...]
  transfers between devices with their start and end apart: 73 -> 73, of which waited for: 22 -> 19; matrix products, arithmetic and copies ran while one was open for 5% -> 7% of each run, Pallas kernels for 36% -> 41%
where the time goes in v3:
time: 356 us; the launch traced here: 352 us
  Pallas kernels  160 us (45%)
  starting transfers between devices  94.3 us (26%)
  waiting for transfers between devices  49.1 us (14%)
  local copies, waits for them, and re-layouts  27.7 us (8%)
  other arithmetic  17.2 us (5%)
    ppermute x24, starting transfers between devices, exchange(): lax.ppermute(value, axis, [(place, place ^ distance) for place in range(c...  35.6 us
    ppermute x10, starting transfers between devices, from_behind(): lax.ppermute(value, axis, [(source, source + steps) for source in range(i...  34.9 us
    pallas_call x4, Pallas kernels, scan_backward(): pl.pallas_call(functools.partial(scan_back_kernel, s.head, s.heads, s.sta...  33.5 us
    ppermute x24, waiting for transfers between devices, exchange(): lax.ppermute(value, axis, [(place, place ^ distance) for place in range(c...  27.1 us
    pallas_call x2, Pallas kernels, out_backward(): pl.pallas_call(functools.partial(out_back_kernel, s.head, s.heads, s.stat...  23.3 us
    pallas_call x4, Pallas kernels, scan_forward(): pl.pallas_call(functools.partial(scan_kernel, s.head, s.state, s.gate_gai...  18.5 us
    ppermute x12, starting transfers between devices, across(): return lax.ppermute(value, (SECTION, WSHARD), pairs)  18.2 us
    ppermute x12, waiting for transfers between devices, across(): return lax.ppermute(value, (SECTION, WSHARD), pairs)  17.2 us
  transfers between devices with their start and end apart: 73, of which 19 were waited for; matrix products, arithmetic and copies ran while one was open for 7% of the time, Pallas kernels for 41%

profile of v3, /device:TPU:0, one launch (start us, length us, event | category | flops | bytes accessed | tf_op | source)
XLA Modules:
  0.0 351.6 jit_solution(6698712234502915240)
XLA Ops:
  7.5 2.7 collective-permute-start.11
  11.2 4.6 %collective-permute-start.2 = (s32[1,128]{1,0:T(1,128)S(1)}, s32[1,128]{1,0:T(1,128)S(1)}, u32[]{:S(2)}, u32[]{:S(2)}) collective-permute-start(s32[1,128]{1,0:T(1,128)S(1)} %get-tuple-element.373), channel_id=1, source_target_pairs={{0,4},{4,8},{8,12},{1,5},{5,9},{9,13},{2,6},{6,10},{10,14},{3,7},{... | collective-permute-start | bytes 1544 | tf_op jit(solution)/shard_map/ppermute | solution.py:35
  15.8 2.7 dynamic-slice_bitcast_fusion
  18.5 3.0 broadcast_select_fusion.5
  34.3 5.9 %collective-permute-done.13.rest_3_ = bf16[1184,256]{1,0:T(8,128)(2,1)S(1)} collective-permute-done((bf16[1184,256]{1,0:T(8,128)(2,1)S(1)}, bf16[1184,256]{1,0:T(8,128)(2,1)S(1)}, u32[]{:S(2)}, u32[]{:S(2)}) %collective-permute-start.13) | collective-permute-done | bytes 606240 | tf_op jit(solution)/shard_map/ppermute | solution.py:1035
  43.6 5.6 %shard_map.209 = (bf16[512,1152]{1,0:T(8,128)(2,1)S(1)}, bf16[512,2304]{1,0:T(8,128)(2,1)S(1)}, bf16[512,128]{1,0:T(8,128)(2,1)S(1)}, bf16[8,2304]{1,0:T(8,128)(2,1)S(1)}) custom-call(bf16[512,1024]{1,0:T(8,128)(2,1)S(1)} %get-tuple-element.191.input_ref, f32[1,14592]{1,0:T(1,128)S(1)} %get-tuple-element.192.vector_ref, ...), custom_call_target="tpu_custom_call" | custom-call | flops 20700000256 | bytes 65536 | tf_op jit(solution)/shard_map/pallas_call | solution.py:604
  51.1 3.5 collective-permute-start.15
  57.8 8.1 %shard_map.210 = (bf16[2048,512]{1,0:T(8,128)(2,1)S(1)}, bf16[512,2048]{1,0:T(8,128)(2,1)}, bf16[512,512]{1,0:T(8,128)(2,1)S(1)}, f32[96,512]{1,0:T(8,128)S(1)},...) custom-call(bf16[512,2304]{1,0:T(8,128)(2,1)S(1)} %get-tuple-element.202.mixed_ref.mixed_bc_ref, ...), custom_call_target="tpu_custom_call" | custom-call | flops 29325000704 | bytes 65536 | tf_op jit(solution)/shard_map/pallas_call | solution.py:516
  72.7 3.8 %collective-permute-start.16 = (bf16[2048,128]{1,0:T(8,128)(2,1)}, bf16[2048,128]{1,0:T(8,128)(2,1)S(1)}, u32[]{:S(2)}, u32[]{:S(2)}) collective-permute-start(bf16[2048,128]{1,0:T(8,128)(2,1)} %copy-done.59), channel_id=1, source_target_pairs={{0,4},{4,8},{8,12},{1,5},{5,9},{9,13},{2,6},{6,10},{10,14},{3,7},{... | collective-permute-start | bytes 1572872 | tf_op jit(solution)/shard_map/ppermute | solution.py:35
  80.6 4.9 %shard_map.211.gate_ref = bf16[512,2048]{1,0:T(8,128)(2,1)S(1)} custom-call(bf16[512,1152]{1,0:T(8,128)(2,1)S(1)} %copy-done.75, bf16[4384,128]{1,0:T(8,128)(2,1)S(1)} %get-tuple-element.195.up_ref, s32[5]{0:T(128)S(1)} %stack.41.where_ref, bf16[2048,256]{1,0:T(8,128)(2,1)S(1)} %copy-done.12, bf16[2048,256]{1,0:T(8,128)(2,1)} %collective-permute-done.17.rest_1_, ...), custom_call_target="tpu_custom_call" | custom-call | flops 12419999744 | bytes 65536 | tf_op jit(solution)/shard_map/pallas_call | solution.py:621
  85.6 4.6 %shard_map.212 = (bf16[512,2048]{1,0:T(8,128)(2,1)S(1)}, bf16[512,2048]{1,0:T(8,128)(2,1)S(1)}) custom-call(bf16[2048,512]{1,0:T(8,128)(2,1)S(1)} %copy-done.89, bf16[512,512]{1,0:T(8,128)(2,1)S(1)} %copy-done.94, f32[96,512]{1,0:T(8,128)S(1)} %copy-done.100, f32[96,512]{1,0:T(8,128)S(1)} %copy-done.100, f32[2,8,256]{2,1,0:T(8,128)S(1)} %copy-done.71, ...), custom_call_target="tpu_custom_call" | custom-call | flops 22424999936 | bytes 65536 | tf_op jit(solution)/shard_map/pallas_call | solution.py:571
  90.2 3.0 collective-permute-done.25.rest_1_
  96.4 4.6 %shard_map.213 = (bf16[512,2048]{1,0:T(8,128)(2,1)S(1)}, bf16[512,2048]{1,0:T(8,128)(2,1)S(1)}) custom-call(bf16[2048,512]{1,0:T(8,128)(2,1)S(1)} %copy-done.89, bf16[512,512]{1,0:T(8,128)(2,1)S(1)} %copy-done.94, f32[96,512]{1,0:T(8,128)S(1)} %copy-done.100, f32[96,512]{1,0:T(8,128)S(1)} %copy-done.100, ...), custom_call_target="tpu_custom_call", output_to_operand_aliasing={{0}: (11, {}), {1}: (12, {})} | custom-call | flops 22424999936 | bytes 65536 | tf_op jit(solution)/shard_map/pallas_call | solution.py:571
  101.2 6.4 %shard_map.214 = (bf16[512,128]{1,0:T(8,128)(2,1)S(1)}, bf16[512,1024]{1,0:T(8,128)(2,1)S(1)}) custom-call(bf16[512,2048]{1,0:T(8,128)(2,1)S(1)} %get-tuple-element.223.normed_ref.refs_2_, bf16[512,1024]{1,0:T(8,128)(2,1)S(1)} %copy-done.9, bf16[2048,128]{1,0:T(8,128)(2,1)S(1)} %copy-done.18, f32[512,128]{1,0:T(8,128)S(1)} %copy-done.61, ...), custom_call_target="tpu_custom_call" | custom-call | flops 13799999488 | bytes 65536 | tf_op jit(solution)/shard_map/pallas_call | solution.py:636
  107.6 3.8 %collective-permute-done.27.rest_3_ = bf16[1184,256]{1,0:T(8,128)(2,1)S(1)} collective-permute-done((bf16[1184,256]{1,0:T(8,128)(2,1)S(1)}, bf16[1184,256]{1,0:T(8,128)(2,1)S(1)}, u32[]{:S(2)}, u32[]{:S(2)}) %collective-permute-start.27) | collective-permute-done | bytes 606240 | tf_op jit(solution)/shard_map/ppermute | solution.py:1035
  111.5 3.1 collective-permute-done.31.rest_1_
  117.0 6.1 %shard_map.215 = (bf16[512,1152]{1,0:T(8,128)(2,1)S(1)}, bf16[512,2304]{1,0:T(8,128)(2,1)S(1)}, bf16[512,128]{1,0:T(8,128)(2,1)S(1)}, bf16[8,2304]{1,0:T(8,128)(2,1)}) custom-call(bf16[512,1024]{1,0:T(8,128)(2,1)S(1)} %get-tuple-element.230.input_ref, f32[1,14592]{1,0:T(1,128)S(1)} %copy-done.37, bf16[1024,128]{1,0:T(8,128)(2,1)S(1)} %copy-done.29, ...), custom_call_target="tpu_custom_call" | custom-call | flops 20700000256 | bytes 65536 | tf_op jit(solution)/shard_map/pallas_call | solution.py:604
  126.2 3.5 collective-permute-start.29
  135.4 8.1 %shard_map.216 = (bf16[2048,512]{1,0:T(8,128)(2,1)S(1)}, bf16[512,2048]{1,0:T(8,128)(2,1)}, bf16[512,512]{1,0:T(8,128)(2,1)S(1)}, f32[96,512]{1,0:T(8,128)S(1)},...) custom-call(bf16[512,2304]{1,0:T(8,128)(2,1)S(1)} %copy-done.87, bf16[512,2304]{1,0:T(8,128)(2,1)S(1)} %copy-done.87, ...), custom_call_target="tpu_custom_call" | custom-call | flops 29325000704 | bytes 65536 | tf_op jit(solution)/shard_map/pallas_call | solution.py:516
  143.5 12.5 %collective-permute-start.30 = (bf16[2048,128]{1,0:T(8,128)(2,1)S(1)}, bf16[2048,128]{1,0:T(8,128)(2,1)S(1)}, u32[]{:S(2)}, u32[]{:S(2)}) collective-permute-start(bf16[2048,128]{1,0:T(8,128)(2,1)S(1)} %get-tuple-element.246), channel_id=1, source_target_pairs={{0,4},{4,8},{8,12},{1,5},{5,9},{9,13},{2,6},{6,10},{10,14},{3,7},{... | collective-permute-start | bytes 1572872 | tf_op jit(solution)/shard_map/ppermute | solution.py:35
  156.7 4.0 %shard_map.217.gate_ref = bf16[512,2048]{1,0:T(8,128)(2,1)S(1)} custom-call(bf16[512,1152]{1,0:T(8,128)(2,1)S(1)} %copy-done.78, bf16[4384,128]{1,0:T(8,128)(2,1)S(1)} %copy-done.7, s32[5]{0:T(128)S(1)} %stack.41.where_ref, bf16[2048,256]{1,0:T(8,128)(2,1)S(1)} %copy-done.16, bf16[2048,256]{1,0:T(8,128)(2,1)S(1)} %copy-done.33, ...), custom_call_target="tpu_custom_call" | custom-call | flops 12419999744 | bytes 65536 | tf_op jit(solution)/shard_map/pallas_call | solution.py:621
  160.7 4.6 %shard_map.218 = (bf16[512,2048]{1,0:T(8,128)(2,1)S(1)}, bf16[512,2048]{1,0:T(8,128)(2,1)S(1)}) custom-call(bf16[2048,512]{1,0:T(8,128)(2,1)S(1)} %get-tuple-element.243.values_ref, bf16[512,512]{1,0:T(8,128)(2,1)S(1)} %get-tuple-element.244.bc_ref.slope_bc_ref, f32[96,512]{1,0:T(8,128)S(1)} %get-tuple-element.245.step_ref.decay_ref.sig_ref, ...), custom_call_target="tpu_custom_call" | custom-call | flops 22424999936 | bytes 65536 | tf_op jit(solution)/shard_map/pallas_call | solution.py:571
  166.7 4.6 %shard_map.219 = (bf16[512,2048]{1,0:T(8,128)(2,1)S(1)}, bf16[512,2048]{1,0:T(8,128)(2,1)S(1)}) custom-call(bf16[2048,512]{1,0:T(8,128)(2,1)S(1)} %get-tuple-element.243.values_ref, bf16[512,512]{1,0:T(8,128)(2,1)S(1)} %get-tuple-element.244.bc_ref.slope_bc_ref, ...), custom_call_target="tpu_custom_call", output_to_operand_aliasing={{0}: (11, {}), {1}: (12, {})} | custom-call | flops 22424999936 | bytes 65536 | tf_op jit(solution)/shard_map/pallas_call | solution.py:571
  171.4 3.7 %shard_map.220 = (bf16[512,128]{1,0:T(8,128)(2,1)S(1)}, bf16[512,1024]{1,0:T(8,128)(2,1)S(1)}) custom-call(bf16[512,2048]{1,0:T(8,128)(2,1)S(1)} %get-tuple-element.256.normed_ref.refs_2_, bf16[512,1024]{1,0:T(8,128)(2,1)S(1)} %get-tuple-element.230.input_ref, bf16[2048,128]{1,0:T(8,128)(2,1)S(1)} %copy-done.20, f32[512,128]{1,0:T(8,128)S(1)} %copy-done.62, ...), custom_call_target="tpu_custom_call" | custom-call | flops 13799999488 | bytes 65536 | tf_op jit(solution)/shard_map/pallas_call | solution.py:636
  176.8 11.0 %shard_map.221 = (bf16[512,2048]{1,0:T(8,128)(2,1)S(1)}, bf16[2048,512]{1,0:T(8,128)(2,1)S(1)}, bf16[512,128]{1,0:T(8,128)(2,1)S(1)}, bf16[2048,128]{1,0:T(8,128)(2,1)S(1)}, bf16[2048,128]{1,0:T(8,128)(2,1)S(1)}) custom-call(bf16[512,1024]{1,0:T(8,128)(2,1)S(1)} %copy-done.14, f32[512,128]{1,0:T(8,128)S(1)} %copy-done.62, bf16[128,1024]{1,0:T(8,128)(2,1)S(1)} %copy-done.31, ...), custom_call_target="tpu_custom_call" | custom-call | flops 46575001600 | bytes 65536 | tf_op jit(solution)/shard_map/pallas_call | solution.py:651
  189.1 8.4 %shard_map.222 = (bf16[512,2048]{1,0:T(8,128)(2,1)S(1)}, bf16[512,256]{1,0:T(8,128)(2,1)S(1)}, bf16[512,128]{1,0:T(8,128)(2,1)S(1)}, bf16[8,2304]{1,0:T(8,128)(2,1)S(1)}) custom-call(bf16[2048,512]{1,0:T(8,128)(2,1)S(1)} %get-tuple-element.243.values_ref, bf16[2048,512]{1,0:T(8,128)(2,1)S(1)} %get-tuple-element.267.grad_ref, ...), custom_call_target="tpu_custom_call" | custom-call | flops 29325000704 | bytes 65536 | tf_op jit(solution)/shard_map/pallas_call | solution.py:744
  199.3 4.0 %shard_map.225.part_ref = f32[512,1152]{1,0:T(8,128)S(1)} custom-call(bf16[512,2048]{1,0:T(8,128)(2,1)S(1)} %get-tuple-element.279.grad_ref.refs_4_, bf16[4384,128]{1,0:T(8,128)(2,1)S(1)} %copy-done.7, s32[5]{0:T(128)S(1)} %stack.41.where_ref, bf16[2048,256]{1,0:T(8,128)(2,1)S(1)} %copy-done.16, bf16[2048,256]{1,0:T(8,128)(2,1)S(1)} %copy-done.33, ...), custom_call_target="tpu_custom_call" | custom-call | flops 12074999808 | bytes 65536 | tf_op jit(solution)/shard_map/pallas_call | solution.py:678
  205.1 8.3 %shard_map.223 = (bf16[512,2048]{1,0:T(8,128)(2,1)S(1)}, bf16[512,256]{1,0:T(8,128)(2,1)S(1)}, bf16[512,128]{1,0:T(8,128)(2,1)S(1)}) custom-call(bf16[2048,512]{1,0:T(8,128)(2,1)S(1)} %get-tuple-element.243.values_ref, bf16[2048,512]{1,0:T(8,128)(2,1)S(1)} %get-tuple-element.267.grad_ref, ...), custom_call_target="tpu_custom_call", output_to_operand_aliasing={{0}: (15, {}), {1}: (16, {}), {2}: (17, {})} | custom-call | flops 29325000704 | bytes 65536 | tf_op jit(solution)/shard_map/pallas_call | solution.py:744
  213.4 4.4 %shard_map.224.grad_ref.refs_2_ = bf16[512,2304]{1,0:T(8,128)(2,1)S(1)} custom-call(bf16[512,2048]{1,0:T(8,128)(2,1)S(1)} %get-tuple-element.274.grad_ref, bf16[512,256]{1,0:T(8,128)(2,1)S(1)} %get-tuple-element.275.grad_bc_ref, bf16[512,2048]{1,0:T(8,128)(2,1)S(1)} %copy-done.85, bf16[512,512]{1,0:T(8,128)(2,1)S(1)} %get-tuple-element.244.bc_ref.slope_bc_ref, ...), custom_call_target="tpu_custom_call" | custom-call | flops 15180000256 | bytes 65536 | tf_op jit(solution)/shard_map/pallas_call | solution.py:767
  221.4 4.5 %shard_map.227.up_ref.refs_0_.up_stream_ref = bf16[512,1024]{1,0:T(8,128)(2,1)S(1)} custom-call(bf16[512,2304]{1,0:T(8,128)(2,1)S(1)} %shard_map.224.grad_ref.refs_2_, bf16[512,128]{1,0:T(8,128)(2,1)S(1)} %get-tuple-element.278.raw_ref.refs_3_, f32[512,1152]{1,0:T(8,128)S(1)} %shard_map.225.part_ref, bf16[512,1024]{1,0:T(8,128)(2,1)S(1)} %get-tuple-element.230.input_ref, ...), custom_call_target="tpu_custom_call" | custom-call | flops 16215000064 | bytes 65536 | tf_op jit(solution)/shard_map/pallas_call | solution.py:709
  231.7 12.3 %shard_map.230 = (bf16[512,2048]{1,0:T(8,128)(2,1)S(1)}, bf16[2048,512]{1,0:T(8,128)(2,1)S(1)}, bf16[512,128]{1,0:T(8,128)(2,1)S(1)}, bf16[2048,128]{1,0:T(8,128)(2,1)S(1)}, bf16[2048,128]{1,0:T(8,128)(2,1)S(1)}) custom-call(bf16[512,1024]{1,0:T(8,128)(2,1)S(1)} %shard_map.227.up_ref.refs_0_.up_stream_ref, f32[512,128]{1,0:T(8,128)S(1)} %copy-done.62, ...), custom_call_target="tpu_custom_call" | custom-call | flops 46575001600 | bytes 65536 | tf_op jit(solution)/shard_map/pallas_call | solution.py:651
  245.3 8.6 %shard_map.231 = (bf16[512,2048]{1,0:T(8,128)(2,1)S(1)}, bf16[512,256]{1,0:T(8,128)(2,1)S(1)}, bf16[512,128]{1,0:T(8,128)(2,1)S(1)}, bf16[8,2304]{1,0:T(8,128)(2,1)S(1)}) custom-call(bf16[2048,512]{1,0:T(8,128)(2,1)S(1)} %copy-done.90, bf16[2048,512]{1,0:T(8,128)(2,1)S(1)} %get-tuple-element.292.grad_ref, bf16[512,512]{1,0:T(8,128)(2,1)S(1)} %copy-done.95, ...), custom_call_target="tpu_custom_call" | custom-call | flops 29325000704 | bytes 65536 | tf_op jit(solution)/shard_map/pallas_call | solution.py:744
  255.2 4.9 %shard_map.234.part_ref = f32[512,1152]{1,0:T(8,128)S(1)} custom-call(bf16[512,2048]{1,0:T(8,128)(2,1)S(1)} %get-tuple-element.308.grad_ref.refs_4_, bf16[4384,128]{1,0:T(8,128)(2,1)S(1)} %get-tuple-element.195.up_ref, s32[5]{0:T(128)S(1)} %stack.41.where_ref, bf16[2048,256]{1,0:T(8,128)(2,1)S(1)} %copy-done.13, ...), custom_call_target="tpu_custom_call" | custom-call | flops 12074999808 | bytes 65536 | tf_op jit(solution)/shard_map/pallas_call | solution.py:678
  262.1 4.6 %collective-permute-start.47 = (bf16[272,128]{1,0:T(8,128)(2,1)S(1)}, bf16[272,128]{1,0:T(8,128)(2,1)S(1)}, u32[]{:S(2)}, u32[]{:S(2)}) collective-permute-start(bf16[272,128]{1,0:T(8,128)(2,1)S(1)} %get-tuple-element.368), channel_id=1, source_target_pairs={{0,4},{4,0},{8,12},{12,8},{1,5},{5,1},{9,13},{13,9},{2,6},{6,2},{1... | collective-permute-start | bytes 208904 | tf_op jit(solution)/shard_map/ppermute | solution.py:1017
  266.7 3.5 collective-permute-start.48
  270.2 8.3 %shard_map.232 = (bf16[512,2048]{1,0:T(8,128)(2,1)S(1)}, bf16[512,256]{1,0:T(8,128)(2,1)S(1)}, bf16[512,128]{1,0:T(8,128)(2,1)S(1)}) custom-call(bf16[2048,512]{1,0:T(8,128)(2,1)S(1)} %copy-done.90, bf16[2048,512]{1,0:T(8,128)(2,1)S(1)} %get-tuple-element.292.grad_ref, ...), custom_call_target="tpu_custom_call", output_to_operand_aliasing={{0}: (15, {}), {1}: (16, {}), {2}: (17, {})} | custom-call | flops 29325000704 | bytes 65536 | tf_op jit(solution)/shard_map/pallas_call | solution.py:744
  279.3 3.8 %collective-permute-start.52 = (bf16[272,128]{1,0:T(8,128)(2,1)S(1)}, bf16[272,128]{1,0:T(8,128)(2,1)S(1)}, u32[]{:S(2)}, u32[]{:S(2)}) collective-permute-start(bf16[272,128]{1,0:T(8,128)(2,1)S(1)} %get-tuple-element.335), channel_id=1, source_target_pairs={{0,8},{4,12},{8,0},{12,4},{1,9},{5,13},{9,1},{13,5},{2,10},{6,14},... | collective-permute-start | bytes 208904 | tf_op jit(solution)/shard_map/ppermute | solution.py:1017
  283.1 4.4 %shard_map.233.grad_ref.refs_2_ = bf16[512,2304]{1,0:T(8,128)(2,1)S(1)} custom-call(bf16[512,2048]{1,0:T(8,128)(2,1)S(1)} %get-tuple-element.300.grad_ref, bf16[512,256]{1,0:T(8,128)(2,1)S(1)} %get-tuple-element.301.grad_bc_ref, bf16[512,2048]{1,0:T(8,128)(2,1)S(1)} %copy-done.84, bf16[512,512]{1,0:T(8,128)(2,1)S(1)} %copy-done.95, ...), custom_call_target="tpu_custom_call" | custom-call | flops 15180000256 | bytes 65536 | tf_op jit(solution)/shard_map/pallas_call | solution.py:767
  295.2 2.7 collective-permute-done.55
  297.9 3.2 collective-permute-done.56
  305.3 4.5 %shard_map.238 = bf16[512,1024]{1,0:T(8,128)(2,1)S(1)} custom-call(bf16[512,2304]{1,0:T(8,128)(2,1)S(1)} %shard_map.233.grad_ref.refs_2_, bf16[512,128]{1,0:T(8,128)(2,1)S(1)} %get-tuple-element.307.raw_ref.refs_3_, f32[512,1152]{1,0:T(8,128)S(1)} %shard_map.234.part_ref, bf16[512,1024]{1,0:T(8,128)(2,1)S(1)} %copy-done.10, ...), custom_call_target="tpu_custom_call" | custom-call | flops 16215000064 | bytes 65536 | tf_op jit(solution)/shard_map/pallas_call | solution.py:709
  310.0 3.2 collective-permute-done.61
  314.0 3.4 collective-permute-start.64
  320.4 3.6 %collective-permute-done.65 = bf16[272,128]{1,0:T(8,128)(2,1)S(1)} collective-permute-done((bf16[272,128]{1,0:T(8,128)(2,1)S(1)}, bf16[272,128]{1,0:T(8,128)(2,1)S(1)}, u32[]{:S(2)}, u32[]{:S(2)}) %collective-permute-start.65) | collective-permute-done | bytes 69664 | tf_op jit(solution)/shard_map/ppermute | solution.py:1017
  325.9 2.8 collective-permute-start.68
  337.5 4.1 %collective-permute-done.69 = bf16[1088,128]{1,0:T(8,128)(2,1)S(1)} collective-permute-done((bf16[1088,128]{1,0:T(8,128)(2,1)S(1)}, bf16[1088,128]{1,0:T(8,128)(2,1)S(1)}, u32[]{:S(2)}, u32[]{:S(2)}) %collective-permute-start.69) | collective-permute-done | bytes 278560 | tf_op jit(solution)/shard_map/ppermute | solution.py:1017
  341.7 4.1 %collective-permute-done.70 = bf16[1088,128]{1,0:T(8,128)(2,1)S(1)} collective-permute-done((bf16[1088,128]{1,0:T(8,128)(2,1)S(1)}, bf16[1088,128]{1,0:T(8,128)(2,1)S(1)}, u32[]{:S(2)}, u32[]{:S(2)}) %collective-permute-start.70) | collective-permute-done | bytes 278560 | tf_op jit(solution)/shard_map/ppermute | solution.py:1017
  346.1 2.7 collective-permute-done.72.refs_3_
  (438 shorter events, 106.0 us)
Async XLA Ops:
  7.5 22.4 %collective-permute-start.11 = (bf16[2336,256]{1,0:T(8,128)(2,1)S(1)}, bf16[2336,256]{1,0:T(8,128)(2,1)S(1)}, u32[]{:S(2)}, u32[]{:S(2)}) collective-permute-start(bf16[2336,256]{1,0:T(8,128)(2,1)S(1)} %get-tuple-element.197.rest_0_), channel_id=1, source_target_pairs={{0,1},{1,0},{2,3},{3,2},{16,18},{17,19},{18,16},{19,17},{4,5},{5,4... | collective-permute-start | bytes 3588104 | tf_op jit(solution)/shard_map/ppermute | solution.py:1035
  10.2 11.2 %collective-permute-start.4 = (bf16[512,1024]{1,0:T(8,128)(2,1)S(1)}, bf16[512,1024]{1,0:T(8,128)(2,1)S(1)}, u32[]{:S(2)}, u32[]{:S(2)}) collective-permute-start(bf16[512,1024]{1,0:T(8,128)(2,1)S(1)} %bitcast.124), channel_id=1, source_target_pairs={{0,16},{16,0},{1,17},{17,1},{2,18},{18,2},{3,19},{19,3},{4,20},{20... | collective-permute-start | bytes 3145736 | tf_op jit(solution)/shard_map/ppermute | solution.py:1012
  10.3 14.3 %collective-permute-start.5 = (f32[3,32]{1,0:T(4,128)S(1)}, f32[3,32]{1,0:T(4,128)S(1)}, u32[]{:S(2)}, u32[]{:S(2)}) collective-permute-start(f32[3,32]{1,0:T(4,128)S(1)} %pad_maximum_fusion), channel_id=1, source_target_pairs={{0,16},{16,0},{1,17},{17,1},{2,18},{18,2},{3,19},{19,3},{4,20},{20... | collective-permute-start | bytes 1160 | tf_op jit(solution)/shard_map/ppermute | solution.py:1012
  11.0 17.6 %collective-permute-start.10 = (f32[1,14592]{1,0:T(1,128)S(1)}, f32[1,14592]{1,0:T(1,128)S(1)}, u32[]{:S(2)}, u32[]{:S(2)}) collective-permute-start(f32[1,14592]{1,0:T(1,128)S(1)} %constant_dynamic-update-slice_fusion), channel_id=1, source_target_pairs={{0,16},{16,0},{1,17},{17,1},{2,18},{18,2},{3,19},{19,3},{4,20},{20... | collective-permute-start | bytes 175112 | tf_op jit(solution)/shard_map/ppermute | solution.py:1012
  11.2 13.7 %collective-permute-start.2 = (s32[1,128]{1,0:T(1,128)S(1)}, s32[1,128]{1,0:T(1,128)S(1)}, u32[]{:S(2)}, u32[]{:S(2)}) collective-permute-start(s32[1,128]{1,0:T(1,128)S(1)} %get-tuple-element.373), channel_id=1, source_target_pairs={{0,4},{4,8},{8,12},{1,5},{5,9},{9,13},{2,6},{6,10},{10,14},{3,7},{... | collective-permute-start | bytes 1544 | tf_op jit(solution)/shard_map/ppermute | solution.py:35
  24.7 17.0 %collective-permute-start.7 = (bf16[4384,128]{1,0:T(8,128)(2,1)S(1)}, bf16[4384,128]{1,0:T(8,128)(2,1)S(1)}, u32[]{:S(2)}, u32[]{:S(2)}) collective-permute-start(bf16[4384,128]{1,0:T(8,128)(2,1)S(1)} %bitcast.115), channel_id=1, source_target_pairs={{0,16},{16,0},{1,17},{17,1},{2,18},{18,2},{3,19},{19,3},{4,20},{20... | collective-permute-start | bytes 3366920 | tf_op jit(solution)/shard_map/ppermute | solution.py:1012
  29.9 13.0 %collective-permute-start.12 = (bf16[2336,256]{1,0:T(8,128)(2,1)S(1)}, bf16[2336,256]{1,0:T(8,128)(2,1)S(1)}, u32[]{:S(2)}, u32[]{:S(2)}) collective-permute-start(bf16[2336,256]{1,0:T(8,128)(2,1)S(1)} %collective-permute-done.11.rest_1_), channel_id=1, source_target_pairs={{0,16},{16,0},{1,17},{17,1},{2,18},{18,2},{3,19},{19,3},{4,20},{20... | collective-permute-start | bytes 3588104 | tf_op jit(solution)/shard_map/ppermute | solution.py:1012
  30.0 10.1 %collective-permute-start.13 = (bf16[1184,256]{1,0:T(8,128)(2,1)S(1)}, bf16[1184,256]{1,0:T(8,128)(2,1)S(1)}, u32[]{:S(2)}, u32[]{:S(2)}) collective-permute-start(bf16[1184,256]{1,0:T(8,128)(2,1)S(1)} %constant_dynamic-slice_fusion.23), channel_id=1, source_target_pairs={{0,2},{1,3},{2,0},{3,1},{16,17},{17,16},{18,19},{19,18},{4,6},{5,7... | collective-permute-start | bytes 1818632 | tf_op jit(solution)/shard_map/ppermute | solution.py:1035
  40.1 15.0 %collective-permute-start.17 = (bf16[2048,256]{1,0:T(8,128)(2,1)S(1)}, bf16[2048,256]{1,0:T(8,128)(2,1)}, u32[]{:S(2)}, u32[]{:S(2)}) collective-permute-start(bf16[2048,256]{1,0:T(8,128)(2,1)S(1)} %get-tuple-element.217.rest_0_), channel_id=1, source_target_pairs={{0,1},{1,0},{2,3},{3,2},{16,18},{17,19},{18,16},{19,17},{4,5},{5,4... | collective-permute-start | bytes 3145736 | tf_op jit(solution)/shard_map/ppermute | solution.py:1035
  50.2 26.3 %collective-permute-start.21 = (bf16[512,1024]{1,0:T(8,128)(2,1)}, bf16[512,1024]{1,0:T(8,128)(2,1)}, u32[]{:S(2)}, u32[]{:S(2)}) collective-permute-start(bf16[512,1024]{1,0:T(8,128)(2,1)} %get-tuple-element.227.rest_0_), channel_id=1, source_target_pairs={{0,1},{1,0},{2,3},{3,2},{16,18},{17,19},{18,16},{19,17},{4,5},{5,4... | collective-permute-start | bytes 3145736 | tf_op jit(solution)/shard_map/ppermute | solution.py:1035
  55.1 24.1 %collective-permute-start.18 = (bf16[2048,256]{1,0:T(8,128)(2,1)}, bf16[2048,256]{1,0:T(8,128)(2,1)}, u32[]{:S(2)}, u32[]{:S(2)}) collective-permute-start(bf16[2048,256]{1,0:T(8,128)(2,1)} %collective-permute-done.17.rest_1_), channel_id=1, source_target_pairs={{0,16},{16,0},{1,17},{17,1},{2,18},{18,2},{3,19},{19,3},{4,20},{20... | collective-permute-start | bytes 3145736 | tf_op jit(solution)/shard_map/ppermute | solution.py:1012
  56.2 15.0 %collective-permute-start.19 = (bf16[1024,256]{1,0:T(8,128)(2,1)S(1)}, bf16[1024,256]{1,0:T(8,128)(2,1)}, u32[]{:S(2)}, u32[]{:S(2)}) collective-permute-start(bf16[1024,256]{1,0:T(8,128)(2,1)S(1)} %constant_dynamic-slice_fusion.22), channel_id=1, source_target_pairs={{0,2},{1,3},{2,0},{3,1},{16,17},{17,16},{18,19},{19,18},{4,6},{5,7... | collective-permute-start | bytes 1572872 | tf_op jit(solution)/shard_map/ppermute | solution.py:1035
  71.2 22.0 %collective-permute-start.25 = (bf16[2336,256]{1,0:T(8,128)(2,1)S(1)}, bf16[2336,256]{1,0:T(8,128)(2,1)S(1)}, u32[]{:S(2)}, u32[]{:S(2)}) collective-permute-start(bf16[2336,256]{1,0:T(8,128)(2,1)S(1)} %get-tuple-element.236.rest_0_), channel_id=1, source_target_pairs={{0,1},{1,0},{2,3},{3,2},{16,18},{17,19},{18,16},{19,17},{4,5},{5,4... | collective-permute-start | bytes 3588104 | tf_op jit(solution)/shard_map/ppermute | solution.py:1035
  72.7 23.7 %collective-permute-start.16 = (bf16[2048,128]{1,0:T(8,128)(2,1)}, bf16[2048,128]{1,0:T(8,128)(2,1)S(1)}, u32[]{:S(2)}, u32[]{:S(2)}) collective-permute-start(bf16[2048,128]{1,0:T(8,128)(2,1)} %copy-done.59), channel_id=1, source_target_pairs={{0,4},{4,8},{8,12},{1,5},{5,9},{9,13},{2,6},{6,10},{10,14},{3,7},{... | collective-permute-start | bytes 1572872 | tf_op jit(solution)/shard_map/ppermute | solution.py:35
  76.5 24.6 %collective-permute-start.22 = (bf16[512,1024]{1,0:T(8,128)(2,1)}, bf16[512,1024]{1,0:T(8,128)(2,1)S(1)}, u32[]{:S(2)}, u32[]{:S(2)}) collective-permute-start(bf16[512,1024]{1,0:T(8,128)(2,1)} %collective-permute-done.21.rest_1_), channel_id=1, source_target_pairs={{0,16},{16,0},{1,17},{17,1},{2,18},{18,2},{3,19},{19,3},{4,20},{20... | collective-permute-start | bytes 3145736 | tf_op jit(solution)/shard_map/ppermute | solution.py:1012
  77.7 17.1 %collective-permute-start.23 = (bf16[256,1024]{1,0:T(8,128)(2,1)S(1)}, bf16[256,1024]{1,0:T(8,128)(2,1)S(1)}, u32[]{:S(2)}, u32[]{:S(2)}) collective-permute-start(bf16[256,1024]{1,0:T(8,128)(2,1)S(1)} %constant_dynamic-slice_fusion.21), channel_id=1, source_target_pairs={{0,2},{1,3},{2,0},{3,1},{16,17},{17,16},{18,19},{19,18},{4,6},{5,7... | collective-permute-start | bytes 1572872 | tf_op jit(solution)/shard_map/ppermute | solution.py:1035
  93.2 21.3 %collective-permute-start.31 = (bf16[2048,256]{1,0:T(8,128)(2,1)S(1)}, bf16[2048,256]{1,0:T(8,128)(2,1)S(1)}, u32[]{:S(2)}, u32[]{:S(2)}) collective-permute-start(bf16[2048,256]{1,0:T(8,128)(2,1)S(1)} %copy-done.15), channel_id=1, source_target_pairs={{0,1},{1,0},{2,3},{3,2},{16,18},{17,19},{18,16},{19,17},{4,5},{5,4... | collective-permute-start | bytes 3145736 | tf_op jit(solution)/shard_map/ppermute | solution.py:1035
  94.7 22.2 %collective-permute-start.26 = (bf16[2336,256]{1,0:T(8,128)(2,1)S(1)}, bf16[2336,256]{1,0:T(8,128)(2,1)S(1)}, u32[]{:S(2)}, u32[]{:S(2)}) collective-permute-start(bf16[2336,256]{1,0:T(8,128)(2,1)S(1)} %collective-permute-done.25.rest_1_), channel_id=1, source_target_pairs={{0,16},{16,0},{1,17},{17,1},{2,18},{18,2},{3,19},{19,3},{4,20},{20... | collective-permute-start | bytes 3588104 | tf_op jit(solution)/shard_map/ppermute | solution.py:1012
  94.8 16.7 %collective-permute-start.27 = (bf16[1184,256]{1,0:T(8,128)(2,1)S(1)}, bf16[1184,256]{1,0:T(8,128)(2,1)S(1)}, u32[]{:S(2)}, u32[]{:S(2)}) collective-permute-start(bf16[1184,256]{1,0:T(8,128)(2,1)S(1)} %constant_dynamic-slice_fusion.20), channel_id=1, source_target_pairs={{0,2},{1,3},{2,0},{3,1},{16,17},{17,16},{18,19},{19,18},{4,6},{5,7... | collective-permute-start | bytes 1818632 | tf_op jit(solution)/shard_map/ppermute | solution.py:1035
  115.4 16.0 %collective-permute-start.33 = (bf16[1024,256]{1,0:T(8,128)(2,1)}, bf16[1024,256]{1,0:T(8,128)(2,1)}, u32[]{:S(2)}, u32[]{:S(2)}) collective-permute-start(bf16[1024,256]{1,0:T(8,128)(2,1)} %constant_dynamic-slice_fusion.19), channel_id=1, source_target_pairs={{0,2},{1,3},{2,0},{3,1},{16,17},{17,16},{18,19},{19,18},{4,6},{5,7... | collective-permute-start | bytes 1572872 | tf_op jit(solution)/shard_map/ppermute | solution.py:1035
  129.8 26.2 %collective-permute-start.35 = (bf16[512,1024]{1,0:T(8,128)(2,1)}, bf16[512,1024]{1,0:T(8,128)(2,1)S(1)}, u32[]{:S(2)}, u32[]{:S(2)}) collective-permute-start(bf16[512,1024]{1,0:T(8,128)(2,1)} %get-tuple-element.260.rest_0_), channel_id=1, source_target_pairs={{0,1},{1,0},{2,3},{3,2},{16,18},{17,19},{18,16},{19,17},{4,5},{5,4... | collective-permute-start | bytes 3145736 | tf_op jit(solution)/shard_map/ppermute | solution.py:1035
  131.3 25.3 %collective-permute-start.32 = (bf16[2048,256]{1,0:T(8,128)(2,1)}, bf16[2048,256]{1,0:T(8,128)(2,1)S(1)}, u32[]{:S(2)}, u32[]{:S(2)}) collective-permute-start(bf16[2048,256]{1,0:T(8,128)(2,1)} %copy-done.32), channel_id=1, source_target_pairs={{0,16},{16,0},{1,17},{17,1},{2,18},{18,2},{3,19},{19,3},{4,20},{20... | collective-permute-start | bytes 3145736 | tf_op jit(solution)/shard_map/ppermute | solution.py:1012
  131.4 25.3 %collective-permute-start.34 = (bf16[1024,256]{1,0:T(8,128)(2,1)}, bf16[1024,256]{1,0:T(8,128)(2,1)S(1)}, u32[]{:S(2)}, u32[]{:S(2)}) collective-permute-start(bf16[1024,256]{1,0:T(8,128)(2,1)} %collective-permute-done.33.rest_3_), channel_id=1, source_target_pairs={{0,16},{16,0},{1,17},{17,1},{2,18},{18,2},{3,19},{19,3},{4,20},{20... | collective-permute-start | bytes 1572872 | tf_op jit(solution)/shard_map/ppermute | solution.py:1012
  143.5 23.2 %collective-permute-start.30 = (bf16[2048,128]{1,0:T(8,128)(2,1)S(1)}, bf16[2048,128]{1,0:T(8,128)(2,1)S(1)}, u32[]{:S(2)}, u32[]{:S(2)}) collective-permute-start(bf16[2048,128]{1,0:T(8,128)(2,1)S(1)} %get-tuple-element.246), channel_id=1, source_target_pairs={{0,4},{4,8},{8,12},{1,5},{5,9},{9,13},{2,6},{6,10},{10,14},{3,7},{... | collective-permute-start | bytes 1572872 | tf_op jit(solution)/shard_map/ppermute | solution.py:35
  156.0 15.4 %collective-permute-start.36 = (bf16[512,1024]{1,0:T(8,128)(2,1)S(1)}, bf16[512,1024]{1,0:T(8,128)(2,1)S(1)}, u32[]{:S(2)}, u32[]{:S(2)}) collective-permute-start(bf16[512,1024]{1,0:T(8,128)(2,1)S(1)} %collective-permute-done.35.rest_1_), channel_id=1, source_target_pairs={{0,16},{16,0},{1,17},{17,1},{2,18},{18,2},{3,19},{19,3},{4,20},{20... | collective-permute-start | bytes 3145736 | tf_op jit(solution)/shard_map/ppermute | solution.py:1012
  156.1 9.3 %collective-permute-start.37 = (bf16[256,1024]{1,0:T(8,128)(2,1)S(1)}, bf16[256,1024]{1,0:T(8,128)(2,1)S(1)}, u32[]{:S(2)}, u32[]{:S(2)}) collective-permute-start(bf16[256,1024]{1,0:T(8,128)(2,1)S(1)} %constant_dynamic-slice_fusion.18), channel_id=1, source_target_pairs={{0,2},{1,3},{2,0},{3,1},{16,17},{17,16},{18,19},{19,18},{4,6},{5,7... | collective-permute-start | bytes 1572872 | tf_op jit(solution)/shard_map/ppermute | solution.py:1035
  187.8 17.3 %collective-permute-start.40 = (bf16[2048,128]{1,0:T(8,128)(2,1)S(1)}, bf16[2048,128]{1,0:T(8,128)(2,1)S(1)}, u32[]{:S(2)}, u32[]{:S(2)}) collective-permute-start(bf16[2048,128]{1,0:T(8,128)(2,1)S(1)} %get-tuple-element.268), channel_id=1, source_target_pairs={{4,0},{8,4},{12,8},{5,1},{9,5},{13,9},{6,2},{10,6},{14,10},{7,3},{... | collective-permute-start | bytes 1572872 | tf_op jit(solution)/shard_map/ppermute | solution.py:35
  197.5 15.9 %collective-permute-start.41 = (bf16[8,2304]{1,0:T(8,128)(2,1)S(1)}, bf16[8,2304]{1,0:T(8,128)(2,1)S(1)}, u32[]{:S(2)}, u32[]{:S(2)}) collective-permute-start(bf16[8,2304]{1,0:T(8,128)(2,1)S(1)} %get-tuple-element.276), channel_id=1, source_target_pairs={{4,0},{8,4},{12,8},{5,1},{9,5},{13,9},{6,2},{10,6},{14,10},{7,3},{... | collective-permute-start | bytes 110600 | tf_op jit(solution)/shard_map/ppermute | solution.py:35
  199.2 26.8 %collective-permute-start.39 = (bf16[512,1024]{1,0:T(8,128)(2,1)S(1)}, bf16[512,1024]{1,0:T(8,128)(2,1)S(1)}, u32[]{:S(2)}, u32[]{:S(2)}) collective-permute-start(bf16[512,1024]{1,0:T(8,128)(2,1)S(1)} %broadcast_select_fusion.9), channel_id=1, source_target_pairs={{0,16},{16,0},{1,17},{17,1},{2,18},{18,2},{3,19},{19,3},{4,20},{20... | collective-permute-start | bytes 3145736 | tf_op jit(solution)/shard_map/ppermute | solution.py:1012
  228.0 33.9 %collective-permute-start.43 = (bf16[1088,128]{1,0:T(8,128)(2,1)S(1)}, bf16[1088,128]{1,0:T(8,128)(2,1)S(1)}, u32[]{:S(2)}, u32[]{:S(2)}) collective-permute-start(bf16[1088,128]{1,0:T(8,128)(2,1)S(1)} %get-tuple-element.356), channel_id=1, source_target_pairs={{0,1},{1,0},{2,3},{3,2},{4,5},{5,4},{6,7},{7,6},{8,9},{9,8},{10,11... | collective-permute-start | bytes 835592 | tf_op jit(solution)/shard_map/ppermute | solution.py:1017
  228.8 33.1 %collective-permute-start.44 = (bf16[1088,128]{1,0:T(8,128)(2,1)S(1)}, bf16[1088,128]{1,0:T(8,128)(2,1)S(1)}, u32[]{:S(2)}, u32[]{:S(2)}) collective-permute-start(bf16[1088,128]{1,0:T(8,128)(2,1)S(1)} %get-tuple-element.355), channel_id=1, source_target_pairs={{0,2},{1,3},{2,0},{3,1},{4,6},{5,7},{6,4},{7,5},{8,10},{9,11},{10,... | collective-permute-start | bytes 835592 | tf_op jit(solution)/shard_map/ppermute | solution.py:1017
  230.4 31.6 %collective-permute-start.45 = (bf16[1088,128]{1,0:T(8,128)(2,1)S(1)}, bf16[1088,128]{1,0:T(8,128)(2,1)S(1)}, u32[]{:S(2)}, u32[]{:S(2)}) collective-permute-start(bf16[1088,128]{1,0:T(8,128)(2,1)S(1)} %get-tuple-element.354), channel_id=1, source_target_pairs={{0,3},{1,2},{2,1},{3,0},{4,7},{5,6},{6,5},{7,4},{8,11},{9,10},{10,... | collective-permute-start | bytes 835592 | tf_op jit(solution)/shard_map/ppermute | solution.py:1017
  244.0 26.2 %collective-permute-start.46 = (bf16[2048,128]{1,0:T(8,128)(2,1)S(1)}, bf16[2048,128]{1,0:T(8,128)(2,1)S(1)}, u32[]{:S(2)}, u32[]{:S(2)}) collective-permute-start(bf16[2048,128]{1,0:T(8,128)(2,1)S(1)} %get-tuple-element.293), channel_id=1, source_target_pairs={{4,0},{8,4},{12,8},{5,1},{9,5},{13,9},{6,2},{10,6},{14,10},{7,3},{... | collective-permute-start | bytes 1572872 | tf_op jit(solution)/shard_map/ppermute | solution.py:35
  253.9 29.2 %collective-permute-start.50 = (bf16[8,2304]{1,0:T(8,128)(2,1)S(1)}, bf16[8,2304]{1,0:T(8,128)(2,1)S(1)}, u32[]{:S(2)}, u32[]{:S(2)}) collective-permute-start(bf16[8,2304]{1,0:T(8,128)(2,1)S(1)} %get-tuple-element.302), channel_id=1, source_target_pairs={{4,0},{8,4},{12,8},{5,1},{9,5},{13,9},{6,2},{10,6},{14,10},{7,3},{... | collective-permute-start | bytes 110600 | tf_op jit(solution)/shard_map/ppermute | solution.py:35
  262.1 16.4 %collective-permute-start.47 = (bf16[272,128]{1,0:T(8,128)(2,1)S(1)}, bf16[272,128]{1,0:T(8,128)(2,1)S(1)}, u32[]{:S(2)}, u32[]{:S(2)}) collective-permute-start(bf16[272,128]{1,0:T(8,128)(2,1)S(1)} %get-tuple-element.368), channel_id=1, source_target_pairs={{0,4},{4,0},{8,12},{12,8},{1,5},{5,1},{9,13},{13,9},{2,6},{6,2},{1... | collective-permute-start | bytes 208904 | tf_op jit(solution)/shard_map/ppermute | solution.py:1017
  266.7 11.8 %collective-permute-start.48 = (bf16[272,128]{1,0:T(8,128)(2,1)S(1)}, bf16[272,128]{1,0:T(8,128)(2,1)S(1)}, u32[]{:S(2)}, u32[]{:S(2)}) collective-permute-start(bf16[272,128]{1,0:T(8,128)(2,1)S(1)} %get-tuple-element.367), channel_id=1, source_target_pairs={{0,8},{4,12},{8,0},{12,4},{1,9},{5,13},{9,1},{13,5},{2,10},{6,14},... | collective-permute-start | bytes 208904 | tf_op jit(solution)/shard_map/ppermute | solution.py:1017
  270.2 8.3 %collective-permute-start.49 = (bf16[272,128]{1,0:T(8,128)(2,1)S(1)}, bf16[272,128]{1,0:T(8,128)(2,1)S(1)}, u32[]{:S(2)}, u32[]{:S(2)}) collective-permute-start(bf16[272,128]{1,0:T(8,128)(2,1)S(1)} %get-tuple-element.366), channel_id=1, source_target_pairs={{0,12},{4,8},{8,4},{12,0},{1,13},{5,9},{9,5},{13,1},{2,14},{6,10},... | collective-permute-start | bytes 208904 | tf_op jit(solution)/shard_map/ppermute | solution.py:1017
  278.6 8.9 %collective-permute-start.51 = (bf16[272,128]{1,0:T(8,128)(2,1)S(1)}, bf16[272,128]{1,0:T(8,128)(2,1)S(1)}, u32[]{:S(2)}, u32[]{:S(2)}) collective-permute-start(bf16[272,128]{1,0:T(8,128)(2,1)S(1)} %get-tuple-element.335), channel_id=1, source_target_pairs={{0,4},{4,0},{8,12},{12,8},{1,5},{5,1},{9,13},{13,9},{2,6},{6,2},{1... | collective-permute-start | bytes 208904 | tf_op jit(solution)/shard_map/ppermute | solution.py:1017
  289.2 8.7 %collective-permute-start.55 = (bf16[1088,128]{1,0:T(8,128)(2,1)S(1)}, bf16[1088,128]{1,0:T(8,128)(2,1)S(1)}, u32[]{:S(2)}, u32[]{:S(2)}) collective-permute-start(bf16[1088,128]{1,0:T(8,128)(2,1)S(1)} %bitcast.120), channel_id=1, source_target_pairs={{0,1},{1,0},{2,3},{3,2},{4,5},{5,4},{6,7},{7,6},{8,9},{9,8},{10,11... | collective-permute-start | bytes 835592 | tf_op jit(solution)/shard_map/ppermute | solution.py:1017
  289.8 11.3 %collective-permute-start.56 = (bf16[1088,128]{1,0:T(8,128)(2,1)S(1)}, bf16[1088,128]{1,0:T(8,128)(2,1)S(1)}, u32[]{:S(2)}, u32[]{:S(2)}) collective-permute-start(bf16[1088,128]{1,0:T(8,128)(2,1)S(1)} %bitcast.121), channel_id=1, source_target_pairs={{0,2},{1,3},{2,0},{3,1},{4,6},{5,7},{6,4},{7,5},{8,10},{9,11},{10,... | collective-permute-start | bytes 835592 | tf_op jit(solution)/shard_map/ppermute | solution.py:1017
  291.4 9.8 %collective-permute-start.57 = (bf16[1088,128]{1,0:T(8,128)(2,1)S(1)}, bf16[1088,128]{1,0:T(8,128)(2,1)S(1)}, u32[]{:S(2)}, u32[]{:S(2)}) collective-permute-start(bf16[1088,128]{1,0:T(8,128)(2,1)S(1)} %bitcast.122), channel_id=1, source_target_pairs={{0,3},{1,2},{2,1},{3,0},{4,7},{5,6},{6,5},{7,4},{8,11},{9,10},{10,... | collective-permute-start | bytes 835592 | tf_op jit(solution)/shard_map/ppermute | solution.py:1017
  303.3 9.9 %collective-permute-start.61 = (bf16[1088,128]{1,0:T(8,128)(2,1)S(1)}, bf16[1088,128]{1,0:T(8,128)(2,1)S(1)}, u32[]{:S(2)}, u32[]{:S(2)}) collective-permute-start(bf16[1088,128]{1,0:T(8,128)(2,1)S(1)} %get-tuple-element.351), channel_id=1, source_target_pairs={{0,2},{1,3},{2,0},{3,1},{4,6},{5,7},{6,4},{7,5},{8,10},{9,11},{10,... | collective-permute-start | bytes 835592 | tf_op jit(solution)/shard_map/ppermute | solution.py:1017
  303.8 9.3 %collective-permute-start.62 = (bf16[1088,128]{1,0:T(8,128)(2,1)S(1)}, bf16[1088,128]{1,0:T(8,128)(2,1)S(1)}, u32[]{:S(2)}, u32[]{:S(2)}) collective-permute-start(bf16[1088,128]{1,0:T(8,128)(2,1)S(1)} %get-tuple-element.350), channel_id=1, source_target_pairs={{0,3},{1,2},{2,1},{3,0},{4,7},{5,6},{6,5},{7,4},{8,11},{9,10},{10,... | collective-permute-start | bytes 835592 | tf_op jit(solution)/shard_map/ppermute | solution.py:1017
  317.9 17.8 %collective-permute-start.58 = (bf16[512,1024]{1,0:T(8,128)(2,1)S(1)}, bf16[512,1024]{1,0:T(8,128)(2,1)S(1)}, u32[]{:S(2)}, u32[]{:S(2)}) collective-permute-start(bf16[512,1024]{1,0:T(8,128)(2,1)S(1)} %broadcast_select_fusion.7), channel_id=1, source_target_pairs={{0,16},{16,0},{1,17},{17,1},{2,18},{18,2},{3,19},{19,3},{4,20},{20... | collective-permute-start | bytes 3145736 | tf_op jit(solution)/shard_map/ppermute | solution.py:1012
  330.1 15.9 %collective-permute-start.59 = (bf16[4352,128]{1,0:T(8,128)(2,1)S(1)}, bf16[4352,128]{1,0:T(8,128)(2,1)S(1)}, u32[]{:S(2)}, u32[]{:S(2)}) collective-permute-start(bf16[4352,128]{1,0:T(8,128)(2,1)S(1)} %bitcast.108), channel_id=1, source_target_pairs={{0,16},{16,0},{1,17},{17,1},{2,18},{18,2},{3,19},{19,3},{4,20},{20... | collective-permute-start | bytes 3342344 | tf_op jit(solution)/shard_map/ppermute | solution.py:1012
  332.0 9.7 %collective-permute-start.69 = (bf16[1088,128]{1,0:T(8,128)(2,1)S(1)}, bf16[1088,128]{1,0:T(8,128)(2,1)S(1)}, u32[]{:S(2)}, u32[]{:S(2)}) collective-permute-start(bf16[1088,128]{1,0:T(8,128)(2,1)S(1)} %bitcast.116), channel_id=1, source_target_pairs={{0,1},{1,0},{2,3},{3,2},{4,5},{5,4},{6,7},{7,6},{8,9},{9,8},{10,11... | collective-permute-start | bytes 835592 | tf_op jit(solution)/shard_map/ppermute | solution.py:1017
  333.0 12.8 %collective-permute-start.70 = (bf16[1088,128]{1,0:T(8,128)(2,1)S(1)}, bf16[1088,128]{1,0:T(8,128)(2,1)S(1)}, u32[]{:S(2)}, u32[]{:S(2)}) collective-permute-start(bf16[1088,128]{1,0:T(8,128)(2,1)S(1)} %bitcast.117), channel_id=1, source_target_pairs={{0,2},{1,3},{2,0},{3,1},{4,6},{5,7},{6,4},{7,5},{8,10},{9,11},{10,... | collective-permute-start | bytes 835592 | tf_op jit(solution)/shard_map/ppermute | solution.py:1017
  334.1 11.8 %collective-permute-start.71 = (bf16[1088,128]{1,0:T(8,128)(2,1)S(1)}, bf16[1088,128]{1,0:T(8,128)(2,1)S(1)}, u32[]{:S(2)}, u32[]{:S(2)}) collective-permute-start(bf16[1088,128]{1,0:T(8,128)(2,1)S(1)} %bitcast.118), channel_id=1, source_target_pairs={{0,3},{1,2},{2,1},{3,0},{4,7},{5,6},{6,5},{7,4},{8,11},{9,10},{10,... | collective-permute-start | bytes 835592 | tf_op jit(solution)/shard_map/ppermute | solution.py:1017
  (144 other events, 1067.6 us)

commit v4 on v3

--- a/solution.py
+++ b/solution.py
@@ -318,7 +318,7 @@
         out_ref[:, here] = (input_ref[:, here].astype(F32) + dot(left, right)).astype(BF16)
 
 
-def gate_in_back_kernel(count, grad_ref, up_ref, where_ref, *rest):
+def gate_in_back_kernel(count, grad_ref, where_ref, *rest):
     parts, out_ref = rest[:count], rest[count]
     grad = grad_ref[...]
     half = grad.shape[1] // 2
@@ -327,14 +327,11 @@
     for place in range(4):
         product = dot(grad[:, :half], lower[place]) + dot(grad[:, half:], upper[place])
         out_ref[:, place * columns : (place + 1) * columns] = product
-    out_ref[:, 4 * columns :] = dot(grad, up_ref[...])
-
-
-def narrow_back_kernel(main, extra, grad_ref, raw_ref, part_ref, lane_ref, up_ref, narrow_ref):
-    before = up_ref.shape[0] - main - extra
-    total = part_ref[...] + dot(grad_ref[...], up_ref[before : before + main])
-    total = total + dot(raw_ref[...][:, :extra], up_ref[before + main :])
-    narrow_ref[...] = (total * lane_ref[...]).astype(BF16)
+
+
+def narrow_back_kernel(extra, grad_gate_ref, grad_ref, raw_ref, lane_ref, up_ref, narrow_ref):
+    left = jnp.concatenate([grad_gate_ref[...], grad_ref[...], raw_ref[...][:, :extra]], axis=1)
+    narrow_ref[...] = (dot(left, up_ref[...]) * lane_ref[...]).astype(BF16)
 
 
 def mixed_in_back_kernel(
@@ -674,31 +671,29 @@
 
 def gate_in_backward(sizes, grad_gate, level):
     s = sizes
-    width = 4 * s.columns + LANES
+    width = 4 * s.columns
     return pl.pallas_call(
         functools.partial(gate_in_back_kernel, len(level.gate)),
         grid=(1,),
-        in_specs=whole_specs(grad_gate) + gate_specs(s, level),
+        in_specs=whole_specs(grad_gate) + gate_specs(s, level)[1:],
         out_specs=whole((s.rows, width)),
         out_shape=shape_of((s.rows, width), F32),
         compiler_params=PARAMS,
         cost_estimate=cost(3.5),
-    )(grad_gate, level.in_up, level.where, *level.gate)
-
-
-def narrow_backward(sizes, grad_mixed, raw, part, level, lane_mask):
-    s = sizes
-    args = [grad_mixed, raw, part, lane_mask, level.in_up]
-    in_specs = whole_specs(*args)
-    in_specs[2] = spec((s.rows, LANES), lambda _: (0, part.shape[1] // LANES - 1))
+    )(grad_gate, level.where, *level.gate)
+
+
+def narrow_backward(sizes, grad_gate, grad_mixed, raw, level, lane_mask):
+    s = sizes
+    args = [grad_gate, grad_mixed, raw, lane_mask, level.in_up]
     return pl.pallas_call(
-        functools.partial(narrow_back_kernel, s.mixed, s.heads),
+        functools.partial(narrow_back_kernel, s.heads),
         grid=(1,),
-        in_specs=in_specs,
+        in_specs=whole_specs(*args),
         out_specs=whole((s.rows, LANES)),
         out_shape=shape_of((s.rows, LANES)),
         compiler_params=PARAMS,
-        cost_estimate=cost(0.9),
+        cost_estimate=cost(1.3),
     )(*args)
 
 
@@ -710,7 +705,7 @@
         functools.partial(mixed_in_back_kernel, s.mixed, s.heads, s.norm_gain, len(level.mixed)),
         grid=(s.spans,),
         in_specs=[
-            rows(s.mixed), rows(LANES), rows(width + LANES), rows(width), rows(width), whole(level.vector.shape),
+            rows(s.mixed), rows(LANES), rows(width), rows(width), rows(width), whole(level.vector.shape),
             rows(LANES), *whole_specs(level.in_down), SMALL, *whole_specs(*level.mixed),
         ],
         out_specs=rows(width),
@@ -986,26 +981,23 @@
     grad_values, grad_maps, raw = outputs[:3]
     grad_values = yield grad_values, grad_values
     grad_mixed = conv_backward(s, grad_values, grad_maps, conv, later, level, tokens)
-    part = gate_in_backward(s, grad_gate, level)
     grad_mixed = yield grad_mixed, grad_mixed
-    narrow = narrow_backward(s, grad_mixed, raw, part, level, lane_mask)
+    narrow = narrow_backward(s, grad_gate, grad_mixed, raw, level, lane_mask)
     buffer = late_grads(s, kept, narrow, grad_mixed, raw, early_rows, buffer, all_rows)
     grad_mixed = yield buffer, grad_mixed
+    part = gate_in_backward(s, tie(grad_gate, grad_mixed), level)
     return mixed_in_backward(s, grad_mixed, raw, part, kept.inputs, upstream, narrow, level)
 
 
 def make_level(sizes, vector, numbers, adapters, where):
     s = sizes
-    in_down, in_up, out_down, out_up = adapters
+    in_down, in_up = adapters
     dt_bias, a_log, skip_gain = numbers
     rate = -jnp.exp(a_log)[:, None]
     lane = jnp.arange(LANES)[None, :]
     table = jnp.where(lane == 1, skip_gain[:, None], jnp.where(lane == 2, dt_bias[:, None], rate))
     table = jnp.where(lane == 0, rate * LOG2E, table)
-    return Bag(
-        vector=vector, heads=table, in_down=in_down, in_up=in_up, out_down=out_down,
-        out_up=out_up, where=where, mixed_where=where,
-    )
+    return Bag(vector=vector, heads=table, in_down=in_down, in_up=in_up, where=where, mixed_where=where)
 
 
 def swap(value):
@@ -1126,23 +1118,24 @@
     weights.start(0)
     weights.start(1, weights.forward(0))
     weights.finish(0)
-    rest = (layer_input, out_grad, doc_index, doc_adapter, norm_gain, conv_weight, conv_bias, dt_bias, a_log, skip_gain)
+    rest = (layer_input, doc_index, doc_adapter, norm_gain, conv_weight, conv_bias, dt_bias, a_log, skip_gain)
     rest, gate_gain, adapters = tie((rest, gate_gain, adapters), weights.later)
-    layer_input, out_grad, doc_index, doc_adapter, norm_gain, conv_weight, conv_bias, dt_bias, a_log, skip_gain = rest
-    inputs, grads, doc_ids, table = pick(layer_input), pick(out_grad), pick(doc_index), pick(doc_adapter)[0]
+    layer_input, doc_index, doc_adapter, norm_gain, conv_weight, conv_bias, dt_bias, a_log, skip_gain = rest
+    inputs, doc_ids, table = pick(layer_input), pick(doc_index), pick(doc_adapter)[0]
     tokens, lane_mask = token_tables(doc_ids[None, :], table)
     vectors = both_layers(jnp.concatenate([conv_weight[0].reshape(1, -1), conv_bias, gate_gain, norm_gain], axis=1))
     numbers = both_layers(jnp.concatenate([dt_bias, a_log, skip_gain], axis=0))
     in_down, in_up, out_down, out_up = adapters
-    both = [both_layers(array) for array in (in_down[0], in_up[0].T, out_down[0], out_up[0])]
+    both = [both_layers(array) for array in (in_down[0], in_up[0].T)]
+    out_adapters = [(array[0], swap(array[0])) for array in (out_down, out_up)]
     where = jnp.stack([place, place ^ (1 + section), place ^ (2 - section), place ^ 3, section]).astype(jnp.int32)
     levels = [
         make_level(sizes, vectors[layer], numbers[layer], [pair[layer] for pair in both], where)
         for layer in range(2)
     ]
-    small = [inputs, grads, lane_mask, tokens.__dict__, weights.own[1:]] + [level.__dict__ for level in levels]
+    small = [inputs, lane_mask, tokens.__dict__, weights.own[1:]] + [level.__dict__ for level in levels]
     small, weights.parts[0] = lax.optimization_barrier((small, weights.parts[0]))
-    inputs, grads, lane_mask, token_fields, weights.own[1:], *level_fields = small
+    inputs, lane_mask, token_fields, weights.own[1:], *level_fields = small
     tokens, levels = Bag(**token_fields), [Bag(**fields) for fields in level_fields]
     levels[0].mixed = weights.parts[0]
     levels[0].gate_first = levels[1].gate_first = False
@@ -1158,6 +1151,15 @@
                 token = next(stages)
             except StopIteration as end:
                 rows_now, stored = end.value
+            if (layer, stage) == (0, 0):
+                chosen = [
+                    [jnp.where(section == choice, tie(here, token), there) for choice in range(2)]
+                    for here, there in out_adapters
+                ]
+                for choice in range(2):
+                    levels[choice].out_down, levels[choice].out_up = chosen[0][choice], chosen[1][choice]
+            if (layer, stage) == (1, 0):
+                grads = pick(tie(out_grad, token))
             move = ends.get((layer, stage))
             if move is not None:
                 weights.finish(move, token)

time: 356 us -> 352 us (0.989)
  local copies, waits for them, and re-layouts: 27.7 us -> 19 us
  waiting for transfers between devices: 49.1 us -> 56.4 us
    ppermute x12, waiting for transfers between devices: 17.2 us -> 25.1 us  [across(): return lax.ppermute(value, (SECTION, WSHARD), pairs)]
    unnamed x242 -> x244, local copies, waits for them, and re-layouts: 16.1 us -> 10.7 us
  transfers between devices with their start and end apart: 73 -> 73, of which waited for: 19 -> 19; matrix products, arithmetic and copies ran while one was open for 7% -> 6% of each run, Pallas kernels for 41% -> 40%
where the time goes in v4:
time: 352 us; the launch traced here: 347 us
  Pallas kernels  158 us (45%)
  starting transfers between devices  93.6 us (27%)
  waiting for transfers between devices  56.4 us (16%)
  local copies, waits for them, and re-layouts  19 us (5%)
  other arithmetic  17 us (5%)
    ppermute x10, starting transfers between devices, from_behind(): lax.ppermute(value, axis, [(source, source + steps) for source in range(i...  37.6 us
    ppermute x24, starting transfers between devices, exchange(): lax.ppermute(value, axis, [(place, place ^ distance) for place in range(c...  33.9 us
    pallas_call x4, Pallas kernels, scan_backward(): pl.pallas_call(functools.partial(scan_back_kernel, s.head, s.heads, s.sta...  33.3 us
    ppermute x12, waiting for transfers between devices, across(): return lax.ppermute(value, (SECTION, WSHARD), pairs)  25.1 us
    ppermute x24, waiting for transfers between devices, exchange(): lax.ppermute(value, axis, [(place, place ^ distance) for place in range(c...  23.6 us
    pallas_call x2, Pallas kernels, out_backward(): pl.pallas_call(functools.partial(out_back_kernel, s.head, s.heads, s.stat...  22.5 us
    pallas_call x4, Pallas kernels, scan_forward(): pl.pallas_call(functools.partial(scan_kernel, s.head, s.state, s.gate_gai...  18.4 us
    ppermute x12, starting transfers between devices, across(): return lax.ppermute(value, (SECTION, WSHARD), pairs)  17.5 us
  transfers between devices with their start and end apart: 73, of which 19 were waited for; matrix products, arithmetic and copies ran while one was open for 6% of the time, Pallas kernels for 40%

profile of v4, /device:TPU:0, one launch (start us, length us, event | category | flops | bytes accessed | tf_op | source)
XLA Modules:
  0.0 346.6 jit_solution(104312869002209286)
XLA Ops:
  5.3 2.9 broadcast_select_fusion
  9.2 2.7 collective-permute-start.9
  12.9 4.2 %collective-permute-start.2 = (s32[1,128]{1,0:T(1,128)S(1)}, s32[1,128]{1,0:T(1,128)S(1)}, u32[]{:S(2)}, u32[]{:S(2)}) collective-permute-start(s32[1,128]{1,0:T(1,128)S(1)} %get-tuple-element.371), channel_id=1, source_target_pairs={{0,4},{4,8},{8,12},{1,5},{5,9},{9,13},{2,6},{6,10},{10,14},{3,7},{... | collective-permute-start | bytes 1544 | tf_op jit(solution)/shard_map/ppermute | solution.py:35
  17.0 2.7 broadcast_select_fusion.5
  29.8 7.8 %collective-permute-done.11.rest_3_ = bf16[1184,256]{1,0:T(8,128)(2,1)S(1)} collective-permute-done((bf16[1184,256]{1,0:T(8,128)(2,1)S(1)}, bf16[1184,256]{1,0:T(8,128)(2,1)S(1)}, u32[]{:S(2)}, u32[]{:S(2)}) %collective-permute-start.11) | collective-permute-done | bytes 606240 | tf_op jit(solution)/shard_map/ppermute | solution.py:1027
  40.4 5.6 %shard_map.209 = (bf16[512,1152]{1,0:T(8,128)(2,1)S(1)}, bf16[512,2304]{1,0:T(8,128)(2,1)S(1)}, bf16[512,128]{1,0:T(8,128)(2,1)S(1)}, bf16[8,2304]{1,0:T(8,128)(2,1)S(1)}) custom-call(bf16[512,1024]{1,0:T(8,128)(2,1)S(1)} %dynamic-slice_bitcast_fusion.1.input_ref, f32[1,14592]{1,0:T(1,128)S(1)} %get-tuple-element.188.vector_ref, ...), custom_call_target="tpu_custom_call" | custom-call | flops 20700000256 | bytes 65536 | tf_op jit(solution)/shard_map/pallas_call | solution.py:601
  46.9 4.5 %collective-permute-start.13 = (bf16[8,2304]{1,0:T(8,128)(2,1)S(1)}, bf16[8,2304]{1,0:T(8,128)(2,1)S(1)}, u32[]{:S(2)}, u32[]{:S(2)}) collective-permute-start(bf16[8,2304]{1,0:T(8,128)(2,1)S(1)} %get-tuple-element.199), channel_id=1, source_target_pairs={{0,4},{4,8},{8,12},{1,5},{5,9},{9,13},{2,6},{6,10},{10,14},{3,7},{... | collective-permute-start | bytes 110600 | tf_op jit(solution)/shard_map/ppermute | solution.py:35
  54.1 8.0 %shard_map.210 = (bf16[2048,512]{1,0:T(8,128)(2,1)S(1)}, bf16[512,2048]{1,0:T(8,128)(2,1)}, bf16[512,512]{1,0:T(8,128)(2,1)S(1)}, f32[96,512]{1,0:T(8,128)S(1)},...) custom-call(bf16[512,2304]{1,0:T(8,128)(2,1)S(1)} %get-tuple-element.198.mixed_ref.mixed_bc_ref, ...), custom_call_target="tpu_custom_call" | custom-call | flops 29325000704 | bytes 65536 | tf_op jit(solution)/shard_map/pallas_call | solution.py:513
  62.1 5.3 %collective-permute-done.17.rest_3_ = bf16[1024,256]{1,0:T(8,128)(2,1)S(1)} collective-permute-done((bf16[1024,256]{1,0:T(8,128)(2,1)S(1)}, bf16[1024,256]{1,0:T(8,128)(2,1)S(1)}, u32[]{:S(2)}, u32[]{:S(2)}) %collective-permute-start.17) | collective-permute-done | bytes 524320 | tf_op jit(solution)/shard_map/ppermute | solution.py:1027
  69.9 4.8 %collective-permute-start.14 = (bf16[2048,128]{1,0:T(8,128)(2,1)S(1)}, bf16[2048,128]{1,0:T(8,128)(2,1)S(1)}, u32[]{:S(2)}, u32[]{:S(2)}) collective-permute-start(bf16[2048,128]{1,0:T(8,128)(2,1)S(1)} %get-tuple-element.209), channel_id=1, source_target_pairs={{0,4},{4,8},{8,12},{1,5},{5,9},{9,13},{2,6},{6,10},{10,14},{3,7},{... | collective-permute-start | bytes 1572872 | tf_op jit(solution)/shard_map/ppermute | solution.py:35
  76.5 3.5 %shard_map.211.gate_ref = bf16[512,2048]{1,0:T(8,128)(2,1)S(1)} custom-call(bf16[512,1152]{1,0:T(8,128)(2,1)S(1)} %get-tuple-element.210.normed_ref.refs_5_.refs_0_.refs_4_, bf16[4384,128]{1,0:T(8,128)(2,1)S(1)} %get-tuple-element.191.up_ref, s32[5]{0:T(128)S(1)} %copy-done.40, bf16[2048,256]{1,0:T(8,128)(2,1)S(1)} %get-tuple-element.213.rest_0_, ...), custom_call_target="tpu_custom_call" | custom-call | flops 12419999744 | bytes 65536 | tf_op jit(solution)/shard_map/pallas_call | solution.py:618
  80.1 4.6 %shard_map.212 = (bf16[512,2048]{1,0:T(8,128)(2,1)S(1)}, bf16[512,2048]{1,0:T(8,128)(2,1)S(1)}) custom-call(bf16[2048,512]{1,0:T(8,128)(2,1)S(1)} %get-tuple-element.204.values_ref, bf16[512,512]{1,0:T(8,128)(2,1)S(1)} %get-tuple-element.205.bc_ref.slope_bc_ref, f32[96,512]{1,0:T(8,128)S(1)} %get-tuple-element.206.step_ref.decay_ref.sig_ref, ...), custom_call_target="tpu_custom_call" | custom-call | flops 22424999936 | bytes 65536 | tf_op jit(solution)/shard_map/pallas_call | solution.py:568
  85.5 5.1 %collective-permute-done.25.rest_1_ = bf16[2336,256]{1,0:T(8,128)(2,1)} collective-permute-done((bf16[2336,256]{1,0:T(8,128)(2,1)S(1)}, bf16[2336,256]{1,0:T(8,128)(2,1)}, u32[]{:S(2)}, u32[]{:S(2)}) %collective-permute-start.25) | collective-permute-done | bytes 1196064 | tf_op jit(solution)/shard_map/ppermute | solution.py:1027
  94.8 4.6 %shard_map.213 = (bf16[512,2048]{1,0:T(8,128)(2,1)S(1)}, bf16[512,2048]{1,0:T(8,128)(2,1)S(1)}) custom-call(bf16[2048,512]{1,0:T(8,128)(2,1)S(1)} %get-tuple-element.204.values_ref, bf16[512,512]{1,0:T(8,128)(2,1)S(1)} %get-tuple-element.205.bc_ref.slope_bc_ref, ...), custom_call_target="tpu_custom_call", output_to_operand_aliasing={{0}: (11, {}), {1}: (12, {})} | custom-call | flops 22424999936 | bytes 65536 | tf_op jit(solution)/shard_map/pallas_call | solution.py:568
  100.3 3.7 %shard_map.214 = (bf16[512,128]{1,0:T(8,128)(2,1)S(1)}, bf16[512,1024]{1,0:T(8,128)(2,1)S(1)}) custom-call(bf16[512,2048]{1,0:T(8,128)(2,1)S(1)} %get-tuple-element.219.normed_ref.refs_2_, bf16[512,1024]{1,0:T(8,128)(2,1)S(1)} %dynamic-slice_bitcast_fusion.1.input_ref, bf16[2048,128]{1,0:T(8,128)(2,1)S(1)} %get-tuple-element.356.down_ref.down_out_ref, ...), custom_call_target="tpu_custom_call" | custom-call | flops 13799999488 | bytes 65536 | tf_op jit(solution)/shard_map/pallas_call | solution.py:633
  104.7 5.2 %collective-permute-done.27.rest_3_ = bf16[1184,256]{1,0:T(8,128)(2,1)} collective-permute-done((bf16[1184,256]{1,0:T(8,128)(2,1)S(1)}, bf16[1184,256]{1,0:T(8,128)(2,1)}, u32[]{:S(2)}, u32[]{:S(2)}) %collective-permute-start.27) | collective-permute-done | bytes 606240 | tf_op jit(solution)/shard_map/ppermute | solution.py:1027
  119.7 7.2 %shard_map.215 = (bf16[512,1152]{1,0:T(8,128)(2,1)S(1)}, bf16[512,2304]{1,0:T(8,128)(2,1)S(1)}, bf16[512,128]{1,0:T(8,128)(2,1)S(1)}, bf16[8,2304]{1,0:T(8,128)(2,1)S(1)}) custom-call(bf16[512,1024]{1,0:T(8,128)(2,1)S(1)} %get-tuple-element.228.input_ref, f32[1,14592]{1,0:T(1,128)S(1)} %copy-done.33, bf16[1024,128]{1,0:T(8,128)(2,1)S(1)} %get-tuple-element.230.down_ref, ...), custom_call_target="tpu_custom_call" | custom-call | flops 20700000256 | bytes 65536 | tf_op jit(solution)/shard_map/pallas_call | solution.py:601
  127.0 4.7 %collective-permute-start.29 = (bf16[8,2304]{1,0:T(8,128)(2,1)S(1)}, bf16[8,2304]{1,0:T(8,128)(2,1)S(1)}, u32[]{:S(2)}, u32[]{:S(2)}) collective-permute-start(bf16[8,2304]{1,0:T(8,128)(2,1)S(1)} %get-tuple-element.238), channel_id=1, source_target_pairs={{0,4},{4,8},{8,12},{1,5},{5,9},{9,13},{2,6},{6,10},{10,14},{3,7},{... | collective-permute-start | bytes 110600 | tf_op jit(solution)/shard_map/ppermute | solution.py:35
  133.3 8.1 %shard_map.216 = (bf16[2048,512]{1,0:T(8,128)(2,1)S(1)}, bf16[512,2048]{1,0:T(8,128)(2,1)}, bf16[512,512]{1,0:T(8,128)(2,1)S(1)}, f32[96,512]{1,0:T(8,128)S(1)},...) custom-call(bf16[512,2304]{1,0:T(8,128)(2,1)S(1)} %get-tuple-element.237.mixed_ref.mixed_bc_ref, ...), custom_call_target="tpu_custom_call" | custom-call | flops 29325000704 | bytes 65536 | tf_op jit(solution)/shard_map/pallas_call | solution.py:513
  141.3 12.8 %collective-permute-start.30 = (bf16[2048,128]{1,0:T(8,128)(2,1)S(1)}, bf16[2048,128]{1,0:T(8,128)(2,1)S(1)}, u32[]{:S(2)}, u32[]{:S(2)}) collective-permute-start(bf16[2048,128]{1,0:T(8,128)(2,1)S(1)} %get-tuple-element.244), channel_id=1, source_target_pairs={{0,4},{4,8},{8,12},{1,5},{5,9},{9,13},{2,6},{6,10},{10,14},{3,7},{... | collective-permute-start | bytes 1572872 | tf_op jit(solution)/shard_map/ppermute | solution.py:35
  155.1 5.0 %shard_map.217.gate_ref = bf16[512,2048]{1,0:T(8,128)(2,1)S(1)} custom-call(bf16[512,1152]{1,0:T(8,128)(2,1)S(1)} %get-tuple-element.245.normed_ref.refs_5_.refs_0_.refs_4_, bf16[4384,128]{1,0:T(8,128)(2,1)S(1)} %copy-done.8, s32[5]{0:T(128)S(1)} %copy-done.42, bf16[2048,256]{1,0:T(8,128)(2,1)} %get-tuple-element.248.rest_0_, ...), custom_call_target="tpu_custom_call" | custom-call | flops 12419999744 | bytes 65536 | tf_op jit(solution)/shard_map/pallas_call | solution.py:618
  160.2 4.6 %shard_map.218 = (bf16[512,2048]{1,0:T(8,128)(2,1)S(1)}, bf16[512,2048]{1,0:T(8,128)(2,1)S(1)}) custom-call(bf16[2048,512]{1,0:T(8,128)(2,1)S(1)} %get-tuple-element.241.values_ref, bf16[512,512]{1,0:T(8,128)(2,1)S(1)} %get-tuple-element.242.bc_ref.slope_bc_ref, f32[96,512]{1,0:T(8,128)S(1)} %get-tuple-element.243.step_ref.decay_ref.sig_ref, ...), custom_call_target="tpu_custom_call" | custom-call | flops 22424999936 | bytes 65536 | tf_op jit(solution)/shard_map/pallas_call | solution.py:568
  166.0 4.6 %shard_map.219 = (bf16[512,2048]{1,0:T(8,128)(2,1)S(1)}, bf16[512,2048]{1,0:T(8,128)(2,1)S(1)}) custom-call(bf16[2048,512]{1,0:T(8,128)(2,1)S(1)} %get-tuple-element.241.values_ref, bf16[512,512]{1,0:T(8,128)(2,1)S(1)} %get-tuple-element.242.bc_ref.slope_bc_ref, ...), custom_call_target="tpu_custom_call", output_to_operand_aliasing={{0}: (11, {}), {1}: (12, {})} | custom-call | flops 22424999936 | bytes 65536 | tf_op jit(solution)/shard_map/pallas_call | solution.py:568
  170.6 3.7 %shard_map.220 = (bf16[512,128]{1,0:T(8,128)(2,1)S(1)}, bf16[512,1024]{1,0:T(8,128)(2,1)S(1)}) custom-call(bf16[512,2048]{1,0:T(8,128)(2,1)S(1)} %get-tuple-element.254.normed_ref.refs_2_, bf16[512,1024]{1,0:T(8,128)(2,1)S(1)} %get-tuple-element.228.input_ref, bf16[2048,128]{1,0:T(8,128)(2,1)S(1)} %copy-done.19, f32[512,128]{1,0:T(8,128)S(1)} %copy-done.71, ...), custom_call_target="tpu_custom_call" | custom-call | flops 13799999488 | bytes 65536 | tf_op jit(solution)/shard_map/pallas_call | solution.py:633
  174.3 11.1 %shard_map.221 = (bf16[512,2048]{1,0:T(8,128)(2,1)S(1)}, bf16[2048,512]{1,0:T(8,128)(2,1)S(1)}, bf16[512,128]{1,0:T(8,128)(2,1)S(1)}, bf16[2048,128]{1,0:T(8,128)(2,1)S(1)}, bf16[2048,128]{1,0:T(8,128)(2,1)S(1)}) custom-call(bf16[512,1024]{1,0:T(8,128)(2,1)S(1)} %dynamic-slice_bitcast_fusion.up_ref.up_stream_ref.refs_0_, f32[512,128]{1,0:T(8,128)S(1)} %copy-done.71, ...), custom_call_target="tpu_custom_call" | custom-call | flops 46575001600 | bytes 65536 | tf_op jit(solution)/shard_map/pallas_call | solution.py:648
  186.7 8.3 %shard_map.222 = (bf16[512,2048]{1,0:T(8,128)(2,1)S(1)}, bf16[512,256]{1,0:T(8,128)(2,1)S(1)}, bf16[512,128]{1,0:T(8,128)(2,1)S(1)}, bf16[8,2304]{1,0:T(8,128)(2,1)S(1)}) custom-call(bf16[2048,512]{1,0:T(8,128)(2,1)S(1)} %get-tuple-element.241.values_ref, bf16[2048,512]{1,0:T(8,128)(2,1)S(1)} %get-tuple-element.263.grad_ref, ...), custom_call_target="tpu_custom_call" | custom-call | flops 29325000704 | bytes 65536 | tf_op jit(solution)/shard_map/pallas_call | solution.py:739
  198.5 3.1 collective-permute-done.40.grad_state_ref
  201.6 8.2 %shard_map.223 = (bf16[512,2048]{1,0:T(8,128)(2,1)S(1)}, bf16[512,256]{1,0:T(8,128)(2,1)S(1)}, bf16[512,128]{1,0:T(8,128)(2,1)S(1)}) custom-call(bf16[2048,512]{1,0:T(8,128)(2,1)S(1)} %get-tuple-element.241.values_ref, bf16[2048,512]{1,0:T(8,128)(2,1)S(1)} %get-tuple-element.263.grad_ref, ...), custom_call_target="tpu_custom_call", output_to_operand_aliasing={{0}: (15, {}), {1}: (16, {}), {2}: (17, {})} | custom-call | flops 29325000704 | bytes 65536 | tf_op jit(solution)/shard_map/pallas_call | solution.py:739
  209.9 4.4 %shard_map.224.grad_ref.refs_2_ = bf16[512,2304]{1,0:T(8,128)(2,1)S(1)} custom-call(bf16[512,2048]{1,0:T(8,128)(2,1)S(1)} %get-tuple-element.270.grad_ref, bf16[512,256]{1,0:T(8,128)(2,1)S(1)} %get-tuple-element.271.grad_bc_ref, bf16[512,2048]{1,0:T(8,128)(2,1)S(1)} %copy-done.92, bf16[512,512]{1,0:T(8,128)(2,1)S(1)} %get-tuple-element.242.bc_ref.slope_bc_ref, ...), custom_call_target="tpu_custom_call" | custom-call | flops 15180000256 | bytes 65536 | tf_op jit(solution)/shard_map/pallas_call | solution.py:762
  218.3 3.9 %shard_map.225.part_ref = f32[512,1024]{1,0:T(8,128)S(1)} custom-call(bf16[512,2048]{1,0:T(8,128)(2,1)S(1)} %get-tuple-element.276.grad_ref.grad_gate_ref.refs_4_, s32[5]{0:T(128)S(1)} %copy-done.42, bf16[2048,256]{1,0:T(8,128)(2,1)} %get-tuple-element.248.rest_0_, bf16[2048,256]{1,0:T(8,128)(2,1)} %collective-permute-done.31.rest_1_, ...), custom_call_target="tpu_custom_call" | custom-call | flops 12074999808 | bytes 65536 | tf_op jit(solution)/shard_map/pallas_call | solution.py:675
  222.2 5.9 %shard_map.227.up_ref.refs_0_.up_stream_ref = bf16[512,1024]{1,0:T(8,128)(2,1)S(1)} custom-call(bf16[512,2304]{1,0:T(8,128)(2,1)S(1)} %shard_map.224.grad_ref.refs_2_, bf16[512,128]{1,0:T(8,128)(2,1)S(1)} %get-tuple-element.274.raw_ref.refs_3_, f32[512,1024]{1,0:T(8,128)S(1)} %shard_map.225.part_ref, bf16[512,1024]{1,0:T(8,128)(2,1)S(1)} %get-tuple-element.228.input_ref, ...), custom_call_target="tpu_custom_call" | custom-call | flops 16215000064 | bytes 65536 | tf_op jit(solution)/shard_map/pallas_call | solution.py:704
  233.8 11.5 %shard_map.230 = (bf16[512,2048]{1,0:T(8,128)(2,1)S(1)}, bf16[2048,512]{1,0:T(8,128)(2,1)S(1)}, bf16[512,128]{1,0:T(8,128)(2,1)S(1)}, bf16[2048,128]{1,0:T(8,128)(2,1)S(1)}, bf16[2048,128]{1,0:T(8,128)(2,1)S(1)}) custom-call(bf16[512,1024]{1,0:T(8,128)(2,1)S(1)} %shard_map.227.up_ref.refs_0_.up_stream_ref, f32[512,128]{1,0:T(8,128)S(1)} %copy-done.71, ...), custom_call_target="tpu_custom_call" | custom-call | flops 46575001600 | bytes 65536 | tf_op jit(solution)/shard_map/pallas_call | solution.py:648
  246.6 8.3 %shard_map.231 = (bf16[512,2048]{1,0:T(8,128)(2,1)S(1)}, bf16[512,256]{1,0:T(8,128)(2,1)S(1)}, bf16[512,128]{1,0:T(8,128)(2,1)S(1)}, bf16[8,2304]{1,0:T(8,128)(2,1)S(1)}) custom-call(bf16[2048,512]{1,0:T(8,128)(2,1)S(1)} %copy-done.94, bf16[2048,512]{1,0:T(8,128)(2,1)S(1)} %get-tuple-element.289.grad_ref, bf16[512,512]{1,0:T(8,128)(2,1)S(1)} %copy-done.98, ...), custom_call_target="tpu_custom_call" | custom-call | flops 29325000704 | bytes 65536 | tf_op jit(solution)/shard_map/pallas_call | solution.py:739
  258.2 3.3 collective-permute-start.47
  261.6 3.0 collective-permute-start.48
  264.6 8.4 %shard_map.232 = (bf16[512,2048]{1,0:T(8,128)(2,1)S(1)}, bf16[512,256]{1,0:T(8,128)(2,1)S(1)}, bf16[512,128]{1,0:T(8,128)(2,1)S(1)}) custom-call(bf16[2048,512]{1,0:T(8,128)(2,1)S(1)} %copy-done.94, bf16[2048,512]{1,0:T(8,128)(2,1)S(1)} %get-tuple-element.289.grad_ref, ...), custom_call_target="tpu_custom_call", output_to_operand_aliasing={{0}: (15, {}), {1}: (16, {}), {2}: (17, {})} | custom-call | flops 29325000704 | bytes 65536 | tf_op jit(solution)/shard_map/pallas_call | solution.py:739
  273.8 3.8 %collective-permute-start.52 = (bf16[272,128]{1,0:T(8,128)(2,1)S(1)}, bf16[272,128]{1,0:T(8,128)(2,1)S(1)}, u32[]{:S(2)}, u32[]{:S(2)}) collective-permute-start(bf16[272,128]{1,0:T(8,128)(2,1)S(1)} %get-tuple-element.333), channel_id=1, source_target_pairs={{0,8},{4,12},{8,0},{12,4},{1,9},{5,13},{9,1},{13,5},{2,10},{6,14},... | collective-permute-start | bytes 208904 | tf_op jit(solution)/shard_map/ppermute | solution.py:1009
  277.6 4.4 %shard_map.233.grad_ref.refs_2_ = bf16[512,2304]{1,0:T(8,128)(2,1)S(1)} custom-call(bf16[512,2048]{1,0:T(8,128)(2,1)S(1)} %get-tuple-element.297.grad_ref, bf16[512,256]{1,0:T(8,128)(2,1)S(1)} %get-tuple-element.298.grad_bc_ref, bf16[512,2048]{1,0:T(8,128)(2,1)S(1)} %copy-done.91, bf16[512,512]{1,0:T(8,128)(2,1)S(1)} %copy-done.98, ...), custom_call_target="tpu_custom_call" | custom-call | flops 15180000256 | bytes 65536 | tf_op jit(solution)/shard_map/pallas_call | solution.py:762
  291.8 3.0 collective-permute-done.56
  299.0 2.9 shard_map.237.part_ref
  302.0 4.7 %shard_map.238 = bf16[512,1024]{1,0:T(8,128)(2,1)S(1)} custom-call(bf16[512,2304]{1,0:T(8,128)(2,1)S(1)} %shard_map.233.grad_ref.refs_2_, bf16[512,128]{1,0:T(8,128)(2,1)S(1)} %get-tuple-element.305.raw_ref.refs_3_, f32[512,1024]{1,0:T(8,128)S(1)} %shard_map.237.part_ref, bf16[512,1024]{1,0:T(8,128)(2,1)S(1)} %copy-done.16, ...), custom_call_target="tpu_custom_call" | custom-call | flops 16215000064 | bytes 65536 | tf_op jit(solution)/shard_map/pallas_call | solution.py:704
  308.8 2.7 collective-permute-start.64
  314.0 4.2 %collective-permute-done.65 = bf16[272,128]{1,0:T(8,128)(2,1)S(1)} collective-permute-done((bf16[272,128]{1,0:T(8,128)(2,1)S(1)}, bf16[272,128]{1,0:T(8,128)(2,1)S(1)}, u32[]{:S(2)}, u32[]{:S(2)}) %collective-permute-start.65) | collective-permute-done | bytes 69664 | tf_op jit(solution)/shard_map/ppermute | solution.py:1009
  324.3 2.5 collective-permute-done.68
  332.3 4.2 %collective-permute-done.69 = bf16[1088,128]{1,0:T(8,128)(2,1)S(1)} collective-permute-done((bf16[1088,128]{1,0:T(8,128)(2,1)S(1)}, bf16[1088,128]{1,0:T(8,128)(2,1)S(1)}, u32[]{:S(2)}, u32[]{:S(2)}) %collective-permute-start.69) | collective-permute-done | bytes 278560 | tf_op jit(solution)/shard_map/ppermute | solution.py:1009
  336.5 4.2 %collective-permute-done.70 = bf16[1088,128]{1,0:T(8,128)(2,1)S(1)} collective-permute-done((bf16[1088,128]{1,0:T(8,128)(2,1)S(1)}, bf16[1088,128]{1,0:T(8,128)(2,1)S(1)}, u32[]{:S(2)}, u32[]{:S(2)}) %collective-permute-start.70) | collective-permute-done | bytes 278560 | tf_op jit(solution)/shard_map/ppermute | solution.py:1009
  341.0 2.7 collective-permute-done.72.refs_3_
  343.7 2.7 shard_map.239
  (441 shorter events, 96.2 us)
Async XLA Ops:
  9.2 17.7 %collective-permute-start.9 = (bf16[2336,256]{1,0:T(8,128)(2,1)S(1)}, bf16[2336,256]{1,0:T(8,128)(2,1)S(1)}, u32[]{:S(2)}, u32[]{:S(2)}) collective-permute-start(bf16[2336,256]{1,0:T(8,128)(2,1)S(1)} %get-tuple-element.193.rest_0_), channel_id=1, source_target_pairs={{0,1},{1,0},{2,3},{3,2},{16,18},{17,19},{18,16},{19,17},{4,5},{5,4... | collective-permute-start | bytes 3588104 | tf_op jit(solution)/shard_map/ppermute | solution.py:1027
  12.0 10.3 %collective-permute-start.5 = (f32[3,32]{1,0:T(4,128)S(1)}, f32[3,32]{1,0:T(4,128)S(1)}, u32[]{:S(2)}, u32[]{:S(2)}) collective-permute-start(f32[3,32]{1,0:T(4,128)S(1)} %pad_maximum_fusion), channel_id=1, source_target_pairs={{0,16},{16,0},{1,17},{17,1},{2,18},{18,2},{3,19},{19,3},{4,20},{20... | collective-permute-start | bytes 1160 | tf_op jit(solution)/shard_map/ppermute | solution.py:1004
  12.6 14.8 %collective-permute-start.8 = (f32[1,14592]{1,0:T(1,128)S(1)}, f32[1,14592]{1,0:T(1,128)S(1)}, u32[]{:S(2)}, u32[]{:S(2)}) collective-permute-start(f32[1,14592]{1,0:T(1,128)S(1)} %constant_dynamic-update-slice_fusion), channel_id=1, source_target_pairs={{0,16},{16,0},{1,17},{17,1},{2,18},{18,2},{3,19},{19,3},{4,20},{20... | collective-permute-start | bytes 175112 | tf_op jit(solution)/shard_map/ppermute | solution.py:1004
  12.9 12.0 %collective-permute-start.2 = (s32[1,128]{1,0:T(1,128)S(1)}, s32[1,128]{1,0:T(1,128)S(1)}, u32[]{:S(2)}, u32[]{:S(2)}) collective-permute-start(s32[1,128]{1,0:T(1,128)S(1)} %get-tuple-element.371), channel_id=1, source_target_pairs={{0,4},{4,8},{8,12},{1,5},{5,9},{9,13},{2,6},{6,10},{10,14},{3,7},{... | collective-permute-start | bytes 1544 | tf_op jit(solution)/shard_map/ppermute | solution.py:35
  24.1 13.5 %collective-permute-start.7 = (bf16[4384,128]{1,0:T(8,128)(2,1)S(1)}, bf16[4384,128]{1,0:T(8,128)(2,1)S(1)}, u32[]{:S(2)}, u32[]{:S(2)}) collective-permute-start(bf16[4384,128]{1,0:T(8,128)(2,1)S(1)} %bitcast.111), channel_id=1, source_target_pairs={{0,16},{16,0},{1,17},{17,1},{2,18},{18,2},{3,19},{19,3},{4,20},{20... | collective-permute-start | bytes 3366920 | tf_op jit(solution)/shard_map/ppermute | solution.py:1004
  25.5 42.0 %collective-permute-start.19 = (bf16[2048,128]{1,0:T(8,128)(2,1)S(1)}, bf16[2048,128]{1,0:T(8,128)(2,1)S(1)}, u32[]{:S(2)}, u32[]{:S(2)}) collective-permute-start(bf16[2048,128]{1,0:T(8,128)(2,1)S(1)} %bitcast.121), channel_id=1, source_target_pairs={{0,16},{16,0},{1,17},{17,1},{2,18},{18,2},{3,19},{19,3},{4,20},{20... | collective-permute-start | bytes 1572872 | tf_op jit(solution)/shard_map/ppermute | solution.py:1004
  26.9 24.5 %collective-permute-start.20 = (bf16[128,1024]{1,0:T(8,128)(2,1)S(1)}, bf16[128,1024]{1,0:T(8,128)(2,1)S(1)}, u32[]{:S(2)}, u32[]{:S(2)}) collective-permute-start(bf16[128,1024]{1,0:T(8,128)(2,1)S(1)} %bitcast.124), channel_id=1, source_target_pairs={{0,16},{16,0},{1,17},{17,1},{2,18},{18,2},{3,19},{19,3},{4,20},{20... | collective-permute-start | bytes 786440 | tf_op jit(solution)/shard_map/ppermute | solution.py:1004
  27.5 10.1 %collective-permute-start.11 = (bf16[1184,256]{1,0:T(8,128)(2,1)S(1)}, bf16[1184,256]{1,0:T(8,128)(2,1)S(1)}, u32[]{:S(2)}, u32[]{:S(2)}) collective-permute-start(bf16[1184,256]{1,0:T(8,128)(2,1)S(1)} %constant_dynamic-slice_fusion.23), channel_id=1, source_target_pairs={{0,2},{1,3},{2,0},{3,1},{16,17},{17,16},{18,19},{19,18},{4,6},{5,7... | collective-permute-start | bytes 1818632 | tf_op jit(solution)/shard_map/ppermute | solution.py:1027
  29.8 10.6 %collective-permute-start.10 = (bf16[2336,256]{1,0:T(8,128)(2,1)S(1)}, bf16[2336,256]{1,0:T(8,128)(2,1)S(1)}, u32[]{:S(2)}, u32[]{:S(2)}) collective-permute-start(bf16[2336,256]{1,0:T(8,128)(2,1)S(1)} %collective-permute-done.9.rest_1_), channel_id=1, source_target_pairs={{0,16},{16,0},{1,17},{17,1},{2,18},{18,2},{3,19},{19,3},{4,20},{20... | collective-permute-start | bytes 3588104 | tf_op jit(solution)/shard_map/ppermute | solution.py:1004
  37.6 14.9 %collective-permute-start.15 = (bf16[2048,256]{1,0:T(8,128)(2,1)S(1)}, bf16[2048,256]{1,0:T(8,128)(2,1)S(1)}, u32[]{:S(2)}, u32[]{:S(2)}) collective-permute-start(bf16[2048,256]{1,0:T(8,128)(2,1)S(1)} %get-tuple-element.213.rest_0_), channel_id=1, source_target_pairs={{0,1},{1,0},{2,3},{3,2},{16,18},{17,19},{18,16},{19,17},{4,5},{5,4... | collective-permute-start | bytes 3145736 | tf_op jit(solution)/shard_map/ppermute | solution.py:1027
  46.0 28.7 %collective-permute-start.21 = (bf16[512,1024]{1,0:T(8,128)(2,1)S(1)}, bf16[512,1024]{1,0:T(8,128)(2,1)S(1)}, u32[]{:S(2)}, u32[]{:S(2)}) collective-permute-start(bf16[512,1024]{1,0:T(8,128)(2,1)S(1)} %get-tuple-element.225.rest_0_), channel_id=1, source_target_pairs={{0,1},{1,0},{2,3},{3,2},{16,18},{17,19},{18,16},{19,17},{4,5},{5,4... | collective-permute-start | bytes 3145736 | tf_op jit(solution)/shard_map/ppermute | solution.py:1027
  52.5 24.0 %collective-permute-start.16 = (bf16[2048,256]{1,0:T(8,128)(2,1)S(1)}, bf16[2048,256]{1,0:T(8,128)(2,1)S(1)}, u32[]{:S(2)}, u32[]{:S(2)}) collective-permute-start(bf16[2048,256]{1,0:T(8,128)(2,1)S(1)} %collective-permute-done.15.rest_1_), channel_id=1, source_target_pairs={{0,16},{16,0},{1,17},{17,1},{2,18},{18,2},{3,19},{19,3},{4,20},{20... | collective-permute-start | bytes 3145736 | tf_op jit(solution)/shard_map/ppermute | solution.py:1004
  52.5 14.9 %collective-permute-start.17 = (bf16[1024,256]{1,0:T(8,128)(2,1)S(1)}, bf16[1024,256]{1,0:T(8,128)(2,1)S(1)}, u32[]{:S(2)}, u32[]{:S(2)}) collective-permute-start(bf16[1024,256]{1,0:T(8,128)(2,1)S(1)} %constant_dynamic-slice_fusion.22), channel_id=1, source_target_pairs={{0,2},{1,3},{2,0},{3,1},{16,17},{17,16},{18,19},{19,18},{4,6},{5,7... | collective-permute-start | bytes 1572872 | tf_op jit(solution)/shard_map/ppermute | solution.py:1027
  68.4 22.1 %collective-permute-start.25 = (bf16[2336,256]{1,0:T(8,128)(2,1)S(1)}, bf16[2336,256]{1,0:T(8,128)(2,1)}, u32[]{:S(2)}, u32[]{:S(2)}) collective-permute-start(bf16[2336,256]{1,0:T(8,128)(2,1)S(1)} %copy-done.2), channel_id=1, source_target_pairs={{0,1},{1,0},{2,3},{3,2},{16,18},{17,19},{18,16},{19,17},{4,5},{5,4... | collective-permute-start | bytes 3588104 | tf_op jit(solution)/shard_map/ppermute | solution.py:1027
  69.9 24.8 %collective-permute-start.14 = (bf16[2048,128]{1,0:T(8,128)(2,1)S(1)}, bf16[2048,128]{1,0:T(8,128)(2,1)S(1)}, u32[]{:S(2)}, u32[]{:S(2)}) collective-permute-start(bf16[2048,128]{1,0:T(8,128)(2,1)S(1)} %get-tuple-element.209), channel_id=1, source_target_pairs={{0,4},{4,8},{8,12},{1,5},{5,9},{9,13},{2,6},{6,10},{10,14},{3,7},{... | collective-permute-start | bytes 1572872 | tf_op jit(solution)/shard_map/ppermute | solution.py:35
  74.8 25.4 %collective-permute-start.22 = (bf16[512,1024]{1,0:T(8,128)(2,1)S(1)}, bf16[512,1024]{1,0:T(8,128)(2,1)S(1)}, u32[]{:S(2)}, u32[]{:S(2)}) collective-permute-start(bf16[512,1024]{1,0:T(8,128)(2,1)S(1)} %collective-permute-done.21.rest_1_), channel_id=1, source_target_pairs={{0,16},{16,0},{1,17},{17,1},{2,18},{18,2},{3,19},{19,3},{4,20},{20... | collective-permute-start | bytes 3145736 | tf_op jit(solution)/shard_map/ppermute | solution.py:1004
  74.9 18.2 %collective-permute-start.23 = (bf16[256,1024]{1,0:T(8,128)(2,1)S(1)}, bf16[256,1024]{1,0:T(8,128)(2,1)S(1)}, u32[]{:S(2)}, u32[]{:S(2)}) collective-permute-start(bf16[256,1024]{1,0:T(8,128)(2,1)S(1)} %constant_dynamic-slice_fusion.21), channel_id=1, source_target_pairs={{0,2},{1,3},{2,0},{3,1},{16,17},{17,16},{18,19},{19,18},{4,6},{5,7... | collective-permute-start | bytes 1572872 | tf_op jit(solution)/shard_map/ppermute | solution.py:1027
  90.5 21.6 %collective-permute-start.31 = (bf16[2048,256]{1,0:T(8,128)(2,1)}, bf16[2048,256]{1,0:T(8,128)(2,1)}, u32[]{:S(2)}, u32[]{:S(2)}) collective-permute-start(bf16[2048,256]{1,0:T(8,128)(2,1)} %get-tuple-element.248.rest_0_), channel_id=1, source_target_pairs={{0,1},{1,0},{2,3},{3,2},{16,18},{17,19},{18,16},{19,17},{4,5},{5,4... | collective-permute-start | bytes 3145736 | tf_op jit(solution)/shard_map/ppermute | solution.py:1027
  92.0 22.8 %collective-permute-start.26 = (bf16[2336,256]{1,0:T(8,128)(2,1)}, bf16[2336,256]{1,0:T(8,128)(2,1)}, u32[]{:S(2)}, u32[]{:S(2)}) collective-permute-start(bf16[2336,256]{1,0:T(8,128)(2,1)} %collective-permute-done.25.rest_1_), channel_id=1, source_target_pairs={{0,16},{16,0},{1,17},{17,1},{2,18},{18,2},{3,19},{19,3},{4,20},{20... | collective-permute-start | bytes 3588104 | tf_op jit(solution)/shard_map/ppermute | solution.py:1004
  93.2 16.8 %collective-permute-start.27 = (bf16[1184,256]{1,0:T(8,128)(2,1)S(1)}, bf16[1184,256]{1,0:T(8,128)(2,1)}, u32[]{:S(2)}, u32[]{:S(2)}) collective-permute-start(bf16[1184,256]{1,0:T(8,128)(2,1)S(1)} %constant_dynamic-slice_fusion.20), channel_id=1, source_target_pairs={{0,2},{1,3},{2,0},{3,1},{16,17},{17,16},{18,19},{19,18},{4,6},{5,7... | collective-permute-start | bytes 1818632 | tf_op jit(solution)/shard_map/ppermute | solution.py:1027
  109.9 44.2 %collective-permute-start.35 = (bf16[512,1024]{1,0:T(8,128)(2,1)S(1)}, bf16[512,1024]{1,0:T(8,128)(2,1)S(1)}, u32[]{:S(2)}, u32[]{:S(2)}) collective-permute-start(bf16[512,1024]{1,0:T(8,128)(2,1)S(1)} %copy-done.14), channel_id=1, source_target_pairs={{0,1},{1,0},{2,3},{3,2},{16,18},{17,19},{18,16},{19,17},{4,5},{5,4... | collective-permute-start | bytes 3145736 | tf_op jit(solution)/shard_map/ppermute | solution.py:1027
  112.1 43.0 %collective-permute-start.32 = (bf16[2048,256]{1,0:T(8,128)(2,1)}, bf16[2048,256]{1,0:T(8,128)(2,1)S(1)}, u32[]{:S(2)}, u32[]{:S(2)}) collective-permute-start(bf16[2048,256]{1,0:T(8,128)(2,1)} %collective-permute-done.31.rest_1_), channel_id=1, source_target_pairs={{0,16},{16,0},{1,17},{17,1},{2,18},{18,2},{3,19},{19,3},{4,20},{20... | collective-permute-start | bytes 3145736 | tf_op jit(solution)/shard_map/ppermute | solution.py:1004
  113.2 18.5 %collective-permute-start.33 = (bf16[1024,256]{1,0:T(8,128)(2,1)S(1)}, bf16[1024,256]{1,0:T(8,128)(2,1)S(1)}, u32[]{:S(2)}, u32[]{:S(2)}) collective-permute-start(bf16[1024,256]{1,0:T(8,128)(2,1)S(1)} %constant_dynamic-slice_fusion.19), channel_id=1, source_target_pairs={{0,2},{1,3},{2,0},{3,1},{16,17},{17,16},{18,19},{19,18},{4,6},{5,7... | collective-permute-start | bytes 1572872 | tf_op jit(solution)/shard_map/ppermute | solution.py:1027
  131.8 23.3 %collective-permute-start.34 = (bf16[1024,256]{1,0:T(8,128)(2,1)S(1)}, bf16[1024,256]{1,0:T(8,128)(2,1)S(1)}, u32[]{:S(2)}, u32[]{:S(2)}) collective-permute-start(bf16[1024,256]{1,0:T(8,128)(2,1)S(1)} %collective-permute-done.33.rest_3_), channel_id=1, source_target_pairs={{0,16},{16,0},{1,17},{17,1},{2,18},{18,2},{3,19},{19,3},{4,20},{20... | collective-permute-start | bytes 1572872 | tf_op jit(solution)/shard_map/ppermute | solution.py:1004
  141.3 24.6 %collective-permute-start.30 = (bf16[2048,128]{1,0:T(8,128)(2,1)S(1)}, bf16[2048,128]{1,0:T(8,128)(2,1)S(1)}, u32[]{:S(2)}, u32[]{:S(2)}) collective-permute-start(bf16[2048,128]{1,0:T(8,128)(2,1)S(1)} %get-tuple-element.244), channel_id=1, source_target_pairs={{0,4},{4,8},{8,12},{1,5},{5,9},{9,13},{2,6},{6,10},{10,14},{3,7},{... | collective-permute-start | bytes 1572872 | tf_op jit(solution)/shard_map/ppermute | solution.py:35
  154.2 16.4 %collective-permute-start.36 = (bf16[512,1024]{1,0:T(8,128)(2,1)S(1)}, bf16[512,1024]{1,0:T(8,128)(2,1)S(1)}, u32[]{:S(2)}, u32[]{:S(2)}) collective-permute-start(bf16[512,1024]{1,0:T(8,128)(2,1)S(1)} %collective-permute-done.35.rest_1_), channel_id=1, source_target_pairs={{0,16},{16,0},{1,17},{17,1},{2,18},{18,2},{3,19},{19,3},{4,20},{20... | collective-permute-start | bytes 3145736 | tf_op jit(solution)/shard_map/ppermute | solution.py:1004
  154.3 10.5 %collective-permute-start.37 = (bf16[256,1024]{1,0:T(8,128)(2,1)S(1)}, bf16[256,1024]{1,0:T(8,128)(2,1)S(1)}, u32[]{:S(2)}, u32[]{:S(2)}) collective-permute-start(bf16[256,1024]{1,0:T(8,128)(2,1)S(1)} %constant_dynamic-slice_fusion.18), channel_id=1, source_target_pairs={{0,2},{1,3},{2,0},{3,1},{16,17},{17,16},{18,19},{19,18},{4,6},{5,7... | collective-permute-start | bytes 1572872 | tf_op jit(solution)/shard_map/ppermute | solution.py:1027
  185.4 16.2 %collective-permute-start.40 = (bf16[2048,128]{1,0:T(8,128)(2,1)S(1)}, bf16[2048,128]{1,0:T(8,128)(2,1)S(1)}, u32[]{:S(2)}, u32[]{:S(2)}) collective-permute-start(bf16[2048,128]{1,0:T(8,128)(2,1)S(1)} %get-tuple-element.264), channel_id=1, source_target_pairs={{4,0},{8,4},{12,8},{5,1},{9,5},{13,9},{6,2},{10,6},{14,10},{7,3},{... | collective-permute-start | bytes 1572872 | tf_op jit(solution)/shard_map/ppermute | solution.py:35
  195.2 14.7 %collective-permute-start.41 = (bf16[8,2304]{1,0:T(8,128)(2,1)S(1)}, bf16[8,2304]{1,0:T(8,128)(2,1)S(1)}, u32[]{:S(2)}, u32[]{:S(2)}) collective-permute-start(bf16[8,2304]{1,0:T(8,128)(2,1)S(1)} %get-tuple-element.272), channel_id=1, source_target_pairs={{4,0},{8,4},{12,8},{5,1},{9,5},{13,9},{6,2},{10,6},{14,10},{7,3},{... | collective-permute-start | bytes 110600 | tf_op jit(solution)/shard_map/ppermute | solution.py:35
  196.7 31.4 %collective-permute-start.39 = (bf16[512,1024]{1,0:T(8,128)(2,1)S(1)}, bf16[512,1024]{1,0:T(8,128)(2,1)S(1)}, u32[]{:S(2)}, u32[]{:S(2)}) collective-permute-start(bf16[512,1024]{1,0:T(8,128)(2,1)S(1)} %broadcast_select_fusion.9), channel_id=1, source_target_pairs={{0,16},{16,0},{1,17},{17,1},{2,18},{18,2},{3,19},{19,3},{4,20},{20... | collective-permute-start | bytes 3145736 | tf_op jit(solution)/shard_map/ppermute | solution.py:1004
  216.9 12.8 %collective-permute-start.42 = (bf16[4352,128]{1,0:T(8,128)(2,1)S(1)}, bf16[4352,128]{1,0:T(8,128)(2,1)S(1)}, u32[]{:S(2)}, u32[]{:S(2)}) collective-permute-start(bf16[4352,128]{1,0:T(8,128)(2,1)S(1)} %constant_dynamic-slice_fusion.17), channel_id=1, source_target_pairs={{0,16},{16,0},{1,17},{17,1},{2,18},{18,2},{3,19},{19,3},{4,20},{20... | collective-permute-start | bytes 3342344 | tf_op jit(solution)/shard_map/ppermute | solution.py:1004
  230.1 27.9 %collective-permute-start.43 = (bf16[1088,128]{1,0:T(8,128)(2,1)S(1)}, bf16[1088,128]{1,0:T(8,128)(2,1)S(1)}, u32[]{:S(2)}, u32[]{:S(2)}) collective-permute-start(bf16[1088,128]{1,0:T(8,128)(2,1)S(1)} %get-tuple-element.354), channel_id=1, source_target_pairs={{0,1},{1,0},{2,3},{3,2},{4,5},{5,4},{6,7},{7,6},{8,9},{9,8},{10,11... | collective-permute-start | bytes 835592 | tf_op jit(solution)/shard_map/ppermute | solution.py:1009
  230.9 27.1 %collective-permute-start.44 = (bf16[1088,128]{1,0:T(8,128)(2,1)S(1)}, bf16[1088,128]{1,0:T(8,128)(2,1)S(1)}, u32[]{:S(2)}, u32[]{:S(2)}) collective-permute-start(bf16[1088,128]{1,0:T(8,128)(2,1)S(1)} %get-tuple-element.353), channel_id=1, source_target_pairs={{0,2},{1,3},{2,0},{3,1},{4,6},{5,7},{6,4},{7,5},{8,10},{9,11},{10,... | collective-permute-start | bytes 835592 | tf_op jit(solution)/shard_map/ppermute | solution.py:1009
  232.5 25.6 %collective-permute-start.45 = (bf16[1088,128]{1,0:T(8,128)(2,1)S(1)}, bf16[1088,128]{1,0:T(8,128)(2,1)S(1)}, u32[]{:S(2)}, u32[]{:S(2)}) collective-permute-start(bf16[1088,128]{1,0:T(8,128)(2,1)S(1)} %get-tuple-element.352), channel_id=1, source_target_pairs={{0,3},{1,2},{2,1},{3,0},{4,7},{5,6},{6,5},{7,4},{8,11},{9,10},{10,... | collective-permute-start | bytes 835592 | tf_op jit(solution)/shard_map/ppermute | solution.py:1009
  245.3 19.3 %collective-permute-start.46 = (bf16[2048,128]{1,0:T(8,128)(2,1)S(1)}, bf16[2048,128]{1,0:T(8,128)(2,1)S(1)}, u32[]{:S(2)}, u32[]{:S(2)}) collective-permute-start(bf16[2048,128]{1,0:T(8,128)(2,1)S(1)} %get-tuple-element.290), channel_id=1, source_target_pairs={{4,0},{8,4},{12,8},{5,1},{9,5},{13,9},{6,2},{10,6},{14,10},{7,3},{... | collective-permute-start | bytes 1572872 | tf_op jit(solution)/shard_map/ppermute | solution.py:35
  255.0 22.6 %collective-permute-start.50 = (bf16[8,2304]{1,0:T(8,128)(2,1)S(1)}, bf16[8,2304]{1,0:T(8,128)(2,1)S(1)}, u32[]{:S(2)}, u32[]{:S(2)}) collective-permute-start(bf16[8,2304]{1,0:T(8,128)(2,1)S(1)} %get-tuple-element.299), channel_id=1, source_target_pairs={{4,0},{8,4},{12,8},{5,1},{9,5},{13,9},{6,2},{10,6},{14,10},{7,3},{... | collective-permute-start | bytes 110600 | tf_op jit(solution)/shard_map/ppermute | solution.py:35
  258.2 14.8 %collective-permute-start.47 = (bf16[272,128]{1,0:T(8,128)(2,1)S(1)}, bf16[272,128]{1,0:T(8,128)(2,1)S(1)}, u32[]{:S(2)}, u32[]{:S(2)}) collective-permute-start(bf16[272,128]{1,0:T(8,128)(2,1)S(1)} %get-tuple-element.366), channel_id=1, source_target_pairs={{0,4},{4,0},{8,12},{12,8},{1,5},{5,1},{9,13},{13,9},{2,6},{6,2},{1... | collective-permute-start | bytes 208904 | tf_op jit(solution)/shard_map/ppermute | solution.py:1009
  261.6 11.5 %collective-permute-start.48 = (bf16[272,128]{1,0:T(8,128)(2,1)S(1)}, bf16[272,128]{1,0:T(8,128)(2,1)S(1)}, u32[]{:S(2)}, u32[]{:S(2)}) collective-permute-start(bf16[272,128]{1,0:T(8,128)(2,1)S(1)} %get-tuple-element.365), channel_id=1, source_target_pairs={{0,8},{4,12},{8,0},{12,4},{1,9},{5,13},{9,1},{13,5},{2,10},{6,14},... | collective-permute-start | bytes 208904 | tf_op jit(solution)/shard_map/ppermute | solution.py:1009
  273.2 8.9 %collective-permute-start.51 = (bf16[272,128]{1,0:T(8,128)(2,1)S(1)}, bf16[272,128]{1,0:T(8,128)(2,1)S(1)}, u32[]{:S(2)}, u32[]{:S(2)}) collective-permute-start(bf16[272,128]{1,0:T(8,128)(2,1)S(1)} %get-tuple-element.333), channel_id=1, source_target_pairs={{0,4},{4,0},{8,12},{12,8},{1,5},{5,1},{9,13},{13,9},{2,6},{6,2},{1... | collective-permute-start | bytes 208904 | tf_op jit(solution)/shard_map/ppermute | solution.py:1009
  284.6 10.2 %collective-permute-start.56 = (bf16[1088,128]{1,0:T(8,128)(2,1)S(1)}, bf16[1088,128]{1,0:T(8,128)(2,1)S(1)}, u32[]{:S(2)}, u32[]{:S(2)}) collective-permute-start(bf16[1088,128]{1,0:T(8,128)(2,1)S(1)} %bitcast.117), channel_id=1, source_target_pairs={{0,2},{1,3},{2,0},{3,1},{4,6},{5,7},{6,4},{7,5},{8,10},{9,11},{10,... | collective-permute-start | bytes 835592 | tf_op jit(solution)/shard_map/ppermute | solution.py:1009
  295.4 11.4 %collective-permute-start.60 = (bf16[1088,128]{1,0:T(8,128)(2,1)S(1)}, bf16[1088,128]{1,0:T(8,128)(2,1)S(1)}, u32[]{:S(2)}, u32[]{:S(2)}) collective-permute-start(bf16[1088,128]{1,0:T(8,128)(2,1)S(1)} %get-tuple-element.350), channel_id=1, source_target_pairs={{0,1},{1,0},{2,3},{3,2},{4,5},{5,4},{6,7},{7,6},{8,9},{9,8},{10,11... | collective-permute-start | bytes 835592 | tf_op jit(solution)/shard_map/ppermute | solution.py:1009
  297.1 11.4 %collective-permute-start.61 = (bf16[1088,128]{1,0:T(8,128)(2,1)S(1)}, bf16[1088,128]{1,0:T(8,128)(2,1)S(1)}, u32[]{:S(2)}, u32[]{:S(2)}) collective-permute-start(bf16[1088,128]{1,0:T(8,128)(2,1)S(1)} %get-tuple-element.349), channel_id=1, source_target_pairs={{0,2},{1,3},{2,0},{3,1},{4,6},{5,7},{6,4},{7,5},{8,10},{9,11},{10,... | collective-permute-start | bytes 835592 | tf_op jit(solution)/shard_map/ppermute | solution.py:1009
  297.4 11.1 %collective-permute-start.62 = (bf16[1088,128]{1,0:T(8,128)(2,1)S(1)}, bf16[1088,128]{1,0:T(8,128)(2,1)S(1)}, u32[]{:S(2)}, u32[]{:S(2)}) collective-permute-start(bf16[1088,128]{1,0:T(8,128)(2,1)S(1)} %get-tuple-element.348), channel_id=1, source_target_pairs={{0,3},{1,2},{2,1},{3,0},{4,7},{5,6},{6,5},{7,4},{8,11},{9,10},{10,... | collective-permute-start | bytes 835592 | tf_op jit(solution)/shard_map/ppermute | solution.py:1009
  313.3 17.3 %collective-permute-start.58 = (bf16[512,1024]{1,0:T(8,128)(2,1)S(1)}, bf16[512,1024]{1,0:T(8,128)(2,1)S(1)}, u32[]{:S(2)}, u32[]{:S(2)}) collective-permute-start(bf16[512,1024]{1,0:T(8,128)(2,1)S(1)} %broadcast_select_fusion.7), channel_id=1, source_target_pairs={{0,16},{16,0},{1,17},{17,1},{2,18},{18,2},{3,19},{19,3},{4,20},{20... | collective-permute-start | bytes 3145736 | tf_op jit(solution)/shard_map/ppermute | solution.py:1004
  324.3 16.7 %collective-permute-start.59 = (bf16[4352,128]{1,0:T(8,128)(2,1)S(1)}, bf16[4352,128]{1,0:T(8,128)(2,1)S(1)}, u32[]{:S(2)}, u32[]{:S(2)}) collective-permute-start(bf16[4352,128]{1,0:T(8,128)(2,1)S(1)} %bitcast.104), channel_id=1, source_target_pairs={{0,16},{16,0},{1,17},{17,1},{2,18},{18,2},{3,19},{19,3},{4,20},{20... | collective-permute-start | bytes 3342344 | tf_op jit(solution)/shard_map/ppermute | solution.py:1004
  326.8 9.7 %collective-permute-start.69 = (bf16[1088,128]{1,0:T(8,128)(2,1)S(1)}, bf16[1088,128]{1,0:T(8,128)(2,1)S(1)}, u32[]{:S(2)}, u32[]{:S(2)}) collective-permute-start(bf16[1088,128]{1,0:T(8,128)(2,1)S(1)} %bitcast.112), channel_id=1, source_target_pairs={{0,1},{1,0},{2,3},{3,2},{4,5},{5,4},{6,7},{7,6},{8,9},{9,8},{10,11... | collective-permute-start | bytes 835592 | tf_op jit(solution)/shard_map/ppermute | solution.py:1009
  328.3 12.4 %collective-permute-start.70 = (bf16[1088,128]{1,0:T(8,128)(2,1)S(1)}, bf16[1088,128]{1,0:T(8,128)(2,1)S(1)}, u32[]{:S(2)}, u32[]{:S(2)}) collective-permute-start(bf16[1088,128]{1,0:T(8,128)(2,1)S(1)} %bitcast.113), channel_id=1, source_target_pairs={{0,2},{1,3},{2,0},{3,1},{4,6},{5,7},{6,4},{7,5},{8,10},{9,11},{10,... | collective-permute-start | bytes 835592 | tf_op jit(solution)/shard_map/ppermute | solution.py:1009
  328.9 11.8 %collective-permute-start.71 = (bf16[1088,128]{1,0:T(8,128)(2,1)S(1)}, bf16[1088,128]{1,0:T(8,128)(2,1)S(1)}, u32[]{:S(2)}, u32[]{:S(2)}) collective-permute-start(bf16[1088,128]{1,0:T(8,128)(2,1)S(1)} %bitcast.114), channel_id=1, source_target_pairs={{0,3},{1,2},{2,1},{3,0},{4,7},{5,6},{6,5},{7,4},{8,11},{9,10},{10,... | collective-permute-start | bytes 835592 | tf_op jit(solution)/shard_map/ppermute | solution.py:1009
  (145 other events, 1731.3 us)

commit v5 on v4

--- a/solution.py
+++ b/solution.py
@@ -184,7 +184,7 @@
             normed_ref[rows, :] = (gated * rms_rate(gated) * vector_ref[:, gain : gain + gated.shape[1]]).astype(BF16)
             return 0
 
-        lax.fori_loop(0, SPAN // 16, rows_at, 0, unroll=4)
+        lax.fori_loop(0, SPAN // 16, rows_at, 0, unroll=8)
 
 
 def out_back_kernel(
@@ -218,7 +218,7 @@
         grad_mixed_ref[rows, :] = (grad_gated * silu).astype(BF16)
         return 0
 
-    lax.fori_loop(0, SPAN // 16, rows_at, 0, unroll=4)
+    lax.fori_loop(0, SPAN // 16, rows_at, 0, unroll=8)
     carry = jnp.exp2(decay_ref[...]) * token_ref[0][:1]
     out_map = bc_ref[:, state:]
     wide = 512
@@ -487,7 +487,7 @@
 
 
 def cost(microseconds):
-    return pl.CostEstimate(flops=int(microseconds * 3.45e+09), bytes_accessed=1 << 16, transcendentals=0)
+    return pl.CostEstimate(flops=int(microseconds * 2.3e+09), bytes_accessed=1 << 16, transcendentals=0)
 
 
 class Sizes:

time: 352 us -> 350 us (level)
    unnamed x244 -> x220, local copies, waits for them, and re-layouts: 10.7 us -> 9.34 us
  transfers between devices with their start and end apart: 73 -> 73, of which waited for: 19 -> 19; matrix products, arithmetic and copies ran while one was open for 6% -> 5% of each run, Pallas kernels for 40% -> 41%
where the time goes in v5:
time: 350 us; the launch traced here: 344 us
  Pallas kernels  157 us (45%)
  starting transfers between devices  94.2 us (27%)
  waiting for transfers between devices  56.7 us (16%)
  local copies, waits for them, and re-layouts  17.6 us (5%)
  other arithmetic  15.6 us (4%)
    ppermute x10, starting transfers between devices, from_behind(): lax.ppermute(value, axis, [(source, source + steps) for source in range(i...  38.2 us
    ppermute x24, starting transfers between devices, exchange(): lax.ppermute(value, axis, [(place, place ^ distance) for place in range(c...  34 us
    pallas_call x4, Pallas kernels, scan_backward(): pl.pallas_call(functools.partial(scan_back_kernel, s.head, s.heads, s.sta...  33.4 us
    ppermute x12, waiting for transfers between devices, across(): return lax.ppermute(value, (SECTION, WSHARD), pairs)  25.4 us
    ppermute x24, waiting for transfers between devices, exchange(): lax.ppermute(value, axis, [(place, place ^ distance) for place in range(c...  23.7 us
    pallas_call x2, Pallas kernels, out_backward(): pl.pallas_call(functools.partial(out_back_kernel, s.head, s.heads, s.stat...  22.9 us
    pallas_call x4, Pallas kernels, scan_forward(): pl.pallas_call(functools.partial(scan_kernel, s.head, s.state, s.gate_gai...  17.8 us
    ppermute x12, starting transfers between devices, across(): return lax.ppermute(value, (SECTION, WSHARD), pairs)  17.4 us
  transfers between devices with their start and end apart: 73, of which 19 were waited for; matrix products, arithmetic and copies ran while one was open for 5% of the time, Pallas kernels for 41%

profile of v5, /device:TPU:0, one launch (start us, length us, event | category | flops | bytes accessed | tf_op | source)
XLA Modules:
  0.0 344.4 jit_solution(14843124826538544505)
XLA Ops:
  5.3 2.9 broadcast_select_fusion
  9.2 2.7 collective-permute-start.9
  12.9 4.1 %collective-permute-start.2 = (s32[1,128]{1,0:T(1,128)S(1)}, s32[1,128]{1,0:T(1,128)S(1)}, u32[]{:S(2)}, u32[]{:S(2)}) collective-permute-start(s32[1,128]{1,0:T(1,128)S(1)} %get-tuple-element.371), channel_id=1, source_target_pairs={{0,4},{4,8},{8,12},{1,5},{5,9},{9,13},{2,6},{6,10},{10,14},{3,7},{... | collective-permute-start | bytes 1544 | tf_op jit(solution)/shard_map/ppermute | solution.py:35
  17.0 2.7 broadcast_select_fusion.5
  29.8 7.8 %collective-permute-done.11.rest_3_ = bf16[1184,256]{1,0:T(8,128)(2,1)S(1)} collective-permute-done((bf16[1184,256]{1,0:T(8,128)(2,1)S(1)}, bf16[1184,256]{1,0:T(8,128)(2,1)S(1)}, u32[]{:S(2)}, u32[]{:S(2)}) %collective-permute-start.11) | collective-permute-done | bytes 606240 | tf_op jit(solution)/shard_map/ppermute | solution.py:1027
  40.4 5.6 %shard_map.209 = (bf16[512,1152]{1,0:T(8,128)(2,1)S(1)}, bf16[512,2304]{1,0:T(8,128)(2,1)S(1)}, bf16[512,128]{1,0:T(8,128)(2,1)S(1)}, bf16[8,2304]{1,0:T(8,128)(2,1)S(1)}) custom-call(bf16[512,1024]{1,0:T(8,128)(2,1)S(1)} %dynamic-slice_bitcast_fusion.1.input_ref, f32[1,14592]{1,0:T(1,128)S(1)} %get-tuple-element.188.vector_ref, ...), custom_call_target="tpu_custom_call" | custom-call | flops 13799999488 | bytes 65536 | tf_op jit(solution)/shard_map/pallas_call | solution.py:601
  46.9 4.5 %collective-permute-start.13 = (bf16[8,2304]{1,0:T(8,128)(2,1)S(1)}, bf16[8,2304]{1,0:T(8,128)(2,1)S(1)}, u32[]{:S(2)}, u32[]{:S(2)}) collective-permute-start(bf16[8,2304]{1,0:T(8,128)(2,1)S(1)} %get-tuple-element.199), channel_id=1, source_target_pairs={{0,4},{4,8},{8,12},{1,5},{5,9},{9,13},{2,6},{6,10},{10,14},{3,7},{... | collective-permute-start | bytes 110600 | tf_op jit(solution)/shard_map/ppermute | solution.py:35
  54.1 8.0 %shard_map.210 = (bf16[2048,512]{1,0:T(8,128)(2,1)S(1)}, bf16[512,2048]{1,0:T(8,128)(2,1)}, bf16[512,512]{1,0:T(8,128)(2,1)S(1)}, f32[96,512]{1,0:T(8,128)S(1)},...) custom-call(bf16[512,2304]{1,0:T(8,128)(2,1)S(1)} %get-tuple-element.198.mixed_ref.mixed_bc_ref, ...), custom_call_target="tpu_custom_call" | custom-call | flops 19549999104 | bytes 65536 | tf_op jit(solution)/shard_map/pallas_call | solution.py:513
  62.1 5.3 %collective-permute-done.17.rest_3_ = bf16[1024,256]{1,0:T(8,128)(2,1)S(1)} collective-permute-done((bf16[1024,256]{1,0:T(8,128)(2,1)S(1)}, bf16[1024,256]{1,0:T(8,128)(2,1)S(1)}, u32[]{:S(2)}, u32[]{:S(2)}) %collective-permute-start.17) | collective-permute-done | bytes 524320 | tf_op jit(solution)/shard_map/ppermute | solution.py:1027
  69.9 4.8 %collective-permute-start.14 = (bf16[2048,128]{1,0:T(8,128)(2,1)S(1)}, bf16[2048,128]{1,0:T(8,128)(2,1)S(1)}, u32[]{:S(2)}, u32[]{:S(2)}) collective-permute-start(bf16[2048,128]{1,0:T(8,128)(2,1)S(1)} %get-tuple-element.209), channel_id=1, source_target_pairs={{0,4},{4,8},{8,12},{1,5},{5,9},{9,13},{2,6},{6,10},{10,14},{3,7},{... | collective-permute-start | bytes 1572872 | tf_op jit(solution)/shard_map/ppermute | solution.py:35
  76.5 3.5 %shard_map.211.gate_ref = bf16[512,2048]{1,0:T(8,128)(2,1)S(1)} custom-call(bf16[512,1152]{1,0:T(8,128)(2,1)S(1)} %get-tuple-element.210.normed_ref.refs_5_.refs_0_.refs_4_, bf16[4384,128]{1,0:T(8,128)(2,1)S(1)} %get-tuple-element.191.up_ref, s32[5]{0:T(128)S(1)} %copy-done.39, bf16[2048,256]{1,0:T(8,128)(2,1)S(1)} %get-tuple-element.213.rest_0_, ...), custom_call_target="tpu_custom_call" | custom-call | flops 8280000000 | bytes 65536 | tf_op jit(solution)/shard_map/pallas_call | solution.py:618
  80.1 4.4 %shard_map.212 = (bf16[512,2048]{1,0:T(8,128)(2,1)S(1)}, bf16[512,2048]{1,0:T(8,128)(2,1)S(1)}) custom-call(bf16[2048,512]{1,0:T(8,128)(2,1)S(1)} %get-tuple-element.204.values_ref, bf16[512,512]{1,0:T(8,128)(2,1)S(1)} %get-tuple-element.205.bc_ref.slope_bc_ref, f32[96,512]{1,0:T(8,128)S(1)} %get-tuple-element.206.step_ref.decay_ref.sig_ref, ...), custom_call_target="tpu_custom_call" | custom-call | flops 14949999616 | bytes 65536 | tf_op jit(solution)/shard_map/pallas_call | solution.py:568
  85.3 5.2 %collective-permute-done.25.rest_1_ = bf16[2336,256]{1,0:T(8,128)(2,1)} collective-permute-done((bf16[2336,256]{1,0:T(8,128)(2,1)S(1)}, bf16[2336,256]{1,0:T(8,128)(2,1)}, u32[]{:S(2)}, u32[]{:S(2)}) %collective-permute-start.25) | collective-permute-done | bytes 1196064 | tf_op jit(solution)/shard_map/ppermute | solution.py:1027
  94.8 4.5 %shard_map.213 = (bf16[512,2048]{1,0:T(8,128)(2,1)S(1)}, bf16[512,2048]{1,0:T(8,128)(2,1)S(1)}) custom-call(bf16[2048,512]{1,0:T(8,128)(2,1)S(1)} %get-tuple-element.204.values_ref, bf16[512,512]{1,0:T(8,128)(2,1)S(1)} %get-tuple-element.205.bc_ref.slope_bc_ref, ...), custom_call_target="tpu_custom_call", output_to_operand_aliasing={{0}: (11, {}), {1}: (12, {})} | custom-call | flops 14949999616 | bytes 65536 | tf_op jit(solution)/shard_map/pallas_call | solution.py:568
  100.1 3.7 %shard_map.214 = (bf16[512,128]{1,0:T(8,128)(2,1)S(1)}, bf16[512,1024]{1,0:T(8,128)(2,1)S(1)}) custom-call(bf16[512,2048]{1,0:T(8,128)(2,1)S(1)} %get-tuple-element.219.normed_ref.refs_2_, bf16[512,1024]{1,0:T(8,128)(2,1)S(1)} %dynamic-slice_bitcast_fusion.1.input_ref, bf16[2048,128]{1,0:T(8,128)(2,1)S(1)} %get-tuple-element.356.down_ref.down_out_ref, ...), custom_call_target="tpu_custom_call" | custom-call | flops 9200000000 | bytes 65536 | tf_op jit(solution)/shard_map/pallas_call | solution.py:633
  104.5 5.4 %collective-permute-done.27.rest_3_ = bf16[1184,256]{1,0:T(8,128)(2,1)} collective-permute-done((bf16[1184,256]{1,0:T(8,128)(2,1)S(1)}, bf16[1184,256]{1,0:T(8,128)(2,1)}, u32[]{:S(2)}, u32[]{:S(2)}) %collective-permute-start.27) | collective-permute-done | bytes 606240 | tf_op jit(solution)/shard_map/ppermute | solution.py:1027
  119.7 7.2 %shard_map.215 = (bf16[512,1152]{1,0:T(8,128)(2,1)S(1)}, bf16[512,2304]{1,0:T(8,128)(2,1)S(1)}, bf16[512,128]{1,0:T(8,128)(2,1)S(1)}, bf16[8,2304]{1,0:T(8,128)(2,1)S(1)}) custom-call(bf16[512,1024]{1,0:T(8,128)(2,1)S(1)} %get-tuple-element.228.input_ref, f32[1,14592]{1,0:T(1,128)S(1)} %copy-done.32, bf16[1024,128]{1,0:T(8,128)(2,1)S(1)} %get-tuple-element.230.down_ref, ...), custom_call_target="tpu_custom_call" | custom-call | flops 13799999488 | bytes 65536 | tf_op jit(solution)/shard_map/pallas_call | solution.py:601
  127.0 4.7 %collective-permute-start.29 = (bf16[8,2304]{1,0:T(8,128)(2,1)S(1)}, bf16[8,2304]{1,0:T(8,128)(2,1)S(1)}, u32[]{:S(2)}, u32[]{:S(2)}) collective-permute-start(bf16[8,2304]{1,0:T(8,128)(2,1)S(1)} %get-tuple-element.238), channel_id=1, source_target_pairs={{0,4},{4,8},{8,12},{1,5},{5,9},{9,13},{2,6},{6,10},{10,14},{3,7},{... | collective-permute-start | bytes 110600 | tf_op jit(solution)/shard_map/ppermute | solution.py:35
  133.3 8.1 %shard_map.216 = (bf16[2048,512]{1,0:T(8,128)(2,1)S(1)}, bf16[512,2048]{1,0:T(8,128)(2,1)}, bf16[512,512]{1,0:T(8,128)(2,1)S(1)}, f32[96,512]{1,0:T(8,128)S(1)},...) custom-call(bf16[512,2304]{1,0:T(8,128)(2,1)S(1)} %get-tuple-element.237.mixed_ref.mixed_bc_ref, ...), custom_call_target="tpu_custom_call" | custom-call | flops 19549999104 | bytes 65536 | tf_op jit(solution)/shard_map/pallas_call | solution.py:513
  141.4 13.4 %collective-permute-start.30 = (bf16[2048,128]{1,0:T(8,128)(2,1)S(1)}, bf16[2048,128]{1,0:T(8,128)(2,1)S(1)}, u32[]{:S(2)}, u32[]{:S(2)}) collective-permute-start(bf16[2048,128]{1,0:T(8,128)(2,1)S(1)} %get-tuple-element.244), channel_id=1, source_target_pairs={{0,4},{4,8},{8,12},{1,5},{5,9},{9,13},{2,6},{6,10},{10,14},{3,7},{... | collective-permute-start | bytes 1572872 | tf_op jit(solution)/shard_map/ppermute | solution.py:35
  155.6 4.5 %shard_map.217.gate_ref = bf16[512,2048]{1,0:T(8,128)(2,1)S(1)} custom-call(bf16[512,1152]{1,0:T(8,128)(2,1)S(1)} %get-tuple-element.245.normed_ref.refs_5_.refs_0_.refs_4_, bf16[4384,128]{1,0:T(8,128)(2,1)S(1)} %copy-done.8, s32[5]{0:T(128)S(1)} %copy-done.41, bf16[2048,256]{1,0:T(8,128)(2,1)} %get-tuple-element.248.rest_0_, ...), custom_call_target="tpu_custom_call" | custom-call | flops 8280000000 | bytes 65536 | tf_op jit(solution)/shard_map/pallas_call | solution.py:618
  160.2 4.4 %shard_map.218 = (bf16[512,2048]{1,0:T(8,128)(2,1)S(1)}, bf16[512,2048]{1,0:T(8,128)(2,1)S(1)}) custom-call(bf16[2048,512]{1,0:T(8,128)(2,1)S(1)} %get-tuple-element.241.values_ref, bf16[512,512]{1,0:T(8,128)(2,1)S(1)} %get-tuple-element.242.bc_ref.slope_bc_ref, f32[96,512]{1,0:T(8,128)S(1)} %get-tuple-element.243.step_ref.decay_ref.sig_ref, ...), custom_call_target="tpu_custom_call" | custom-call | flops 14949999616 | bytes 65536 | tf_op jit(solution)/shard_map/pallas_call | solution.py:568
  165.8 4.5 %shard_map.219 = (bf16[512,2048]{1,0:T(8,128)(2,1)S(1)}, bf16[512,2048]{1,0:T(8,128)(2,1)S(1)}) custom-call(bf16[2048,512]{1,0:T(8,128)(2,1)S(1)} %get-tuple-element.241.values_ref, bf16[512,512]{1,0:T(8,128)(2,1)S(1)} %get-tuple-element.242.bc_ref.slope_bc_ref, ...), custom_call_target="tpu_custom_call", output_to_operand_aliasing={{0}: (11, {}), {1}: (12, {})} | custom-call | flops 14949999616 | bytes 65536 | tf_op jit(solution)/shard_map/pallas_call | solution.py:568
  170.4 3.7 %shard_map.220 = (bf16[512,128]{1,0:T(8,128)(2,1)S(1)}, bf16[512,1024]{1,0:T(8,128)(2,1)S(1)}) custom-call(bf16[512,2048]{1,0:T(8,128)(2,1)S(1)} %get-tuple-element.254.normed_ref.refs_2_, bf16[512,1024]{1,0:T(8,128)(2,1)S(1)} %get-tuple-element.228.input_ref, bf16[2048,128]{1,0:T(8,128)(2,1)S(1)} %copy-done.18, f32[512,128]{1,0:T(8,128)S(1)} %copy-done.64, ...), custom_call_target="tpu_custom_call" | custom-call | flops 9200000000 | bytes 65536 | tf_op jit(solution)/shard_map/pallas_call | solution.py:633
  174.1 11.3 %shard_map.221 = (bf16[512,2048]{1,0:T(8,128)(2,1)S(1)}, bf16[2048,512]{1,0:T(8,128)(2,1)S(1)}, bf16[512,128]{1,0:T(8,128)(2,1)S(1)}, bf16[2048,128]{1,0:T(8,128)(2,1)S(1)}, bf16[2048,128]{1,0:T(8,128)(2,1)S(1)}) custom-call(bf16[512,1024]{1,0:T(8,128)(2,1)S(1)} %dynamic-slice_bitcast_fusion.up_ref.up_stream_ref.refs_0_, f32[512,128]{1,0:T(8,128)S(1)} %copy-done.64, ...), custom_call_target="tpu_custom_call" | custom-call | flops 31050000384 | bytes 65536 | tf_op jit(solution)/shard_map/pallas_call | solution.py:648
  186.7 8.3 %shard_map.222 = (bf16[512,2048]{1,0:T(8,128)(2,1)S(1)}, bf16[512,256]{1,0:T(8,128)(2,1)S(1)}, bf16[512,128]{1,0:T(8,128)(2,1)S(1)}, bf16[8,2304]{1,0:T(8,128)(2,1)S(1)}) custom-call(bf16[2048,512]{1,0:T(8,128)(2,1)S(1)} %get-tuple-element.241.values_ref, bf16[2048,512]{1,0:T(8,128)(2,1)S(1)} %get-tuple-element.263.grad_ref, ...), custom_call_target="tpu_custom_call" | custom-call | flops 19549999104 | bytes 65536 | tf_op jit(solution)/shard_map/pallas_call | solution.py:739
  198.5 3.0 collective-permute-done.40.grad_state_ref
  201.5 8.2 %shard_map.223 = (bf16[512,2048]{1,0:T(8,128)(2,1)S(1)}, bf16[512,256]{1,0:T(8,128)(2,1)S(1)}, bf16[512,128]{1,0:T(8,128)(2,1)S(1)}) custom-call(bf16[2048,512]{1,0:T(8,128)(2,1)S(1)} %get-tuple-element.241.values_ref, bf16[2048,512]{1,0:T(8,128)(2,1)S(1)} %get-tuple-element.263.grad_ref, ...), custom_call_target="tpu_custom_call", output_to_operand_aliasing={{0}: (15, {}), {1}: (16, {}), {2}: (17, {})} | custom-call | flops 19549999104 | bytes 65536 | tf_op jit(solution)/shard_map/pallas_call | solution.py:739
  209.7 4.4 %shard_map.224.grad_ref.refs_2_ = bf16[512,2304]{1,0:T(8,128)(2,1)S(1)} custom-call(bf16[512,2048]{1,0:T(8,128)(2,1)S(1)} %get-tuple-element.270.grad_ref, bf16[512,256]{1,0:T(8,128)(2,1)S(1)} %get-tuple-element.271.grad_bc_ref, bf16[512,2048]{1,0:T(8,128)(2,1)S(1)} %copy-done.82, bf16[512,512]{1,0:T(8,128)(2,1)S(1)} %get-tuple-element.242.bc_ref.slope_bc_ref, ...), custom_call_target="tpu_custom_call" | custom-call | flops 10119999488 | bytes 65536 | tf_op jit(solution)/shard_map/pallas_call | solution.py:762
  216.9 4.0 %shard_map.225.part_ref = f32[512,1024]{1,0:T(8,128)S(1)} custom-call(bf16[512,2048]{1,0:T(8,128)(2,1)S(1)} %get-tuple-element.276.grad_ref.grad_gate_ref.refs_4_, s32[5]{0:T(128)S(1)} %copy-done.41, bf16[2048,256]{1,0:T(8,128)(2,1)} %get-tuple-element.248.rest_0_, bf16[2048,256]{1,0:T(8,128)(2,1)} %collective-permute-done.31.rest_1_, ...), custom_call_target="tpu_custom_call" | custom-call | flops 8049999872 | bytes 65536 | tf_op jit(solution)/shard_map/pallas_call | solution.py:675
  220.9 6.0 %shard_map.227.up_ref.refs_0_.up_stream_ref = bf16[512,1024]{1,0:T(8,128)(2,1)S(1)} custom-call(bf16[512,2304]{1,0:T(8,128)(2,1)S(1)} %shard_map.224.grad_ref.refs_2_, bf16[512,128]{1,0:T(8,128)(2,1)S(1)} %get-tuple-element.274.raw_ref.refs_3_, f32[512,1024]{1,0:T(8,128)S(1)} %shard_map.225.part_ref, bf16[512,1024]{1,0:T(8,128)(2,1)S(1)} %get-tuple-element.228.input_ref, ...), custom_call_target="tpu_custom_call" | custom-call | flops 10810000384 | bytes 65536 | tf_op jit(solution)/shard_map/pallas_call | solution.py:704
  231.3 11.6 %shard_map.230 = (bf16[512,2048]{1,0:T(8,128)(2,1)S(1)}, bf16[2048,512]{1,0:T(8,128)(2,1)S(1)}, bf16[512,128]{1,0:T(8,128)(2,1)S(1)}, bf16[2048,128]{1,0:T(8,128)(2,1)S(1)}, bf16[2048,128]{1,0:T(8,128)(2,1)S(1)}) custom-call(bf16[512,1024]{1,0:T(8,128)(2,1)S(1)} %shard_map.227.up_ref.refs_0_.up_stream_ref, f32[512,128]{1,0:T(8,128)S(1)} %copy-done.64, ...), custom_call_target="tpu_custom_call" | custom-call | flops 31050000384 | bytes 65536 | tf_op jit(solution)/shard_map/pallas_call | solution.py:648
  244.3 8.4 %shard_map.231 = (bf16[512,2048]{1,0:T(8,128)(2,1)S(1)}, bf16[512,256]{1,0:T(8,128)(2,1)S(1)}, bf16[512,128]{1,0:T(8,128)(2,1)S(1)}, bf16[8,2304]{1,0:T(8,128)(2,1)S(1)}) custom-call(bf16[2048,512]{1,0:T(8,128)(2,1)S(1)} %copy-done.84, bf16[2048,512]{1,0:T(8,128)(2,1)S(1)} %get-tuple-element.289.grad_ref, bf16[512,512]{1,0:T(8,128)(2,1)S(1)} %copy-done.88, ...), custom_call_target="tpu_custom_call" | custom-call | flops 19549999104 | bytes 65536 | tf_op jit(solution)/shard_map/pallas_call | solution.py:739
  256.0 3.3 collective-permute-start.47
  259.4 3.0 collective-permute-start.48
  262.4 8.5 %shard_map.232 = (bf16[512,2048]{1,0:T(8,128)(2,1)S(1)}, bf16[512,256]{1,0:T(8,128)(2,1)S(1)}, bf16[512,128]{1,0:T(8,128)(2,1)S(1)}) custom-call(bf16[2048,512]{1,0:T(8,128)(2,1)S(1)} %copy-done.84, bf16[2048,512]{1,0:T(8,128)(2,1)S(1)} %get-tuple-element.289.grad_ref, ...), custom_call_target="tpu_custom_call", output_to_operand_aliasing={{0}: (15, {}), {1}: (16, {}), {2}: (17, {})} | custom-call | flops 19549999104 | bytes 65536 | tf_op jit(solution)/shard_map/pallas_call | solution.py:739
  271.6 3.8 %collective-permute-start.52 = (bf16[272,128]{1,0:T(8,128)(2,1)S(1)}, bf16[272,128]{1,0:T(8,128)(2,1)S(1)}, u32[]{:S(2)}, u32[]{:S(2)}) collective-permute-start(bf16[272,128]{1,0:T(8,128)(2,1)S(1)} %get-tuple-element.333), channel_id=1, source_target_pairs={{0,8},{4,12},{8,0},{12,4},{1,9},{5,13},{9,1},{13,5},{2,10},{6,14},... | collective-permute-start | bytes 208904 | tf_op jit(solution)/shard_map/ppermute | solution.py:1009
  275.4 4.4 %shard_map.233.grad_ref.refs_2_ = bf16[512,2304]{1,0:T(8,128)(2,1)S(1)} custom-call(bf16[512,2048]{1,0:T(8,128)(2,1)S(1)} %get-tuple-element.297.grad_ref, bf16[512,256]{1,0:T(8,128)(2,1)S(1)} %get-tuple-element.298.grad_bc_ref, bf16[512,2048]{1,0:T(8,128)(2,1)S(1)} %copy-done.81, bf16[512,512]{1,0:T(8,128)(2,1)S(1)} %copy-done.88, ...), custom_call_target="tpu_custom_call" | custom-call | flops 10119999488 | bytes 65536 | tf_op jit(solution)/shard_map/pallas_call | solution.py:762
  290.2 3.4 collective-permute-done.56
  297.9 2.9 shard_map.237.part_ref
  300.9 4.8 %shard_map.238 = bf16[512,1024]{1,0:T(8,128)(2,1)S(1)} custom-call(bf16[512,2304]{1,0:T(8,128)(2,1)S(1)} %shard_map.233.grad_ref.refs_2_, bf16[512,128]{1,0:T(8,128)(2,1)S(1)} %get-tuple-element.305.raw_ref.refs_3_, f32[512,1024]{1,0:T(8,128)S(1)} %shard_map.237.part_ref, bf16[512,1024]{1,0:T(8,128)(2,1)S(1)} %copy-done.15, ...), custom_call_target="tpu_custom_call" | custom-call | flops 10810000384 | bytes 65536 | tf_op jit(solution)/shard_map/pallas_call | solution.py:704
  306.8 3.4 collective-permute-start.64
  312.4 4.4 %collective-permute-done.65 = bf16[272,128]{1,0:T(8,128)(2,1)S(1)} collective-permute-done((bf16[272,128]{1,0:T(8,128)(2,1)S(1)}, bf16[272,128]{1,0:T(8,128)(2,1)S(1)}, u32[]{:S(2)}, u32[]{:S(2)}) %collective-permute-start.65) | collective-permute-done | bytes 69664 | tf_op jit(solution)/shard_map/ppermute | solution.py:1009
  318.3 3.0 collective-permute-start.68
  330.0 4.2 %collective-permute-done.69 = bf16[1088,128]{1,0:T(8,128)(2,1)S(1)} collective-permute-done((bf16[1088,128]{1,0:T(8,128)(2,1)S(1)}, bf16[1088,128]{1,0:T(8,128)(2,1)S(1)}, u32[]{:S(2)}, u32[]{:S(2)}) %collective-permute-start.69) | collective-permute-done | bytes 278560 | tf_op jit(solution)/shard_map/ppermute | solution.py:1009
  334.2 4.3 %collective-permute-done.70 = bf16[1088,128]{1,0:T(8,128)(2,1)S(1)} collective-permute-done((bf16[1088,128]{1,0:T(8,128)(2,1)S(1)}, bf16[1088,128]{1,0:T(8,128)(2,1)S(1)}, u32[]{:S(2)}, u32[]{:S(2)}) %collective-permute-start.70) | collective-permute-done | bytes 278560 | tf_op jit(solution)/shard_map/ppermute | solution.py:1009
  338.8 2.7 collective-permute-done.72.refs_3_
  341.5 2.7 shard_map.239
  (417 shorter events, 91.8 us)
Async XLA Ops:
  9.2 17.7 %collective-permute-start.9 = (bf16[2336,256]{1,0:T(8,128)(2,1)S(1)}, bf16[2336,256]{1,0:T(8,128)(2,1)S(1)}, u32[]{:S(2)}, u32[]{:S(2)}) collective-permute-start(bf16[2336,256]{1,0:T(8,128)(2,1)S(1)} %get-tuple-element.193.rest_0_), channel_id=1, source_target_pairs={{0,1},{1,0},{2,3},{3,2},{16,18},{17,19},{18,16},{19,17},{4,5},{5,4... | collective-permute-start | bytes 3588104 | tf_op jit(solution)/shard_map/ppermute | solution.py:1027
  12.1 10.2 %collective-permute-start.5 = (f32[3,32]{1,0:T(4,128)S(1)}, f32[3,32]{1,0:T(4,128)S(1)}, u32[]{:S(2)}, u32[]{:S(2)}) collective-permute-start(f32[3,32]{1,0:T(4,128)S(1)} %pad_maximum_fusion), channel_id=1, source_target_pairs={{0,16},{16,0},{1,17},{17,1},{2,18},{18,2},{3,19},{19,3},{4,20},{20... | collective-permute-start | bytes 1160 | tf_op jit(solution)/shard_map/ppermute | solution.py:1004
  12.6 14.8 %collective-permute-start.8 = (f32[1,14592]{1,0:T(1,128)S(1)}, f32[1,14592]{1,0:T(1,128)S(1)}, u32[]{:S(2)}, u32[]{:S(2)}) collective-permute-start(f32[1,14592]{1,0:T(1,128)S(1)} %constant_dynamic-update-slice_fusion), channel_id=1, source_target_pairs={{0,16},{16,0},{1,17},{17,1},{2,18},{18,2},{3,19},{19,3},{4,20},{20... | collective-permute-start | bytes 175112 | tf_op jit(solution)/shard_map/ppermute | solution.py:1004
  12.9 12.0 %collective-permute-start.2 = (s32[1,128]{1,0:T(1,128)S(1)}, s32[1,128]{1,0:T(1,128)S(1)}, u32[]{:S(2)}, u32[]{:S(2)}) collective-permute-start(s32[1,128]{1,0:T(1,128)S(1)} %get-tuple-element.371), channel_id=1, source_target_pairs={{0,4},{4,8},{8,12},{1,5},{5,9},{9,13},{2,6},{6,10},{10,14},{3,7},{... | collective-permute-start | bytes 1544 | tf_op jit(solution)/shard_map/ppermute | solution.py:35
  24.1 13.5 %collective-permute-start.7 = (bf16[4384,128]{1,0:T(8,128)(2,1)S(1)}, bf16[4384,128]{1,0:T(8,128)(2,1)S(1)}, u32[]{:S(2)}, u32[]{:S(2)}) collective-permute-start(bf16[4384,128]{1,0:T(8,128)(2,1)S(1)} %bitcast.111), channel_id=1, source_target_pairs={{0,16},{16,0},{1,17},{17,1},{2,18},{18,2},{3,19},{19,3},{4,20},{20... | collective-permute-start | bytes 3366920 | tf_op jit(solution)/shard_map/ppermute | solution.py:1004
  25.5 42.0 %collective-permute-start.19 = (bf16[2048,128]{1,0:T(8,128)(2,1)S(1)}, bf16[2048,128]{1,0:T(8,128)(2,1)S(1)}, u32[]{:S(2)}, u32[]{:S(2)}) collective-permute-start(bf16[2048,128]{1,0:T(8,128)(2,1)S(1)} %bitcast.121), channel_id=1, source_target_pairs={{0,16},{16,0},{1,17},{17,1},{2,18},{18,2},{3,19},{19,3},{4,20},{20... | collective-permute-start | bytes 1572872 | tf_op jit(solution)/shard_map/ppermute | solution.py:1004
  26.9 24.5 %collective-permute-start.20 = (bf16[128,1024]{1,0:T(8,128)(2,1)S(1)}, bf16[128,1024]{1,0:T(8,128)(2,1)S(1)}, u32[]{:S(2)}, u32[]{:S(2)}) collective-permute-start(bf16[128,1024]{1,0:T(8,128)(2,1)S(1)} %bitcast.124), channel_id=1, source_target_pairs={{0,16},{16,0},{1,17},{17,1},{2,18},{18,2},{3,19},{19,3},{4,20},{20... | collective-permute-start | bytes 786440 | tf_op jit(solution)/shard_map/ppermute | solution.py:1004
  27.5 10.1 %collective-permute-start.11 = (bf16[1184,256]{1,0:T(8,128)(2,1)S(1)}, bf16[1184,256]{1,0:T(8,128)(2,1)S(1)}, u32[]{:S(2)}, u32[]{:S(2)}) collective-permute-start(bf16[1184,256]{1,0:T(8,128)(2,1)S(1)} %constant_dynamic-slice_fusion.23), channel_id=1, source_target_pairs={{0,2},{1,3},{2,0},{3,1},{16,17},{17,16},{18,19},{19,18},{4,6},{5,7... | collective-permute-start | bytes 1818632 | tf_op jit(solution)/shard_map/ppermute | solution.py:1027
  29.7 10.6 %collective-permute-start.10 = (bf16[2336,256]{1,0:T(8,128)(2,1)S(1)}, bf16[2336,256]{1,0:T(8,128)(2,1)S(1)}, u32[]{:S(2)}, u32[]{:S(2)}) collective-permute-start(bf16[2336,256]{1,0:T(8,128)(2,1)S(1)} %collective-permute-done.9.rest_1_), channel_id=1, source_target_pairs={{0,16},{16,0},{1,17},{17,1},{2,18},{18,2},{3,19},{19,3},{4,20},{20... | collective-permute-start | bytes 3588104 | tf_op jit(solution)/shard_map/ppermute | solution.py:1004
  37.6 14.9 %collective-permute-start.15 = (bf16[2048,256]{1,0:T(8,128)(2,1)S(1)}, bf16[2048,256]{1,0:T(8,128)(2,1)S(1)}, u32[]{:S(2)}, u32[]{:S(2)}) collective-permute-start(bf16[2048,256]{1,0:T(8,128)(2,1)S(1)} %get-tuple-element.213.rest_0_), channel_id=1, source_target_pairs={{0,1},{1,0},{2,3},{3,2},{16,18},{17,19},{18,16},{19,17},{4,5},{5,4... | collective-permute-start | bytes 3145736 | tf_op jit(solution)/shard_map/ppermute | solution.py:1027
  46.0 28.7 %collective-permute-start.21 = (bf16[512,1024]{1,0:T(8,128)(2,1)S(1)}, bf16[512,1024]{1,0:T(8,128)(2,1)S(1)}, u32[]{:S(2)}, u32[]{:S(2)}) collective-permute-start(bf16[512,1024]{1,0:T(8,128)(2,1)S(1)} %get-tuple-element.225.rest_0_), channel_id=1, source_target_pairs={{0,1},{1,0},{2,3},{3,2},{16,18},{17,19},{18,16},{19,17},{4,5},{5,4... | collective-permute-start | bytes 3145736 | tf_op jit(solution)/shard_map/ppermute | solution.py:1027
  52.5 24.0 %collective-permute-start.16 = (bf16[2048,256]{1,0:T(8,128)(2,1)S(1)}, bf16[2048,256]{1,0:T(8,128)(2,1)S(1)}, u32[]{:S(2)}, u32[]{:S(2)}) collective-permute-start(bf16[2048,256]{1,0:T(8,128)(2,1)S(1)} %collective-permute-done.15.rest_1_), channel_id=1, source_target_pairs={{0,16},{16,0},{1,17},{17,1},{2,18},{18,2},{3,19},{19,3},{4,20},{20... | collective-permute-start | bytes 3145736 | tf_op jit(solution)/shard_map/ppermute | solution.py:1004
  52.5 14.9 %collective-permute-start.17 = (bf16[1024,256]{1,0:T(8,128)(2,1)S(1)}, bf16[1024,256]{1,0:T(8,128)(2,1)S(1)}, u32[]{:S(2)}, u32[]{:S(2)}) collective-permute-start(bf16[1024,256]{1,0:T(8,128)(2,1)S(1)} %constant_dynamic-slice_fusion.22), channel_id=1, source_target_pairs={{0,2},{1,3},{2,0},{3,1},{16,17},{17,16},{18,19},{19,18},{4,6},{5,7... | collective-permute-start | bytes 1572872 | tf_op jit(solution)/shard_map/ppermute | solution.py:1027
  68.4 22.1 %collective-permute-start.25 = (bf16[2336,256]{1,0:T(8,128)(2,1)S(1)}, bf16[2336,256]{1,0:T(8,128)(2,1)}, u32[]{:S(2)}, u32[]{:S(2)}) collective-permute-start(bf16[2336,256]{1,0:T(8,128)(2,1)S(1)} %copy-done.2), channel_id=1, source_target_pairs={{0,1},{1,0},{2,3},{3,2},{16,18},{17,19},{18,16},{19,17},{4,5},{5,4... | collective-permute-start | bytes 3588104 | tf_op jit(solution)/shard_map/ppermute | solution.py:1027
  69.9 24.8 %collective-permute-start.14 = (bf16[2048,128]{1,0:T(8,128)(2,1)S(1)}, bf16[2048,128]{1,0:T(8,128)(2,1)S(1)}, u32[]{:S(2)}, u32[]{:S(2)}) collective-permute-start(bf16[2048,128]{1,0:T(8,128)(2,1)S(1)} %get-tuple-element.209), channel_id=1, source_target_pairs={{0,4},{4,8},{8,12},{1,5},{5,9},{9,13},{2,6},{6,10},{10,14},{3,7},{... | collective-permute-start | bytes 1572872 | tf_op jit(solution)/shard_map/ppermute | solution.py:35
  74.8 25.2 %collective-permute-start.22 = (bf16[512,1024]{1,0:T(8,128)(2,1)S(1)}, bf16[512,1024]{1,0:T(8,128)(2,1)S(1)}, u32[]{:S(2)}, u32[]{:S(2)}) collective-permute-start(bf16[512,1024]{1,0:T(8,128)(2,1)S(1)} %collective-permute-done.21.rest_1_), channel_id=1, source_target_pairs={{0,16},{16,0},{1,17},{17,1},{2,18},{18,2},{3,19},{19,3},{4,20},{20... | collective-permute-start | bytes 3145736 | tf_op jit(solution)/shard_map/ppermute | solution.py:1004
  74.9 18.2 %collective-permute-start.23 = (bf16[256,1024]{1,0:T(8,128)(2,1)S(1)}, bf16[256,1024]{1,0:T(8,128)(2,1)S(1)}, u32[]{:S(2)}, u32[]{:S(2)}) collective-permute-start(bf16[256,1024]{1,0:T(8,128)(2,1)S(1)} %constant_dynamic-slice_fusion.21), channel_id=1, source_target_pairs={{0,2},{1,3},{2,0},{3,1},{16,17},{17,16},{18,19},{19,18},{4,6},{5,7... | collective-permute-start | bytes 1572872 | tf_op jit(solution)/shard_map/ppermute | solution.py:1027
  90.5 21.6 %collective-permute-start.31 = (bf16[2048,256]{1,0:T(8,128)(2,1)}, bf16[2048,256]{1,0:T(8,128)(2,1)}, u32[]{:S(2)}, u32[]{:S(2)}) collective-permute-start(bf16[2048,256]{1,0:T(8,128)(2,1)} %get-tuple-element.248.rest_0_), channel_id=1, source_target_pairs={{0,1},{1,0},{2,3},{3,2},{16,18},{17,19},{18,16},{19,17},{4,5},{5,4... | collective-permute-start | bytes 3145736 | tf_op jit(solution)/shard_map/ppermute | solution.py:1027
  92.0 22.8 %collective-permute-start.26 = (bf16[2336,256]{1,0:T(8,128)(2,1)}, bf16[2336,256]{1,0:T(8,128)(2,1)}, u32[]{:S(2)}, u32[]{:S(2)}) collective-permute-start(bf16[2336,256]{1,0:T(8,128)(2,1)} %collective-permute-done.25.rest_1_), channel_id=1, source_target_pairs={{0,16},{16,0},{1,17},{17,1},{2,18},{18,2},{3,19},{19,3},{4,20},{20... | collective-permute-start | bytes 3588104 | tf_op jit(solution)/shard_map/ppermute | solution.py:1004
  93.1 16.8 %collective-permute-start.27 = (bf16[1184,256]{1,0:T(8,128)(2,1)S(1)}, bf16[1184,256]{1,0:T(8,128)(2,1)}, u32[]{:S(2)}, u32[]{:S(2)}) collective-permute-start(bf16[1184,256]{1,0:T(8,128)(2,1)S(1)} %constant_dynamic-slice_fusion.20), channel_id=1, source_target_pairs={{0,2},{1,3},{2,0},{3,1},{16,17},{17,16},{18,19},{19,18},{4,6},{5,7... | collective-permute-start | bytes 1818632 | tf_op jit(solution)/shard_map/ppermute | solution.py:1027
  109.9 44.8 %collective-permute-start.35 = (bf16[512,1024]{1,0:T(8,128)(2,1)S(1)}, bf16[512,1024]{1,0:T(8,128)(2,1)S(1)}, u32[]{:S(2)}, u32[]{:S(2)}) collective-permute-start(bf16[512,1024]{1,0:T(8,128)(2,1)S(1)} %copy-done.13), channel_id=1, source_target_pairs={{0,1},{1,0},{2,3},{3,2},{16,18},{17,19},{18,16},{19,17},{4,5},{5,4... | collective-permute-start | bytes 3145736 | tf_op jit(solution)/shard_map/ppermute | solution.py:1027
  112.1 43.5 %collective-permute-start.32 = (bf16[2048,256]{1,0:T(8,128)(2,1)}, bf16[2048,256]{1,0:T(8,128)(2,1)S(1)}, u32[]{:S(2)}, u32[]{:S(2)}) collective-permute-start(bf16[2048,256]{1,0:T(8,128)(2,1)} %collective-permute-done.31.rest_1_), channel_id=1, source_target_pairs={{0,16},{16,0},{1,17},{17,1},{2,18},{18,2},{3,19},{19,3},{4,20},{20... | collective-permute-start | bytes 3145736 | tf_op jit(solution)/shard_map/ppermute | solution.py:1004
  113.2 18.6 %collective-permute-start.33 = (bf16[1024,256]{1,0:T(8,128)(2,1)S(1)}, bf16[1024,256]{1,0:T(8,128)(2,1)S(1)}, u32[]{:S(2)}, u32[]{:S(2)}) collective-permute-start(bf16[1024,256]{1,0:T(8,128)(2,1)S(1)} %constant_dynamic-slice_fusion.19), channel_id=1, source_target_pairs={{0,2},{1,3},{2,0},{3,1},{16,17},{17,16},{18,19},{19,18},{4,6},{5,7... | collective-permute-start | bytes 1572872 | tf_op jit(solution)/shard_map/ppermute | solution.py:1027
  131.8 23.8 %collective-permute-start.34 = (bf16[1024,256]{1,0:T(8,128)(2,1)S(1)}, bf16[1024,256]{1,0:T(8,128)(2,1)S(1)}, u32[]{:S(2)}, u32[]{:S(2)}) collective-permute-start(bf16[1024,256]{1,0:T(8,128)(2,1)S(1)} %collective-permute-done.33.rest_3_), channel_id=1, source_target_pairs={{0,16},{16,0},{1,17},{17,1},{2,18},{18,2},{3,19},{19,3},{4,20},{20... | collective-permute-start | bytes 1572872 | tf_op jit(solution)/shard_map/ppermute | solution.py:1004
  141.4 24.4 %collective-permute-start.30 = (bf16[2048,128]{1,0:T(8,128)(2,1)S(1)}, bf16[2048,128]{1,0:T(8,128)(2,1)S(1)}, u32[]{:S(2)}, u32[]{:S(2)}) collective-permute-start(bf16[2048,128]{1,0:T(8,128)(2,1)S(1)} %get-tuple-element.244), channel_id=1, source_target_pairs={{0,4},{4,8},{8,12},{1,5},{5,9},{9,13},{2,6},{6,10},{10,14},{3,7},{... | collective-permute-start | bytes 1572872 | tf_op jit(solution)/shard_map/ppermute | solution.py:35
  154.8 15.5 %collective-permute-start.36 = (bf16[512,1024]{1,0:T(8,128)(2,1)S(1)}, bf16[512,1024]{1,0:T(8,128)(2,1)S(1)}, u32[]{:S(2)}, u32[]{:S(2)}) collective-permute-start(bf16[512,1024]{1,0:T(8,128)(2,1)S(1)} %collective-permute-done.35.rest_1_), channel_id=1, source_target_pairs={{0,16},{16,0},{1,17},{17,1},{2,18},{18,2},{3,19},{19,3},{4,20},{20... | collective-permute-start | bytes 3145736 | tf_op jit(solution)/shard_map/ppermute | solution.py:1004
  154.9 9.7 %collective-permute-start.37 = (bf16[256,1024]{1,0:T(8,128)(2,1)S(1)}, bf16[256,1024]{1,0:T(8,128)(2,1)S(1)}, u32[]{:S(2)}, u32[]{:S(2)}) collective-permute-start(bf16[256,1024]{1,0:T(8,128)(2,1)S(1)} %constant_dynamic-slice_fusion.18), channel_id=1, source_target_pairs={{0,2},{1,3},{2,0},{3,1},{16,17},{17,16},{18,19},{19,18},{4,6},{5,7... | collective-permute-start | bytes 1572872 | tf_op jit(solution)/shard_map/ppermute | solution.py:1027
  185.3 16.2 %collective-permute-start.40 = (bf16[2048,128]{1,0:T(8,128)(2,1)S(1)}, bf16[2048,128]{1,0:T(8,128)(2,1)S(1)}, u32[]{:S(2)}, u32[]{:S(2)}) collective-permute-start(bf16[2048,128]{1,0:T(8,128)(2,1)S(1)} %get-tuple-element.264), channel_id=1, source_target_pairs={{4,0},{8,4},{12,8},{5,1},{9,5},{13,9},{6,2},{10,6},{14,10},{7,3},{... | collective-permute-start | bytes 1572872 | tf_op jit(solution)/shard_map/ppermute | solution.py:35
  195.0 14.7 %collective-permute-start.41 = (bf16[8,2304]{1,0:T(8,128)(2,1)S(1)}, bf16[8,2304]{1,0:T(8,128)(2,1)S(1)}, u32[]{:S(2)}, u32[]{:S(2)}) collective-permute-start(bf16[8,2304]{1,0:T(8,128)(2,1)S(1)} %get-tuple-element.272), channel_id=1, source_target_pairs={{4,0},{8,4},{12,8},{5,1},{9,5},{13,9},{6,2},{10,6},{14,10},{7,3},{... | collective-permute-start | bytes 110600 | tf_op jit(solution)/shard_map/ppermute | solution.py:35
  196.6 30.3 %collective-permute-start.39 = (bf16[512,1024]{1,0:T(8,128)(2,1)S(1)}, bf16[512,1024]{1,0:T(8,128)(2,1)S(1)}, u32[]{:S(2)}, u32[]{:S(2)}) collective-permute-start(bf16[512,1024]{1,0:T(8,128)(2,1)S(1)} %broadcast_select_fusion.9), channel_id=1, source_target_pairs={{0,16},{16,0},{1,17},{17,1},{2,18},{18,2},{3,19},{19,3},{4,20},{20... | collective-permute-start | bytes 3145736 | tf_op jit(solution)/shard_map/ppermute | solution.py:1004
  216.8 10.4 %collective-permute-start.42 = (bf16[4352,128]{1,0:T(8,128)(2,1)S(1)}, bf16[4352,128]{1,0:T(8,128)(2,1)S(1)}, u32[]{:S(2)}, u32[]{:S(2)}) collective-permute-start(bf16[4352,128]{1,0:T(8,128)(2,1)S(1)} %constant_dynamic-slice_fusion.17), channel_id=1, source_target_pairs={{0,16},{16,0},{1,17},{17,1},{2,18},{18,2},{3,19},{19,3},{4,20},{20... | collective-permute-start | bytes 3342344 | tf_op jit(solution)/shard_map/ppermute | solution.py:1004
  227.6 28.1 %collective-permute-start.43 = (bf16[1088,128]{1,0:T(8,128)(2,1)S(1)}, bf16[1088,128]{1,0:T(8,128)(2,1)S(1)}, u32[]{:S(2)}, u32[]{:S(2)}) collective-permute-start(bf16[1088,128]{1,0:T(8,128)(2,1)S(1)} %get-tuple-element.354), channel_id=1, source_target_pairs={{0,1},{1,0},{2,3},{3,2},{4,5},{5,4},{6,7},{7,6},{8,9},{9,8},{10,11... | collective-permute-start | bytes 835592 | tf_op jit(solution)/shard_map/ppermute | solution.py:1009
  228.4 27.4 %collective-permute-start.44 = (bf16[1088,128]{1,0:T(8,128)(2,1)S(1)}, bf16[1088,128]{1,0:T(8,128)(2,1)S(1)}, u32[]{:S(2)}, u32[]{:S(2)}) collective-permute-start(bf16[1088,128]{1,0:T(8,128)(2,1)S(1)} %get-tuple-element.353), channel_id=1, source_target_pairs={{0,2},{1,3},{2,0},{3,1},{4,6},{5,7},{6,4},{7,5},{8,10},{9,11},{10,... | collective-permute-start | bytes 835592 | tf_op jit(solution)/shard_map/ppermute | solution.py:1009
  230.0 25.8 %collective-permute-start.45 = (bf16[1088,128]{1,0:T(8,128)(2,1)S(1)}, bf16[1088,128]{1,0:T(8,128)(2,1)S(1)}, u32[]{:S(2)}, u32[]{:S(2)}) collective-permute-start(bf16[1088,128]{1,0:T(8,128)(2,1)S(1)} %get-tuple-element.352), channel_id=1, source_target_pairs={{0,3},{1,2},{2,1},{3,0},{4,7},{5,6},{6,5},{7,4},{8,11},{9,10},{10,... | collective-permute-start | bytes 835592 | tf_op jit(solution)/shard_map/ppermute | solution.py:1009
  243.0 19.4 %collective-permute-start.46 = (bf16[2048,128]{1,0:T(8,128)(2,1)S(1)}, bf16[2048,128]{1,0:T(8,128)(2,1)S(1)}, u32[]{:S(2)}, u32[]{:S(2)}) collective-permute-start(bf16[2048,128]{1,0:T(8,128)(2,1)S(1)} %get-tuple-element.290), channel_id=1, source_target_pairs={{4,0},{8,4},{12,8},{5,1},{9,5},{13,9},{6,2},{10,6},{14,10},{7,3},{... | collective-permute-start | bytes 1572872 | tf_op jit(solution)/shard_map/ppermute | solution.py:35
  252.7 22.7 %collective-permute-start.50 = (bf16[8,2304]{1,0:T(8,128)(2,1)S(1)}, bf16[8,2304]{1,0:T(8,128)(2,1)S(1)}, u32[]{:S(2)}, u32[]{:S(2)}) collective-permute-start(bf16[8,2304]{1,0:T(8,128)(2,1)S(1)} %get-tuple-element.299), channel_id=1, source_target_pairs={{4,0},{8,4},{12,8},{5,1},{9,5},{13,9},{6,2},{10,6},{14,10},{7,3},{... | collective-permute-start | bytes 110600 | tf_op jit(solution)/shard_map/ppermute | solution.py:35
  256.0 14.8 %collective-permute-start.47 = (bf16[272,128]{1,0:T(8,128)(2,1)S(1)}, bf16[272,128]{1,0:T(8,128)(2,1)S(1)}, u32[]{:S(2)}, u32[]{:S(2)}) collective-permute-start(bf16[272,128]{1,0:T(8,128)(2,1)S(1)} %get-tuple-element.366), channel_id=1, source_target_pairs={{0,4},{4,0},{8,12},{12,8},{1,5},{5,1},{9,13},{13,9},{2,6},{6,2},{1... | collective-permute-start | bytes 208904 | tf_op jit(solution)/shard_map/ppermute | solution.py:1009
  259.4 11.5 %collective-permute-start.48 = (bf16[272,128]{1,0:T(8,128)(2,1)S(1)}, bf16[272,128]{1,0:T(8,128)(2,1)S(1)}, u32[]{:S(2)}, u32[]{:S(2)}) collective-permute-start(bf16[272,128]{1,0:T(8,128)(2,1)S(1)} %get-tuple-element.365), channel_id=1, source_target_pairs={{0,8},{4,12},{8,0},{12,4},{1,9},{5,13},{9,1},{13,5},{2,10},{6,14},... | collective-permute-start | bytes 208904 | tf_op jit(solution)/shard_map/ppermute | solution.py:1009
  282.4 11.3 %collective-permute-start.56 = (bf16[1088,128]{1,0:T(8,128)(2,1)S(1)}, bf16[1088,128]{1,0:T(8,128)(2,1)S(1)}, u32[]{:S(2)}, u32[]{:S(2)}) collective-permute-start(bf16[1088,128]{1,0:T(8,128)(2,1)S(1)} %bitcast.117), channel_id=1, source_target_pairs={{0,2},{1,3},{2,0},{3,1},{4,6},{5,7},{6,4},{7,5},{8,10},{9,11},{10,... | collective-permute-start | bytes 835592 | tf_op jit(solution)/shard_map/ppermute | solution.py:1009
  283.9 9.7 %collective-permute-start.57 = (bf16[1088,128]{1,0:T(8,128)(2,1)S(1)}, bf16[1088,128]{1,0:T(8,128)(2,1)S(1)}, u32[]{:S(2)}, u32[]{:S(2)}) collective-permute-start(bf16[1088,128]{1,0:T(8,128)(2,1)S(1)} %bitcast.118), channel_id=1, source_target_pairs={{0,3},{1,2},{2,1},{3,0},{4,7},{5,6},{6,5},{7,4},{8,11},{9,10},{10,... | collective-permute-start | bytes 835592 | tf_op jit(solution)/shard_map/ppermute | solution.py:1009
  294.2 11.4 %collective-permute-start.60 = (bf16[1088,128]{1,0:T(8,128)(2,1)S(1)}, bf16[1088,128]{1,0:T(8,128)(2,1)S(1)}, u32[]{:S(2)}, u32[]{:S(2)}) collective-permute-start(bf16[1088,128]{1,0:T(8,128)(2,1)S(1)} %get-tuple-element.350), channel_id=1, source_target_pairs={{0,1},{1,0},{2,3},{3,2},{4,5},{5,4},{6,7},{7,6},{8,9},{9,8},{10,11... | collective-permute-start | bytes 835592 | tf_op jit(solution)/shard_map/ppermute | solution.py:1009
  295.7 10.5 %collective-permute-start.61 = (bf16[1088,128]{1,0:T(8,128)(2,1)S(1)}, bf16[1088,128]{1,0:T(8,128)(2,1)S(1)}, u32[]{:S(2)}, u32[]{:S(2)}) collective-permute-start(bf16[1088,128]{1,0:T(8,128)(2,1)S(1)} %get-tuple-element.349), channel_id=1, source_target_pairs={{0,2},{1,3},{2,0},{3,1},{4,6},{5,7},{6,4},{7,5},{8,10},{9,11},{10,... | collective-permute-start | bytes 835592 | tf_op jit(solution)/shard_map/ppermute | solution.py:1009
  296.4 9.9 %collective-permute-start.62 = (bf16[1088,128]{1,0:T(8,128)(2,1)S(1)}, bf16[1088,128]{1,0:T(8,128)(2,1)S(1)}, u32[]{:S(2)}, u32[]{:S(2)}) collective-permute-start(bf16[1088,128]{1,0:T(8,128)(2,1)S(1)} %get-tuple-element.348), channel_id=1, source_target_pairs={{0,3},{1,2},{2,1},{3,0},{4,7},{5,6},{6,5},{7,4},{8,11},{9,10},{10,... | collective-permute-start | bytes 835592 | tf_op jit(solution)/shard_map/ppermute | solution.py:1009
  311.0 17.3 %collective-permute-start.58 = (bf16[512,1024]{1,0:T(8,128)(2,1)S(1)}, bf16[512,1024]{1,0:T(8,128)(2,1)S(1)}, u32[]{:S(2)}, u32[]{:S(2)}) collective-permute-start(bf16[512,1024]{1,0:T(8,128)(2,1)S(1)} %broadcast_select_fusion.7), channel_id=1, source_target_pairs={{0,16},{16,0},{1,17},{17,1},{2,18},{18,2},{3,19},{19,3},{4,20},{20... | collective-permute-start | bytes 3145736 | tf_op jit(solution)/shard_map/ppermute | solution.py:1004
  322.9 15.9 %collective-permute-start.59 = (bf16[4352,128]{1,0:T(8,128)(2,1)S(1)}, bf16[4352,128]{1,0:T(8,128)(2,1)S(1)}, u32[]{:S(2)}, u32[]{:S(2)}) collective-permute-start(bf16[4352,128]{1,0:T(8,128)(2,1)S(1)} %bitcast.104), channel_id=1, source_target_pairs={{0,16},{16,0},{1,17},{17,1},{2,18},{18,2},{3,19},{19,3},{4,20},{20... | collective-permute-start | bytes 3342344 | tf_op jit(solution)/shard_map/ppermute | solution.py:1004
  324.6 9.7 %collective-permute-start.69 = (bf16[1088,128]{1,0:T(8,128)(2,1)S(1)}, bf16[1088,128]{1,0:T(8,128)(2,1)S(1)}, u32[]{:S(2)}, u32[]{:S(2)}) collective-permute-start(bf16[1088,128]{1,0:T(8,128)(2,1)S(1)} %bitcast.112), channel_id=1, source_target_pairs={{0,1},{1,0},{2,3},{3,2},{4,5},{5,4},{6,7},{7,6},{8,9},{9,8},{10,11... | collective-permute-start | bytes 835592 | tf_op jit(solution)/shard_map/ppermute | solution.py:1009
  326.0 12.6 %collective-permute-start.70 = (bf16[1088,128]{1,0:T(8,128)(2,1)S(1)}, bf16[1088,128]{1,0:T(8,128)(2,1)S(1)}, u32[]{:S(2)}, u32[]{:S(2)}) collective-permute-start(bf16[1088,128]{1,0:T(8,128)(2,1)S(1)} %bitcast.113), channel_id=1, source_target_pairs={{0,2},{1,3},{2,0},{3,1},{4,6},{5,7},{6,4},{7,5},{8,10},{9,11},{10,... | collective-permute-start | bytes 835592 | tf_op jit(solution)/shard_map/ppermute | solution.py:1009
  326.7 11.8 %collective-permute-start.71 = (bf16[1088,128]{1,0:T(8,128)(2,1)S(1)}, bf16[1088,128]{1,0:T(8,128)(2,1)S(1)}, u32[]{:S(2)}, u32[]{:S(2)}) collective-permute-start(bf16[1088,128]{1,0:T(8,128)(2,1)S(1)} %bitcast.114), channel_id=1, source_target_pairs={{0,3},{1,2},{2,1},{3,0},{4,7},{5,6},{6,5},{7,4},{8,11},{9,10},{10,... | collective-permute-start | bytes 835592 | tf_op jit(solution)/shard_map/ppermute | solution.py:1009
  (133 other events, 1606.7 us)
